TPU v7x, 32 devices: a whole 2x2x4 slice. The times are simulated.
32 devices in a mesh: groups: 2 (over x), vocab: 16 (over z, y, core).
Axes of the slice: x: 2, y: 2, z: 4, core: 2. Of those that a mesh axis runs over, the one named last changes fastest.
Arguments:
- initial_residual_vector: bfloat16 [64, 5376], P(('groups', 'vocab')), parts along dimension 0, may hold values from -50 to 50
- later_layer_deltas: bfloat16 [64, 5376], P(('groups', 'vocab')), parts along dimension 0, may hold values from -400 to 400
- closing_rescale_weight: float32 [5376], replicated, may hold values from 0.5 to 1.5
- shared_lexicon_matrix: bfloat16 [16384, 5376], P('vocab'), may hold values from -3 to 3
- class_heat_lookup: float32 [8], replicated, may hold values from 0.3 to 2
- heat_class: int32 [2, 64], P(None, 'groups'), parts along dimension 1, may hold values from 0 to 7
- drawn_identifiers: int32 [2, 64], P(None, 'groups'), parts along dimension 1, may hold values from 0 to 16383
Outputs:
- logprobs: float32 [2, 64, 16384], P(None, 'groups', 'vocab'), parts along dimension 1
- next_embedded: bfloat16 [64, 5376], P(('groups', 'vocab')), parts along dimension 0
There are 2 independent parts, one for each index of `groups`. A program takes and returns all parts, laid end to end along the dimension named above; an argument that names none is the same for every part. Nothing has to cross between parts.
All inputs are finite; a program needn't handle non-finite values.
Results may differ from a plain program's by a relative error of at most 0.0012.
Values may be sent and summed in bfloat16 or wider, within the bound.
No kernel may reach another device: no remote copies, remote signals or barrier semaphores. Data moves between devices by JAX's collectives and lax.ppermute only.
A program may use at most 64 MiB of HBM per device.

v0:
```python
import math

import jax
import jax.numpy as jnp
from jax import lax
from jax.sharding import PartitionSpec as P


def quadratic_rescaled(hidden, closing_rescale_weight):
    squares = jnp.mean(hidden * hidden, axis=-1, keepdims=True)
    return (hidden * lax.rsqrt(squares + 1e-06) * closing_rescale_weight).astype(jnp.bfloat16)


def sequence_heat_factors(class_for_sequence, class_heat_lookup):
    check_agreement = (
        class_for_sequence[:, None]
        == jnp.arange(class_heat_lookup.shape[0], dtype=jnp.int32)[None, :]
    )
    return jnp.sum(
        jnp.where(
            check_agreement, class_heat_lookup[None, :], jnp.zeros_like(class_heat_lookup)[None, :]
        ),
        axis=1,
    )


def logarithmic_likelihood(normed_rows, shared_lexicon_matrix, row_temps):
    logits = lax.dot_general(
        lax.all_gather(normed_rows, "vocab", axis=0, tiled=True),
        shared_lexicon_matrix,
        (((1,), (1,)), ((), ())),
        preferred_element_type=jnp.float32,
    )
    scaled = logits / row_temps[:, None]
    local_peak = jnp.max(scaled, axis=1)
    peak = lax.pmax(local_peak, "vocab")
    total = lax.psum(jnp.sum(jnp.exp(scaled - peak[:, None]), axis=1), "vocab")
    return scaled - peak[:, None] - jnp.log(total)[:, None]


def fetched(token_ids, shared_lexicon_matrix):
    voc_dev = shared_lexicon_matrix.shape[0]
    width = shared_lexicon_matrix.shape[1]
    shards = lax.axis_size("vocab")
    rows_dev = token_ids.shape[0] // shards
    offset = lax.axis_index("vocab") * voc_dev
    local_ids = token_ids - offset
    owned = (local_ids >= 0) & (local_ids < voc_dev)
    picked = jnp.take(shared_lexicon_matrix, jnp.clip(local_ids, 0, voc_dev - 1), axis=0)
    picked = jnp.where(owned[:, None], picked, jnp.zeros_like(picked)).reshape(
        shards, rows_dev, width
    )
    arrived = lax.all_to_all(picked, "vocab", split_axis=0, concat_axis=0, tiled=True)
    gathered = jnp.sum(arrived.astype(jnp.float32), axis=0)
    return (gathered * math.sqrt(width)).astype(jnp.bfloat16)


def body(
    initial_residual_vector,
    later_layer_deltas,
    closing_rescale_weight,
    shared_lexicon_matrix,
    class_heat_lookup,
    heat_class,
    drawn_identifiers,
):
    opening_draw = logarithmic_likelihood(
        quadratic_rescaled(initial_residual_vector.astype(jnp.float32), closing_rescale_weight),
        shared_lexicon_matrix,
        sequence_heat_factors(heat_class[0], class_heat_lookup),
    )
    input_two = fetched(drawn_identifiers[0], shared_lexicon_matrix)
    later_residual_vector = input_two.astype(jnp.float32) + later_layer_deltas.astype(jnp.float32)
    subsequent_draw = logarithmic_likelihood(
        quadratic_rescaled(later_residual_vector, closing_rescale_weight),
        shared_lexicon_matrix,
        sequence_heat_factors(heat_class[1], class_heat_lookup),
    )
    return (
        jnp.stack([opening_draw, subsequent_draw]),
        fetched(drawn_identifiers[1], shared_lexicon_matrix),
    )


def solution(mesh):
    in_specs = (
        P(("groups", "vocab"), None),
        P(("groups", "vocab"), None),
        P(),
        P("vocab", None),
        P(),
        P(None, "groups"),
        P(None, "groups"),
    )
    out_specs = (P(None, "groups", "vocab"), P(("groups", "vocab"), None))
    return jax.shard_map(body, mesh=mesh, in_specs=in_specs, out_specs=out_specs, check_vma=False)
```

profile of v0, /device:TPU:0, one launch (start us, length us, event | category | flops | bytes accessed | tf_op | source)
XLA Modules:
  0.0 154.6 jit_solution(5731276404816652246)
XLA Ops:
  0.6 0.8 and_bitcast_fusion
  1.4 0.8 compare_and_fusion
  2.2 6.6 %gather_fusion = bf16[32,5376]{1,0:T(8,128)(2,1)S(1)} fusion(bf16[1024,5376]{1,0:T(8,128)(2,1)} %param.12, s32[1024]{0:T(1024)S(1)} %pad_clamp_fusion.1), kind=kCustom, calls=%fused_computation.clone | custom fusion | bytes 688256 | tf_op jit(solution)/shard_map/jit(_take)/gather | solution.py:49
  8.8 0.1 select_select_fusion.1
  8.9 0.8 reshape.77
  9.8 7.4 %all-to-all-start = ((bf16[16,2,5376]{2,1,0:T(2,128)(2,1)}), bf16[16,2,5376]{2,1,0:T(2,128)(2,1)S(1)}, u32[]{:S(2)}, u32[]{:S(2)}) async-start(bf16[16,2,5376]{2,1,0:T(2,128)(2,1)} %reshape.77), calls=%async_computation | async-start | bytes 688128 | tf_op jit(solution)/shard_map/all_to_all | solution.py:53
  17.2 6.6 %gather_fusion.1 = bf16[32,5376]{1,0:T(8,128)(2,1)S(1)} fusion(bf16[1024,5376]{1,0:T(8,128)(2,1)} %param.12, s32[1024]{0:T(1024)S(1)} %pad_clamp_fusion), kind=kCustom, calls=%fused_computation.1.clone | custom fusion | bytes 688256 | tf_op jit(solution)/shard_map/jit(_take)/gather | solution.py:49
  23.8 0.1 select_select_fusion
  23.9 0.9 reshape.78
  24.8 0.8 slice_bitcast_fusion
  25.6 0.7 select_reduce_fusion.1
  26.3 0.9 fusion
  27.2 1.3 all-to-all-done
  28.5 4.7 %all-to-all-start.1 = ((bf16[16,2,5376]{2,1,0:T(2,128)(2,1)}), bf16[16,2,5376]{2,1,0:T(2,128)(2,1)S(1)}, u32[]{:S(2)}, u32[]{:S(2)}) async-start(bf16[16,2,5376]{2,1,0:T(2,128)(2,1)} %reshape.78), calls=%async_computation.1 | async-start | bytes 688128 | tf_op jit(solution)/shard_map/all_to_all | solution.py:53
  33.2 0.3 convert_reduce_fusion.1
  33.5 0.9 multiply_reduce_fusion
  34.4 0.9 fusion.3
  35.3 22.8 %all-gather = bf16[16,2,5376]{2,1,0:T(2,128)(2,1)S(1)} all-gather(bf16[1,2,5376]{2,1,0:T(2,128)(2,1)S(1)} %get-tuple-element.13), channel_id=1, replica_groups=mesh['groups'=2,'vocab'=16] {'vocab'}, dimensions={0}, use_global_device_ids=true | all-gather | bytes 365568 | tf_op jit(solution)/shard_map/all_gather | solution.py:29
  58.0 0.1 reshape.98
  58.2 0.0 all-to-all-done.1
  58.2 0.3 convert_reduce_fusion
  58.5 0.6 multiply_convert_fusion
  59.1 18.4 %all-gather.1 = bf16[16,2,5376]{2,1,0:T(2,128)(2,1)S(1)} all-gather(bf16[1,2,5376]{2,1,0:T(2,128)(2,1)S(1)} %get-tuple-element.14), channel_id=1, replica_groups=mesh['groups'=2,'vocab'=16] {'vocab'}, dimensions={0}, use_global_device_ids=true | all-gather | bytes 365568 | tf_op jit(solution)/shard_map/all_gather | solution.py:29
  77.5 0.1 reshape.100
  77.6 7.5 %fusion.6 = (f32[32]{0:T(128)S(1)}, f32[32,1024]{1,0:T(8,128)S(1)}) fusion(f32[32]{0:T(128)S(1)} %get-tuple-element.3, bf16[32,5376]{1,0:T(8,128)(2,1)S(1)} %reshape.98, bf16[1024,5376]{1,0:T(8,128)(2,1)} %param.12), kind=kOutput, calls=%fused_computation.44 | convolution fusion | flops 352387040 | bytes 11485440 | tf_op jit(solution)/shard_map/dot_general | solution.py:28
  85.1 7.5 %fusion.5 = (f32[32]{0:T(128)S(1)}, f32[32,1024]{1,0:T(8,128)S(1)}) fusion(f32[32]{0:T(128)S(1)} %get-tuple-element.4, bf16[32,5376]{1,0:T(8,128)(2,1)S(1)} %reshape.100, bf16[1024,5376]{1,0:T(8,128)(2,1)} %param.12), kind=kOutput, calls=%fused_computation.43 | convolution fusion | flops 352387040 | bytes 11485440 | tf_op jit(solution)/shard_map/dot_general | solution.py:28
  92.7 31.2 %all-reduce.1 = (f32[32]{0:T(128)S(1)}, f32[32]{0:T(128)S(1)}) all-reduce(f32[32]{0:T(128)S(1)} %get-tuple-element.21, f32[32]{0:T(128)S(1)} %get-tuple-element.23), channel_id=1, replica_groups=mesh['groups'=2,'vocab'=16] {'vocab'}, use_global_device_ids=true, to_apply=%region_10.12 | all-reduce | flops 64 | bytes 512 | tf_op jit(solution)/shard_map/pmax | solution.py:36
  123.9 0.2 exponential_reduce_fusion
  124.1 0.2 exponential_reduce_fusion.1
  124.3 29.5 %all-reduce = (f32[32]{0:T(128)S(1)}, f32[32]{0:T(128)S(1)}) all-reduce(f32[32]{0:T(128)S(1)} %exponential_reduce_fusion, f32[32]{0:T(128)S(1)} %exponential_reduce_fusion.1), channel_id=1, replica_groups=mesh['groups'=2,'vocab'=16] {'vocab'}, use_global_device_ids=true, to_apply=%region_12.14 | all-reduce | flops 64 | bytes 512 | tf_op jit(solution)/shard_map/psum | solution.py:37
  153.8 0.1 subtract_bitcast_fusion
  153.9 0.7 pad_maximum_fusion
  (6 shorter events, 0.0 us)
Async XLA Ops:
  9.8 18.8 %all-to-all-start = ((bf16[16,2,5376]{2,1,0:T(2,128)(2,1)}), bf16[16,2,5376]{2,1,0:T(2,128)(2,1)S(1)}, u32[]{:S(2)}, u32[]{:S(2)}) async-start(bf16[16,2,5376]{2,1,0:T(2,128)(2,1)} %reshape.77), calls=%async_computation | async-start | bytes 688128 | tf_op jit(solution)/shard_map/all_to_all | solution.py:53
  28.5 29.6 %all-to-all-start.1 = ((bf16[16,2,5376]{2,1,0:T(2,128)(2,1)}), bf16[16,2,5376]{2,1,0:T(2,128)(2,1)S(1)}, u32[]{:S(2)}, u32[]{:S(2)}) async-start(bf16[16,2,5376]{2,1,0:T(2,128)(2,1)} %reshape.78), calls=%async_computation.1 | async-start | bytes 688128 | tf_op jit(solution)/shard_map/all_to_all | solution.py:53
where the time goes:
time: 155 us
  blocking collectives  102 us (66%)
  local copies, waits for them, and re-layouts  16 us (10%)
  matrix products  15.1 us (10%)
  starting transfers between devices  12.1 us (8%)
  other arithmetic  7.6 us (5%)
    all_gather x2, blocking collectives, logarithmic_likelihood(): lax.all_gather(normed_rows, 'vocab', axis=0, tiled=True)  41.1 us
    pmax x1, blocking collectives, logarithmic_likelihood(): peak = lax.pmax(local_peak, 'vocab')  31.2 us
    psum x1, blocking collectives, logarithmic_likelihood(): total = lax.psum(jnp.sum(jnp.exp(scaled - peak[:, None]), axis=1), 'vocab')  29.5 us
    dot_general x2, matrix products, logarithmic_likelihood(): lax.dot_general(lax.all_gather(normed_rows, 'vocab', axis=0, tiled=True),...  15.1 us
    gather x2, local copies, waits for them, and re-layouts, fetched(): jnp.take(shared_lexicon_matrix, jnp.clip(local_ids, 0, voc_dev - 1), axis=0)  13.3 us
    all_to_all x2, starting transfers between devices, fetched(): lax.all_to_all(picked, 'vocab', split_axis=0, concat_axis=0, tiled=True)  12.1 us
  transfers between devices with their start and end apart: 2, of which 1 were waited for; matrix products, arithmetic and copies ran while one was open for 8% of the time, Pallas kernels for 0%

commit v1 on v0

v1 whole, which is shorter than its diff:
```python
import functools
import math

import jax
import jax.numpy as jnp
from jax import lax
from jax.experimental import pallas as pl
from jax.experimental.pallas import tpu as pltpu
from jax.sharding import PartitionSpec as P

BLOCK = 16


def gather_kernel(step, ids_ref, table_ref, keep_ref, send_ref, slots, rows, sems):
    count = ids_ref.shape[1]
    half = count // 2
    voc_dev = table_ref.shape[0]
    shards = lax.axis_size("vocab")
    rows_dev = count // shards
    me = lax.axis_index("vocab")
    offset = me * voc_dev

    def copy(r, local):
        base = pl.multiple_of(local // BLOCK * BLOCK, BLOCK)
        return pltpu.make_async_copy(table_ref.at[pl.ds(base, BLOCK)], slots.at[r], sems.at[r])

    for r in range(count):
        local = ids_ref[step, r] - offset

        @pl.when((local >= 0) & (local < voc_dev))
        def _(r=r, local=local):
            copy(r, local).start()

    rows[...] = jnp.zeros_like(rows)
    for r in range(count):
        local = ids_ref[step, r] - offset

        @pl.when((local >= 0) & (local < voc_dev))
        def _(r=r, local=local):
            copy(r, local).wait()
            block = slots[r].astype(jnp.float32)
            lane = lax.broadcasted_iota(jnp.int32, block.shape, 0)
            picked = jnp.sum(jnp.where(lane == local % BLOCK, block, 0.0), axis=0, keepdims=True)
            way = (r // rows_dev) ^ me
            place = (way % 2 * 2 + way // 2 % 2) * (shards // 4) + way // 4
            rows[pl.ds(place * rows_dev + r % rows_dev, 1), :] = picked

    keep_ref[...] = rows[:half].astype(keep_ref.dtype)
    send_ref[...] = rows[half:].astype(send_ref.dtype)


def gathered(ids, table, step):
    count = ids.shape[1]
    width = table.shape[1]
    out = jax.ShapeDtypeStruct((count // 2, width), table.dtype)
    return pl.pallas_call(
        functools.partial(gather_kernel, step),
        out_shape=(out, out),
        in_specs=[pl.BlockSpec(memory_space=pltpu.SMEM), pl.BlockSpec(memory_space=pl.ANY)],
        out_specs=(pl.BlockSpec(memory_space=pltpu.VMEM),) * 2,
        scratch_shapes=[
            pltpu.VMEM((count, BLOCK, width), table.dtype),
            pltpu.VMEM((count, width), jnp.float32),
            pltpu.SemaphoreType.DMA((count,)),
        ],
        compiler_params=pltpu.CompilerParams(vmem_limit_bytes=48 * 2**20),
        name="pick_rows",
    )(ids, table)


def swapped(bit):
    pairs = [(i, i ^ bit) for i in range(lax.axis_size("vocab"))]
    return lambda x: lax.ppermute(x, "vocab", pairs)


def crossed(rows, bit, rows_dev):
    blocks = rows.shape[0] // rows_dev
    parts = rows.reshape(blocks // (2 * bit), 2, bit * rows_dev, rows.shape[1])
    return parts[:, ::-1].reshape(rows.shape)


def norm_kernel(first_ref, picked_ref, delta_ref, gain_ref, out_ref):
    width = first_ref.shape[1]
    quarter = first_ref.shape[0]
    gain = gain_ref[...]

    def rescaled(hidden):
        squares = jnp.mean(hidden * hidden, axis=-1, keepdims=True)
        return hidden * lax.rsqrt(squares + 1e-06) * gain

    one = rescaled(first_ref[...].astype(jnp.float32))
    embedded = (picked_ref[...].astype(jnp.float32) * math.sqrt(width)).astype(jnp.bfloat16)
    two = rescaled(embedded.astype(jnp.float32) + delta_ref[...].astype(jnp.float32))
    out_ref[...] = jnp.concatenate([one, two], axis=0).astype(out_ref.dtype)


def normed(first, picked, delta, gain):
    rows, width = first.shape
    return pl.pallas_call(
        norm_kernel,
        out_shape=jax.ShapeDtypeStruct((2 * rows, width), jnp.bfloat16),
        compiler_params=pltpu.CompilerParams(vmem_limit_bytes=32 * 2**20),
        name="norm",
    )(first, picked, delta, gain.reshape(1, width))


def head_kernel(own_ref, got_ref, table_ref, temps_ref, out_ref, peak_ref, total_ref):
    i = pl.program_id(0)
    rows = out_ref.shape[1]
    shards = lax.axis_size("vocab")
    rows_dev = rows // shards
    quarter = rows // 4
    me = lax.axis_index("vocab")
    dims = (((1,), (1,)), ((), ()))
    states = jnp.concatenate([own_ref[...], got_ref[...]], axis=0)
    logits = lax.dot_general(states, table_ref[...], dims, preferred_element_type=jnp.float32)
    for c in range(2):
        for y in range(2):
            for step in range(2):
                for z in range(shards // 4):
                    place = ((c * 2 + y) * 2 + step) * quarter + z * rows_dev
                    row = ((z * 4 + y * 2 + c) ^ me) * rows_dev
                    for j in range(rows_dev):
                        out_ref[step, pl.ds(row + j, 1), :] = logits[place + j : place + j + 1]
    scaled = out_ref[...] / temps_ref[...]
    out_ref[...] = scaled
    top = jnp.max(scaled, axis=2, keepdims=True)

    @pl.when(i == 0)
    def _():
        peak_ref[...] = jnp.full_like(peak_ref, -jnp.inf)
        total_ref[...] = jnp.zeros_like(total_ref)

    before = peak_ref[...]
    peak = jnp.maximum(before, top)
    total_ref[...] = total_ref[...] * jnp.exp(before - peak) + jnp.sum(
        jnp.exp(scaled - peak), axis=2, keepdims=True
    )
    peak_ref[...] = peak


def head(own, got, table, temps):
    steps, rows = temps.shape[:2]
    voc_dev, width = table.shape
    tile = min(256, voc_dev)
    stat = jax.ShapeDtypeStruct((steps, rows, 1), jnp.float32)
    stat_spec = pl.BlockSpec((steps, rows, 1), lambda i: (0, 0, 0))
    return pl.pallas_call(
        head_kernel,
        grid=(voc_dev // tile,),
        out_shape=(jax.ShapeDtypeStruct((steps, rows, voc_dev), jnp.float32), stat, stat),
        in_specs=[
            pl.BlockSpec(own.shape, lambda i: (0, 0)),
            pl.BlockSpec(got.shape, lambda i: (0, 0)),
            pl.BlockSpec((tile, width), lambda i: (i, 0)),
            stat_spec,
        ],
        out_specs=(
            pl.BlockSpec((steps, rows, tile), lambda i: (0, 0, i)),
            stat_spec,
            stat_spec,
        ),
        compiler_params=pltpu.CompilerParams(vmem_limit_bytes=32 * 2**20),
        name="head",
    )(own, got, table, temps)


def row_temps(classes, lookup):
    levels = jnp.arange(lookup.shape[0], dtype=jnp.int32)
    return jnp.sum(jnp.where(classes[..., None] == levels, lookup, 0.0), axis=-1)


def body(first, deltas, gain, table, lookup, classes, ids):
    shards = lax.axis_size("vocab")
    rows_dev, width = first.shape
    high = [1 << k for k in range(shards.bit_length() - 2, 1, -1)]
    core, chip = swapped(1), swapped(2)

    keep, send = gathered(ids, table, 0)
    keep = keep + core(send)
    quarter = keep.shape[0] // 2
    picked = keep[:quarter] + chip(keep[quarter:])
    for bit in high:
        parcel = jnp.concatenate([picked, first, deltas], axis=0)
        got = swapped(bit)(parcel)
        cut = quarter + first.shape[0]
        picked = picked + crossed(got[:quarter], bit // 4, rows_dev)
        first = jnp.concatenate([first, got[quarter:cut]], axis=0)
        deltas = jnp.concatenate([deltas, got[cut:]], axis=0)
    order = (len(high), rows_dev, width)
    first = ordered(first, len(high), rows_dev)
    deltas = ordered(deltas, len(high), rows_dev)
    states = normed(first, picked, deltas, gain)
    states = jnp.concatenate([states, chip(states)], axis=0)
    others = core(states)
    temps = row_temps(classes, lookup)[..., None]
    scaled, peak, total = head(states, others, table, temps)

    stats = jnp.stack([peak[..., 0], total[..., 0]])
    for bit in high + [2, 1]:
        got = swapped(bit)(stats)
        top = jnp.maximum(stats[0], got[0])
        stats = jnp.stack(
            [top, stats[1] * jnp.exp(stats[0] - top) + got[1] * jnp.exp(got[0] - top)]
        )
    logprobs = scaled - stats[0][..., None] - jnp.log(stats[1])[..., None]

    keep, send = gathered(ids, table, 1)
    keep = keep + core(send)
    keep = keep[:quarter] + chip(keep[quarter:])
    for bit in high:
        half = keep.shape[0] // 2
        keep = keep[:half] + swapped(bit)(keep[half:])
    embedded = (keep.astype(jnp.float32) * math.sqrt(width)).astype(jnp.bfloat16)
    return logprobs, embedded


def ordered(rows, bits, rows_dev):
    width = rows.shape[1]
    blocks = rows.reshape((2,) * bits + (rows_dev, width))
    axes = tuple(range(bits - 1, -1, -1)) + (bits, bits + 1)
    return blocks.transpose(axes).reshape(rows.shape)


def solution(mesh):
    in_specs = (
        P(("groups", "vocab"), None),
        P(("groups", "vocab"), None),
        P(),
        P("vocab", None),
        P(),
        P(None, "groups"),
        P(None, "groups"),
    )
    out_specs = (P(None, "groups", "vocab"), P(("groups", "vocab"), None))
    return jax.shard_map(body, mesh=mesh, in_specs=in_specs, out_specs=out_specs, check_vma=False)
```

time: 155 us -> 65.4 us (0.42)
  blocking collectives: 102 us -> 0 us
  waiting for transfers between devices: 1.34 us -> 28 us
  matrix products: 15.1 us -> 0 us
  Pallas kernels: 0 us -> 9.86 us
  local copies, waits for them, and re-layouts: 16 us -> 6.47 us
  starting transfers between devices: 12.1 us -> 17.6 us
  other arithmetic: 7.6 us -> 2.31 us
    all_gather x2 -> x0, blocking collectives: 41.1 us -> none  [logarithmic_likelihood(): lax.all_gather(normed_rows, 'vocab', axis=0, tiled=True)]
    pmax x1 -> x0, blocking collectives: 31.2 us -> none  [logarithmic_likelihood(): peak = lax.pmax(local_peak, 'vocab')]
    psum x1 -> x0, blocking collectives: 29.5 us -> none  [logarithmic_likelihood(): total = lax.psum(jnp.sum(jnp.exp(scaled - peak[:, None]), axis=1), 'vocab')]
    ppermute x0 -> x14, waiting for transfers between devices: none -> 28 us  [swapped(): return lambda x: lax.ppermute(x, 'vocab', pairs)]
    ppermute x0 -> x14, starting transfers between devices: none -> 17.6 us  [swapped(): return lambda x: lax.ppermute(x, 'vocab', pairs)]
    dot_general x2 -> x0, matrix products: 15.1 us -> none  [logarithmic_likelihood(): lax.dot_general(lax.all_gather(normed_rows, 'vocab', axis=0, tiled=True),...]
    gather x2 -> x0, local copies, waits for them, and re-layouts: 13.3 us -> none  [fetched(): jnp.take(shared_lexicon_matrix, jnp.clip(local_ids, 0, voc_dev - 1), axis=0)]
    all_to_all x2 -> x0, starting transfers between devices: 12.1 us -> none  [fetched(): lax.all_to_all(picked, 'vocab', split_axis=0, concat_axis=0, tiled=True)]
  transfers between devices with their start and end apart: 2 -> 14, of which waited for: 1 -> 11; matrix products, arithmetic and copies ran while one was open for 8% -> 3% of each run, Pallas kernels for 0% -> 11%
where the time goes in v1:
time: 65.4 us; the launch traced here: 65.2 us
  waiting for transfers between devices  28 us (43%)
  starting transfers between devices  17.6 us (27%)
  Pallas kernels  9.86 us (15%)
  local copies, waits for them, and re-layouts  6.47 us (10%)
  other arithmetic  2.31 us (4%)
  between operations  0.96 us (1%)
    ppermute x14, waiting for transfers between devices, swapped(): return lambda x: lax.ppermute(x, 'vocab', pairs)  28 us
    ppermute x14, starting transfers between devices, swapped(): return lambda x: lax.ppermute(x, 'vocab', pairs)  17.6 us
    pallas_call x1, Pallas kernels, head(): pl.pallas_call(head_kernel, grid=(voc_dev // tile,), out_shape=(jax.Shape...  5.12 us
    unnamed x16, local copies, waits for them, and re-layouts  4.83 us
    pallas_call x2, Pallas kernels, gathered(): pl.pallas_call(functools.partial(gather_kernel, step), out_shape=(out, ou...  4.56 us
  transfers between devices with their start and end apart: 14, of which 11 were waited for; matrix products, arithmetic and copies ran while one was open for 3% of the time, Pallas kernels for 11%

profile of v1, /device:TPU:0, one launch (start us, length us, event | category | flops | bytes accessed | tf_op | source)
XLA Modules:
  0.0 65.2 jit_solution(18004929059058912721)
XLA Ops:
  0.6 0.7 %copy-done.1 = s32[2,32]{1,0:T(2,128)S(1)} copy-done((s32[2,32]{1,0:T(2,128)S(1)}, s32[2,32]{1,0:T(2,128)}, u32[]{:S(2)}) %copy-start.1) | copy-done | bytes 280
  1.3 2.3 %pick_rows.2 = (bf16[16,5376]{1,0:T(8,128)(2,1)S(1)}, bf16[16,5376]{1,0:T(8,128)(2,1)S(1)}) custom-call(s32[2,32]{1,0:T(2,128)S(1)} %copy-done.1, bf16[1024,5376]{1,0:T(8,128)(2,1)} %table_ref.5), custom_call_target="tpu_custom_call" | custom-call | tf_op jit(solution)/shard_map/pick_rows/pallas_call | solution.py:56
  3.7 0.1 collective-permute-start
  3.8 1.4 %collective-permute-done = bf16[16,5376]{1,0:T(8,128)(2,1)S(1)} collective-permute-done((bf16[16,5376]{1,0:T(8,128)(2,1)S(1)}, bf16[16,5376]{1,0:T(8,128)(2,1)S(1)}, u32[]{:S(2)}, u32[]{:S(2)}) %collective-permute-start) | collective-permute-done | bytes 172064 | tf_op jit(solution)/shard_map/ppermute | solution.py:73
  5.2 2.9 %collective-permute-start.1 = (bf16[8,5376]{1,0:T(8,128)(2,1)S(1)}, bf16[8,5376]{1,0:T(8,128)(2,1)S(1)}, u32[]{:S(2)}, u32[]{:S(2)}) collective-permute-start(bf16[8,5376]{1,0:T(8,128)(2,1)S(1)} %slice.93), channel_id=1, source_target_pairs={{0,2},{1,3},{2,0},{3,1},{4,6},{5,7},{6,4},{7,5},{8,10},{9,11},{10,... | collective-permute-start | bytes 258056 | tf_op jit(solution)/shard_map/ppermute | solution.py:73
  8.1 2.8 %collective-permute-done.1 = bf16[8,5376]{1,0:T(8,128)(2,1)S(1)} collective-permute-done((bf16[8,5376]{1,0:T(8,128)(2,1)S(1)}, bf16[8,5376]{1,0:T(8,128)(2,1)S(1)}, u32[]{:S(2)}, u32[]{:S(2)}) %collective-permute-start.1) | collective-permute-done | bytes 86048 | tf_op jit(solution)/shard_map/ppermute | solution.py:73
  11.0 2.9 %collective-permute-start.2 = (bf16[12,5376]{1,0:T(8,128)(2,1)S(1)}, bf16[12,5376]{1,0:T(8,128)(2,1)S(1)}, u32[]{:S(2)}, u32[]{:S(2)}) collective-permute-start(bf16[12,5376]{1,0:T(8,128)(2,1)S(1)} %pad_maximum_fusion.1), channel_id=1, source_target_pairs={{0,8},{1,9},{2,10},{3,11},{4,12},{5,13},{6,14},{7,15},{8,0},{9,1},... | collective-permute-start | bytes 387080 | tf_op jit(solution)/shard_map/ppermute | solution.py:73
  13.9 7.6 %collective-permute-done.2 = bf16[12,5376]{1,0:T(8,128)(2,1)S(1)} collective-permute-done((bf16[12,5376]{1,0:T(8,128)(2,1)S(1)}, bf16[12,5376]{1,0:T(8,128)(2,1)S(1)}, u32[]{:S(2)}, u32[]{:S(2)}) %collective-permute-start.2) | collective-permute-done | bytes 129056 | tf_op jit(solution)/shard_map/ppermute | solution.py:73
  21.8 0.1 concatenate.21
  21.9 0.7 %collective-permute-start.3 = (bf16[16,5376]{1,0:T(8,128)(2,1)S(1)}, bf16[16,5376]{1,0:T(8,128)(2,1)S(1)}, u32[]{:S(2)}, u32[]{:S(2)}) collective-permute-start(bf16[16,5376]{1,0:T(8,128)(2,1)S(1)} %concatenate.21), channel_id=1, source_target_pairs={{0,4},{1,5},{2,6},{3,7},{4,0},{5,1},{6,2},{7,3},{8,12},{9,13},{10,... | collective-permute-start | bytes 516104 | tf_op jit(solution)/shard_map/ppermute | solution.py:73
  22.6 4.8 %collective-permute-done.3 = bf16[16,5376]{1,0:T(8,128)(2,1)S(1)} collective-permute-done((bf16[16,5376]{1,0:T(8,128)(2,1)S(1)}, bf16[16,5376]{1,0:T(8,128)(2,1)S(1)}, u32[]{:S(2)}, u32[]{:S(2)}) %collective-permute-start.3) | collective-permute-done | bytes 172064 | tf_op jit(solution)/shard_map/ppermute | solution.py:73
  27.4 0.1 pad_maximum_fusion.2
  28.1 0.2 norm.1
  28.3 1.6 %collective-permute-start.4 = (bf16[16,5376]{1,0:T(8,128)(2,1)S(1)}, bf16[16,5376]{1,0:T(8,128)(2,1)S(1)}, u32[]{:S(2)}, u32[]{:S(2)}) collective-permute-start(bf16[16,5376]{1,0:T(8,128)(2,1)S(1)} %norm.1), channel_id=1, source_target_pairs={{0,2},{1,3},{2,0},{3,1},{4,6},{5,7},{6,4},{7,5},{8,10},{9,11},{10,... | collective-permute-start | bytes 516104 | tf_op jit(solution)/shard_map/ppermute | solution.py:73
  29.9 3.9 %collective-permute-done.4 = bf16[16,5376]{1,0:T(8,128)(2,1)S(1)} collective-permute-done((bf16[16,5376]{1,0:T(8,128)(2,1)S(1)}, bf16[16,5376]{1,0:T(8,128)(2,1)S(1)}, u32[]{:S(2)}, u32[]{:S(2)}) %collective-permute-start.4) | collective-permute-done | bytes 172064 | tf_op jit(solution)/shard_map/ppermute | solution.py:73
  33.8 0.1 collective-permute-start.5
  33.9 2.2 %pick_rows.3 = (bf16[16,5376]{1,0:T(8,128)(2,1)S(1)}, bf16[16,5376]{1,0:T(8,128)(2,1)S(1)}) custom-call(s32[2,32]{1,0:T(2,128)S(1)} %copy-done.2, bf16[1024,5376]{1,0:T(8,128)(2,1)} %table_ref.5), custom_call_target="tpu_custom_call" | custom-call | tf_op jit(solution)/shard_map/pick_rows/pallas_call | solution.py:56
  36.1 0.6 collective-permute-start.10
  36.7 0.1 select_reduce_fusion
  36.8 0.1 copy.56.temps_ref
  36.9 0.9 %collective-permute-done.10 = bf16[16,5376]{1,0:T(8,128)(2,1)S(1)} collective-permute-done((bf16[16,5376]{1,0:T(8,128)(2,1)S(1)}, bf16[16,5376]{1,0:T(8,128)(2,1)S(1)}, u32[]{:S(2)}, u32[]{:S(2)}) %collective-permute-start.10) | collective-permute-done | bytes 172064 | tf_op jit(solution)/shard_map/ppermute | solution.py:73
  37.8 1.6 %collective-permute-start.11 = (bf16[8,5376]{1,0:T(8,128)(2,1)S(1)}, bf16[8,5376]{1,0:T(8,128)(2,1)S(1)}, u32[]{:S(2)}, u32[]{:S(2)}) collective-permute-start(bf16[8,5376]{1,0:T(8,128)(2,1)S(1)} %slice.109), channel_id=1, source_target_pairs={{0,2},{1,3},{2,0},{3,1},{4,6},{5,7},{6,4},{7,5},{8,10},{9,11},{10,... | collective-permute-start | bytes 258056 | tf_op jit(solution)/shard_map/ppermute | solution.py:73
  39.4 4.1 %copy-done = bf16[1024,5376]{1,0:T(8,128)(2,1)S(1)} copy-done((bf16[1024,5376]{1,0:T(8,128)(2,1)S(1)}, bf16[1024,5376]{1,0:T(8,128)(2,1)}, u32[]{:S(2)}) %copy-start) | copy-done | bytes 11010072
  43.5 5.1 %head.1 = (f32[2,32,1024]{2,1,0:T(8,128)S(1)}, f32[2,32,1]{2,1,0:T(8,128)S(1)}, f32[2,32,1]{2,1,0:T(8,128)S(1)}) custom-call(bf16[32,5376]{1,0:T(8,128)(2,1)S(1)} %pad_maximum_fusion.own_ref, bf16[32,5376]{1,0:T(8,128)(2,1)S(1)} %collective-permute-done.5.got_ref, bf16[1024,5376]{1,0:T(8,128)(2,1)S(1)} %copy-done, f32[2,32,1]{2,1,0:T(8,128)S(1)} %copy.56.temps_ref), custom_call_target="tpu_custom_call" | custom-call | tf_op jit(solution)/shard_map/head/pallas_call | solution.py:148
  48.7 0.1 reduce
  48.8 0.1 reduce.1
  48.9 3.6 %collective-permute-start.6 = (f32[2,2,32]{2,1,0:T(2,128)S(1)}, f32[2,2,32]{2,1,0:T(2,128)S(1)}, u32[]{:S(2)}, u32[]{:S(2)}) collective-permute-start(f32[2,2,32]{2,1,0:T(2,128)S(1)} %pad_maximum_fusion.4), channel_id=1, source_target_pairs={{0,8},{1,9},{2,10},{3,11},{4,12},{5,13},{6,14},{7,15},{8,0},{9,1},... | collective-permute-start | bytes 1544 | tf_op jit(solution)/shard_map/ppermute | solution.py:73
  52.5 0.1 collective-permute-start.12
  52.6 1.4 %collective-permute-done.6 = f32[2,2,32]{2,1,0:T(2,128)S(1)} collective-permute-done((f32[2,2,32]{2,1,0:T(2,128)S(1)}, f32[2,2,32]{2,1,0:T(2,128)S(1)}, u32[]{:S(2)}, u32[]{:S(2)}) %collective-permute-start.6) | collective-permute-done | bytes 544 | tf_op jit(solution)/shard_map/ppermute | solution.py:73
  54.0 1.6 %collective-permute-start.7 = (f32[2,2,32]{2,1,0:T(2,128)S(1)}, f32[2,2,32]{2,1,0:T(2,128)S(1)}, u32[]{:S(2)}, u32[]{:S(2)}) collective-permute-start(f32[2,2,32]{2,1,0:T(2,128)S(1)} %pad_maximum_fusion.5), channel_id=1, source_target_pairs={{0,4},{1,5},{2,6},{3,7},{4,0},{5,1},{6,2},{7,3},{8,12},{9,13},{10,... | collective-permute-start | bytes 1544 | tf_op jit(solution)/shard_map/ppermute | solution.py:73
  55.6 2.1 %collective-permute-done.12 = bf16[4,5376]{1,0:T(4,128)(2,1)S(1)} collective-permute-done((bf16[4,5376]{1,0:T(4,128)(2,1)S(1)}, bf16[4,5376]{1,0:T(4,128)(2,1)S(1)}, u32[]{:S(2)}, u32[]{:S(2)}) %collective-permute-start.12) | collective-permute-done | bytes 43040 | tf_op jit(solution)/shard_map/ppermute | solution.py:73
  57.8 1.4 %collective-permute-start.13 = (bf16[2,5376]{1,0:T(2,128)(2,1)S(1)}, bf16[2,5376]{1,0:T(2,128)(2,1)S(1)}, u32[]{:S(2)}, u32[]{:S(2)}) collective-permute-start(bf16[2,5376]{1,0:T(2,128)(2,1)S(1)} %slice.113), channel_id=1, source_target_pairs={{0,4},{1,5},{2,6},{3,7},{4,0},{5,1},{6,2},{7,3},{8,12},{9,13},{10,... | collective-permute-start | bytes 64520 | tf_op jit(solution)/shard_map/ppermute | solution.py:73
  59.2 0.5 collective-permute-start.8
  59.6 2.0 %collective-permute-done.13 = bf16[2,5376]{1,0:T(2,128)(2,1)S(1)} collective-permute-done((bf16[2,5376]{1,0:T(2,128)(2,1)S(1)}, bf16[2,5376]{1,0:T(2,128)(2,1)S(1)}, u32[]{:S(2)}, u32[]{:S(2)}) %collective-permute-start.13) | collective-permute-done | bytes 21536 | tf_op jit(solution)/shard_map/ppermute | solution.py:73
  61.6 0.6 multiply_convert_fusion
  62.3 0.1 copy.57
  62.4 0.4 collective-permute-done.8
  62.8 0.1 collective-permute-start.9
  62.9 0.1 copy.62
  63.0 0.1 copy.58
  63.1 0.1 copy.64
  63.2 0.1 copy.59
  63.3 0.1 copy.66
  63.4 0.7 %collective-permute-done.9 = f32[2,2,32]{2,1,0:T(2,128)S(1)} collective-permute-done((f32[2,2,32]{2,1,0:T(2,128)S(1)}, f32[2,2,32]{2,1,0:T(2,128)S(1)}, u32[]{:S(2)}, u32[]{:S(2)}) %collective-permute-start.9) | collective-permute-done | bytes 544 | tf_op jit(solution)/shard_map/ppermute | solution.py:73
  64.1 0.1 copy.60
  64.2 0.1 copy.68
  64.2 0.1 maximum_reduce_fusion
  64.4 0.8 %subtract_subtract_fusion = f32[2,32,1024]{2,1,0:T(8,128)} fusion(f32[2,32,1024]{2,1,0:T(8,128)S(1)} %get-tuple-element.11, f32[2,32]{1,0:T(2,128)S(1)} %get-tuple-element.17, f32[2,32]{1,0:T(2,128)S(1)} %get-tuple-element.16), kind=kLoop, calls=%fused_computation.1 | loop fusion | flops 131072 | bytes 524800 | tf_op jit(solution)/shard_map/sub | solution.py:206
  (55 shorter events, 1.0 us)
Async XLA Ops:
  0.6 0.7 %copy-start.1 = (s32[2,32]{1,0:T(2,128)S(1)}, s32[2,32]{1,0:T(2,128)}, u32[]{:S(2)}) copy-start(s32[2,32]{1,0:T(2,128)} %ids_ref.3) | copy-start | bytes 772
  1.3 9.6 %copy-start.3 = (bf16[2,5376]{1,0:T(2,128)(2,1)S(1)}, bf16[2,5376]{1,0:T(2,128)(2,1)}, u32[]{:S(2)}) copy-start(bf16[2,5376]{1,0:T(2,128)(2,1)} %param.8) | copy-start | bytes 64516
  1.3 9.6 %copy-start.4 = (bf16[2,5376]{1,0:T(2,128)(2,1)S(1)}, bf16[2,5376]{1,0:T(2,128)(2,1)}, u32[]{:S(2)}) copy-start(bf16[2,5376]{1,0:T(2,128)(2,1)} %param.7) | copy-start | bytes 64516
  1.3 21.3 %copy-start.5 = (f32[5376]{0:T(1024)S(1)}, f32[5376]{0:T(1024)}, u32[]{:S(2)}) copy-start(f32[5376]{0:T(1024)} %param.9) | copy-start | bytes 64516
  1.3 32.5 %copy-start.2 = (s32[2,32]{1,0:T(2,128)S(1)}, s32[2,32]{1,0:T(2,128)}, u32[]{:S(2)}) copy-start(s32[2,32]{1,0:T(2,128)} %ids_ref.3) | copy-start | bytes 772
  3.7 33.1 %copy-start.6 = (s32[2,32]{1,0:T(2,128)S(1)}, s32[2,32]{1,0:T(2,128)}, u32[]{:S(2)}) copy-start(s32[2,32]{1,0:T(2,128)} %param.12) | copy-start | bytes 772
  3.7 33.1 %copy-start.7 = (f32[8]{0:T(128)S(1)}, f32[8]{0:T(128)}, u32[]{:S(2)}) copy-start(f32[8]{0:T(128)} %param.11) | copy-start | bytes 100
  3.7 1.5 %collective-permute-start = (bf16[16,5376]{1,0:T(8,128)(2,1)S(1)}, bf16[16,5376]{1,0:T(8,128)(2,1)S(1)}, u32[]{:S(2)}, u32[]{:S(2)}) collective-permute-start(bf16[16,5376]{1,0:T(8,128)(2,1)S(1)} %get-tuple-element.10), channel_id=1, source_target_pairs={{0,1},{1,0},{2,3},{3,2},{4,5},{5,4},{6,7},{7,6},{8,9},{9,8},{10,11... | collective-permute-start | bytes 516104 | tf_op jit(solution)/shard_map/ppermute | solution.py:73
  5.2 5.7 %collective-permute-start.1 = (bf16[8,5376]{1,0:T(8,128)(2,1)S(1)}, bf16[8,5376]{1,0:T(8,128)(2,1)S(1)}, u32[]{:S(2)}, u32[]{:S(2)}) collective-permute-start(bf16[8,5376]{1,0:T(8,128)(2,1)S(1)} %slice.93), channel_id=1, source_target_pairs={{0,2},{1,3},{2,0},{3,1},{4,6},{5,7},{6,4},{7,5},{8,10},{9,11},{10,... | collective-permute-start | bytes 258056 | tf_op jit(solution)/shard_map/ppermute | solution.py:73
  11.0 10.6 %collective-permute-start.2 = (bf16[12,5376]{1,0:T(8,128)(2,1)S(1)}, bf16[12,5376]{1,0:T(8,128)(2,1)S(1)}, u32[]{:S(2)}, u32[]{:S(2)}) collective-permute-start(bf16[12,5376]{1,0:T(8,128)(2,1)S(1)} %pad_maximum_fusion.1), channel_id=1, source_target_pairs={{0,8},{1,9},{2,10},{3,11},{4,12},{5,13},{6,14},{7,15},{8,0},{9,1},... | collective-permute-start | bytes 387080 | tf_op jit(solution)/shard_map/ppermute | solution.py:73
  21.9 5.5 %collective-permute-start.3 = (bf16[16,5376]{1,0:T(8,128)(2,1)S(1)}, bf16[16,5376]{1,0:T(8,128)(2,1)S(1)}, u32[]{:S(2)}, u32[]{:S(2)}) collective-permute-start(bf16[16,5376]{1,0:T(8,128)(2,1)S(1)} %concatenate.21), channel_id=1, source_target_pairs={{0,4},{1,5},{2,6},{3,7},{4,0},{5,1},{6,2},{7,3},{8,12},{9,13},{10,... | collective-permute-start | bytes 516104 | tf_op jit(solution)/shard_map/ppermute | solution.py:73
  28.3 5.5 %collective-permute-start.4 = (bf16[16,5376]{1,0:T(8,128)(2,1)S(1)}, bf16[16,5376]{1,0:T(8,128)(2,1)S(1)}, u32[]{:S(2)}, u32[]{:S(2)}) collective-permute-start(bf16[16,5376]{1,0:T(8,128)(2,1)S(1)} %norm.1), channel_id=1, source_target_pairs={{0,2},{1,3},{2,0},{3,1},{4,6},{5,7},{6,4},{7,5},{8,10},{9,11},{10,... | collective-permute-start | bytes 516104 | tf_op jit(solution)/shard_map/ppermute | solution.py:73
  33.8 5.6 %collective-permute-start.5 = (bf16[32,5376]{1,0:T(8,128)(2,1)S(1)}, bf16[32,5376]{1,0:T(8,128)(2,1)S(1)}, u32[]{:S(2)}, u32[]{:S(2)}) collective-permute-start(bf16[32,5376]{1,0:T(8,128)(2,1)S(1)} %pad_maximum_fusion.own_ref), channel_id=1, source_target_pairs={{0,1},{1,0},{2,3},{3,2},{4,5},{5,4},{6,7},{7,6},{8,9},{9,8},{10,11... | collective-permute-start | bytes 1032200 | tf_op jit(solution)/shard_map/ppermute | solution.py:73
  36.1 1.7 %collective-permute-start.10 = (bf16[16,5376]{1,0:T(8,128)(2,1)S(1)}, bf16[16,5376]{1,0:T(8,128)(2,1)S(1)}, u32[]{:S(2)}, u32[]{:S(2)}) collective-permute-start(bf16[16,5376]{1,0:T(8,128)(2,1)S(1)} %get-tuple-element.15), channel_id=1, source_target_pairs={{0,1},{1,0},{2,3},{3,2},{4,5},{5,4},{6,7},{7,6},{8,9},{9,8},{10,11... | collective-permute-start | bytes 516104 | tf_op jit(solution)/shard_map/ppermute | solution.py:73
  37.8 14.6 %collective-permute-start.11 = (bf16[8,5376]{1,0:T(8,128)(2,1)S(1)}, bf16[8,5376]{1,0:T(8,128)(2,1)S(1)}, u32[]{:S(2)}, u32[]{:S(2)}) collective-permute-start(bf16[8,5376]{1,0:T(8,128)(2,1)S(1)} %slice.109), channel_id=1, source_target_pairs={{0,2},{1,3},{2,0},{3,1},{4,6},{5,7},{6,4},{7,5},{8,10},{9,11},{10,... | collective-permute-start | bytes 258056 | tf_op jit(solution)/shard_map/ppermute | solution.py:73
  39.4 4.1 %copy-start = (bf16[1024,5376]{1,0:T(8,128)(2,1)S(1)}, bf16[1024,5376]{1,0:T(8,128)(2,1)}, u32[]{:S(2)}) copy-start(bf16[1024,5376]{1,0:T(8,128)(2,1)} %table_ref.5) | copy-start | bytes 33030148
  48.9 5.2 %collective-permute-start.6 = (f32[2,2,32]{2,1,0:T(2,128)S(1)}, f32[2,2,32]{2,1,0:T(2,128)S(1)}, u32[]{:S(2)}, u32[]{:S(2)}) collective-permute-start(f32[2,2,32]{2,1,0:T(2,128)S(1)} %pad_maximum_fusion.4), channel_id=1, source_target_pairs={{0,8},{1,9},{2,10},{3,11},{4,12},{5,13},{6,14},{7,15},{8,0},{9,1},... | collective-permute-start | bytes 1544 | tf_op jit(solution)/shard_map/ppermute | solution.py:73
  52.5 5.2 %collective-permute-start.12 = (bf16[4,5376]{1,0:T(4,128)(2,1)S(1)}, bf16[4,5376]{1,0:T(4,128)(2,1)S(1)}, u32[]{:S(2)}, u32[]{:S(2)}) collective-permute-start(bf16[4,5376]{1,0:T(4,128)(2,1)S(1)} %slice.111), channel_id=1, source_target_pairs={{0,8},{1,9},{2,10},{3,11},{4,12},{5,13},{6,14},{7,15},{8,0},{9,1},... | collective-permute-start | bytes 129032 | tf_op jit(solution)/shard_map/ppermute | solution.py:73
  54.0 5.1 %collective-permute-start.7 = (f32[2,2,32]{2,1,0:T(2,128)S(1)}, f32[2,2,32]{2,1,0:T(2,128)S(1)}, u32[]{:S(2)}, u32[]{:S(2)}) collective-permute-start(f32[2,2,32]{2,1,0:T(2,128)S(1)} %pad_maximum_fusion.5), channel_id=1, source_target_pairs={{0,4},{1,5},{2,6},{3,7},{4,0},{5,1},{6,2},{7,3},{8,12},{9,13},{10,... | collective-permute-start | bytes 1544 | tf_op jit(solution)/shard_map/ppermute | solution.py:73
  57.8 3.9 %collective-permute-start.13 = (bf16[2,5376]{1,0:T(2,128)(2,1)S(1)}, bf16[2,5376]{1,0:T(2,128)(2,1)S(1)}, u32[]{:S(2)}, u32[]{:S(2)}) collective-permute-start(bf16[2,5376]{1,0:T(2,128)(2,1)S(1)} %slice.113), channel_id=1, source_target_pairs={{0,4},{1,5},{2,6},{3,7},{4,0},{5,1},{6,2},{7,3},{8,12},{9,13},{10,... | collective-permute-start | bytes 64520 | tf_op jit(solution)/shard_map/ppermute | solution.py:73
  59.2 3.7 %collective-permute-start.8 = (f32[2,2,32]{2,1,0:T(2,128)S(1)}, f32[2,2,32]{2,1,0:T(2,128)S(1)}, u32[]{:S(2)}, u32[]{:S(2)}) collective-permute-start(f32[2,2,32]{2,1,0:T(2,128)S(1)} %pad_maximum_fusion.6), channel_id=1, source_target_pairs={{0,2},{1,3},{2,0},{3,1},{4,6},{5,7},{6,4},{7,5},{8,10},{9,11},{10,... | collective-permute-start | bytes 1544 | tf_op jit(solution)/shard_map/ppermute | solution.py:73
  62.8 1.2 %collective-permute-start.9 = (f32[2,2,32]{2,1,0:T(2,128)S(1)}, f32[2,2,32]{2,1,0:T(2,128)S(1)}, u32[]{:S(2)}, u32[]{:S(2)}) collective-permute-start(f32[2,2,32]{2,1,0:T(2,128)S(1)} %pad_maximum_fusion.7), channel_id=1, source_target_pairs={{0,1},{1,0},{2,3},{3,2},{4,5},{5,4},{6,7},{7,6},{8,9},{9,8},{10,11... | collective-permute-start | bytes 1544 | tf_op jit(solution)/shard_map/ppermute | solution.py:73

commit v2 on v0

v2 whole, which is shorter than its diff:
```python
import functools
import math

import jax
import jax.numpy as jnp
from jax import lax
from jax.experimental import pallas as pl
from jax.experimental.pallas import tpu as pltpu
from jax.sharding import PartitionSpec as P

BLOCK = 16
MIB = 2**20


def reversed_bits(value, bits):
    out = 0
    for k in range(bits):
        out = out * 2 + (value >> k & 1)
    return out


def table_rows(rows, shards):
    bits = shards.bit_length() - 3
    dev = rows // shards
    return [
        (reversed_bits(q, bits) * 4 + y * 2 + c) * dev + j
        for c in range(2)
        for y in range(2)
        for q in range(shards // 4)
        for j in range(dev)
    ]


def pick_kernel(ids_ref, table_ref, *refs):
    outs, (listed, slots, rows, sems) = refs[:2], refs[2:]
    steps, count = ids_ref.shape
    held = slots.shape[1]
    voc_dev = table_ref.shape[0]
    shards = lax.axis_size("vocab")
    bits = shards.bit_length() - 3
    rows_dev = count // shards
    me = lax.axis_index("vocab")
    offset = me * voc_dev
    low = me % 4

    def copy(step, n):
        local = listed[step, n] // count
        base = pl.multiple_of(local // BLOCK * BLOCK, BLOCK)
        slot = n % held
        return pltpu.make_async_copy(
            table_ref.at[pl.ds(base, BLOCK)], slots.at[step, slot], sems.at[step, slot]
        )

    def start(step, first, found):
        @pl.loop(first, jnp.minimum(found, first + held))
        def _(n):
            copy(step, n).start()

    def finish(step, first, found):
        @pl.loop(first, jnp.minimum(found, first + held))
        def _(n):
            entry = listed[step, n]
            r = entry % count
            copy(step, n).wait()
            block = slots[step, n % held].astype(jnp.float32)
            sub = lax.broadcasted_iota(jnp.int32, block.shape, 0)
            picked = jnp.sum(
                jnp.where(sub == entry // count % BLOCK, block, 0.0), axis=0, keepdims=True
            )
            owner = r // rows_dev
            way = owner % 4 ^ low
            chip = owner // 4 if step == 0 else owner // 4 ^ me // 4
            order = sum((chip >> k) % 2 << (bits - 1 - k) for k in range(bits))
            place = ((way % 2 * steps + step) * 2 + way // 2) * (shards // 4) + order
            rows[pl.ds(place * rows_dev + r % rows_dev, 1), :] = picked

    counts = []
    for step in range(steps):
        found = jnp.int32(0)
        for r in range(count):
            local = ids_ref[step, r] - offset
            listed[step, found] = local * count + r
            found = found + ((local >= 0) & (local < voc_dev)).astype(jnp.int32)
        counts.append(found)
        start(step, 0, found)
    rows[...] = jnp.zeros_like(rows)
    for step, found in enumerate(counts):
        finish(step, 0, found)
        for first in range(held, count, held):
            start(step, first, found)
            finish(step, first, found)

    for half, out in enumerate(outs):
        out[...] = rows[half * count : (half + 1) * count].astype(out.dtype)


def picked_rows(ids, table):
    steps, count = ids.shape
    width = table.shape[1]
    held = min(count, 32)
    out = jax.ShapeDtypeStruct((count * steps // 2, width), table.dtype)
    return pl.pallas_call(
        pick_kernel,
        out_shape=(out, out),
        in_specs=[pl.BlockSpec(memory_space=pltpu.SMEM), pl.BlockSpec(memory_space=pl.ANY)],
        out_specs=(pl.BlockSpec(memory_space=pltpu.VMEM),) * 2,
        scratch_shapes=[
            pltpu.SMEM((steps, count + 1), jnp.int32),
            pltpu.VMEM((steps, held, BLOCK, width), table.dtype),
            pltpu.VMEM((steps * count, width), jnp.float32),
            pltpu.SemaphoreType.DMA((steps, held)),
        ],
        compiler_params=pltpu.CompilerParams(vmem_limit_bytes=24 * MIB),
        name="pick",
    )(ids, pltpu.with_memory_space_constraint(table, pltpu.HBM))


def swapped(rows, bit):
    pairs = [(i, i ^ bit) for i in range(lax.axis_size("vocab"))]
    return lax.ppermute(rows, "vocab", pairs)


def load_kernel(table_ref, after_ref, out_ref, sems):
    parts = sems.shape[0]
    part = table_ref.shape[0] // parts
    copies = [
        pltpu.make_async_copy(
            table_ref.at[pl.ds(k * part, part)], out_ref.at[pl.ds(k * part, part)], sems.at[k]
        )
        for k in range(parts)
    ]
    for copy in copies:
        copy.start()
    for copy in copies:
        copy.wait()


def loaded(table, after):
    return pl.pallas_call(
        load_kernel,
        out_shape=jax.ShapeDtypeStruct(table.shape, table.dtype),
        in_specs=[pl.BlockSpec(memory_space=pl.ANY)] * 2,
        out_specs=pl.BlockSpec(memory_space=pltpu.VMEM),
        scratch_shapes=[pltpu.SemaphoreType.DMA((8,))],
        compiler_params=pltpu.CompilerParams(vmem_limit_bytes=4 * MIB),
        cost_estimate=pl.CostEstimate(
            flops=0, bytes_accessed=table.size * table.dtype.itemsize, transcendentals=0
        ),
        name="load",
    )(pltpu.with_memory_space_constraint(table, pltpu.HBM), after)


def norm_kernel(
    places, first_ref, own_ref, got_ref, delta_ref, gain_ref, class_ref, heat_ref, out_ref, temps_ref
):
    temps = jnp.ones(temps_ref.shape, jnp.float32)
    lane = lax.broadcasted_iota(jnp.int32, temps.shape, 1)
    for place, (step, row) in enumerate(places):
        temps = jnp.where(lane == place, heat_ref[class_ref[step, row]], temps)
    temps_ref[...] = temps
    width = first_ref.shape[1]
    gain = gain_ref[...]

    def rescaled(hidden):
        squares = jnp.mean(hidden * hidden, axis=-1, keepdims=True)
        return hidden * lax.rsqrt(squares + 1e-06) * gain

    me = lax.axis_index("vocab")
    bits = lax.axis_size("vocab").bit_length() - 3

    def in_order(rows):
        for k in range(bits):
            size = rows.shape[0] >> k + 1
            parts = [rows[i * size : (i + 1) * size] for i in range(2 << k)]
            other = [parts[i ^ 1] for i in range(2 << k)]
            rows = jnp.where(
                me // 4 >> k & 1 != 0, jnp.concatenate(other), jnp.concatenate(parts)
            )
        return rows

    one = rescaled(in_order(first_ref[...].astype(jnp.float32)))
    picked = own_ref[...].astype(jnp.float32) + got_ref[...].astype(jnp.float32)
    embedded = (picked * math.sqrt(width)).astype(jnp.bfloat16)
    two = rescaled(
        embedded.astype(jnp.float32) + in_order(delta_ref[...].astype(jnp.float32))
    )
    out_ref[...] = jnp.concatenate([one, two], axis=0).astype(out_ref.dtype)


def normed(first, own, got, delta, gain, classes, lookup, places):
    rows, width = first.shape
    smem, vmem = pl.BlockSpec(memory_space=pltpu.SMEM), pl.BlockSpec(memory_space=pltpu.VMEM)
    return pl.pallas_call(
        functools.partial(norm_kernel, places),
        out_shape=(
            jax.ShapeDtypeStruct((2 * rows, width), jnp.bfloat16),
            jax.ShapeDtypeStruct((1, len(places)), jnp.float32),
        ),
        in_specs=[vmem] * 5 + [smem] * 2,
        out_specs=(vmem, vmem),
        compiler_params=pltpu.CompilerParams(vmem_limit_bytes=8 * MIB),
        name="norm",
    )(first, own, got, delta, gain.reshape(1, width), classes, lookup)


def head_kernel(own_ref, got_ref, table_ref, temps_ref, scaled_ref, stats_ref):
    me = lax.axis_index("vocab")
    half, width = own_ref.shape
    dims = (((1,), (1,)), ((), ()))
    own, got = own_ref[...], got_ref[...]
    block = half // 2

    def chips(rows):
        return jnp.where(
            me // 2 % 2 == 1, jnp.concatenate([rows[block:], rows[:block]], axis=0), rows
        )

    own, got = chips(own), chips(got)
    states = jnp.where(
        me % 2 == 1, jnp.concatenate([got, own], axis=0), jnp.concatenate([own, got], axis=0)
    )
    logits = lax.dot_general(table_ref[...], states, dims, preferred_element_type=jnp.float32)
    scaled = logits / temps_ref[...]
    scaled_ref[...] = scaled
    peak = jnp.max(scaled, axis=0, keepdims=True)
    stats_ref[0:1, :] = peak
    stats_ref[1:2, :] = jnp.sum(jnp.exp(scaled - peak), axis=0, keepdims=True)


def head(own, got, table, temps):
    voc_dev, width = table.shape
    rows = 2 * own.shape[0]
    return pl.pallas_call(
        head_kernel,
        out_shape=(
            jax.ShapeDtypeStruct((voc_dev, rows), jnp.float32),
            jax.ShapeDtypeStruct((2, rows), jnp.float32),
        ),
        compiler_params=pltpu.CompilerParams(vmem_limit_bytes=30 * MIB),
        name="head",
    )(own, got, table, temps)


def turn_kernel(order, scaled_ref, out_ref):
    turned = scaled_ref[...].T
    for place, (step, row) in enumerate(order):
        out_ref[step, row : row + 1, :] = turned[place : place + 1]


def turned(scaled, order, steps):
    voc_dev, rows = scaled.shape
    return pl.pallas_call(
        functools.partial(turn_kernel, order),
        out_shape=jax.ShapeDtypeStruct((steps, rows // steps, voc_dev), jnp.float32),
        compiler_params=pltpu.CompilerParams(vmem_limit_bytes=8 * MIB),
        name="turn",
    )(scaled)


def finish_kernel(order, scaled_ref, own_ref, got_ref, out_ref):
    own, got = own_ref[...], got_ref[...]
    peak = jnp.maximum(own[0:1], got[0:1])
    total = own[1:2] * jnp.exp(own[0:1] - peak) + got[1:2] * jnp.exp(got[0:1] - peak)
    both = jnp.concatenate([peak, jnp.log(total)], axis=0)
    rows = both.shape[1]
    spread = jnp.broadcast_to(both[:, None, :], (2, 128, rows))
    peak, log = spread[0].T, spread[1].T
    voc_dev = out_ref.shape[2]
    peak = jnp.concatenate([peak] * (voc_dev // 128), axis=1)
    log = jnp.concatenate([log] * (voc_dev // 128), axis=1)
    for place, (step, row) in enumerate(order):
        at = slice(place, place + 1)
        out_ref[step, row : row + 1, :] = scaled_ref[step, row : row + 1, :] - peak[at] - log[at]


def finished(scaled, own, got, order):
    return pl.pallas_call(
        functools.partial(finish_kernel, order),
        out_shape=jax.ShapeDtypeStruct(scaled.shape, jnp.float32),
        compiler_params=pltpu.CompilerParams(vmem_limit_bytes=8 * MIB),
        name="finish",
    )(scaled, own, got)


def merged(own, got):
    peak = jnp.maximum(own[0], got[0])
    total = own[1] * jnp.exp(own[0] - peak) + got[1] * jnp.exp(got[0] - peak)
    return jnp.stack([peak, total])


def body(first, deltas, gain, table, lookup, classes, ids):
    shards = lax.axis_size("vocab")
    rows_dev, width = first.shape
    steps, rows = ids.shape
    quarter = rows // 4
    high = [1 << k for k in range(shards.bit_length() - 2, 1, -1)]

    keep, send = picked_rows(ids, table)
    keep = (keep + swapped(send, 1)).reshape(steps, 2, quarter, width)
    own = keep[0, 0] + swapped(keep[0, 1], 2)
    following = keep[1, 0] + swapped(keep[1, 1], 2)
    state, delta = first, deltas
    for k, bit in enumerate(high):
        held = state.shape[0]
        moved = swapped(jnp.concatenate([state, delta], axis=0), bit)
        got = swapped(own, bit)
        state = jnp.concatenate([state, moved[:held]], axis=0)
        delta = jnp.concatenate([delta, moved[held:]], axis=0)
        if k < len(high) - 1:
            own = own + got
    order = table_rows(rows, shards)
    places = [
        (step, order[pair * quarter + k])
        for pair in range(4)
        for step in range(steps)
        for k in range(quarter)
    ]
    states, temps = normed(state, own, got, delta, gain, classes, lookup, places)
    states = jnp.concatenate([states, swapped(states, 2)], axis=0)
    scaled, stats = head(states, swapped(states, 1), loaded(table, temps), temps)
    scaled = turned(scaled, places, steps)
    exchange = high + [2, 1]
    for bit in exchange[:-1]:
        stats = merged(stats, swapped(stats, bit))
    logprobs = finished(scaled, stats, swapped(stats, exchange[-1]), places)

    for bit in reversed(high):
        half = following.shape[0] // 2
        following = following[:half] + swapped(following[half:], bit)
    embedded = (following.astype(jnp.float32) * math.sqrt(width)).astype(jnp.bfloat16)
    return logprobs, embedded


def solution(mesh):
    in_specs = (
        P(("groups", "vocab"), None),
        P(("groups", "vocab"), None),
        P(),
        P("vocab", None),
        P(),
        P(None, "groups"),
        P(None, "groups"),
    )
    out_specs = (P(None, "groups", "vocab"), P(("groups", "vocab"), None))
    return jax.shard_map(body, mesh=mesh, in_specs=in_specs, out_specs=out_specs, check_vma=False)
```

time: 155 us -> 59.2 us (0.38)
  blocking collectives: 102 us -> 0 us
  waiting for transfers between devices: 1.34 us -> 29 us
  local copies, waits for them, and re-layouts: 16 us -> 0.87 us
  matrix products: 15.1 us -> 0 us
  Pallas kernels: 0 us -> 11.9 us
  other arithmetic: 7.6 us -> 1.93 us
  starting transfers between devices: 12.1 us -> 14.6 us
    all_gather x2 -> x0, blocking collectives: 41.1 us -> none  [logarithmic_likelihood(): lax.all_gather(normed_rows, 'vocab', axis=0, tiled=True)]
    pmax x1 -> x0, blocking collectives: 31.2 us -> none  [logarithmic_likelihood(): peak = lax.pmax(local_peak, 'vocab')]
    psum x1 -> x0, blocking collectives: 29.5 us -> none  [logarithmic_likelihood(): total = lax.psum(jnp.sum(jnp.exp(scaled - peak[:, None]), axis=1), 'vocab')]
    ppermute x0 -> x15, waiting for transfers between devices: none -> 29 us  [swapped(): return lax.ppermute(rows, 'vocab', pairs)]
    dot_general x2 -> x0, matrix products: 15.1 us -> none  [logarithmic_likelihood(): lax.dot_general(lax.all_gather(normed_rows, 'vocab', axis=0, tiled=True),...]
    ppermute x0 -> x15, starting transfers between devices: none -> 14.6 us  [swapped(): return lax.ppermute(rows, 'vocab', pairs)]
    gather x2 -> x0, local copies, waits for them, and re-layouts: 13.3 us -> none  [fetched(): jnp.take(shared_lexicon_matrix, jnp.clip(local_ids, 0, voc_dev - 1), axis=0)]
    all_to_all x2 -> x0, starting transfers between devices: 12.1 us -> none  [fetched(): lax.all_to_all(picked, 'vocab', split_axis=0, concat_axis=0, tiled=True)]
  transfers between devices with their start and end apart: 2 -> 15, of which waited for: 1 -> 10; matrix products, arithmetic and copies ran while one was open for 8% -> 2% of each run, Pallas kernels for 0% -> 12%
where the time goes in v2:
time: 59.2 us
  waiting for transfers between devices  29 us (49%)
  starting transfers between devices  14.6 us (25%)
  Pallas kernels  11.9 us (20%)
  other arithmetic  1.93 us (3%)
  local copies, waits for them, and re-layouts  0.87 us (1%)
  between operations  0.86 us (1%)
    ppermute x15, waiting for transfers between devices, swapped(): return lax.ppermute(rows, 'vocab', pairs)  29 us
    ppermute x15, starting transfers between devices, swapped(): return lax.ppermute(rows, 'vocab', pairs)  14.6 us
    pallas_call x1, Pallas kernels, loaded(): pl.pallas_call(load_kernel, out_shape=jax.ShapeDtypeStruct(table.shape, t...  4.24 us
    pallas_call x1, Pallas kernels, head(): pl.pallas_call(head_kernel, out_shape=(jax.ShapeDtypeStruct((voc_dev, row...  3.15 us
    pallas_call x1, Pallas kernels, picked_rows(): pl.pallas_call(pick_kernel, out_shape=(out, out), in_specs=[pl.BlockSpec(...  2.54 us
  transfers between devices with their start and end apart: 15, of which 10 were waited for; matrix products, arithmetic and copies ran while one was open for 2% of the time, Pallas kernels for 12%

profile of v2, /device:TPU:0, one launch (start us, length us, event | category | flops | bytes accessed | tf_op | source)
XLA Modules:
  0.0 59.2 jit_solution(12758340045806961115)
XLA Ops:
  0.6 0.0 copy-start.3
  0.6 0.0 copy-start.4
  0.7 0.0 copy-start.5
  0.7 0.0 copy-start.1
  0.7 0.0 copy-start.2
  0.7 0.8 %pad_maximum_fusion.4 = bf16[4,5376]{1,0:T(4,128)(2,1)S(1)} fusion(bf16[2,5376]{1,0:T(2,128)(2,1)} %param.8, bf16[2,5376]{1,0:T(2,128)(2,1)} %param.7), kind=kLoop, calls=%fused_computation.11 | loop fusion | flops 86016 | bytes 86016 | tf_op jit(solution)/shard_map/concatenate | solution.py:305
  1.5 4.1 %collective-permute-start = (bf16[4,5376]{1,0:T(4,128)(2,1)S(1)}, bf16[4,5376]{1,0:T(4,128)(2,1)S(1)}, u32[]{:S(2)}, u32[]{:S(2)}) collective-permute-start(bf16[4,5376]{1,0:T(4,128)(2,1)S(1)} %pad_maximum_fusion.4), channel_id=1, source_target_pairs={{0,8},{1,9},{2,10},{3,11},{4,12},{5,13},{6,14},{7,15},{8,0},{9,1},... | collective-permute-start | bytes 129032 | tf_op jit(solution)/shard_map/ppermute | solution.py:120
  5.6 0.7 %copy-done = s32[2,32]{1,0:T(2,128)S(1)} copy-done((s32[2,32]{1,0:T(2,128)S(1)}, s32[2,32]{1,0:T(2,128)}, u32[]{:S(2)}) %copy-start) | copy-done | bytes 280
  6.3 2.5 %pick.1 = (bf16[32,5376]{1,0:T(8,128)(2,1)S(1)}, bf16[32,5376]{1,0:T(8,128)(2,1)S(1)}) custom-call(s32[2,32]{1,0:T(2,128)S(1)} %copy-done, bf16[1024,5376]{1,0:T(8,128)(2,1)} %table_ref.3), custom_call_target="tpu_custom_call" | custom-call | tf_op jit(solution)/shard_map/pick/pallas_call | solution.py:102
  8.8 0.1 collective-permute-start.2
  8.9 0.0 copy-done.5
  8.9 0.0 collective-permute-done
  9.0 1.6 %collective-permute-done.2 = bf16[32,5376]{1,0:T(8,128)(2,1)S(1)} collective-permute-done((bf16[32,5376]{1,0:T(8,128)(2,1)S(1)}, bf16[32,5376]{1,0:T(8,128)(2,1)S(1)}, u32[]{:S(2)}, u32[]{:S(2)}) %collective-permute-start.2) | collective-permute-done | bytes 344096 | tf_op jit(solution)/shard_map/ppermute | solution.py:120
  10.5 0.1 add.33
  10.7 1.8 %collective-permute-start.12 = (bf16[8,5376]{1,0:T(8,128)(2,1)S(1)}, bf16[8,5376]{1,0:T(8,128)(2,1)S(1)}, u32[]{:S(2)}, u32[]{:S(2)}) collective-permute-start(bf16[8,5376]{1,0:T(8,128)(2,1)S(1)} %get-tuple-element.20), channel_id=1, source_target_pairs={{0,2},{1,3},{2,0},{3,1},{4,6},{5,7},{6,4},{7,5},{8,10},{9,11},{10,... | collective-permute-start | bytes 258056 | tf_op jit(solution)/shard_map/ppermute | solution.py:120
  12.5 0.3 collective-permute-start.3
  12.8 0.1 pad_maximum_fusion
  12.9 2.0 %collective-permute-start.1 = (bf16[8,5376]{1,0:T(8,128)(2,1)S(1)}, bf16[8,5376]{1,0:T(8,128)(2,1)S(1)}, u32[]{:S(2)}, u32[]{:S(2)}) collective-permute-start(bf16[8,5376]{1,0:T(8,128)(2,1)S(1)} %pad_maximum_fusion), channel_id=1, source_target_pairs={{0,4},{1,5},{2,6},{3,7},{4,0},{5,1},{6,2},{7,3},{8,12},{9,13},{10,... | collective-permute-start | bytes 258056 | tf_op jit(solution)/shard_map/ppermute | solution.py:120
  14.8 0.9 %collective-permute-done.12 = bf16[8,5376]{1,0:T(8,128)(2,1)S(1)} collective-permute-done((bf16[8,5376]{1,0:T(8,128)(2,1)S(1)}, bf16[8,5376]{1,0:T(8,128)(2,1)S(1)}, u32[]{:S(2)}, u32[]{:S(2)}) %collective-permute-start.12) | collective-permute-done | bytes 86048 | tf_op jit(solution)/shard_map/ppermute | solution.py:120
  15.8 1.4 %collective-permute-done.3 = bf16[8,5376]{1,0:T(8,128)(2,1)S(1)} collective-permute-done((bf16[8,5376]{1,0:T(8,128)(2,1)S(1)}, bf16[8,5376]{1,0:T(8,128)(2,1)S(1)}, u32[]{:S(2)}, u32[]{:S(2)}) %collective-permute-start.3) | collective-permute-done | bytes 86048 | tf_op jit(solution)/shard_map/ppermute | solution.py:120
  17.2 0.4 collective-permute-start.4
  17.6 0.0 collective-permute-done.1
  17.6 6.8 %collective-permute-done.4 = bf16[8,5376]{1,0:T(8,128)(2,1)S(1)} collective-permute-done((bf16[8,5376]{1,0:T(8,128)(2,1)S(1)}, bf16[8,5376]{1,0:T(8,128)(2,1)S(1)}, u32[]{:S(2)}, u32[]{:S(2)}) %collective-permute-start.4) | collective-permute-done | bytes 86048 | tf_op jit(solution)/shard_map/ppermute | solution.py:120
  24.4 0.3 collective-permute-start.5
  24.7 0.1 pad_maximum_fusion.1
  24.9 4.1 %collective-permute-done.5.got_ref = bf16[8,5376]{1,0:T(8,128)(2,1)S(1)} collective-permute-done((bf16[8,5376]{1,0:T(8,128)(2,1)S(1)}, bf16[8,5376]{1,0:T(8,128)(2,1)S(1)}, u32[]{:S(2)}, u32[]{:S(2)}) %collective-permute-start.5) | collective-permute-done | bytes 86048 | tf_op jit(solution)/shard_map/ppermute | solution.py:120
  29.0 0.9 %norm.1 = (bf16[16,5376]{1,0:T(8,128)(2,1)S(1)}, f32[1,64]{1,0:T(1,128)S(1)}) custom-call(bf16[8,5376]{1,0:T(8,128)(2,1)S(1)} %get-tuple-element.28.first_ref, bf16[8,5376]{1,0:T(8,128)(2,1)S(1)} %add.35.own_ref, bf16[8,5376]{1,0:T(8,128)(2,1)S(1)} %collective-permute-done.5.got_ref, bf16[8,5376]{1,0:T(8,128)(2,1)S(1)} %get-tuple-element.29.delta_ref, ...), custom_call_target="tpu_custom_call" | custom-call | tf_op jit(solution)/shard_map/norm/pallas_call | solution.py:193
  29.9 1.5 %collective-permute-start.6 = (bf16[16,5376]{1,0:T(8,128)(2,1)S(1)}, bf16[16,5376]{1,0:T(8,128)(2,1)S(1)}, u32[]{:S(2)}, u32[]{:S(2)}) collective-permute-start(bf16[16,5376]{1,0:T(8,128)(2,1)S(1)} %get-tuple-element.10), channel_id=1, source_target_pairs={{0,2},{1,3},{2,0},{3,1},{4,6},{5,7},{6,4},{7,5},{8,10},{9,11},{10,... | collective-permute-start | bytes 516104 | tf_op jit(solution)/shard_map/ppermute | solution.py:120
  31.4 3.9 %collective-permute-done.6 = bf16[16,5376]{1,0:T(8,128)(2,1)S(1)} collective-permute-done((bf16[16,5376]{1,0:T(8,128)(2,1)S(1)}, bf16[16,5376]{1,0:T(8,128)(2,1)S(1)}, u32[]{:S(2)}, u32[]{:S(2)}) %collective-permute-start.6) | collective-permute-done | bytes 172064 | tf_op jit(solution)/shard_map/ppermute | solution.py:120
  35.4 0.1 collective-permute-start.7
  35.4 4.2 %load.1.table_ref = bf16[1024,5376]{1,0:T(8,128)(2,1)S(1)} custom-call(bf16[1024,5376]{1,0:T(8,128)(2,1)} %table_ref.3, f32[1,64]{1,0:T(1,128)S(1)} %get-tuple-element.11.after_ref.temps_ref), custom_call_target="tpu_custom_call" | custom-call | bytes 11010048 | tf_op jit(solution)/shard_map/load/pallas_call | solution.py:139
  39.7 0.0 collective-permute-done.7.got_ref
  39.7 3.2 %head.1 = (f32[1024,64]{1,0:T(8,128)S(1)}, f32[2,64]{1,0:T(2,128)S(1)}) custom-call(bf16[32,5376]{1,0:T(8,128)(2,1)S(1)} %constant_dynamic-update-slice_fusion.own_ref, bf16[32,5376]{1,0:T(8,128)(2,1)S(1)} %collective-permute-done.7.got_ref, bf16[1024,5376]{1,0:T(8,128)(2,1)S(1)} %load.1.table_ref, f32[1,64]{1,0:T(1,128)S(1)} %get-tuple-element.11.after_ref.temps_ref), custom_call_target="tpu_custom_call" | custom-call | tf_op jit(solution)/shard_map/head/pallas_call | solution.py:233
  42.9 0.1 collective-permute-start.8
  42.9 4.5 %collective-permute-done.8 = f32[2,64]{1,0:T(2,128)S(1)} collective-permute-done((f32[2,64]{1,0:T(2,128)S(1)}, f32[2,64]{1,0:T(2,128)S(1)}, u32[]{:S(2)}, u32[]{:S(2)}) %collective-permute-start.8) | collective-permute-done | bytes 544 | tf_op jit(solution)/shard_map/ppermute | solution.py:120
  47.4 0.3 collective-permute-start.9
  47.7 1.9 %collective-permute-start.13 = (bf16[4,5376]{1,0:T(4,128)(2,1)S(1)}, bf16[4,5376]{1,0:T(4,128)(2,1)S(1)}, u32[]{:S(2)}, u32[]{:S(2)}) collective-permute-start(bf16[4,5376]{1,0:T(4,128)(2,1)S(1)} %slice.93), channel_id=1, source_target_pairs={{0,4},{1,5},{2,6},{3,7},{4,0},{5,1},{6,2},{7,3},{8,12},{9,13},{10,... | collective-permute-start | bytes 129032 | tf_op jit(solution)/shard_map/ppermute | solution.py:120
  49.6 1.4 %collective-permute-done.9 = f32[2,64]{1,0:T(2,128)S(1)} collective-permute-done((f32[2,64]{1,0:T(2,128)S(1)}, f32[2,64]{1,0:T(2,128)S(1)}, u32[]{:S(2)}, u32[]{:S(2)}) %collective-permute-start.9) | collective-permute-done | bytes 544 | tf_op jit(solution)/shard_map/ppermute | solution.py:120
  51.1 1.5 %collective-permute-start.10 = (f32[2,64]{1,0:T(2,128)S(1)}, f32[2,64]{1,0:T(2,128)S(1)}, u32[]{:S(2)}, u32[]{:S(2)}) collective-permute-start(f32[2,64]{1,0:T(2,128)S(1)} %pad_maximum_fusion.6), channel_id=1, source_target_pairs={{0,2},{1,3},{2,0},{3,1},{4,6},{5,7},{6,4},{7,5},{8,10},{9,11},{10,... | collective-permute-start | bytes 1544 | tf_op jit(solution)/shard_map/ppermute | solution.py:120
  52.6 0.0 collective-permute-done.13
  52.7 0.2 collective-permute-start.14
  52.9 1.8 %collective-permute-done.10 = f32[2,64]{1,0:T(2,128)S(1)} collective-permute-done((f32[2,64]{1,0:T(2,128)S(1)}, f32[2,64]{1,0:T(2,128)S(1)}, u32[]{:S(2)}, u32[]{:S(2)}) %collective-permute-start.10) | collective-permute-done | bytes 544 | tf_op jit(solution)/shard_map/ppermute | solution.py:120
  54.7 0.1 collective-permute-start.11
  54.8 2.6 %collective-permute-done.14 = bf16[2,5376]{1,0:T(2,128)(2,1)S(1)} collective-permute-done((bf16[2,5376]{1,0:T(2,128)(2,1)S(1)}, bf16[2,5376]{1,0:T(2,128)(2,1)S(1)}, u32[]{:S(2)}, u32[]{:S(2)}) %collective-permute-start.14) | collective-permute-done | bytes 21536 | tf_op jit(solution)/shard_map/ppermute | solution.py:120
  57.4 0.6 %multiply_convert_fusion = bf16[2,5376]{1,0:T(2,128)(2,1)} fusion(bf16[2,5376]{1,0:T(2,128)(2,1)S(1)} %collective-permute-done.14, bf16[4,5376]{1,0:T(4,128)(2,1)S(1)} %slice_add_fusion), kind=kLoop, calls=%fused_computation.12 | loop fusion | flops 43008 | bytes 64512 | tf_op jit(solution)/shard_map/convert_element_type | solution.py:330
  58.1 0.2 turn.1.scaled_ref
  58.3 0.0 collective-permute-done.11.got_ref
  58.3 0.9 %finish.1 = f32[2,32,1024]{2,1,0:T(8,128)} custom-call(f32[2,32,1024]{2,1,0:T(8,128)S(1)} %turn.1.scaled_ref, f32[2,64]{1,0:T(2,128)S(1)} %pad_maximum_fusion.7.own_ref, f32[2,64]{1,0:T(2,128)S(1)} %collective-permute-done.11.got_ref), custom_call_target="tpu_custom_call" | custom-call | tf_op jit(solution)/shard_map/finish/pallas_call | solution.py:277
  (22 shorter events, 0.3 us)
Async XLA Ops:
  0.6 12.1 %copy-start.3 = (bf16[2,5376]{1,0:T(2,128)(2,1)S(1)}, bf16[2,5376]{1,0:T(2,128)(2,1)}, u32[]{:S(2)}) copy-start(bf16[2,5376]{1,0:T(2,128)(2,1)} %param.8) | copy-start | bytes 64516
  0.6 12.1 %copy-start.4 = (bf16[2,5376]{1,0:T(2,128)(2,1)S(1)}, bf16[2,5376]{1,0:T(2,128)(2,1)}, u32[]{:S(2)}) copy-start(bf16[2,5376]{1,0:T(2,128)(2,1)} %param.7) | copy-start | bytes 64516
  0.7 8.3 %copy-start.5 = (f32[5376]{0:T(1024)S(1)}, f32[5376]{0:T(1024)}, u32[]{:S(2)}) copy-start(f32[5376]{0:T(1024)} %param.9) | copy-start | bytes 64516
  0.7 28.3 %copy-start.1 = (s32[2,32]{1,0:T(2,128)S(1)}, s32[2,32]{1,0:T(2,128)}, u32[]{:S(2)}) copy-start(s32[2,32]{1,0:T(2,128)} %class_ref.1) | copy-start | bytes 772
  0.7 28.3 %copy-start.2 = (f32[8]{0:T(128)S(1)}, f32[8]{0:T(128)}, u32[]{:S(2)}) copy-start(f32[8]{0:T(128)} %heat_ref.1) | copy-start | bytes 100
  1.5 7.4 %collective-permute-start = (bf16[4,5376]{1,0:T(4,128)(2,1)S(1)}, bf16[4,5376]{1,0:T(4,128)(2,1)S(1)}, u32[]{:S(2)}, u32[]{:S(2)}) collective-permute-start(bf16[4,5376]{1,0:T(4,128)(2,1)S(1)} %pad_maximum_fusion.4), channel_id=1, source_target_pairs={{0,8},{1,9},{2,10},{3,11},{4,12},{5,13},{6,14},{7,15},{8,0},{9,1},... | collective-permute-start | bytes 129032 | tf_op jit(solution)/shard_map/ppermute | solution.py:120
  5.6 0.7 %copy-start = (s32[2,32]{1,0:T(2,128)S(1)}, s32[2,32]{1,0:T(2,128)}, u32[]{:S(2)}) copy-start(s32[2,32]{1,0:T(2,128)} %ids_ref.1) | copy-start | bytes 772
  8.8 1.7 %collective-permute-start.2 = (bf16[32,5376]{1,0:T(8,128)(2,1)S(1)}, bf16[32,5376]{1,0:T(8,128)(2,1)S(1)}, u32[]{:S(2)}, u32[]{:S(2)}) collective-permute-start(bf16[32,5376]{1,0:T(8,128)(2,1)S(1)} %get-tuple-element.9), channel_id=1, source_target_pairs={{0,1},{1,0},{2,3},{3,2},{4,5},{5,4},{6,7},{7,6},{8,9},{9,8},{10,11... | collective-permute-start | bytes 1032200 | tf_op jit(solution)/shard_map/ppermute | solution.py:120
  10.7 5.1 %collective-permute-start.12 = (bf16[8,5376]{1,0:T(8,128)(2,1)S(1)}, bf16[8,5376]{1,0:T(8,128)(2,1)S(1)}, u32[]{:S(2)}, u32[]{:S(2)}) collective-permute-start(bf16[8,5376]{1,0:T(8,128)(2,1)S(1)} %get-tuple-element.20), channel_id=1, source_target_pairs={{0,2},{1,3},{2,0},{3,1},{4,6},{5,7},{6,4},{7,5},{8,10},{9,11},{10,... | collective-permute-start | bytes 258056 | tf_op jit(solution)/shard_map/ppermute | solution.py:120
  12.5 4.7 %collective-permute-start.3 = (bf16[8,5376]{1,0:T(8,128)(2,1)S(1)}, bf16[8,5376]{1,0:T(8,128)(2,1)S(1)}, u32[]{:S(2)}, u32[]{:S(2)}) collective-permute-start(bf16[8,5376]{1,0:T(8,128)(2,1)S(1)} %get-tuple-element.21), channel_id=1, source_target_pairs={{0,2},{1,3},{2,0},{3,1},{4,6},{5,7},{6,4},{7,5},{8,10},{9,11},{10,... | collective-permute-start | bytes 258056 | tf_op jit(solution)/shard_map/ppermute | solution.py:120
  12.9 4.7 %collective-permute-start.1 = (bf16[8,5376]{1,0:T(8,128)(2,1)S(1)}, bf16[8,5376]{1,0:T(8,128)(2,1)S(1)}, u32[]{:S(2)}, u32[]{:S(2)}) collective-permute-start(bf16[8,5376]{1,0:T(8,128)(2,1)S(1)} %pad_maximum_fusion), channel_id=1, source_target_pairs={{0,4},{1,5},{2,6},{3,7},{4,0},{5,1},{6,2},{7,3},{8,12},{9,13},{10,... | collective-permute-start | bytes 258056 | tf_op jit(solution)/shard_map/ppermute | solution.py:120
  17.2 7.2 %collective-permute-start.4 = (bf16[8,5376]{1,0:T(8,128)(2,1)S(1)}, bf16[8,5376]{1,0:T(8,128)(2,1)S(1)}, u32[]{:S(2)}, u32[]{:S(2)}) collective-permute-start(bf16[8,5376]{1,0:T(8,128)(2,1)S(1)} %get-tuple-element.19), channel_id=1, source_target_pairs={{0,8},{1,9},{2,10},{3,11},{4,12},{5,13},{6,14},{7,15},{8,0},{9,1},... | collective-permute-start | bytes 258056 | tf_op jit(solution)/shard_map/ppermute | solution.py:120
  24.4 4.6 %collective-permute-start.5 = (bf16[8,5376]{1,0:T(8,128)(2,1)S(1)}, bf16[8,5376]{1,0:T(8,128)(2,1)S(1)}, u32[]{:S(2)}, u32[]{:S(2)}) collective-permute-start(bf16[8,5376]{1,0:T(8,128)(2,1)S(1)} %add.35.own_ref), channel_id=1, source_target_pairs={{0,4},{1,5},{2,6},{3,7},{4,0},{5,1},{6,2},{7,3},{8,12},{9,13},{10,... | collective-permute-start | bytes 258056 | tf_op jit(solution)/shard_map/ppermute | solution.py:120
  29.9 5.5 %collective-permute-start.6 = (bf16[16,5376]{1,0:T(8,128)(2,1)S(1)}, bf16[16,5376]{1,0:T(8,128)(2,1)S(1)}, u32[]{:S(2)}, u32[]{:S(2)}) collective-permute-start(bf16[16,5376]{1,0:T(8,128)(2,1)S(1)} %get-tuple-element.10), channel_id=1, source_target_pairs={{0,2},{1,3},{2,0},{3,1},{4,6},{5,7},{6,4},{7,5},{8,10},{9,11},{10,... | collective-permute-start | bytes 516104 | tf_op jit(solution)/shard_map/ppermute | solution.py:120
  35.4 4.3 %collective-permute-start.7 = (bf16[32,5376]{1,0:T(8,128)(2,1)S(1)}, bf16[32,5376]{1,0:T(8,128)(2,1)S(1)}, u32[]{:S(2)}, u32[]{:S(2)}) collective-permute-start(bf16[32,5376]{1,0:T(8,128)(2,1)S(1)} %constant_dynamic-update-slice_fusion.own_ref), channel_id=1, source_target_pairs={{0,1},{1,0},{2,3},{3,2},{4,5},{5,4},{6,7},{7,6},{8,9},{9,8},{10,11... | collective-permute-start | bytes 1032200 | tf_op jit(solution)/shard_map/ppermute | solution.py:120
  42.9 4.5 %collective-permute-start.8 = (f32[2,64]{1,0:T(2,128)S(1)}, f32[2,64]{1,0:T(2,128)S(1)}, u32[]{:S(2)}, u32[]{:S(2)}) collective-permute-start(f32[2,64]{1,0:T(2,128)S(1)} %get-tuple-element.13), channel_id=1, source_target_pairs={{0,8},{1,9},{2,10},{3,11},{4,12},{5,13},{6,14},{7,15},{8,0},{9,1},... | collective-permute-start | bytes 1544 | tf_op jit(solution)/shard_map/ppermute | solution.py:120
  47.4 3.6 %collective-permute-start.9 = (f32[2,64]{1,0:T(2,128)S(1)}, f32[2,64]{1,0:T(2,128)S(1)}, u32[]{:S(2)}, u32[]{:S(2)}) collective-permute-start(f32[2,64]{1,0:T(2,128)S(1)} %pad_maximum_fusion.5), channel_id=1, source_target_pairs={{0,4},{1,5},{2,6},{3,7},{4,0},{5,1},{6,2},{7,3},{8,12},{9,13},{10,... | collective-permute-start | bytes 1544 | tf_op jit(solution)/shard_map/ppermute | solution.py:120
  47.7 4.9 %collective-permute-start.13 = (bf16[4,5376]{1,0:T(4,128)(2,1)S(1)}, bf16[4,5376]{1,0:T(4,128)(2,1)S(1)}, u32[]{:S(2)}, u32[]{:S(2)}) collective-permute-start(bf16[4,5376]{1,0:T(4,128)(2,1)S(1)} %slice.93), channel_id=1, source_target_pairs={{0,4},{1,5},{2,6},{3,7},{4,0},{5,1},{6,2},{7,3},{8,12},{9,13},{10,... | collective-permute-start | bytes 129032 | tf_op jit(solution)/shard_map/ppermute | solution.py:120
  51.1 3.6 %collective-permute-start.10 = (f32[2,64]{1,0:T(2,128)S(1)}, f32[2,64]{1,0:T(2,128)S(1)}, u32[]{:S(2)}, u32[]{:S(2)}) collective-permute-start(f32[2,64]{1,0:T(2,128)S(1)} %pad_maximum_fusion.6), channel_id=1, source_target_pairs={{0,2},{1,3},{2,0},{3,1},{4,6},{5,7},{6,4},{7,5},{8,10},{9,11},{10,... | collective-permute-start | bytes 1544 | tf_op jit(solution)/shard_map/ppermute | solution.py:120
  52.7 4.8 %collective-permute-start.14 = (bf16[2,5376]{1,0:T(2,128)(2,1)S(1)}, bf16[2,5376]{1,0:T(2,128)(2,1)S(1)}, u32[]{:S(2)}, u32[]{:S(2)}) collective-permute-start(bf16[2,5376]{1,0:T(2,128)(2,1)S(1)} %slice.95), channel_id=1, source_target_pairs={{0,8},{1,9},{2,10},{3,11},{4,12},{5,13},{6,14},{7,15},{8,0},{9,1},... | collective-permute-start | bytes 64520 | tf_op jit(solution)/shard_map/ppermute | solution.py:120
  54.7 3.6 %collective-permute-start.11 = (f32[2,64]{1,0:T(2,128)S(1)}, f32[2,64]{1,0:T(2,128)S(1)}, u32[]{:S(2)}, u32[]{:S(2)}) collective-permute-start(f32[2,64]{1,0:T(2,128)S(1)} %pad_maximum_fusion.7.own_ref), channel_id=1, source_target_pairs={{0,1},{1,0},{2,3},{3,2},{4,5},{5,4},{6,7},{7,6},{8,9},{9,8},{10,11... | collective-permute-start | bytes 1544 | tf_op jit(solution)/shard_map/ppermute | solution.py:120

commit v3 on v2

v3 whole, which is shorter than its diff:
```python
import functools
import math

import jax
import jax.numpy as jnp
from jax import lax
from jax.experimental import pallas as pl
from jax.experimental.pallas import tpu as pltpu
from jax.sharding import PartitionSpec as P

BLOCK = 16
MIB = 2**20


def reversed_bits(value, bits):
    out = 0
    for k in range(bits):
        out = out * 2 + (value >> k & 1)
    return out


def table_rows(rows, shards):
    bits = shards.bit_length() - 3
    dev = rows // shards
    return [
        (reversed_bits(q, bits) * 4 + y * 2 + c) * dev + j
        for c in range(2)
        for y in range(2)
        for q in range(shards // 4)
        for j in range(dev)
    ]


def pick_kernel(step, ids_ref, table_ref, after_ref, *refs):
    outs, (ids, listed, slots, rows, ids_sem, sems) = refs[:2], refs[2:]
    count = ids_ref.shape[1]
    held = slots.shape[0]
    voc_dev = table_ref.shape[0]
    shards = lax.axis_size("vocab")
    bits = shards.bit_length() - 3
    rows_dev = count // shards
    me = lax.axis_index("vocab")
    offset = me * voc_dev
    low = me % 4
    fetch = pltpu.make_async_copy(ids_ref, ids, ids_sem)
    fetch.start()
    rows[...] = jnp.zeros_like(rows)
    fetch.wait()

    def copy(n):
        base = pl.multiple_of(listed[n] // count // BLOCK * BLOCK, BLOCK)
        slot = n % held
        return pltpu.make_async_copy(
            table_ref.at[pl.ds(base, BLOCK)], slots.at[slot], sems.at[slot]
        )

    found = jnp.int32(0)
    for r in range(count):
        local = ids[step, r] - offset
        listed[found] = local * count + r
        found = found + ((local >= 0) & (local < voc_dev)).astype(jnp.int32)

    for first in range(0, count, held):
        last = jnp.minimum(found, first + held)

        @pl.loop(first, last)
        def _(n):
            copy(n).start()

        @pl.loop(first, last)
        def _(n):
            entry = listed[n]
            r = entry % count
            copy(n).wait()
            block = slots[n % held].astype(jnp.float32)
            sub = lax.broadcasted_iota(jnp.int32, block.shape, 0)
            picked = jnp.sum(
                jnp.where(sub == entry // count % BLOCK, block, 0.0), axis=0, keepdims=True
            )
            owner = r // rows_dev
            way = owner % 4 ^ low
            chip = owner // 4 if step == 0 else owner // 4 ^ me // 4
            order = sum((chip >> k) % 2 << (bits - 1 - k) for k in range(bits))
            place = (way % 2 * 2 + way // 2) * (shards // 4) + order
            rows[pl.ds(place * rows_dev + r % rows_dev, 1), :] = picked

    half = count // 2
    for part, out in enumerate(outs):
        out[...] = rows[part * half : (part + 1) * half].astype(out.dtype)


def picked_rows(ids, table, step, after):
    count = ids.shape[1]
    width = table.shape[1]
    held = min(count, 32)
    out = jax.ShapeDtypeStruct((count // 2, width), table.dtype)
    return pl.pallas_call(
        functools.partial(pick_kernel, step),
        out_shape=(out, out),
        in_specs=[pl.BlockSpec(memory_space=pl.ANY)] * 3,
        out_specs=(pl.BlockSpec(memory_space=pltpu.VMEM),) * 2,
        scratch_shapes=[
            pltpu.SMEM(ids.shape, jnp.int32),
            pltpu.SMEM((count + 1,), jnp.int32),
            pltpu.VMEM((held, BLOCK, width), table.dtype),
            pltpu.VMEM((count, width), jnp.float32),
            pltpu.SemaphoreType.DMA,
            pltpu.SemaphoreType.DMA((held,)),
        ],
        compiler_params=pltpu.CompilerParams(vmem_limit_bytes=16 * MIB),
        name="pick",
    )(in_hbm(ids), in_hbm(table), after)


def in_hbm(array):
    return pltpu.with_memory_space_constraint(array, pltpu.HBM)


def fold_kernel(keep_ref, got_ref, first_ref, delta_ref, own_ref, send_ref, beside_ref):
    total = keep_ref[...].astype(jnp.float32) + got_ref[...].astype(jnp.float32)
    half = own_ref.shape[0]
    own_ref[...] = total[:half].astype(own_ref.dtype)
    send_ref[...] = total[half:].astype(send_ref.dtype)
    beside_ref[...] = jnp.concatenate(
        [first_ref[...].astype(jnp.float32), delta_ref[...].astype(jnp.float32)], axis=0
    ).astype(beside_ref.dtype)


def folded(keep, got, first, deltas):
    rows, width = keep.shape
    vmem = pl.BlockSpec(memory_space=pltpu.VMEM)
    part = jax.ShapeDtypeStruct((rows // 2, width), keep.dtype)
    return pl.pallas_call(
        fold_kernel,
        out_shape=(part, part, jax.ShapeDtypeStruct((2 * first.shape[0], width), keep.dtype)),
        in_specs=[vmem] * 4,
        out_specs=(vmem,) * 3,
        compiler_params=pltpu.CompilerParams(vmem_limit_bytes=12 * MIB),
        name="fold",
    )(keep, got, first, deltas)


def swapped(rows, bit):
    pairs = [(i, i ^ bit) for i in range(lax.axis_size("vocab"))]
    return lax.ppermute(rows, "vocab", pairs)


def load_kernel(places, table_ref, class_ref, heat_ref, after_ref, out_ref, temps_ref, sems):
    parts = sems.shape[0]
    part = table_ref.shape[0] // parts
    copies = [
        pltpu.make_async_copy(
            table_ref.at[pl.ds(k * part, part)], out_ref.at[pl.ds(k * part, part)], sems.at[k]
        )
        for k in range(parts)
    ]
    for copy in copies:
        copy.start()
    temps = jnp.ones(temps_ref.shape, jnp.float32)
    lane = lax.broadcasted_iota(jnp.int32, temps.shape, 1)
    for place, (step, row) in enumerate(places):
        temps = jnp.where(lane == place, heat_ref[class_ref[step, row]], temps)
    temps_ref[...] = temps
    for copy in copies:
        copy.wait()


def loaded(table, classes, lookup, places, after):
    hbm, smem, vmem = (pl.BlockSpec(memory_space=m) for m in (pl.ANY, pltpu.SMEM, pltpu.VMEM))
    return pl.pallas_call(
        functools.partial(load_kernel, places),
        out_shape=(
            jax.ShapeDtypeStruct(table.shape, table.dtype),
            jax.ShapeDtypeStruct((1, len(places)), jnp.float32),
        ),
        in_specs=[hbm, smem, smem, hbm],
        out_specs=(vmem, vmem),
        scratch_shapes=[pltpu.SemaphoreType.DMA((8,))],
        compiler_params=pltpu.CompilerParams(vmem_limit_bytes=4 * MIB),
        cost_estimate=pl.CostEstimate(
            flops=0, bytes_accessed=table.size * table.dtype.itemsize, transcendentals=0
        ),
        name="load",
    )(in_hbm(table), classes, lookup, after)


def norm_kernel(first_ref, own_ref, got_ref, delta_ref, gain_ref, after_ref, out_ref):
    width = first_ref.shape[1]
    gain = gain_ref[...]

    def rescaled(hidden):
        squares = jnp.mean(hidden * hidden, axis=-1, keepdims=True)
        return hidden * lax.rsqrt(squares + 1e-06) * gain

    me = lax.axis_index("vocab")
    bits = lax.axis_size("vocab").bit_length() - 3

    def in_order(rows):
        for k in range(bits):
            size = rows.shape[0] >> k + 1
            parts = [rows[i * size : (i + 1) * size] for i in range(2 << k)]
            other = [parts[i ^ 1] for i in range(2 << k)]
            rows = jnp.where(
                me // 4 >> k & 1 != 0, jnp.concatenate(other), jnp.concatenate(parts)
            )
        return rows

    one = rescaled(in_order(first_ref[...].astype(jnp.float32)))
    picked = own_ref[...].astype(jnp.float32) + got_ref[...].astype(jnp.float32)
    embedded = (picked * math.sqrt(width)).astype(jnp.bfloat16)
    two = rescaled(
        embedded.astype(jnp.float32) + in_order(delta_ref[...].astype(jnp.float32))
    )
    out_ref[...] = jnp.concatenate([one, two], axis=0).astype(out_ref.dtype)


def normed(first, own, got, delta, gain, after):
    rows, width = first.shape
    vmem = pl.BlockSpec(memory_space=pltpu.VMEM)
    return pl.pallas_call(
        norm_kernel,
        out_shape=jax.ShapeDtypeStruct((2 * rows, width), jnp.bfloat16),
        in_specs=[vmem] * 5 + [pl.BlockSpec(memory_space=pl.ANY)],
        out_specs=vmem,
        compiler_params=pltpu.CompilerParams(vmem_limit_bytes=12 * MIB),
        name="norm",
    )(first, own, got, delta, gain.reshape(1, width), after)


def head_kernel(own_ref, got_ref, table_ref, temps_ref, after_ref, scaled_ref, stats_ref):
    me = lax.axis_index("vocab")
    half, width = own_ref.shape
    dims = (((1,), (1,)), ((), ()))
    own, got = own_ref[...], got_ref[...]
    block = half // 2

    def chips(rows):
        return jnp.where(
            me // 2 % 2 == 1, jnp.concatenate([rows[block:], rows[:block]], axis=0), rows
        )

    own, got = chips(own), chips(got)
    states = jnp.where(
        me % 2 == 1, jnp.concatenate([got, own], axis=0), jnp.concatenate([own, got], axis=0)
    )
    logits = lax.dot_general(table_ref[...], states, dims, preferred_element_type=jnp.float32)
    scaled = logits / temps_ref[...]
    scaled_ref[...] = scaled
    peak = jnp.max(scaled, axis=0, keepdims=True)
    stats_ref[0:1, :] = peak
    stats_ref[1:2, :] = jnp.sum(jnp.exp(scaled - peak), axis=0, keepdims=True)


def head(own, got, table, temps, after):
    voc_dev, width = table.shape
    rows = 2 * own.shape[0]
    return pl.pallas_call(
        head_kernel,
        out_shape=(
            jax.ShapeDtypeStruct((voc_dev, rows), jnp.float32),
            jax.ShapeDtypeStruct((2, rows), jnp.float32),
        ),
        in_specs=[pl.BlockSpec(memory_space=pltpu.VMEM)] * 4 + [pl.BlockSpec(memory_space=pl.ANY)],
        out_specs=(pl.BlockSpec(memory_space=pltpu.VMEM),) * 2,
        compiler_params=pltpu.CompilerParams(vmem_limit_bytes=30 * MIB),
        name="head",
    )(own, got, table, temps, after)


def turn_kernel(order, scaled_ref, out_ref):
    turned = scaled_ref[...].T
    for place, (step, row) in enumerate(order):
        out_ref[step, row : row + 1, :] = turned[place : place + 1]


def turned(scaled, order, steps):
    voc_dev, rows = scaled.shape
    return pl.pallas_call(
        functools.partial(turn_kernel, order),
        out_shape=jax.ShapeDtypeStruct((steps, rows // steps, voc_dev), jnp.float32),
        compiler_params=pltpu.CompilerParams(vmem_limit_bytes=12 * MIB),
        name="turn",
    )(scaled)


def finish_kernel(order, scaled_ref, own_ref, got_ref, out_ref):
    own, got = own_ref[...], got_ref[...]
    peak = jnp.maximum(own[0:1], got[0:1])
    total = own[1:2] * jnp.exp(own[0:1] - peak) + got[1:2] * jnp.exp(got[0:1] - peak)
    both = jnp.concatenate([peak, jnp.log(total)], axis=0)
    rows = both.shape[1]
    spread = jnp.broadcast_to(both[:, None, :], (2, 128, rows))
    peak, log = spread[0].T, spread[1].T
    voc_dev = out_ref.shape[2]
    peak = jnp.concatenate([peak] * (voc_dev // 128), axis=1)
    log = jnp.concatenate([log] * (voc_dev // 128), axis=1)
    for place, (step, row) in enumerate(order):
        at = slice(place, place + 1)
        out_ref[step, row : row + 1, :] = scaled_ref[step, row : row + 1, :] - peak[at] - log[at]


def finished(scaled, own, got, order):
    return pl.pallas_call(
        functools.partial(finish_kernel, order),
        out_shape=jax.ShapeDtypeStruct(scaled.shape, jnp.float32),
        compiler_params=pltpu.CompilerParams(vmem_limit_bytes=12 * MIB),
        name="finish",
    )(scaled, own, got)


def merged(own, got):
    peak = jnp.maximum(own[0], got[0])
    total = own[1] * jnp.exp(own[0] - peak) + got[1] * jnp.exp(got[0] - peak)
    return jnp.stack([peak, total])


def body(first, deltas, gain, table, lookup, classes, ids):
    shards = lax.axis_size("vocab")
    rows_dev, width = first.shape
    steps, rows = ids.shape
    quarter = rows // 4
    high = [1 << k for k in range(shards.bit_length() - 2, 1, -1)]

    order = table_rows(rows, shards)
    places = [
        (step, order[pair * quarter + k])
        for pair in range(4)
        for step in range(steps)
        for k in range(quarter)
    ]

    keep, send = picked_rows(ids, table, 0, ids)
    own, send, beside = folded(keep, swapped(send, 1), first, deltas)
    keep, away = picked_rows(ids, table, 1, own)
    own = own + swapped(send, 2)
    keep = keep + swapped(away, 1)
    following = keep[:quarter] + swapped(keep[quarter:], 2)
    state, delta = beside[:rows_dev], beside[rows_dev:]
    for k, bit in enumerate(high):
        held = state.shape[0]
        moved = swapped(beside, bit)
        got = swapped(own, bit)
        state = jnp.concatenate([state, moved[:held]], axis=0)
        delta = jnp.concatenate([delta, moved[held:]], axis=0)
        beside = jnp.concatenate([state, delta], axis=0)
        if k < len(high) - 1:
            own = own + got
    head_table, temps = loaded(table, classes, lookup, places, own)
    states = normed(state, own, got, delta, gain, temps)
    states = jnp.concatenate([states, swapped(states, 2)], axis=0)
    others = swapped(states, 1)
    for bit in reversed(high):
        half = following.shape[0] // 2
        following = following[:half] + swapped(following[half:], bit)
    embedded = (following.astype(jnp.float32) * math.sqrt(width)).astype(jnp.bfloat16)
    scaled, stats = head(states, others, head_table, temps, following)
    scaled = turned(scaled, places, steps)
    exchange = high + [2, 1]
    for bit in exchange[:-1]:
        stats = merged(stats, swapped(stats, bit))
    logprobs = finished(scaled, stats, swapped(stats, exchange[-1]), places)
    return logprobs, embedded


def solution(mesh):
    in_specs = (
        P(("groups", "vocab"), None),
        P(("groups", "vocab"), None),
        P(),
        P("vocab", None),
        P(),
        P(None, "groups"),
        P(None, "groups"),
    )
    out_specs = (P(None, "groups", "vocab"), P(("groups", "vocab"), None))
    return jax.shard_map(body, mesh=mesh, in_specs=in_specs, out_specs=out_specs, check_vma=False)
```

time: 59.2 us -> 53.8 us (0.909); the launches traced: 59.2 us -> 53 us
  waiting for transfers between devices: 29 us -> 19.7 us
  starting transfers between devices: 14.6 us -> 17 us
  Pallas kernels: 11.9 us -> 14.1 us
  other arithmetic: 1.93 us -> 1.12 us
  local copies, waits for them, and re-layouts: 0.87 us -> 0.2 us
    ppermute x15 -> x16, waiting for transfers between devices: 29 us -> 19.7 us  [swapped(): return lax.ppermute(rows, 'vocab', pairs)]
    ppermute x15 -> x16, starting transfers between devices: 14.6 us -> 17 us  [swapped(): return lax.ppermute(rows, 'vocab', pairs)]
    pallas_call x3 -> x5, Pallas kernels: 7.64 us -> 9.84 us  [the longest x1 4.79 us: loaded(): pl.pallas_call(functools.partial(load_kernel, places), out_shape=(jax.Sha...]
    concatenate x2, other arithmetic: 0.92 us -> 0.14 us  [the longest x1 0.1 us: body(): beside = jnp.concatenate([state, delta], axis=0)]
    unnamed x13 -> x10, local copies, waits for them, and re-layouts: 0.71 us -> 0.02 us
  transfers between devices with their start and end apart: 15 -> 16, of which waited for: 10 -> 10; matrix products, arithmetic and copies ran while one was open for 2% -> 2% of each run, Pallas kernels for 12% -> 14%
where the time goes in v3:
time: 53.8 us; the launch traced here: 53 us
  waiting for transfers between devices  19.7 us (37%)
  starting transfers between devices  17 us (32%)
  Pallas kernels  14.1 us (26%)
  other arithmetic  1.12 us (2%)
  between operations  0.9 us (2%)
    ppermute x16, waiting for transfers between devices, swapped(): return lax.ppermute(rows, 'vocab', pairs)  19.7 us
    ppermute x16, starting transfers between devices, swapped(): return lax.ppermute(rows, 'vocab', pairs)  17 us
    pallas_call x1, Pallas kernels, loaded(): pl.pallas_call(functools.partial(load_kernel, places), out_shape=(jax.Sha...  4.79 us
    pallas_call x2, Pallas kernels, picked_rows(): pl.pallas_call(functools.partial(pick_kernel, step), out_shape=(out, out)...  4.68 us
    pallas_call x1, Pallas kernels, head(): pl.pallas_call(head_kernel, out_shape=(jax.ShapeDtypeStruct((voc_dev, row...  3.15 us
  transfers between devices with their start and end apart: 16, of which 10 were waited for; matrix products, arithmetic and copies ran while one was open for 2% of the time, Pallas kernels for 14%

profile of v3, /device:TPU:0, one launch (start us, length us, event | category | flops | bytes accessed | tf_op | source)
XLA Modules:
  0.0 53.0 jit_solution(6294304197119903821)
XLA Ops:
  0.6 0.0 copy-start.1
  0.6 0.0 copy-start
  0.7 0.0 copy-start.4
  0.7 0.0 copy-start.2
  0.7 2.4 %pick.2 = (bf16[16,5376]{1,0:T(8,128)(2,1)S(1)}, bf16[16,5376]{1,0:T(8,128)(2,1)S(1)}) custom-call(s32[2,32]{1,0:T(2,128)} %ids_ref.3, bf16[1024,5376]{1,0:T(8,128)(2,1)} %table_ref.5, s32[2,32]{1,0:T(2,128)} %ids_ref.3), custom_call_target="tpu_custom_call" | custom-call | tf_op jit(solution)/shard_map/pick/pallas_call | solution.py:97
  3.0 0.6 %collective-permute-start = (bf16[16,5376]{1,0:T(8,128)(2,1)S(1)}, bf16[16,5376]{1,0:T(8,128)(2,1)S(1)}, u32[]{:S(2)}, u32[]{:S(2)}) collective-permute-start(bf16[16,5376]{1,0:T(8,128)(2,1)S(1)} %get-tuple-element.14), channel_id=1, source_target_pairs={{0,1},{1,0},{2,3},{3,2},{4,5},{5,4},{6,7},{7,6},{8,9},{9,8},{10,11... | collective-permute-start | bytes 516104 | tf_op jit(solution)/shard_map/ppermute | solution.py:145
  3.7 1.0 %collective-permute-done.got_ref = bf16[16,5376]{1,0:T(8,128)(2,1)S(1)} collective-permute-done((bf16[16,5376]{1,0:T(8,128)(2,1)S(1)}, bf16[16,5376]{1,0:T(8,128)(2,1)S(1)}, u32[]{:S(2)}, u32[]{:S(2)}) %collective-permute-start) | collective-permute-done | bytes 172064 | tf_op jit(solution)/shard_map/ppermute | solution.py:145
  4.7 0.1 fold.1
  4.8 3.9 %collective-permute-start.1 = (bf16[4,5376]{1,0:T(4,128)(2,1)S(1)}, bf16[4,5376]{1,0:T(4,128)(2,1)S(1)}, u32[]{:S(2)}, u32[]{:S(2)}) collective-permute-start(bf16[4,5376]{1,0:T(4,128)(2,1)S(1)} %get-tuple-element.15), channel_id=1, source_target_pairs={{0,8},{1,9},{2,10},{3,11},{4,12},{5,13},{6,14},{7,15},{8,0},{9,1},... | collective-permute-start | bytes 129032 | tf_op jit(solution)/shard_map/ppermute | solution.py:145
  8.7 1.7 %collective-permute-start.3 = (bf16[8,5376]{1,0:T(8,128)(2,1)S(1)}, bf16[8,5376]{1,0:T(8,128)(2,1)S(1)}, u32[]{:S(2)}, u32[]{:S(2)}) collective-permute-start(bf16[8,5376]{1,0:T(8,128)(2,1)S(1)} %get-tuple-element.17), channel_id=1, source_target_pairs={{0,2},{1,3},{2,0},{3,1},{4,6},{5,7},{6,4},{7,5},{8,10},{9,11},{10,... | collective-permute-start | bytes 258056 | tf_op jit(solution)/shard_map/ppermute | solution.py:145
  10.4 2.3 %pick.3 = (bf16[16,5376]{1,0:T(8,128)(2,1)S(1)}, bf16[16,5376]{1,0:T(8,128)(2,1)S(1)}) custom-call(s32[2,32]{1,0:T(2,128)} %ids_ref.3, bf16[1024,5376]{1,0:T(8,128)(2,1)} %table_ref.5, bf16[8,5376]{1,0:T(8,128)(2,1)S(1)} %get-tuple-element.16.after_ref), custom_call_target="tpu_custom_call" | custom-call | tf_op jit(solution)/shard_map/pick/pallas_call | solution.py:97
  12.7 0.1 collective-permute-start.8
  12.8 0.0 collective-permute-done.1
  12.9 0.1 pad_maximum_fusion.1
  13.0 1.1 %collective-permute-start.2 = (bf16[8,5376]{1,0:T(8,128)(2,1)S(1)}, bf16[8,5376]{1,0:T(8,128)(2,1)S(1)}, u32[]{:S(2)}, u32[]{:S(2)}) collective-permute-start(bf16[8,5376]{1,0:T(8,128)(2,1)S(1)} %pad_maximum_fusion.1), channel_id=1, source_target_pairs={{0,4},{1,5},{2,6},{3,7},{4,0},{5,1},{6,2},{7,3},{8,12},{9,13},{10,... | collective-permute-start | bytes 258056 | tf_op jit(solution)/shard_map/ppermute | solution.py:145
  14.1 0.0 copy-done.4
  14.1 0.0 collective-permute-done.3
  14.2 1.8 %collective-permute-start.4 = (bf16[8,5376]{1,0:T(8,128)(2,1)S(1)}, bf16[8,5376]{1,0:T(8,128)(2,1)S(1)}, u32[]{:S(2)}, u32[]{:S(2)}) collective-permute-start(bf16[8,5376]{1,0:T(8,128)(2,1)S(1)} %add.33), channel_id=1, source_target_pairs={{0,8},{1,9},{2,10},{3,11},{4,12},{5,13},{6,14},{7,15},{8,0},{9,1},... | collective-permute-start | bytes 258056 | tf_op jit(solution)/shard_map/ppermute | solution.py:145
  16.0 0.0 collective-permute-done.8
  16.1 1.7 %collective-permute-start.9 = (bf16[8,5376]{1,0:T(8,128)(2,1)S(1)}, bf16[8,5376]{1,0:T(8,128)(2,1)S(1)}, u32[]{:S(2)}, u32[]{:S(2)}) collective-permute-start(bf16[8,5376]{1,0:T(8,128)(2,1)S(1)} %slice.89), channel_id=1, source_target_pairs={{0,2},{1,3},{2,0},{3,1},{4,6},{5,7},{6,4},{7,5},{8,10},{9,11},{10,... | collective-permute-start | bytes 258056 | tf_op jit(solution)/shard_map/ppermute | solution.py:145
  17.7 1.2 %collective-permute-done.2 = bf16[8,5376]{1,0:T(8,128)(2,1)S(1)} collective-permute-done((bf16[8,5376]{1,0:T(8,128)(2,1)S(1)}, bf16[8,5376]{1,0:T(8,128)(2,1)S(1)}, u32[]{:S(2)}, u32[]{:S(2)}) %collective-permute-start.2) | collective-permute-done | bytes 86048 | tf_op jit(solution)/shard_map/ppermute | solution.py:145
  18.9 2.2 %collective-permute-done.4 = bf16[8,5376]{1,0:T(8,128)(2,1)S(1)} collective-permute-done((bf16[8,5376]{1,0:T(8,128)(2,1)S(1)}, bf16[8,5376]{1,0:T(8,128)(2,1)S(1)}, u32[]{:S(2)}, u32[]{:S(2)}) %collective-permute-start.4) | collective-permute-done | bytes 86048 | tf_op jit(solution)/shard_map/ppermute | solution.py:145
  21.2 0.1 collective-permute-start.5
  21.3 0.0 collective-permute-done.9
  21.3 2.1 %collective-permute-start.10 = (bf16[4,5376]{1,0:T(4,128)(2,1)S(1)}, bf16[4,5376]{1,0:T(4,128)(2,1)S(1)}, u32[]{:S(2)}, u32[]{:S(2)}) collective-permute-start(bf16[4,5376]{1,0:T(4,128)(2,1)S(1)} %slice.91), channel_id=1, source_target_pairs={{0,4},{1,5},{2,6},{3,7},{4,0},{5,1},{6,2},{7,3},{8,12},{9,13},{10,... | collective-permute-start | bytes 129032 | tf_op jit(solution)/shard_map/ppermute | solution.py:145
  23.4 0.1 pad_maximum_fusion.2
  23.6 4.8 %load.1 = (bf16[1024,5376]{1,0:T(8,128)(2,1)S(1)}, f32[1,64]{1,0:T(1,128)S(1)}) custom-call(bf16[1024,5376]{1,0:T(8,128)(2,1)} %table_ref.5, s32[2,32]{1,0:T(2,128)S(1)} %copy-done.2, f32[8]{0:T(128)S(1)} %copy-done.3, bf16[8,5376]{1,0:T(8,128)(2,1)S(1)} %add.34.after_ref.own_ref), custom_call_target="tpu_custom_call" | custom-call | bytes 11010048 | tf_op jit(solution)/shard_map/load/pallas_call | solution.py:170
  28.4 0.0 collective-permute-done.5.got_ref
  28.4 0.3 norm.1
  28.7 1.4 %collective-permute-start.6 = (bf16[16,5376]{1,0:T(8,128)(2,1)S(1)}, bf16[16,5376]{1,0:T(8,128)(2,1)S(1)}, u32[]{:S(2)}, u32[]{:S(2)}) collective-permute-start(bf16[16,5376]{1,0:T(8,128)(2,1)S(1)} %norm.1), channel_id=1, source_target_pairs={{0,2},{1,3},{2,0},{3,1},{4,6},{5,7},{6,4},{7,5},{8,10},{9,11},{10,... | collective-permute-start | bytes 516104 | tf_op jit(solution)/shard_map/ppermute | solution.py:145
  30.1 0.0 collective-permute-done.10
  30.2 0.5 %collective-permute-start.11 = (bf16[2,5376]{1,0:T(2,128)(2,1)S(1)}, bf16[2,5376]{1,0:T(2,128)(2,1)S(1)}, u32[]{:S(2)}, u32[]{:S(2)}) collective-permute-start(bf16[2,5376]{1,0:T(2,128)(2,1)S(1)} %slice.93), channel_id=1, source_target_pairs={{0,8},{1,9},{2,10},{3,11},{4,12},{5,13},{6,14},{7,15},{8,0},{9,1},... | collective-permute-start | bytes 64520 | tf_op jit(solution)/shard_map/ppermute | solution.py:145
  30.7 3.4 %collective-permute-done.6 = bf16[16,5376]{1,0:T(8,128)(2,1)S(1)} collective-permute-done((bf16[16,5376]{1,0:T(8,128)(2,1)S(1)}, bf16[16,5376]{1,0:T(8,128)(2,1)S(1)}, u32[]{:S(2)}, u32[]{:S(2)}) %collective-permute-start.6) | collective-permute-done | bytes 172064 | tf_op jit(solution)/shard_map/ppermute | solution.py:145
  34.2 0.1 collective-permute-start.7
  34.3 0.7 %collective-permute-done.11 = bf16[2,5376]{1,0:T(2,128)(2,1)S(1)} collective-permute-done((bf16[2,5376]{1,0:T(2,128)(2,1)S(1)}, bf16[2,5376]{1,0:T(2,128)(2,1)S(1)}, u32[]{:S(2)}, u32[]{:S(2)}) %collective-permute-start.11) | collective-permute-done | bytes 21536 | tf_op jit(solution)/shard_map/ppermute | solution.py:145
  34.9 0.6 %multiply_convert_fusion = (bf16[2,5376]{1,0:T(2,128)(2,1)}, bf16[2,5376]{1,0:T(2,128)(2,1)S(1)}) fusion(bf16[2,5376]{1,0:T(2,128)(2,1)S(1)} %collective-permute-done.11, bf16[4,5376]{1,0:T(4,128)(2,1)S(1)} %slice_add_fusion.1), kind=kLoop, calls=%fused_computation.7 | loop fusion | flops 43008 | bytes 86016 | tf_op jit(solution)/shard_map/convert_element_type | solution.py:355
  35.6 0.3 collective-permute-done.7.got_ref
  35.9 3.1 %head.1 = (f32[1024,64]{1,0:T(8,128)S(1)}, f32[2,64]{1,0:T(2,128)S(1)}) custom-call(bf16[32,5376]{1,0:T(8,128)(2,1)S(1)} %pad_maximum_fusion.own_ref, bf16[32,5376]{1,0:T(8,128)(2,1)S(1)} %collective-permute-done.7.got_ref, bf16[1024,5376]{1,0:T(8,128)(2,1)S(1)} %get-tuple-element.19.table_ref, f32[1,64]{1,0:T(1,128)S(1)} %get-tuple-element.18.after_ref.temps_ref, ...), custom_call_target="tpu_custom_call" | custom-call | tf_op jit(solution)/shard_map/head/pallas_call | solution.py:257
  39.0 0.3 collective-permute-start.12
  39.3 4.2 %collective-permute-done.12 = f32[2,64]{1,0:T(2,128)S(1)} collective-permute-done((f32[2,64]{1,0:T(2,128)S(1)}, f32[2,64]{1,0:T(2,128)S(1)}, u32[]{:S(2)}, u32[]{:S(2)}) %collective-permute-start.12) | collective-permute-done | bytes 544 | tf_op jit(solution)/shard_map/ppermute | solution.py:145
  43.6 0.1 collective-permute-start.13
  43.7 3.5 %collective-permute-done.13 = f32[2,64]{1,0:T(2,128)S(1)} collective-permute-done((f32[2,64]{1,0:T(2,128)S(1)}, f32[2,64]{1,0:T(2,128)S(1)}, u32[]{:S(2)}, u32[]{:S(2)}) %collective-permute-start.13) | collective-permute-done | bytes 544 | tf_op jit(solution)/shard_map/ppermute | solution.py:145
  47.3 1.5 %collective-permute-start.14 = (f32[2,64]{1,0:T(2,128)S(1)}, f32[2,64]{1,0:T(2,128)S(1)}, u32[]{:S(2)}, u32[]{:S(2)}) collective-permute-start(f32[2,64]{1,0:T(2,128)S(1)} %pad_maximum_fusion.6), channel_id=1, source_target_pairs={{0,2},{1,3},{2,0},{3,1},{4,6},{5,7},{6,4},{7,5},{8,10},{9,11},{10,... | collective-permute-start | bytes 1544 | tf_op jit(solution)/shard_map/ppermute | solution.py:145
  48.8 2.1 %collective-permute-done.14 = f32[2,64]{1,0:T(2,128)S(1)} collective-permute-done((f32[2,64]{1,0:T(2,128)S(1)}, f32[2,64]{1,0:T(2,128)S(1)}, u32[]{:S(2)}, u32[]{:S(2)}) %collective-permute-start.14) | collective-permute-done | bytes 544 | tf_op jit(solution)/shard_map/ppermute | solution.py:145
  50.9 0.1 collective-permute-start.15
  51.0 0.2 turn.1.scaled_ref
  51.2 0.9 %collective-permute-done.15.got_ref = f32[2,64]{1,0:T(2,128)S(1)} collective-permute-done((f32[2,64]{1,0:T(2,128)S(1)}, f32[2,64]{1,0:T(2,128)S(1)}, u32[]{:S(2)}, u32[]{:S(2)}) %collective-permute-start.15) | collective-permute-done | bytes 544 | tf_op jit(solution)/shard_map/ppermute | solution.py:145
  52.1 0.9 %finish.1 = f32[2,32,1024]{2,1,0:T(8,128)} custom-call(f32[2,32,1024]{2,1,0:T(8,128)S(1)} %turn.1.scaled_ref, f32[2,64]{1,0:T(2,128)S(1)} %pad_maximum_fusion.7.own_ref, f32[2,64]{1,0:T(2,128)S(1)} %collective-permute-done.15.got_ref), custom_call_target="tpu_custom_call" | custom-call | tf_op jit(solution)/shard_map/finish/pallas_call | solution.py:303
  (24 shorter events, 0.4 us)
Async XLA Ops:
  0.6 4.1 %copy-start.1 = (bf16[2,5376]{1,0:T(2,128)(2,1)S(1)}, bf16[2,5376]{1,0:T(2,128)(2,1)}, u32[]{:S(2)}) copy-start(bf16[2,5376]{1,0:T(2,128)(2,1)} %delta_ref.1) | copy-start | bytes 64516
  0.6 4.1 %copy-start = (bf16[2,5376]{1,0:T(2,128)(2,1)S(1)}, bf16[2,5376]{1,0:T(2,128)(2,1)}, u32[]{:S(2)}) copy-start(bf16[2,5376]{1,0:T(2,128)(2,1)} %first_ref.1) | copy-start | bytes 64516
  0.7 13.4 %copy-start.4 = (f32[5376]{0:T(1024)S(1)}, f32[5376]{0:T(1024)}, u32[]{:S(2)}) copy-start(f32[5376]{0:T(1024)} %param.9) | copy-start | bytes 64516
  0.7 22.9 %copy-start.2 = (s32[2,32]{1,0:T(2,128)S(1)}, s32[2,32]{1,0:T(2,128)}, u32[]{:S(2)}) copy-start(s32[2,32]{1,0:T(2,128)} %class_ref.1) | copy-start | bytes 772
  0.7 22.9 %copy-start.3 = (f32[8]{0:T(128)S(1)}, f32[8]{0:T(128)}, u32[]{:S(2)}) copy-start(f32[8]{0:T(128)} %heat_ref.1) | copy-start | bytes 100
  3.0 1.6 %collective-permute-start = (bf16[16,5376]{1,0:T(8,128)(2,1)S(1)}, bf16[16,5376]{1,0:T(8,128)(2,1)S(1)}, u32[]{:S(2)}, u32[]{:S(2)}) collective-permute-start(bf16[16,5376]{1,0:T(8,128)(2,1)S(1)} %get-tuple-element.14), channel_id=1, source_target_pairs={{0,1},{1,0},{2,3},{3,2},{4,5},{5,4},{6,7},{7,6},{8,9},{9,8},{10,11... | collective-permute-start | bytes 516104 | tf_op jit(solution)/shard_map/ppermute | solution.py:145
  4.8 8.0 %collective-permute-start.1 = (bf16[4,5376]{1,0:T(4,128)(2,1)S(1)}, bf16[4,5376]{1,0:T(4,128)(2,1)S(1)}, u32[]{:S(2)}, u32[]{:S(2)}) collective-permute-start(bf16[4,5376]{1,0:T(4,128)(2,1)S(1)} %get-tuple-element.15), channel_id=1, source_target_pairs={{0,8},{1,9},{2,10},{3,11},{4,12},{5,13},{6,14},{7,15},{8,0},{9,1},... | collective-permute-start | bytes 129032 | tf_op jit(solution)/shard_map/ppermute | solution.py:145
  8.7 5.4 %collective-permute-start.3 = (bf16[8,5376]{1,0:T(8,128)(2,1)S(1)}, bf16[8,5376]{1,0:T(8,128)(2,1)S(1)}, u32[]{:S(2)}, u32[]{:S(2)}) collective-permute-start(bf16[8,5376]{1,0:T(8,128)(2,1)S(1)} %get-tuple-element.17), channel_id=1, source_target_pairs={{0,2},{1,3},{2,0},{3,1},{4,6},{5,7},{6,4},{7,5},{8,10},{9,11},{10,... | collective-permute-start | bytes 258056 | tf_op jit(solution)/shard_map/ppermute | solution.py:145
  12.7 3.2 %collective-permute-start.8 = (bf16[16,5376]{1,0:T(8,128)(2,1)S(1)}, bf16[16,5376]{1,0:T(8,128)(2,1)S(1)}, u32[]{:S(2)}, u32[]{:S(2)}) collective-permute-start(bf16[16,5376]{1,0:T(8,128)(2,1)S(1)} %get-tuple-element.21), channel_id=1, source_target_pairs={{0,1},{1,0},{2,3},{3,2},{4,5},{5,4},{6,7},{7,6},{8,9},{9,8},{10,11... | collective-permute-start | bytes 516104 | tf_op jit(solution)/shard_map/ppermute | solution.py:145
  13.0 5.9 %collective-permute-start.2 = (bf16[8,5376]{1,0:T(8,128)(2,1)S(1)}, bf16[8,5376]{1,0:T(8,128)(2,1)S(1)}, u32[]{:S(2)}, u32[]{:S(2)}) collective-permute-start(bf16[8,5376]{1,0:T(8,128)(2,1)S(1)} %pad_maximum_fusion.1), channel_id=1, source_target_pairs={{0,4},{1,5},{2,6},{3,7},{4,0},{5,1},{6,2},{7,3},{8,12},{9,13},{10,... | collective-permute-start | bytes 258056 | tf_op jit(solution)/shard_map/ppermute | solution.py:145
  14.2 7.0 %collective-permute-start.4 = (bf16[8,5376]{1,0:T(8,128)(2,1)S(1)}, bf16[8,5376]{1,0:T(8,128)(2,1)S(1)}, u32[]{:S(2)}, u32[]{:S(2)}) collective-permute-start(bf16[8,5376]{1,0:T(8,128)(2,1)S(1)} %add.33), channel_id=1, source_target_pairs={{0,8},{1,9},{2,10},{3,11},{4,12},{5,13},{6,14},{7,15},{8,0},{9,1},... | collective-permute-start | bytes 258056 | tf_op jit(solution)/shard_map/ppermute | solution.py:145
  16.1 5.2 %collective-permute-start.9 = (bf16[8,5376]{1,0:T(8,128)(2,1)S(1)}, bf16[8,5376]{1,0:T(8,128)(2,1)S(1)}, u32[]{:S(2)}, u32[]{:S(2)}) collective-permute-start(bf16[8,5376]{1,0:T(8,128)(2,1)S(1)} %slice.89), channel_id=1, source_target_pairs={{0,2},{1,3},{2,0},{3,1},{4,6},{5,7},{6,4},{7,5},{8,10},{9,11},{10,... | collective-permute-start | bytes 258056 | tf_op jit(solution)/shard_map/ppermute | solution.py:145
  21.2 7.2 %collective-permute-start.5 = (bf16[8,5376]{1,0:T(8,128)(2,1)S(1)}, bf16[8,5376]{1,0:T(8,128)(2,1)S(1)}, u32[]{:S(2)}, u32[]{:S(2)}) collective-permute-start(bf16[8,5376]{1,0:T(8,128)(2,1)S(1)} %add.34.after_ref.own_ref), channel_id=1, source_target_pairs={{0,4},{1,5},{2,6},{3,7},{4,0},{5,1},{6,2},{7,3},{8,12},{9,13},{10,... | collective-permute-start | bytes 258056 | tf_op jit(solution)/shard_map/ppermute | solution.py:145
  21.3 8.8 %collective-permute-start.10 = (bf16[4,5376]{1,0:T(4,128)(2,1)S(1)}, bf16[4,5376]{1,0:T(4,128)(2,1)S(1)}, u32[]{:S(2)}, u32[]{:S(2)}) collective-permute-start(bf16[4,5376]{1,0:T(4,128)(2,1)S(1)} %slice.91), channel_id=1, source_target_pairs={{0,4},{1,5},{2,6},{3,7},{4,0},{5,1},{6,2},{7,3},{8,12},{9,13},{10,... | collective-permute-start | bytes 129032 | tf_op jit(solution)/shard_map/ppermute | solution.py:145
  28.7 5.5 %collective-permute-start.6 = (bf16[16,5376]{1,0:T(8,128)(2,1)S(1)}, bf16[16,5376]{1,0:T(8,128)(2,1)S(1)}, u32[]{:S(2)}, u32[]{:S(2)}) collective-permute-start(bf16[16,5376]{1,0:T(8,128)(2,1)S(1)} %norm.1), channel_id=1, source_target_pairs={{0,2},{1,3},{2,0},{3,1},{4,6},{5,7},{6,4},{7,5},{8,10},{9,11},{10,... | collective-permute-start | bytes 516104 | tf_op jit(solution)/shard_map/ppermute | solution.py:145
  30.2 4.8 %collective-permute-start.11 = (bf16[2,5376]{1,0:T(2,128)(2,1)S(1)}, bf16[2,5376]{1,0:T(2,128)(2,1)S(1)}, u32[]{:S(2)}, u32[]{:S(2)}) collective-permute-start(bf16[2,5376]{1,0:T(2,128)(2,1)S(1)} %slice.93), channel_id=1, source_target_pairs={{0,8},{1,9},{2,10},{3,11},{4,12},{5,13},{6,14},{7,15},{8,0},{9,1},... | collective-permute-start | bytes 64520 | tf_op jit(solution)/shard_map/ppermute | solution.py:145
  34.2 1.7 %collective-permute-start.7 = (bf16[32,5376]{1,0:T(8,128)(2,1)S(1)}, bf16[32,5376]{1,0:T(8,128)(2,1)S(1)}, u32[]{:S(2)}, u32[]{:S(2)}) collective-permute-start(bf16[32,5376]{1,0:T(8,128)(2,1)S(1)} %pad_maximum_fusion.own_ref), channel_id=1, source_target_pairs={{0,1},{1,0},{2,3},{3,2},{4,5},{5,4},{6,7},{7,6},{8,9},{9,8},{10,11... | collective-permute-start | bytes 1032200 | tf_op jit(solution)/shard_map/ppermute | solution.py:145
  39.0 4.5 %collective-permute-start.12 = (f32[2,64]{1,0:T(2,128)S(1)}, f32[2,64]{1,0:T(2,128)S(1)}, u32[]{:S(2)}, u32[]{:S(2)}) collective-permute-start(f32[2,64]{1,0:T(2,128)S(1)} %get-tuple-element.23), channel_id=1, source_target_pairs={{0,8},{1,9},{2,10},{3,11},{4,12},{5,13},{6,14},{7,15},{8,0},{9,1},... | collective-permute-start | bytes 1544 | tf_op jit(solution)/shard_map/ppermute | solution.py:145
  43.6 3.6 %collective-permute-start.13 = (f32[2,64]{1,0:T(2,128)S(1)}, f32[2,64]{1,0:T(2,128)S(1)}, u32[]{:S(2)}, u32[]{:S(2)}) collective-permute-start(f32[2,64]{1,0:T(2,128)S(1)} %pad_maximum_fusion.5), channel_id=1, source_target_pairs={{0,4},{1,5},{2,6},{3,7},{4,0},{5,1},{6,2},{7,3},{8,12},{9,13},{10,... | collective-permute-start | bytes 1544 | tf_op jit(solution)/shard_map/ppermute | solution.py:145
  47.3 3.6 %collective-permute-start.14 = (f32[2,64]{1,0:T(2,128)S(1)}, f32[2,64]{1,0:T(2,128)S(1)}, u32[]{:S(2)}, u32[]{:S(2)}) collective-permute-start(f32[2,64]{1,0:T(2,128)S(1)} %pad_maximum_fusion.6), channel_id=1, source_target_pairs={{0,2},{1,3},{2,0},{3,1},{4,6},{5,7},{6,4},{7,5},{8,10},{9,11},{10,... | collective-permute-start | bytes 1544 | tf_op jit(solution)/shard_map/ppermute | solution.py:145
  50.9 1.2 %collective-permute-start.15 = (f32[2,64]{1,0:T(2,128)S(1)}, f32[2,64]{1,0:T(2,128)S(1)}, u32[]{:S(2)}, u32[]{:S(2)}) collective-permute-start(f32[2,64]{1,0:T(2,128)S(1)} %pad_maximum_fusion.7.own_ref), channel_id=1, source_target_pairs={{0,1},{1,0},{2,3},{3,2},{4,5},{5,4},{6,7},{7,6},{8,9},{9,8},{10,11... | collective-permute-start | bytes 1544 | tf_op jit(solution)/shard_map/ppermute | solution.py:145

commit v4 on v3

--- a/solution.py
+++ b/solution.py
@@ -79,8 +79,9 @@
             )
             owner = r // rows_dev
             way = owner % 4 ^ low
-            chip = owner // 4 if step == 0 else owner // 4 ^ me // 4
-            order = sum((chip >> k) % 2 << (bits - 1 - k) for k in range(bits))
+            order = owner // 4 ^ me // 4
+            if step == 0:
+                order = sum((owner // 4 >> k) % 2 << (bits - 1 - k) for k in range(bits))
             place = (way % 2 * 2 + way // 2) * (shards // 4) + order
             rows[pl.ds(place * rows_dev + r % rows_dev, 1), :] = picked
 
@@ -140,6 +141,36 @@
     )(keep, got, first, deltas)
 
 
+def plus_kernel(own_ref, got_ref, after_ref, out_ref):
+    out_ref[...] = own_ref[...] + got_ref[...]
+
+
+def join_kernel(own_ref, got_ref, after_ref, out_ref):
+    half = own_ref.shape[0] // 2
+    own, got = own_ref[...].astype(jnp.float32), got_ref[...].astype(jnp.float32)
+    parts = [own[:half], got[:half], own[half:], got[half:]]
+    out_ref[...] = jnp.concatenate(parts, axis=0).astype(out_ref.dtype)
+
+
+def merge_kernel(own_ref, got_ref, after_ref, out_ref):
+    own, got = own_ref[...], got_ref[...]
+    peak = jnp.maximum(own[0:1], got[0:1])
+    out_ref[0:1, :] = peak
+    out_ref[1:2, :] = own[1:2] * jnp.exp(own[0:1] - peak) + got[1:2] * jnp.exp(got[0:1] - peak)
+
+
+def paired(kernel, own, got, after, rows, name):
+    vmem = pl.BlockSpec(memory_space=pltpu.VMEM)
+    return pl.pallas_call(
+        kernel,
+        out_shape=jax.ShapeDtypeStruct((rows, own.shape[1]), own.dtype),
+        in_specs=[vmem, vmem, pl.BlockSpec(memory_space=pl.ANY)],
+        out_specs=vmem,
+        compiler_params=pltpu.CompilerParams(vmem_limit_bytes=12 * MIB),
+        name=name,
+    )(own, got, after)
+
+
 def swapped(rows, bit):
     pairs = [(i, i ^ bit) for i in range(lax.axis_size("vocab"))]
     return lax.ppermute(rows, "vocab", pairs)
@@ -147,7 +178,7 @@
 
 def load_kernel(places, table_ref, class_ref, heat_ref, after_ref, out_ref, temps_ref, sems):
     parts = sems.shape[0]
-    part = table_ref.shape[0] // parts
+    part = out_ref.shape[0] // parts
     copies = [
         pltpu.make_async_copy(
             table_ref.at[pl.ds(k * part, part)], out_ref.at[pl.ds(k * part, part)], sems.at[k]
@@ -166,19 +197,22 @@
 
 
 def loaded(table, classes, lookup, places, after):
+    held = table.shape[0] // 8 * 5
     hbm, smem, vmem = (pl.BlockSpec(memory_space=m) for m in (pl.ANY, pltpu.SMEM, pltpu.VMEM))
     return pl.pallas_call(
         functools.partial(load_kernel, places),
         out_shape=(
-            jax.ShapeDtypeStruct(table.shape, table.dtype),
+            jax.ShapeDtypeStruct((held, table.shape[1]), table.dtype),
             jax.ShapeDtypeStruct((1, len(places)), jnp.float32),
         ),
         in_specs=[hbm, smem, smem, hbm],
         out_specs=(vmem, vmem),
-        scratch_shapes=[pltpu.SemaphoreType.DMA((8,))],
+        scratch_shapes=[pltpu.SemaphoreType.DMA((5,))],
         compiler_params=pltpu.CompilerParams(vmem_limit_bytes=4 * MIB),
         cost_estimate=pl.CostEstimate(
-            flops=0, bytes_accessed=table.size * table.dtype.itemsize, transcendentals=0
+            flops=0,
+            bytes_accessed=held * table.shape[1] * table.dtype.itemsize,
+            transcendentals=0,
         ),
         name="load",
     )(in_hbm(table), classes, lookup, after)
@@ -227,9 +261,22 @@
     )(first, own, got, delta, gain.reshape(1, width), after)
 
 
-def head_kernel(own_ref, got_ref, table_ref, temps_ref, after_ref, scaled_ref, stats_ref):
+def head_kernel(
+    own_ref, got_ref, held_ref, table_ref, temps_ref, after_ref, scaled_ref, stats_ref, rest, sems
+):
     me = lax.axis_index("vocab")
     half, width = own_ref.shape
+    first = held_ref.shape[0]
+    parts = sems.shape[0]
+    part = rest.shape[0] // parts
+    copies = [
+        pltpu.make_async_copy(
+            table_ref.at[pl.ds(first + k * part, part)], rest.at[pl.ds(k * part, part)], sems.at[k]
+        )
+        for k in range(parts)
+    ]
+    for copy in copies:
+        copy.start()
     dims = (((1,), (1,)), ((), ()))
     own, got = own_ref[...], got_ref[...]
     block = half // 2
@@ -243,28 +290,40 @@
     states = jnp.where(
         me % 2 == 1, jnp.concatenate([got, own], axis=0), jnp.concatenate([own, got], axis=0)
     )
-    logits = lax.dot_general(table_ref[...], states, dims, preferred_element_type=jnp.float32)
-    scaled = logits / temps_ref[...]
-    scaled_ref[...] = scaled
+
+    def scaled_part(rows):
+        logits = lax.dot_general(rows, states, dims, preferred_element_type=jnp.float32)
+        return logits / temps_ref[...]
+
+    scaled_ref[:first, :] = scaled_part(held_ref[...])
+    for copy in copies:
+        copy.wait()
+    scaled_ref[first:, :] = scaled_part(rest[...])
+    scaled = scaled_ref[...]
     peak = jnp.max(scaled, axis=0, keepdims=True)
     stats_ref[0:1, :] = peak
     stats_ref[1:2, :] = jnp.sum(jnp.exp(scaled - peak), axis=0, keepdims=True)
 
 
-def head(own, got, table, temps, after):
+def head(own, got, held, table, temps, after):
     voc_dev, width = table.shape
     rows = 2 * own.shape[0]
+    vmem, anywhere = pl.BlockSpec(memory_space=pltpu.VMEM), pl.BlockSpec(memory_space=pl.ANY)
     return pl.pallas_call(
         head_kernel,
         out_shape=(
             jax.ShapeDtypeStruct((voc_dev, rows), jnp.float32),
             jax.ShapeDtypeStruct((2, rows), jnp.float32),
         ),
-        in_specs=[pl.BlockSpec(memory_space=pltpu.VMEM)] * 4 + [pl.BlockSpec(memory_space=pl.ANY)],
-        out_specs=(pl.BlockSpec(memory_space=pltpu.VMEM),) * 2,
+        in_specs=[vmem] * 3 + [anywhere, vmem, anywhere],
+        out_specs=(vmem,) * 2,
+        scratch_shapes=[
+            pltpu.VMEM((voc_dev - held.shape[0], width), table.dtype),
+            pltpu.SemaphoreType.DMA((3,)),
+        ],
         compiler_params=pltpu.CompilerParams(vmem_limit_bytes=30 * MIB),
         name="head",
-    )(own, got, table, temps, after)
+    )(own, got, held, in_hbm(table), temps, after)
 
 
 def turn_kernel(order, scaled_ref, out_ref):
@@ -331,34 +390,34 @@
 
     keep, send = picked_rows(ids, table, 0, ids)
     own, send, beside = folded(keep, swapped(send, 1), first, deltas)
-    keep, away = picked_rows(ids, table, 1, own)
     own = own + swapped(send, 2)
-    keep = keep + swapped(away, 1)
-    following = keep[:quarter] + swapped(keep[quarter:], 2)
-    state, delta = beside[:rows_dev], beside[rows_dev:]
+    held_table, temps = loaded(table, classes, lookup, places, own)
     for k, bit in enumerate(high):
-        held = state.shape[0]
+        held = beside.shape[0] // 2
         moved = swapped(beside, bit)
         got = swapped(own, bit)
-        state = jnp.concatenate([state, moved[:held]], axis=0)
-        delta = jnp.concatenate([delta, moved[held:]], axis=0)
-        beside = jnp.concatenate([state, delta], axis=0)
         if k < len(high) - 1:
-            own = own + got
-    head_table, temps = loaded(table, classes, lookup, places, own)
-    states = normed(state, own, got, delta, gain, temps)
+            beside = paired(join_kernel, beside, moved, own, 4 * held, "join")
+            own = paired(plus_kernel, own, got, temps, quarter, "plus")
+    state = jnp.concatenate([beside[:held], moved[:held]], axis=0)
+    delta = jnp.concatenate([beside[held:], moved[held:]], axis=0)
+    keep, send = picked_rows(ids, table, 1, own)
+    states = normed(state, own, got, delta, gain, send)
+    keep = keep + swapped(send, 1)
+    following = keep[:quarter] + swapped(keep[quarter:], 2)
     states = jnp.concatenate([states, swapped(states, 2)], axis=0)
     others = swapped(states, 1)
-    for bit in reversed(high):
+    scaled, stats = head(states, others, held_table, table, temps, following)
+    scaled = turned(scaled, places, steps)
+    for bit in high:
         half = following.shape[0] // 2
         following = following[:half] + swapped(following[half:], bit)
     embedded = (following.astype(jnp.float32) * math.sqrt(width)).astype(jnp.bfloat16)
-    scaled, stats = head(states, others, head_table, temps, following)
-    scaled = turned(scaled, places, steps)
-    exchange = high + [2, 1]
-    for bit in exchange[:-1]:
+    for bit in high[:-1]:
         stats = merged(stats, swapped(stats, bit))
-    logprobs = finished(scaled, stats, swapped(stats, exchange[-1]), places)
+    stats = paired(merge_kernel, stats, swapped(stats, high[-1]), following, 2, "merge")
+    stats = merged(stats, swapped(stats, 2))
+    logprobs = finished(scaled, stats, swapped(stats, 1), places)
     return logprobs, embedded
 
 

time: 53.8 us -> 52.5 us (0.976); the launches traced: 53 us -> 52.4 us
  waiting for transfers between devices: 19.7 us -> 13.9 us
  starting transfers between devices: 17 us -> 21 us
  Pallas kernels: 14.1 us -> 15.5 us
    ppermute x16, waiting for transfers between devices: 19.7 us -> 13.9 us  [swapped(): return lax.ppermute(rows, 'vocab', pairs)]
    ppermute x16, starting transfers between devices: 17 us -> 21 us  [swapped(): return lax.ppermute(rows, 'vocab', pairs)]
    pallas_call x1, Pallas kernels: 3.15 us -> 5.44 us  [head(): pl.pallas_call(head_kernel, out_shape=(jax.ShapeDtypeStruct((voc_dev, row...]
    pallas_call x1, Pallas kernels: 4.79 us -> 3.59 us  [loaded(): pl.pallas_call(functools.partial(load_kernel, places), out_shape=(jax.Sha...]
  transfers between devices with their start and end apart: 16 -> 16, of which waited for: 10 -> 9; matrix products, arithmetic and copies ran while one was open for 2% -> 2% of each run, Pallas kernels for 14% -> 23%
where the time goes in v4:
time: 52.5 us; the launch traced here: 52.4 us
  starting transfers between devices  21 us (40%)
  Pallas kernels  15.5 us (30%)
  waiting for transfers between devices  13.9 us (26%)
  other arithmetic  0.9 us (2%)
  between operations  0.88 us (2%)
    ppermute x16, starting transfers between devices, swapped(): return lax.ppermute(rows, 'vocab', pairs)  21 us
    ppermute x16, waiting for transfers between devices, swapped(): return lax.ppermute(rows, 'vocab', pairs)  13.9 us
    pallas_call x1, Pallas kernels, head(): pl.pallas_call(head_kernel, out_shape=(jax.ShapeDtypeStruct((voc_dev, row...  5.44 us
    pallas_call x2, Pallas kernels, picked_rows(): pl.pallas_call(functools.partial(pick_kernel, step), out_shape=(out, out)...  4.95 us
    pallas_call x1, Pallas kernels, loaded(): pl.pallas_call(functools.partial(load_kernel, places), out_shape=(jax.Sha...  3.59 us
  transfers between devices with their start and end apart: 16, of which 9 were waited for; matrix products, arithmetic and copies ran while one was open for 2% of the time, Pallas kernels for 23%

profile of v4, /device:TPU:0, one launch (start us, length us, event | category | flops | bytes accessed | tf_op | source)
XLA Modules:
  0.0 52.4 jit_solution(13582185677478614611)
XLA Ops:
  0.6 0.0 copy-start
  0.6 0.0 copy-start.1
  0.7 0.0 copy-start.4
  0.7 0.0 copy-start.2
  0.7 0.0 copy-start.3
  0.7 2.5 %pick.2 = (bf16[16,5376]{1,0:T(8,128)(2,1)S(1)}, bf16[16,5376]{1,0:T(8,128)(2,1)S(1)}) custom-call(s32[2,32]{1,0:T(2,128)} %ids_ref.3, bf16[1024,5376]{1,0:T(8,128)(2,1)} %table_ref.7, s32[2,32]{1,0:T(2,128)} %ids_ref.3), custom_call_target="tpu_custom_call" | custom-call | tf_op jit(solution)/shard_map/pick/pallas_call | solution.py:98
  3.2 0.5 collective-permute-start
  3.7 1.0 %collective-permute-done.got_ref = bf16[16,5376]{1,0:T(8,128)(2,1)S(1)} collective-permute-done((bf16[16,5376]{1,0:T(8,128)(2,1)S(1)}, bf16[16,5376]{1,0:T(8,128)(2,1)S(1)}, u32[]{:S(2)}, u32[]{:S(2)}) %collective-permute-start) | collective-permute-done | bytes 172064 | tf_op jit(solution)/shard_map/ppermute | solution.py:176
  4.8 0.0 copy-done
  4.8 0.1 fold.1
  4.9 2.7 %collective-permute-start.2 = (bf16[8,5376]{1,0:T(8,128)(2,1)S(1)}, bf16[8,5376]{1,0:T(8,128)(2,1)S(1)}, u32[]{:S(2)}, u32[]{:S(2)}) collective-permute-start(bf16[8,5376]{1,0:T(8,128)(2,1)S(1)} %get-tuple-element.17), channel_id=1, source_target_pairs={{0,2},{1,3},{2,0},{3,1},{4,6},{5,7},{6,4},{7,5},{8,10},{9,11},{10,... | collective-permute-start | bytes 258056 | tf_op jit(solution)/shard_map/ppermute | solution.py:176
  7.5 2.2 %collective-permute-start.1 = (bf16[4,5376]{1,0:T(4,128)(2,1)S(1)}, bf16[4,5376]{1,0:T(4,128)(2,1)S(1)}, u32[]{:S(2)}, u32[]{:S(2)}) collective-permute-start(bf16[4,5376]{1,0:T(4,128)(2,1)S(1)} %get-tuple-element.15.own_ref), channel_id=1, source_target_pairs={{0,8},{1,9},{2,10},{3,11},{4,12},{5,13},{6,14},{7,15},{8,0},{9,1},... | collective-permute-start | bytes 129032 | tf_op jit(solution)/shard_map/ppermute | solution.py:176
  9.8 0.6 %collective-permute-done.2 = bf16[8,5376]{1,0:T(8,128)(2,1)S(1)} collective-permute-done((bf16[8,5376]{1,0:T(8,128)(2,1)S(1)}, bf16[8,5376]{1,0:T(8,128)(2,1)S(1)}, u32[]{:S(2)}, u32[]{:S(2)}) %collective-permute-start.2) | collective-permute-done | bytes 86048 | tf_op jit(solution)/shard_map/ppermute | solution.py:176
  10.4 2.9 %collective-permute-start.4 = (bf16[8,5376]{1,0:T(8,128)(2,1)S(1)}, bf16[8,5376]{1,0:T(8,128)(2,1)S(1)}, u32[]{:S(2)}, u32[]{:S(2)}) collective-permute-start(bf16[8,5376]{1,0:T(8,128)(2,1)S(1)} %add.23.after_ref.own_ref), channel_id=1, source_target_pairs={{0,8},{1,9},{2,10},{3,11},{4,12},{5,13},{6,14},{7,15},{8,0},{9,1},... | collective-permute-start | bytes 258056 | tf_op jit(solution)/shard_map/ppermute | solution.py:176
  13.3 0.0 collective-permute-done.1.got_ref
  13.3 1.9 %collective-permute-start.3 = (bf16[8,5376]{1,0:T(8,128)(2,1)S(1)}, bf16[8,5376]{1,0:T(8,128)(2,1)S(1)}, u32[]{:S(2)}, u32[]{:S(2)}) collective-permute-start(bf16[8,5376]{1,0:T(8,128)(2,1)S(1)} %join.1), channel_id=1, source_target_pairs={{0,4},{1,5},{2,6},{3,7},{4,0},{5,1},{6,2},{7,3},{8,12},{9,13},{10,... | collective-permute-start | bytes 258056 | tf_op jit(solution)/shard_map/ppermute | solution.py:176
  15.3 3.6 %load.1 = (bf16[640,5376]{1,0:T(8,128)(2,1)S(1)}, f32[1,64]{1,0:T(1,128)S(1)}) custom-call(bf16[1024,5376]{1,0:T(8,128)(2,1)} %table_ref.7, s32[2,32]{1,0:T(2,128)S(1)} %copy-done.2, f32[8]{0:T(128)S(1)} %copy-done.3, bf16[8,5376]{1,0:T(8,128)(2,1)S(1)} %add.23.after_ref.own_ref), custom_call_target="tpu_custom_call" | custom-call | bytes 6881280 | tf_op jit(solution)/shard_map/load/pallas_call | solution.py:202
  18.9 0.0 collective-permute-done.4.got_ref
  18.9 0.2 collective-permute-start.5
  19.2 2.4 %pick.3 = (bf16[16,5376]{1,0:T(8,128)(2,1)S(1)}, bf16[16,5376]{1,0:T(8,128)(2,1)S(1)}) custom-call(s32[2,32]{1,0:T(2,128)} %ids_ref.3, bf16[1024,5376]{1,0:T(8,128)(2,1)} %table_ref.7, bf16[8,5376]{1,0:T(8,128)(2,1)S(1)} %plus.1.after_ref.own_ref), custom_call_target="tpu_custom_call" | custom-call | tf_op jit(solution)/shard_map/pick/pallas_call | solution.py:98
  21.6 0.1 collective-permute-start.8
  21.7 0.0 collective-permute-done.3
  21.7 0.1 pad_maximum_fusion.1
  21.8 1.7 %collective-permute-done.5.got_ref = bf16[8,5376]{1,0:T(8,128)(2,1)S(1)} collective-permute-done((bf16[8,5376]{1,0:T(8,128)(2,1)S(1)}, bf16[8,5376]{1,0:T(8,128)(2,1)S(1)}, u32[]{:S(2)}, u32[]{:S(2)}) %collective-permute-start.5) | collective-permute-done | bytes 86048 | tf_op jit(solution)/shard_map/ppermute | solution.py:176
  23.5 0.3 norm.1
  23.8 1.8 %collective-permute-start.6 = (bf16[16,5376]{1,0:T(8,128)(2,1)S(1)}, bf16[16,5376]{1,0:T(8,128)(2,1)S(1)}, u32[]{:S(2)}, u32[]{:S(2)}) collective-permute-start(bf16[16,5376]{1,0:T(8,128)(2,1)S(1)} %norm.1), channel_id=1, source_target_pairs={{0,2},{1,3},{2,0},{3,1},{4,6},{5,7},{6,4},{7,5},{8,10},{9,11},{10,... | collective-permute-start | bytes 516104 | tf_op jit(solution)/shard_map/ppermute | solution.py:176
  25.6 0.0 collective-permute-done.8
  25.6 0.4 collective-permute-start.9
  26.0 3.9 %collective-permute-done.6 = bf16[16,5376]{1,0:T(8,128)(2,1)S(1)} collective-permute-done((bf16[16,5376]{1,0:T(8,128)(2,1)S(1)}, bf16[16,5376]{1,0:T(8,128)(2,1)S(1)}, u32[]{:S(2)}, u32[]{:S(2)}) %collective-permute-start.6) | collective-permute-done | bytes 172064 | tf_op jit(solution)/shard_map/ppermute | solution.py:176
  29.9 0.1 collective-permute-start.7
  30.0 0.8 %collective-permute-done.9 = bf16[8,5376]{1,0:T(8,128)(2,1)S(1)} collective-permute-done((bf16[8,5376]{1,0:T(8,128)(2,1)S(1)}, bf16[8,5376]{1,0:T(8,128)(2,1)S(1)}, u32[]{:S(2)}, u32[]{:S(2)}) %collective-permute-start.9) | collective-permute-done | bytes 86048 | tf_op jit(solution)/shard_map/ppermute | solution.py:176
  30.9 2.1 %collective-permute-start.12 = (bf16[4,5376]{1,0:T(4,128)(2,1)S(1)}, bf16[4,5376]{1,0:T(4,128)(2,1)S(1)}, u32[]{:S(2)}, u32[]{:S(2)}) collective-permute-start(bf16[4,5376]{1,0:T(4,128)(2,1)S(1)} %slice.83), channel_id=1, source_target_pairs={{0,8},{1,9},{2,10},{3,11},{4,12},{5,13},{6,14},{7,15},{8,0},{9,1},... | collective-permute-start | bytes 129032 | tf_op jit(solution)/shard_map/ppermute | solution.py:176
  33.0 0.0 collective-permute-done.7.got_ref
  33.0 5.4 %head.1 = (f32[1024,64]{1,0:T(8,128)S(1)}, f32[2,64]{1,0:T(2,128)S(1)}) custom-call(bf16[32,5376]{1,0:T(8,128)(2,1)S(1)} %pad_maximum_fusion.own_ref, bf16[32,5376]{1,0:T(8,128)(2,1)S(1)} %collective-permute-done.7.got_ref, bf16[640,5376]{1,0:T(8,128)(2,1)S(1)} %get-tuple-element.20.held_ref, bf16[1024,5376]{1,0:T(8,128)(2,1)} %table_ref.7, ...), custom_call_target="tpu_custom_call" | custom-call | tf_op jit(solution)/shard_map/head/pallas_call | solution.py:312
  38.4 0.9 %collective-permute-start.10 = (f32[2,64]{1,0:T(2,128)S(1)}, f32[2,64]{1,0:T(2,128)S(1)}, u32[]{:S(2)}, u32[]{:S(2)}) collective-permute-start(f32[2,64]{1,0:T(2,128)S(1)} %get-tuple-element.23), channel_id=1, source_target_pairs={{0,8},{1,9},{2,10},{3,11},{4,12},{5,13},{6,14},{7,15},{8,0},{9,1},... | collective-permute-start | bytes 1544 | tf_op jit(solution)/shard_map/ppermute | solution.py:176
  39.4 0.0 collective-permute-done.12
  39.4 1.7 %collective-permute-start.13 = (bf16[2,5376]{1,0:T(2,128)(2,1)S(1)}, bf16[2,5376]{1,0:T(2,128)(2,1)S(1)}, u32[]{:S(2)}, u32[]{:S(2)}) collective-permute-start(bf16[2,5376]{1,0:T(2,128)(2,1)S(1)} %slice.85), channel_id=1, source_target_pairs={{0,4},{1,5},{2,6},{3,7},{4,0},{5,1},{6,2},{7,3},{8,12},{9,13},{10,... | collective-permute-start | bytes 64520 | tf_op jit(solution)/shard_map/ppermute | solution.py:176
  41.1 1.8 %collective-permute-done.10 = f32[2,64]{1,0:T(2,128)S(1)} collective-permute-done((f32[2,64]{1,0:T(2,128)S(1)}, f32[2,64]{1,0:T(2,128)S(1)}, u32[]{:S(2)}, u32[]{:S(2)}) %collective-permute-start.10) | collective-permute-done | bytes 544 | tf_op jit(solution)/shard_map/ppermute | solution.py:176
  43.0 1.6 %collective-permute-start.11 = (f32[2,64]{1,0:T(2,128)S(1)}, f32[2,64]{1,0:T(2,128)S(1)}, u32[]{:S(2)}, u32[]{:S(2)}) collective-permute-start(f32[2,64]{1,0:T(2,128)S(1)} %pad_maximum_fusion.3.own_ref), channel_id=1, source_target_pairs={{0,4},{1,5},{2,6},{3,7},{4,0},{5,1},{6,2},{7,3},{8,12},{9,13},{10,... | collective-permute-start | bytes 1544 | tf_op jit(solution)/shard_map/ppermute | solution.py:176
  44.6 0.0 collective-permute-done.13
  44.6 0.6 %multiply_convert_fusion = (bf16[2,5376]{1,0:T(2,128)(2,1)}, bf16[2,5376]{1,0:T(2,128)(2,1)S(1)}) fusion(bf16[2,5376]{1,0:T(2,128)(2,1)S(1)} %collective-permute-done.13, bf16[4,5376]{1,0:T(4,128)(2,1)S(1)} %slice_add_fusion.1), kind=kLoop, calls=%fused_computation.5 | loop fusion | flops 43008 | bytes 86016 | tf_op jit(solution)/shard_map/convert_element_type | solution.py:415
  45.3 1.3 %collective-permute-done.11.got_ref = f32[2,64]{1,0:T(2,128)S(1)} collective-permute-done((f32[2,64]{1,0:T(2,128)S(1)}, f32[2,64]{1,0:T(2,128)S(1)}, u32[]{:S(2)}, u32[]{:S(2)}) %collective-permute-start.11) | collective-permute-done | bytes 544 | tf_op jit(solution)/shard_map/ppermute | solution.py:176
  46.6 1.8 %collective-permute-start.14 = (f32[2,64]{1,0:T(2,128)S(1)}, f32[2,64]{1,0:T(2,128)S(1)}, u32[]{:S(2)}, u32[]{:S(2)}) collective-permute-start(f32[2,64]{1,0:T(2,128)S(1)} %merge.1), channel_id=1, source_target_pairs={{0,2},{1,3},{2,0},{3,1},{4,6},{5,7},{6,4},{7,5},{8,10},{9,11},{10,... | collective-permute-start | bytes 1544 | tf_op jit(solution)/shard_map/ppermute | solution.py:176
  48.4 1.8 %collective-permute-done.14 = f32[2,64]{1,0:T(2,128)S(1)} collective-permute-done((f32[2,64]{1,0:T(2,128)S(1)}, f32[2,64]{1,0:T(2,128)S(1)}, u32[]{:S(2)}, u32[]{:S(2)}) %collective-permute-start.14) | collective-permute-done | bytes 544 | tf_op jit(solution)/shard_map/ppermute | solution.py:176
  50.3 0.1 collective-permute-start.15
  50.4 0.2 turn.1.scaled_ref
  50.6 0.9 %collective-permute-done.15.got_ref = f32[2,64]{1,0:T(2,128)S(1)} collective-permute-done((f32[2,64]{1,0:T(2,128)S(1)}, f32[2,64]{1,0:T(2,128)S(1)}, u32[]{:S(2)}, u32[]{:S(2)}) %collective-permute-start.15) | collective-permute-done | bytes 544 | tf_op jit(solution)/shard_map/ppermute | solution.py:176
  51.5 0.9 %finish.1 = f32[2,32,1024]{2,1,0:T(8,128)} custom-call(f32[2,32,1024]{2,1,0:T(8,128)S(1)} %turn.1.scaled_ref, f32[2,64]{1,0:T(2,128)S(1)} %pad_maximum_fusion.4.own_ref, f32[2,64]{1,0:T(2,128)S(1)} %collective-permute-done.15.got_ref), custom_call_target="tpu_custom_call" | custom-call | tf_op jit(solution)/shard_map/finish/pallas_call | solution.py:362
  (22 shorter events, 0.4 us)
Async XLA Ops:
  0.6 4.2 %copy-start = (bf16[2,5376]{1,0:T(2,128)(2,1)S(1)}, bf16[2,5376]{1,0:T(2,128)(2,1)}, u32[]{:S(2)}) copy-start(bf16[2,5376]{1,0:T(2,128)(2,1)} %first_ref.1) | copy-start | bytes 64516
  0.6 4.2 %copy-start.1 = (bf16[2,5376]{1,0:T(2,128)(2,1)S(1)}, bf16[2,5376]{1,0:T(2,128)(2,1)}, u32[]{:S(2)}) copy-start(bf16[2,5376]{1,0:T(2,128)(2,1)} %delta_ref.1) | copy-start | bytes 64516
  0.7 9.1 %copy-start.4 = (f32[5376]{0:T(1024)S(1)}, f32[5376]{0:T(1024)}, u32[]{:S(2)}) copy-start(f32[5376]{0:T(1024)} %param.9) | copy-start | bytes 64516
  0.7 14.6 %copy-start.2 = (s32[2,32]{1,0:T(2,128)S(1)}, s32[2,32]{1,0:T(2,128)}, u32[]{:S(2)}) copy-start(s32[2,32]{1,0:T(2,128)} %class_ref.1) | copy-start | bytes 772
  0.7 14.6 %copy-start.3 = (f32[8]{0:T(128)S(1)}, f32[8]{0:T(128)}, u32[]{:S(2)}) copy-start(f32[8]{0:T(128)} %heat_ref.1) | copy-start | bytes 100
  3.2 1.6 %collective-permute-start = (bf16[16,5376]{1,0:T(8,128)(2,1)S(1)}, bf16[16,5376]{1,0:T(8,128)(2,1)S(1)}, u32[]{:S(2)}, u32[]{:S(2)}) collective-permute-start(bf16[16,5376]{1,0:T(8,128)(2,1)S(1)} %get-tuple-element.14), channel_id=1, source_target_pairs={{0,1},{1,0},{2,3},{3,2},{4,5},{5,4},{6,7},{7,6},{8,9},{9,8},{10,11... | collective-permute-start | bytes 516104 | tf_op jit(solution)/shard_map/ppermute | solution.py:176
  4.9 5.5 %collective-permute-start.2 = (bf16[8,5376]{1,0:T(8,128)(2,1)S(1)}, bf16[8,5376]{1,0:T(8,128)(2,1)S(1)}, u32[]{:S(2)}, u32[]{:S(2)}) collective-permute-start(bf16[8,5376]{1,0:T(8,128)(2,1)S(1)} %get-tuple-element.17), channel_id=1, source_target_pairs={{0,2},{1,3},{2,0},{3,1},{4,6},{5,7},{6,4},{7,5},{8,10},{9,11},{10,... | collective-permute-start | bytes 258056 | tf_op jit(solution)/shard_map/ppermute | solution.py:176
  7.5 5.7 %collective-permute-start.1 = (bf16[4,5376]{1,0:T(4,128)(2,1)S(1)}, bf16[4,5376]{1,0:T(4,128)(2,1)S(1)}, u32[]{:S(2)}, u32[]{:S(2)}) collective-permute-start(bf16[4,5376]{1,0:T(4,128)(2,1)S(1)} %get-tuple-element.15.own_ref), channel_id=1, source_target_pairs={{0,8},{1,9},{2,10},{3,11},{4,12},{5,13},{6,14},{7,15},{8,0},{9,1},... | collective-permute-start | bytes 129032 | tf_op jit(solution)/shard_map/ppermute | solution.py:176
  10.4 8.5 %collective-permute-start.4 = (bf16[8,5376]{1,0:T(8,128)(2,1)S(1)}, bf16[8,5376]{1,0:T(8,128)(2,1)S(1)}, u32[]{:S(2)}, u32[]{:S(2)}) collective-permute-start(bf16[8,5376]{1,0:T(8,128)(2,1)S(1)} %add.23.after_ref.own_ref), channel_id=1, source_target_pairs={{0,8},{1,9},{2,10},{3,11},{4,12},{5,13},{6,14},{7,15},{8,0},{9,1},... | collective-permute-start | bytes 258056 | tf_op jit(solution)/shard_map/ppermute | solution.py:176
  13.3 8.3 %collective-permute-start.3 = (bf16[8,5376]{1,0:T(8,128)(2,1)S(1)}, bf16[8,5376]{1,0:T(8,128)(2,1)S(1)}, u32[]{:S(2)}, u32[]{:S(2)}) collective-permute-start(bf16[8,5376]{1,0:T(8,128)(2,1)S(1)} %join.1), channel_id=1, source_target_pairs={{0,4},{1,5},{2,6},{3,7},{4,0},{5,1},{6,2},{7,3},{8,12},{9,13},{10,... | collective-permute-start | bytes 258056 | tf_op jit(solution)/shard_map/ppermute | solution.py:176
  18.9 4.6 %collective-permute-start.5 = (bf16[8,5376]{1,0:T(8,128)(2,1)S(1)}, bf16[8,5376]{1,0:T(8,128)(2,1)S(1)}, u32[]{:S(2)}, u32[]{:S(2)}) collective-permute-start(bf16[8,5376]{1,0:T(8,128)(2,1)S(1)} %plus.1.after_ref.own_ref), channel_id=1, source_target_pairs={{0,4},{1,5},{2,6},{3,7},{4,0},{5,1},{6,2},{7,3},{8,12},{9,13},{10,... | collective-permute-start | bytes 258056 | tf_op jit(solution)/shard_map/ppermute | solution.py:176
  21.6 4.0 %collective-permute-start.8 = (bf16[16,5376]{1,0:T(8,128)(2,1)S(1)}, bf16[16,5376]{1,0:T(8,128)(2,1)S(1)}, u32[]{:S(2)}, u32[]{:S(2)}) collective-permute-start(bf16[16,5376]{1,0:T(8,128)(2,1)S(1)} %get-tuple-element.19.after_ref), channel_id=1, source_target_pairs={{0,1},{1,0},{2,3},{3,2},{4,5},{5,4},{6,7},{7,6},{8,9},{9,8},{10,11... | collective-permute-start | bytes 516104 | tf_op jit(solution)/shard_map/ppermute | solution.py:176
  23.8 6.1 %collective-permute-start.6 = (bf16[16,5376]{1,0:T(8,128)(2,1)S(1)}, bf16[16,5376]{1,0:T(8,128)(2,1)S(1)}, u32[]{:S(2)}, u32[]{:S(2)}) collective-permute-start(bf16[16,5376]{1,0:T(8,128)(2,1)S(1)} %norm.1), channel_id=1, source_target_pairs={{0,2},{1,3},{2,0},{3,1},{4,6},{5,7},{6,4},{7,5},{8,10},{9,11},{10,... | collective-permute-start | bytes 516104 | tf_op jit(solution)/shard_map/ppermute | solution.py:176
  25.6 5.2 %collective-permute-start.9 = (bf16[8,5376]{1,0:T(8,128)(2,1)S(1)}, bf16[8,5376]{1,0:T(8,128)(2,1)S(1)}, u32[]{:S(2)}, u32[]{:S(2)}) collective-permute-start(bf16[8,5376]{1,0:T(8,128)(2,1)S(1)} %slice.81), channel_id=1, source_target_pairs={{0,2},{1,3},{2,0},{3,1},{4,6},{5,7},{6,4},{7,5},{8,10},{9,11},{10,... | collective-permute-start | bytes 258056 | tf_op jit(solution)/shard_map/ppermute | solution.py:176
  29.9 3.1 %collective-permute-start.7 = (bf16[32,5376]{1,0:T(8,128)(2,1)S(1)}, bf16[32,5376]{1,0:T(8,128)(2,1)S(1)}, u32[]{:S(2)}, u32[]{:S(2)}) collective-permute-start(bf16[32,5376]{1,0:T(8,128)(2,1)S(1)} %pad_maximum_fusion.own_ref), channel_id=1, source_target_pairs={{0,1},{1,0},{2,3},{3,2},{4,5},{5,4},{6,7},{7,6},{8,9},{9,8},{10,11... | collective-permute-start | bytes 1032200 | tf_op jit(solution)/shard_map/ppermute | solution.py:176
  30.9 8.5 %collective-permute-start.12 = (bf16[4,5376]{1,0:T(4,128)(2,1)S(1)}, bf16[4,5376]{1,0:T(4,128)(2,1)S(1)}, u32[]{:S(2)}, u32[]{:S(2)}) collective-permute-start(bf16[4,5376]{1,0:T(4,128)(2,1)S(1)} %slice.83), channel_id=1, source_target_pairs={{0,8},{1,9},{2,10},{3,11},{4,12},{5,13},{6,14},{7,15},{8,0},{9,1},... | collective-permute-start | bytes 129032 | tf_op jit(solution)/shard_map/ppermute | solution.py:176
  38.4 4.5 %collective-permute-start.10 = (f32[2,64]{1,0:T(2,128)S(1)}, f32[2,64]{1,0:T(2,128)S(1)}, u32[]{:S(2)}, u32[]{:S(2)}) collective-permute-start(f32[2,64]{1,0:T(2,128)S(1)} %get-tuple-element.23), channel_id=1, source_target_pairs={{0,8},{1,9},{2,10},{3,11},{4,12},{5,13},{6,14},{7,15},{8,0},{9,1},... | collective-permute-start | bytes 1544 | tf_op jit(solution)/shard_map/ppermute | solution.py:176
  39.4 5.2 %collective-permute-start.13 = (bf16[2,5376]{1,0:T(2,128)(2,1)S(1)}, bf16[2,5376]{1,0:T(2,128)(2,1)S(1)}, u32[]{:S(2)}, u32[]{:S(2)}) collective-permute-start(bf16[2,5376]{1,0:T(2,128)(2,1)S(1)} %slice.85), channel_id=1, source_target_pairs={{0,4},{1,5},{2,6},{3,7},{4,0},{5,1},{6,2},{7,3},{8,12},{9,13},{10,... | collective-permute-start | bytes 64520 | tf_op jit(solution)/shard_map/ppermute | solution.py:176
  43.0 3.6 %collective-permute-start.11 = (f32[2,64]{1,0:T(2,128)S(1)}, f32[2,64]{1,0:T(2,128)S(1)}, u32[]{:S(2)}, u32[]{:S(2)}) collective-permute-start(f32[2,64]{1,0:T(2,128)S(1)} %pad_maximum_fusion.3.own_ref), channel_id=1, source_target_pairs={{0,4},{1,5},{2,6},{3,7},{4,0},{5,1},{6,2},{7,3},{8,12},{9,13},{10,... | collective-permute-start | bytes 1544 | tf_op jit(solution)/shard_map/ppermute | solution.py:176
  46.6 3.6 %collective-permute-start.14 = (f32[2,64]{1,0:T(2,128)S(1)}, f32[2,64]{1,0:T(2,128)S(1)}, u32[]{:S(2)}, u32[]{:S(2)}) collective-permute-start(f32[2,64]{1,0:T(2,128)S(1)} %merge.1), channel_id=1, source_target_pairs={{0,2},{1,3},{2,0},{3,1},{4,6},{5,7},{6,4},{7,5},{8,10},{9,11},{10,... | collective-permute-start | bytes 1544 | tf_op jit(solution)/shard_map/ppermute | solution.py:176
  50.3 1.2 %collective-permute-start.15 = (f32[2,64]{1,0:T(2,128)S(1)}, f32[2,64]{1,0:T(2,128)S(1)}, u32[]{:S(2)}, u32[]{:S(2)}) collective-permute-start(f32[2,64]{1,0:T(2,128)S(1)} %pad_maximum_fusion.4.own_ref), channel_id=1, source_target_pairs={{0,1},{1,0},{2,3},{3,2},{4,5},{5,4},{6,7},{7,6},{8,9},{9,8},{10,11... | collective-permute-start | bytes 1544 | tf_op jit(solution)/shard_map/ppermute | solution.py:176

commit v5 on v3

--- a/solution.py
+++ b/solution.py
@@ -79,8 +79,9 @@
             )
             owner = r // rows_dev
             way = owner % 4 ^ low
-            chip = owner // 4 if step == 0 else owner // 4 ^ me // 4
-            order = sum((chip >> k) % 2 << (bits - 1 - k) for k in range(bits))
+            order = owner // 4 ^ me // 4
+            if step == 0:
+                order = sum((owner // 4 >> k) % 2 << (bits - 1 - k) for k in range(bits))
             place = (way % 2 * 2 + way // 2) * (shards // 4) + order
             rows[pl.ds(place * rows_dev + r % rows_dev, 1), :] = picked
 
@@ -140,20 +141,55 @@
     )(keep, got, first, deltas)
 
 
+def plus_kernel(own_ref, got_ref, *refs):
+    out_ref = refs[-1]
+    out_ref[...] = own_ref[...] + got_ref[...]
+
+
+def join_kernel(own_ref, got_ref, *refs):
+    out_ref = refs[-1]
+    half = own_ref.shape[0] // 2
+    own, got = own_ref[...].astype(jnp.float32), got_ref[...].astype(jnp.float32)
+    parts = [own[:half], got[:half], own[half:], got[half:]]
+    out_ref[...] = jnp.concatenate(parts, axis=0).astype(out_ref.dtype)
+
+
+def chips_kernel(own_ref, got_ref, *refs):
+    out_ref = refs[-1]
+    own, got = own_ref[...], got_ref[...]
+    upper = lax.axis_index("vocab") // 2 % 2 == 1
+    rows = own.shape[0]
+    out_ref[:rows, :] = jnp.where(upper, got, own)
+    out_ref[rows:, :] = jnp.where(upper, own, got)
+
+
+def merge_kernel(own_ref, got_ref, *refs):
+    out_ref = refs[-1]
+    own, got = own_ref[...], got_ref[...]
+    peak = jnp.maximum(own[0:1], got[0:1])
+    out_ref[0:1, :] = peak
+    out_ref[1:2, :] = own[1:2] * jnp.exp(own[0:1] - peak) + got[1:2] * jnp.exp(got[0:1] - peak)
+
+
+def paired(kernel, own, got, rows, name, *after):
+    vmem = pl.BlockSpec(memory_space=pltpu.VMEM)
+    return pl.pallas_call(
+        kernel,
+        out_shape=jax.ShapeDtypeStruct((rows, own.shape[1]), own.dtype),
+        in_specs=[vmem] * 2 + [pl.BlockSpec(memory_space=pl.ANY)] * len(after),
+        out_specs=vmem,
+        compiler_params=pltpu.CompilerParams(vmem_limit_bytes=12 * MIB),
+        name=name,
+    )(own, got, *after)
+
+
 def swapped(rows, bit):
     pairs = [(i, i ^ bit) for i in range(lax.axis_size("vocab"))]
     return lax.ppermute(rows, "vocab", pairs)
 
 
 def load_kernel(places, table_ref, class_ref, heat_ref, after_ref, out_ref, temps_ref, sems):
-    parts = sems.shape[0]
-    part = table_ref.shape[0] // parts
-    copies = [
-        pltpu.make_async_copy(
-            table_ref.at[pl.ds(k * part, part)], out_ref.at[pl.ds(k * part, part)], sems.at[k]
-        )
-        for k in range(parts)
-    ]
+    copies = part_copies(table_ref, out_ref, sems, 0)
     for copy in copies:
         copy.start()
     temps = jnp.ones(temps_ref.shape, jnp.float32)
@@ -165,6 +201,25 @@
         copy.wait()
 
 
+def more_kernel(table_ref, held_ref, after_ref, out_ref, token_ref, sems):
+    copies = part_copies(table_ref, out_ref, sems, table_ref.shape[0] // 2)
+    for copy in copies:
+        copy.start()
+    token_ref[...] = jnp.zeros_like(token_ref)
+    for copy in copies:
+        copy.wait()
+
+
+def part_copies(table_ref, out_ref, sems, first):
+    parts = sems.shape[0]
+    part = table_ref.shape[0] // 2 // parts
+    rows = [pl.ds(first + k * part, part) for k in range(parts)]
+    return [
+        pltpu.make_async_copy(table_ref.at[at], out_ref.at[at], sems.at[k])
+        for k, at in enumerate(rows)
+    ]
+
+
 def loaded(table, classes, lookup, places, after):
     hbm, smem, vmem = (pl.BlockSpec(memory_space=m) for m in (pl.ANY, pltpu.SMEM, pltpu.VMEM))
     return pl.pallas_call(
@@ -175,16 +230,32 @@
         ),
         in_specs=[hbm, smem, smem, hbm],
         out_specs=(vmem, vmem),
-        scratch_shapes=[pltpu.SemaphoreType.DMA((8,))],
+        scratch_shapes=[pltpu.SemaphoreType.DMA((4,))],
         compiler_params=pltpu.CompilerParams(vmem_limit_bytes=4 * MIB),
-        cost_estimate=pl.CostEstimate(
-            flops=0, bytes_accessed=table.size * table.dtype.itemsize, transcendentals=0
-        ),
         name="load",
     )(in_hbm(table), classes, lookup, after)
 
 
-def norm_kernel(first_ref, own_ref, got_ref, delta_ref, gain_ref, after_ref, out_ref):
+def loaded_more(table, held, after):
+    anywhere, vmem = pl.BlockSpec(memory_space=pl.ANY), pl.BlockSpec(memory_space=pltpu.VMEM)
+    return pl.pallas_call(
+        more_kernel,
+        out_shape=(
+            jax.ShapeDtypeStruct(table.shape, table.dtype),
+            jax.ShapeDtypeStruct((8, 128), jnp.float32),
+        ),
+        in_specs=[anywhere, vmem, anywhere],
+        out_specs=(vmem, vmem),
+        input_output_aliases={1: 0},
+        scratch_shapes=[pltpu.SemaphoreType.DMA((4,))],
+        compiler_params=pltpu.CompilerParams(vmem_limit_bytes=4 * MIB),
+        name="more",
+    )(in_hbm(table), held, after)
+
+
+def norm_kernel(
+    first_ref, own_ref, got_ref, delta_ref, gain_ref, after_ref, also_ref, out_ref
+):
     width = first_ref.shape[1]
     gain = gain_ref[...]
 
@@ -214,32 +285,23 @@
     out_ref[...] = jnp.concatenate([one, two], axis=0).astype(out_ref.dtype)
 
 
-def normed(first, own, got, delta, gain, after):
+def normed(first, own, got, delta, gain, after, also):
     rows, width = first.shape
     vmem = pl.BlockSpec(memory_space=pltpu.VMEM)
     return pl.pallas_call(
         norm_kernel,
         out_shape=jax.ShapeDtypeStruct((2 * rows, width), jnp.bfloat16),
-        in_specs=[vmem] * 5 + [pl.BlockSpec(memory_space=pl.ANY)],
+        in_specs=[vmem] * 5 + [pl.BlockSpec(memory_space=pl.ANY)] * 2,
         out_specs=vmem,
         compiler_params=pltpu.CompilerParams(vmem_limit_bytes=12 * MIB),
         name="norm",
-    )(first, own, got, delta, gain.reshape(1, width), after)
-
-
-def head_kernel(own_ref, got_ref, table_ref, temps_ref, after_ref, scaled_ref, stats_ref):
+    )(first, own, got, delta, gain.reshape(1, width), after, also)
+
+
+def head_kernel(own_ref, got_ref, table_ref, temps_ref, scaled_ref, stats_ref):
     me = lax.axis_index("vocab")
-    half, width = own_ref.shape
     dims = (((1,), (1,)), ((), ()))
     own, got = own_ref[...], got_ref[...]
-    block = half // 2
-
-    def chips(rows):
-        return jnp.where(
-            me // 2 % 2 == 1, jnp.concatenate([rows[block:], rows[:block]], axis=0), rows
-        )
-
-    own, got = chips(own), chips(got)
     states = jnp.where(
         me % 2 == 1, jnp.concatenate([got, own], axis=0), jnp.concatenate([own, got], axis=0)
     )
@@ -251,7 +313,7 @@
     stats_ref[1:2, :] = jnp.sum(jnp.exp(scaled - peak), axis=0, keepdims=True)
 
 
-def head(own, got, table, temps, after):
+def head(own, got, table, temps):
     voc_dev, width = table.shape
     rows = 2 * own.shape[0]
     return pl.pallas_call(
@@ -260,11 +322,11 @@
             jax.ShapeDtypeStruct((voc_dev, rows), jnp.float32),
             jax.ShapeDtypeStruct((2, rows), jnp.float32),
         ),
-        in_specs=[pl.BlockSpec(memory_space=pltpu.VMEM)] * 4 + [pl.BlockSpec(memory_space=pl.ANY)],
+        in_specs=[pl.BlockSpec(memory_space=pltpu.VMEM)] * 4,
         out_specs=(pl.BlockSpec(memory_space=pltpu.VMEM),) * 2,
         compiler_params=pltpu.CompilerParams(vmem_limit_bytes=30 * MIB),
         name="head",
-    )(own, got, table, temps, after)
+    )(own, got, table, temps)
 
 
 def turn_kernel(order, scaled_ref, out_ref):
@@ -331,34 +393,38 @@
 
     keep, send = picked_rows(ids, table, 0, ids)
     own, send, beside = folded(keep, swapped(send, 1), first, deltas)
-    keep, away = picked_rows(ids, table, 1, own)
     own = own + swapped(send, 2)
-    keep = keep + swapped(away, 1)
+    keep, send = picked_rows(ids, table, 1, own)
+    keep = keep + swapped(send, 1)
     following = keep[:quarter] + swapped(keep[quarter:], 2)
-    state, delta = beside[:rows_dev], beside[rows_dev:]
     for k, bit in enumerate(high):
-        held = state.shape[0]
+        held = beside.shape[0] // 2
         moved = swapped(beside, bit)
         got = swapped(own, bit)
-        state = jnp.concatenate([state, moved[:held]], axis=0)
-        delta = jnp.concatenate([delta, moved[held:]], axis=0)
-        beside = jnp.concatenate([state, delta], axis=0)
         if k < len(high) - 1:
-            own = own + got
-    head_table, temps = loaded(table, classes, lookup, places, own)
-    states = normed(state, own, got, delta, gain, temps)
-    states = jnp.concatenate([states, swapped(states, 2)], axis=0)
+            beside = paired(join_kernel, beside, moved, 4 * held, "join", own)
+            own = paired(plus_kernel, own, got, quarter, "plus", send)
+    state = jnp.concatenate([beside[:held], moved[:held]], axis=0)
+    delta = jnp.concatenate([beside[held:], moved[held:]], axis=0)
+    held_table, temps = loaded(table, classes, lookup, places, own)
+    states = normed(state, own, got, delta, gain, temps, following)
+    held_table, token = loaded_more(table, held_table, states)
+    half = quarter // 2
+    away = swapped(following[half:], high[0])
+    states = paired(chips_kernel, states, swapped(states, 2), rows, "chips", token, away)
     others = swapped(states, 1)
-    for bit in reversed(high):
+    scaled, stats = head(states, others, held_table, temps)
+    following = paired(plus_kernel, following[:half], away, half, "plus", stats)
+    scaled = turned(scaled, places, steps)
+    for bit in high[1:]:
         half = following.shape[0] // 2
         following = following[:half] + swapped(following[half:], bit)
     embedded = (following.astype(jnp.float32) * math.sqrt(width)).astype(jnp.bfloat16)
-    scaled, stats = head(states, others, head_table, temps, following)
-    scaled = turned(scaled, places, steps)
-    exchange = high + [2, 1]
-    for bit in exchange[:-1]:
+    for bit in high[:-1]:
         stats = merged(stats, swapped(stats, bit))
-    logprobs = finished(scaled, stats, swapped(stats, exchange[-1]), places)
+    stats = paired(merge_kernel, stats, swapped(stats, high[-1]), 2, "merge", following)
+    stats = merged(stats, swapped(stats, 2))
+    logprobs = finished(scaled, stats, swapped(stats, 1), places)
     return logprobs, embedded
 
 

time: 53.8 us -> 49.8 us (0.926); the launches traced: 53 us -> 49.5 us
  waiting for transfers between devices: 19.7 us -> 10.9 us
  starting transfers between devices: 17 us -> 21.3 us
  Pallas kernels: 14.1 us -> 15.4 us
    ppermute x16, waiting for transfers between devices: 19.7 us -> 10.9 us  [swapped(): return lax.ppermute(rows, 'vocab', pairs)]
    ppermute x16, starting transfers between devices: 17 us -> 21.3 us  [swapped(): return lax.ppermute(rows, 'vocab', pairs)]
    pallas_call x0 -> x6, Pallas kernels: none -> 2.74 us  [the longest x1 2.62 us: loaded_more(): pl.pallas_call(more_kernel, out_shape=(jax.ShapeDtypeStruct(table.shape,...]
    pallas_call x1, Pallas kernels: 4.79 us -> 3.17 us  [loaded(): pl.pallas_call(functools.partial(load_kernel, places), out_shape=(jax.Sha...]
  transfers between devices with their start and end apart: 16 -> 16, of which waited for: 10 -> 9; matrix products, arithmetic and copies ran while one was open for 2% -> 2% of each run, Pallas kernels for 14% -> 17%
where the time goes in v5:
time: 49.8 us; the launch traced here: 49.5 us
  starting transfers between devices  21.3 us (43%)
  Pallas kernels  15.4 us (31%)
  waiting for transfers between devices  10.9 us (22%)
  between operations  0.89 us (2%)
  other arithmetic  0.85 us (2%)
    ppermute x16, starting transfers between devices, swapped(): return lax.ppermute(rows, 'vocab', pairs)  21.3 us
    ppermute x16, waiting for transfers between devices, swapped(): return lax.ppermute(rows, 'vocab', pairs)  10.9 us
    pallas_call x2, Pallas kernels, picked_rows(): pl.pallas_call(functools.partial(pick_kernel, step), out_shape=(out, out)...  4.86 us
    pallas_call x1, Pallas kernels, loaded(): pl.pallas_call(functools.partial(load_kernel, places), out_shape=(jax.Sha...  3.17 us
    pallas_call x1, Pallas kernels, head(): pl.pallas_call(head_kernel, out_shape=(jax.ShapeDtypeStruct((voc_dev, row...  3.15 us
    pallas_call x1, Pallas kernels, loaded_more(): pl.pallas_call(more_kernel, out_shape=(jax.ShapeDtypeStruct(table.shape,...  2.62 us
  transfers between devices with their start and end apart: 16, of which 9 were waited for; matrix products, arithmetic and copies ran while one was open for 2% of the time, Pallas kernels for 17%

profile of v5, /device:TPU:0, one launch (start us, length us, event | category | flops | bytes accessed | tf_op | source)
XLA Modules:
  0.0 49.5 jit_solution(67363707642205711)
XLA Ops:
  0.6 0.0 copy-start.1
  0.6 0.0 copy-start
  0.7 0.0 copy-start.4
  0.7 2.6 %pick.2 = (bf16[16,5376]{1,0:T(8,128)(2,1)S(1)}, bf16[16,5376]{1,0:T(8,128)(2,1)S(1)}) custom-call(s32[2,32]{1,0:T(2,128)} %ids_ref.3, bf16[1024,5376]{1,0:T(8,128)(2,1)} %table_ref.7, s32[2,32]{1,0:T(2,128)} %ids_ref.3), custom_call_target="tpu_custom_call" | custom-call | tf_op jit(solution)/shard_map/pick/pallas_call | solution.py:98
  3.3 0.2 collective-permute-start
  3.6 1.2 %collective-permute-done.got_ref = bf16[16,5376]{1,0:T(8,128)(2,1)S(1)} collective-permute-done((bf16[16,5376]{1,0:T(8,128)(2,1)S(1)}, bf16[16,5376]{1,0:T(8,128)(2,1)S(1)}, u32[]{:S(2)}, u32[]{:S(2)}) %collective-permute-start) | collective-permute-done | bytes 172064 | tf_op jit(solution)/shard_map/ppermute | solution.py:188
  4.8 0.0 copy-done.1
  4.8 0.1 fold.1
  4.9 2.8 %collective-permute-start.2 = (bf16[8,5376]{1,0:T(8,128)(2,1)S(1)}, bf16[8,5376]{1,0:T(8,128)(2,1)S(1)}, u32[]{:S(2)}, u32[]{:S(2)}) collective-permute-start(bf16[8,5376]{1,0:T(8,128)(2,1)S(1)} %get-tuple-element.19), channel_id=1, source_target_pairs={{0,2},{1,3},{2,0},{3,1},{4,6},{5,7},{6,4},{7,5},{8,10},{9,11},{10,... | collective-permute-start | bytes 258056 | tf_op jit(solution)/shard_map/ppermute | solution.py:188
  7.6 2.5 %collective-permute-start.1 = (bf16[4,5376]{1,0:T(4,128)(2,1)S(1)}, bf16[4,5376]{1,0:T(4,128)(2,1)S(1)}, u32[]{:S(2)}, u32[]{:S(2)}) collective-permute-start(bf16[4,5376]{1,0:T(4,128)(2,1)S(1)} %get-tuple-element.17.own_ref), channel_id=1, source_target_pairs={{0,8},{1,9},{2,10},{3,11},{4,12},{5,13},{6,14},{7,15},{8,0},{9,1},... | collective-permute-start | bytes 129032 | tf_op jit(solution)/shard_map/ppermute | solution.py:188
  10.1 0.0 copy-done.4
  10.2 0.3 collective-permute-done.2
  10.5 2.8 %collective-permute-start.4 = (bf16[8,5376]{1,0:T(8,128)(2,1)S(1)}, bf16[8,5376]{1,0:T(8,128)(2,1)S(1)}, u32[]{:S(2)}, u32[]{:S(2)}) collective-permute-start(bf16[8,5376]{1,0:T(8,128)(2,1)S(1)} %add.20.refs_0_.after_ref.own_ref), channel_id=1, source_target_pairs={{0,8},{1,9},{2,10},{3,11},{4,12},{5,13},{6,14},{7,15},{8,0},{9,1},... | collective-permute-start | bytes 258056 | tf_op jit(solution)/shard_map/ppermute | solution.py:188
  13.3 0.0 collective-permute-done.1.got_ref
  13.4 1.6 %collective-permute-start.3 = (bf16[8,5376]{1,0:T(8,128)(2,1)S(1)}, bf16[8,5376]{1,0:T(8,128)(2,1)S(1)}, u32[]{:S(2)}, u32[]{:S(2)}) collective-permute-start(bf16[8,5376]{1,0:T(8,128)(2,1)S(1)} %join.1), channel_id=1, source_target_pairs={{0,4},{1,5},{2,6},{3,7},{4,0},{5,1},{6,2},{7,3},{8,12},{9,13},{10,... | collective-permute-start | bytes 258056 | tf_op jit(solution)/shard_map/ppermute | solution.py:188
  15.0 2.2 %pick.3 = (bf16[16,5376]{1,0:T(8,128)(2,1)S(1)}, bf16[16,5376]{1,0:T(8,128)(2,1)S(1)}) custom-call(s32[2,32]{1,0:T(2,128)} %ids_ref.3, bf16[1024,5376]{1,0:T(8,128)(2,1)} %table_ref.7, bf16[8,5376]{1,0:T(8,128)(2,1)S(1)} %add.20.refs_0_.after_ref.own_ref), custom_call_target="tpu_custom_call" | custom-call | tf_op jit(solution)/shard_map/pick/pallas_call | solution.py:98
  17.3 0.1 collective-permute-start.6
  17.3 0.0 collective-permute-done.4.got_ref
  17.4 1.2 %collective-permute-start.5 = (bf16[8,5376]{1,0:T(8,128)(2,1)S(1)}, bf16[8,5376]{1,0:T(8,128)(2,1)S(1)}, u32[]{:S(2)}, u32[]{:S(2)}) collective-permute-start(bf16[8,5376]{1,0:T(8,128)(2,1)S(1)} %plus.2.after_ref.own_ref), channel_id=1, source_target_pairs={{0,4},{1,5},{2,6},{3,7},{4,0},{5,1},{6,2},{7,3},{8,12},{9,13},{10,... | collective-permute-start | bytes 258056 | tf_op jit(solution)/shard_map/ppermute | solution.py:188
  18.6 0.0 collective-permute-done.3
  18.6 0.1 collective-permute-done.6
  18.8 1.4 %collective-permute-start.7 = (bf16[8,5376]{1,0:T(8,128)(2,1)S(1)}, bf16[8,5376]{1,0:T(8,128)(2,1)S(1)}, u32[]{:S(2)}, u32[]{:S(2)}) collective-permute-start(bf16[8,5376]{1,0:T(8,128)(2,1)S(1)} %slice.81), channel_id=1, source_target_pairs={{0,2},{1,3},{2,0},{3,1},{4,6},{5,7},{6,4},{7,5},{8,10},{9,11},{10,... | collective-permute-start | bytes 258056 | tf_op jit(solution)/shard_map/ppermute | solution.py:188
  20.2 0.1 pad_maximum_fusion
  20.3 3.2 %load.1 = (bf16[1024,5376]{1,0:T(8,128)(2,1)S(1)}, f32[1,64]{1,0:T(1,128)S(1)}) custom-call(bf16[1024,5376]{1,0:T(8,128)(2,1)} %table_ref.7, s32[2,32]{1,0:T(2,128)S(1)} %copy-done.2, f32[8]{0:T(128)S(1)} %copy-done.3, bf16[8,5376]{1,0:T(8,128)(2,1)S(1)} %plus.2.after_ref.own_ref), custom_call_target="tpu_custom_call" | custom-call | tf_op jit(solution)/shard_map/load/pallas_call | solution.py:225
  23.4 0.0 collective-permute-done.7
  23.5 0.0 collective-permute-done.5.got_ref
  23.5 0.3 norm.1.after_ref.own_ref
  23.8 1.3 %collective-permute-start.8 = (bf16[16,5376]{1,0:T(8,128)(2,1)S(1)}, bf16[16,5376]{1,0:T(8,128)(2,1)S(1)}, u32[]{:S(2)}, u32[]{:S(2)}) collective-permute-start(bf16[16,5376]{1,0:T(8,128)(2,1)S(1)} %norm.1.after_ref.own_ref), channel_id=1, source_target_pairs={{0,2},{1,3},{2,0},{3,1},{4,6},{5,7},{6,4},{7,5},{8,10},{9,11},{10,... | collective-permute-start | bytes 516104 | tf_op jit(solution)/shard_map/ppermute | solution.py:188
  25.2 2.9 %collective-permute-start.9 = (bf16[4,5376]{1,0:T(4,128)(2,1)S(1)}, bf16[4,5376]{1,0:T(4,128)(2,1)S(1)}, u32[]{:S(2)}, u32[]{:S(2)}) collective-permute-start(bf16[4,5376]{1,0:T(4,128)(2,1)S(1)} %get-tuple-element.35), channel_id=1, source_target_pairs={{0,8},{1,9},{2,10},{3,11},{4,12},{5,13},{6,14},{7,15},{8,0},{9,1},... | collective-permute-start | bytes 129032 | tf_op jit(solution)/shard_map/ppermute | solution.py:188
  28.0 2.6 %more.1 = (bf16[1024,5376]{1,0:T(8,128)(2,1)S(1)}, f32[8,128]{1,0:T(8,128)S(1)}) custom-call(bf16[1024,5376]{1,0:T(8,128)(2,1)} %table_ref.7, bf16[1024,5376]{1,0:T(8,128)(2,1)S(1)} %get-tuple-element.23.held_ref, bf16[16,5376]{1,0:T(8,128)(2,1)S(1)} %norm.1.after_ref.own_ref), custom_call_target="tpu_custom_call", output_to_operand_aliasing={{0}: (1, {})} | custom-call | tf_op jit(solution)/shard_map/more/pallas_call | solution.py:241
  30.7 0.0 collective-permute-done.9.refs_1_.got_ref
  30.7 0.0 collective-permute-done.8.got_ref
  30.7 0.1 collective-permute-start.10
  30.8 1.6 %collective-permute-done.10.got_ref = bf16[32,5376]{1,0:T(8,128)(2,1)S(1)} collective-permute-done((bf16[32,5376]{1,0:T(8,128)(2,1)S(1)}, bf16[32,5376]{1,0:T(8,128)(2,1)S(1)}, u32[]{:S(2)}, u32[]{:S(2)}) %collective-permute-start.10) | collective-permute-done | bytes 344096 | tf_op jit(solution)/shard_map/ppermute | solution.py:188
  32.5 3.2 %head.1 = (f32[1024,64]{1,0:T(8,128)S(1)}, f32[2,64]{1,0:T(2,128)S(1)}) custom-call(bf16[32,5376]{1,0:T(8,128)(2,1)S(1)} %chips.1.own_ref, bf16[32,5376]{1,0:T(8,128)(2,1)S(1)} %collective-permute-done.10.got_ref, bf16[1024,5376]{1,0:T(8,128)(2,1)S(1)} %get-tuple-element.25.table_ref, f32[1,64]{1,0:T(1,128)S(1)} %get-tuple-element.21.after_ref.temps_ref), custom_call_target="tpu_custom_call" | custom-call | tf_op jit(solution)/shard_map/head/pallas_call | solution.py:319
  35.6 2.3 %collective-permute-start.11 = (f32[2,64]{1,0:T(2,128)S(1)}, f32[2,64]{1,0:T(2,128)S(1)}, u32[]{:S(2)}, u32[]{:S(2)}) collective-permute-start(f32[2,64]{1,0:T(2,128)S(1)} %get-tuple-element.27.refs_0_), channel_id=1, source_target_pairs={{0,8},{1,9},{2,10},{3,11},{4,12},{5,13},{6,14},{7,15},{8,0},{9,1},... | collective-permute-start | bytes 1544 | tf_op jit(solution)/shard_map/ppermute | solution.py:188
  38.0 0.6 %collective-permute-start.13 = (bf16[2,5376]{1,0:T(2,128)(2,1)S(1)}, bf16[2,5376]{1,0:T(2,128)(2,1)S(1)}, u32[]{:S(2)}, u32[]{:S(2)}) collective-permute-start(bf16[2,5376]{1,0:T(2,128)(2,1)S(1)} %slice.85), channel_id=1, source_target_pairs={{0,4},{1,5},{2,6},{3,7},{4,0},{5,1},{6,2},{7,3},{8,12},{9,13},{10,... | collective-permute-start | bytes 64520 | tf_op jit(solution)/shard_map/ppermute | solution.py:188
  38.6 1.6 %collective-permute-done.11 = f32[2,64]{1,0:T(2,128)S(1)} collective-permute-done((f32[2,64]{1,0:T(2,128)S(1)}, f32[2,64]{1,0:T(2,128)S(1)}, u32[]{:S(2)}, u32[]{:S(2)}) %collective-permute-start.11) | collective-permute-done | bytes 544 | tf_op jit(solution)/shard_map/ppermute | solution.py:188
  40.2 0.6 %collective-permute-start.12 = (f32[2,64]{1,0:T(2,128)S(1)}, f32[2,64]{1,0:T(2,128)S(1)}, u32[]{:S(2)}, u32[]{:S(2)}) collective-permute-start(f32[2,64]{1,0:T(2,128)S(1)} %pad_maximum_fusion.2.own_ref), channel_id=1, source_target_pairs={{0,4},{1,5},{2,6},{3,7},{4,0},{5,1},{6,2},{7,3},{8,12},{9,13},{10,... | collective-permute-start | bytes 1544 | tf_op jit(solution)/shard_map/ppermute | solution.py:188
  40.7 1.1 %collective-permute-done.13 = bf16[2,5376]{1,0:T(2,128)(2,1)S(1)} collective-permute-done((bf16[2,5376]{1,0:T(2,128)(2,1)S(1)}, bf16[2,5376]{1,0:T(2,128)(2,1)S(1)}, u32[]{:S(2)}, u32[]{:S(2)}) %collective-permute-start.13) | collective-permute-done | bytes 21536 | tf_op jit(solution)/shard_map/ppermute | solution.py:188
  41.8 0.6 %multiply_convert_fusion = (bf16[2,5376]{1,0:T(2,128)(2,1)}, bf16[2,5376]{1,0:T(2,128)(2,1)S(1)}) fusion(bf16[2,5376]{1,0:T(2,128)(2,1)S(1)} %collective-permute-done.13, bf16[4,5376]{1,0:T(4,128)(2,1)S(1)} %plus.3), kind=kLoop, calls=%fused_computation.3 | loop fusion | flops 43008 | bytes 86016 | tf_op jit(solution)/shard_map/convert_element_type | solution.py:422
  42.5 1.3 %collective-permute-done.12.got_ref = f32[2,64]{1,0:T(2,128)S(1)} collective-permute-done((f32[2,64]{1,0:T(2,128)S(1)}, f32[2,64]{1,0:T(2,128)S(1)}, u32[]{:S(2)}, u32[]{:S(2)}) %collective-permute-start.12) | collective-permute-done | bytes 544 | tf_op jit(solution)/shard_map/ppermute | solution.py:188
  43.8 0.9 %collective-permute-start.14 = (f32[2,64]{1,0:T(2,128)S(1)}, f32[2,64]{1,0:T(2,128)S(1)}, u32[]{:S(2)}, u32[]{:S(2)}) collective-permute-start(f32[2,64]{1,0:T(2,128)S(1)} %merge.1), channel_id=1, source_target_pairs={{0,2},{1,3},{2,0},{3,1},{4,6},{5,7},{6,4},{7,5},{8,10},{9,11},{10,... | collective-permute-start | bytes 1544 | tf_op jit(solution)/shard_map/ppermute | solution.py:188
  44.7 2.7 %collective-permute-done.14 = f32[2,64]{1,0:T(2,128)S(1)} collective-permute-done((f32[2,64]{1,0:T(2,128)S(1)}, f32[2,64]{1,0:T(2,128)S(1)}, u32[]{:S(2)}, u32[]{:S(2)}) %collective-permute-start.14) | collective-permute-done | bytes 544 | tf_op jit(solution)/shard_map/ppermute | solution.py:188
  47.5 0.1 collective-permute-start.15
  47.6 0.2 turn.1.scaled_ref
  47.8 0.9 %collective-permute-done.15.got_ref = f32[2,64]{1,0:T(2,128)S(1)} collective-permute-done((f32[2,64]{1,0:T(2,128)S(1)}, f32[2,64]{1,0:T(2,128)S(1)}, u32[]{:S(2)}, u32[]{:S(2)}) %collective-permute-start.15) | collective-permute-done | bytes 544 | tf_op jit(solution)/shard_map/ppermute | solution.py:188
  48.7 0.9 %finish.1 = f32[2,32,1024]{2,1,0:T(8,128)} custom-call(f32[2,32,1024]{2,1,0:T(8,128)S(1)} %turn.1.scaled_ref, f32[2,64]{1,0:T(2,128)S(1)} %pad_maximum_fusion.3.own_ref, f32[2,64]{1,0:T(2,128)S(1)} %collective-permute-done.15.got_ref), custom_call_target="tpu_custom_call" | custom-call | tf_op jit(solution)/shard_map/finish/pallas_call | solution.py:365
  (23 shorter events, 0.4 us)
Async XLA Ops:
  0.6 4.2 %copy-start.1 = (bf16[2,5376]{1,0:T(2,128)(2,1)S(1)}, bf16[2,5376]{1,0:T(2,128)(2,1)}, u32[]{:S(2)}) copy-start(bf16[2,5376]{1,0:T(2,128)(2,1)} %delta_ref.1) | copy-start | bytes 64516
  0.6 4.2 %copy-start = (bf16[2,5376]{1,0:T(2,128)(2,1)S(1)}, bf16[2,5376]{1,0:T(2,128)(2,1)}, u32[]{:S(2)}) copy-start(bf16[2,5376]{1,0:T(2,128)(2,1)} %first_ref.1) | copy-start | bytes 64516
  0.7 9.5 %copy-start.4 = (f32[5376]{0:T(1024)S(1)}, f32[5376]{0:T(1024)}, u32[]{:S(2)}) copy-start(f32[5376]{0:T(1024)} %param.9) | copy-start | bytes 64516
  0.7 19.6 %copy-start.2 = (s32[2,32]{1,0:T(2,128)S(1)}, s32[2,32]{1,0:T(2,128)}, u32[]{:S(2)}) copy-start(s32[2,32]{1,0:T(2,128)} %class_ref.1) | copy-start | bytes 772
  0.7 19.6 %copy-start.3 = (f32[8]{0:T(128)S(1)}, f32[8]{0:T(128)}, u32[]{:S(2)}) copy-start(f32[8]{0:T(128)} %heat_ref.1) | copy-start | bytes 100
  3.3 1.5 %collective-permute-start = (bf16[16,5376]{1,0:T(8,128)(2,1)S(1)}, bf16[16,5376]{1,0:T(8,128)(2,1)S(1)}, u32[]{:S(2)}, u32[]{:S(2)}) collective-permute-start(bf16[16,5376]{1,0:T(8,128)(2,1)S(1)} %get-tuple-element.16), channel_id=1, source_target_pairs={{0,1},{1,0},{2,3},{3,2},{4,5},{5,4},{6,7},{7,6},{8,9},{9,8},{10,11... | collective-permute-start | bytes 516104 | tf_op jit(solution)/shard_map/ppermute | solution.py:188
  4.9 5.6 %collective-permute-start.2 = (bf16[8,5376]{1,0:T(8,128)(2,1)S(1)}, bf16[8,5376]{1,0:T(8,128)(2,1)S(1)}, u32[]{:S(2)}, u32[]{:S(2)}) collective-permute-start(bf16[8,5376]{1,0:T(8,128)(2,1)S(1)} %get-tuple-element.19), channel_id=1, source_target_pairs={{0,2},{1,3},{2,0},{3,1},{4,6},{5,7},{6,4},{7,5},{8,10},{9,11},{10,... | collective-permute-start | bytes 258056 | tf_op jit(solution)/shard_map/ppermute | solution.py:188
  7.6 5.7 %collective-permute-start.1 = (bf16[4,5376]{1,0:T(4,128)(2,1)S(1)}, bf16[4,5376]{1,0:T(4,128)(2,1)S(1)}, u32[]{:S(2)}, u32[]{:S(2)}) collective-permute-start(bf16[4,5376]{1,0:T(4,128)(2,1)S(1)} %get-tuple-element.17.own_ref), channel_id=1, source_target_pairs={{0,8},{1,9},{2,10},{3,11},{4,12},{5,13},{6,14},{7,15},{8,0},{9,1},... | collective-permute-start | bytes 129032 | tf_op jit(solution)/shard_map/ppermute | solution.py:188
  10.5 6.8 %collective-permute-start.4 = (bf16[8,5376]{1,0:T(8,128)(2,1)S(1)}, bf16[8,5376]{1,0:T(8,128)(2,1)S(1)}, u32[]{:S(2)}, u32[]{:S(2)}) collective-permute-start(bf16[8,5376]{1,0:T(8,128)(2,1)S(1)} %add.20.refs_0_.after_ref.own_ref), channel_id=1, source_target_pairs={{0,8},{1,9},{2,10},{3,11},{4,12},{5,13},{6,14},{7,15},{8,0},{9,1},... | collective-permute-start | bytes 258056 | tf_op jit(solution)/shard_map/ppermute | solution.py:188
  13.4 5.2 %collective-permute-start.3 = (bf16[8,5376]{1,0:T(8,128)(2,1)S(1)}, bf16[8,5376]{1,0:T(8,128)(2,1)S(1)}, u32[]{:S(2)}, u32[]{:S(2)}) collective-permute-start(bf16[8,5376]{1,0:T(8,128)(2,1)S(1)} %join.1), channel_id=1, source_target_pairs={{0,4},{1,5},{2,6},{3,7},{4,0},{5,1},{6,2},{7,3},{8,12},{9,13},{10,... | collective-permute-start | bytes 258056 | tf_op jit(solution)/shard_map/ppermute | solution.py:188
  17.3 1.5 %collective-permute-start.6 = (bf16[16,5376]{1,0:T(8,128)(2,1)S(1)}, bf16[16,5376]{1,0:T(8,128)(2,1)S(1)}, u32[]{:S(2)}, u32[]{:S(2)}) collective-permute-start(bf16[16,5376]{1,0:T(8,128)(2,1)S(1)} %get-tuple-element.20.refs_0_), channel_id=1, source_target_pairs={{0,1},{1,0},{2,3},{3,2},{4,5},{5,4},{6,7},{7,6},{8,9},{9,8},{10,11... | collective-permute-start | bytes 516104 | tf_op jit(solution)/shard_map/ppermute | solution.py:188
  17.4 6.1 %collective-permute-start.5 = (bf16[8,5376]{1,0:T(8,128)(2,1)S(1)}, bf16[8,5376]{1,0:T(8,128)(2,1)S(1)}, u32[]{:S(2)}, u32[]{:S(2)}) collective-permute-start(bf16[8,5376]{1,0:T(8,128)(2,1)S(1)} %plus.2.after_ref.own_ref), channel_id=1, source_target_pairs={{0,4},{1,5},{2,6},{3,7},{4,0},{5,1},{6,2},{7,3},{8,12},{9,13},{10,... | collective-permute-start | bytes 258056 | tf_op jit(solution)/shard_map/ppermute | solution.py:188
  18.8 4.7 %collective-permute-start.7 = (bf16[8,5376]{1,0:T(8,128)(2,1)S(1)}, bf16[8,5376]{1,0:T(8,128)(2,1)S(1)}, u32[]{:S(2)}, u32[]{:S(2)}) collective-permute-start(bf16[8,5376]{1,0:T(8,128)(2,1)S(1)} %slice.81), channel_id=1, source_target_pairs={{0,2},{1,3},{2,0},{3,1},{4,6},{5,7},{6,4},{7,5},{8,10},{9,11},{10,... | collective-permute-start | bytes 258056 | tf_op jit(solution)/shard_map/ppermute | solution.py:188
  23.8 6.9 %collective-permute-start.8 = (bf16[16,5376]{1,0:T(8,128)(2,1)S(1)}, bf16[16,5376]{1,0:T(8,128)(2,1)S(1)}, u32[]{:S(2)}, u32[]{:S(2)}) collective-permute-start(bf16[16,5376]{1,0:T(8,128)(2,1)S(1)} %norm.1.after_ref.own_ref), channel_id=1, source_target_pairs={{0,2},{1,3},{2,0},{3,1},{4,6},{5,7},{6,4},{7,5},{8,10},{9,11},{10,... | collective-permute-start | bytes 516104 | tf_op jit(solution)/shard_map/ppermute | solution.py:188
  25.2 5.5 %collective-permute-start.9 = (bf16[4,5376]{1,0:T(4,128)(2,1)S(1)}, bf16[4,5376]{1,0:T(4,128)(2,1)S(1)}, u32[]{:S(2)}, u32[]{:S(2)}) collective-permute-start(bf16[4,5376]{1,0:T(4,128)(2,1)S(1)} %get-tuple-element.35), channel_id=1, source_target_pairs={{0,8},{1,9},{2,10},{3,11},{4,12},{5,13},{6,14},{7,15},{8,0},{9,1},... | collective-permute-start | bytes 129032 | tf_op jit(solution)/shard_map/ppermute | solution.py:188
  30.7 1.7 %collective-permute-start.10 = (bf16[32,5376]{1,0:T(8,128)(2,1)S(1)}, bf16[32,5376]{1,0:T(8,128)(2,1)S(1)}, u32[]{:S(2)}, u32[]{:S(2)}) collective-permute-start(bf16[32,5376]{1,0:T(8,128)(2,1)S(1)} %chips.1.own_ref), channel_id=1, source_target_pairs={{0,1},{1,0},{2,3},{3,2},{4,5},{5,4},{6,7},{7,6},{8,9},{9,8},{10,11... | collective-permute-start | bytes 1032200 | tf_op jit(solution)/shard_map/ppermute | solution.py:188
  35.6 4.5 %collective-permute-start.11 = (f32[2,64]{1,0:T(2,128)S(1)}, f32[2,64]{1,0:T(2,128)S(1)}, u32[]{:S(2)}, u32[]{:S(2)}) collective-permute-start(f32[2,64]{1,0:T(2,128)S(1)} %get-tuple-element.27.refs_0_), channel_id=1, source_target_pairs={{0,8},{1,9},{2,10},{3,11},{4,12},{5,13},{6,14},{7,15},{8,0},{9,1},... | collective-permute-start | bytes 1544 | tf_op jit(solution)/shard_map/ppermute | solution.py:188
  38.0 3.9 %collective-permute-start.13 = (bf16[2,5376]{1,0:T(2,128)(2,1)S(1)}, bf16[2,5376]{1,0:T(2,128)(2,1)S(1)}, u32[]{:S(2)}, u32[]{:S(2)}) collective-permute-start(bf16[2,5376]{1,0:T(2,128)(2,1)S(1)} %slice.85), channel_id=1, source_target_pairs={{0,4},{1,5},{2,6},{3,7},{4,0},{5,1},{6,2},{7,3},{8,12},{9,13},{10,... | collective-permute-start | bytes 64520 | tf_op jit(solution)/shard_map/ppermute | solution.py:188
  40.2 3.6 %collective-permute-start.12 = (f32[2,64]{1,0:T(2,128)S(1)}, f32[2,64]{1,0:T(2,128)S(1)}, u32[]{:S(2)}, u32[]{:S(2)}) collective-permute-start(f32[2,64]{1,0:T(2,128)S(1)} %pad_maximum_fusion.2.own_ref), channel_id=1, source_target_pairs={{0,4},{1,5},{2,6},{3,7},{4,0},{5,1},{6,2},{7,3},{8,12},{9,13},{10,... | collective-permute-start | bytes 1544 | tf_op jit(solution)/shard_map/ppermute | solution.py:188
  43.8 3.6 %collective-permute-start.14 = (f32[2,64]{1,0:T(2,128)S(1)}, f32[2,64]{1,0:T(2,128)S(1)}, u32[]{:S(2)}, u32[]{:S(2)}) collective-permute-start(f32[2,64]{1,0:T(2,128)S(1)} %merge.1), channel_id=1, source_target_pairs={{0,2},{1,3},{2,0},{3,1},{4,6},{5,7},{6,4},{7,5},{8,10},{9,11},{10,... | collective-permute-start | bytes 1544 | tf_op jit(solution)/shard_map/ppermute | solution.py:188
  47.5 1.2 %collective-permute-start.15 = (f32[2,64]{1,0:T(2,128)S(1)}, f32[2,64]{1,0:T(2,128)S(1)}, u32[]{:S(2)}, u32[]{:S(2)}) collective-permute-start(f32[2,64]{1,0:T(2,128)S(1)} %pad_maximum_fusion.3.own_ref), channel_id=1, source_target_pairs={{0,1},{1,0},{2,3},{3,2},{4,5},{5,4},{6,7},{7,6},{8,9},{9,8},{10,11... | collective-permute-start | bytes 1544 | tf_op jit(solution)/shard_map/ppermute | solution.py:188

commit v6 on v5

--- a/solution.py
+++ b/solution.py
@@ -31,8 +31,16 @@
     ]
 
 
-def pick_kernel(step, ids_ref, table_ref, after_ref, *refs):
-    outs, (ids, listed, slots, rows, ids_sem, sems) = refs[:2], refs[2:]
+def pick_kernel(step, places, ids_ref, table_ref, *refs):
+    *refs, ids, listed, slots, rows, ids_sem, sems = refs
+    if places:
+        class_ref, heat_ref, *outs, temps_ref, classes, heat, heat_sems = refs
+        heat_copies = [
+            pltpu.make_async_copy(class_ref, classes, heat_sems.at[0]),
+            pltpu.make_async_copy(heat_ref, heat, heat_sems.at[1]),
+        ]
+    else:
+        outs = refs[-2:]
     count = ids_ref.shape[1]
     held = slots.shape[0]
     voc_dev = table_ref.shape[0]
@@ -44,6 +52,9 @@
     low = me % 4
     fetch = pltpu.make_async_copy(ids_ref, ids, ids_sem)
     fetch.start()
+    if places:
+        for fetched in heat_copies:
+            fetched.start()
     rows[...] = jnp.zeros_like(rows)
     fetch.wait()
 
@@ -66,6 +77,15 @@
         @pl.loop(first, last)
         def _(n):
             copy(n).start()
+
+        if places and first == 0:
+            for fetched in heat_copies:
+                fetched.wait()
+            temps = jnp.ones(temps_ref.shape, jnp.float32)
+            lane = lax.broadcasted_iota(jnp.int32, temps.shape, 1)
+            for place, (at, row) in enumerate(places):
+                temps = jnp.where(lane == place, heat[classes[at, row]], temps)
+            temps_ref[...] = temps
 
         @pl.loop(first, last)
         def _(n):
@@ -90,17 +110,25 @@
         out[...] = rows[part * half : (part + 1) * half].astype(out.dtype)
 
 
-def picked_rows(ids, table, step, after):
+def picked_rows(ids, table, step, places, *others):
     count = ids.shape[1]
     width = table.shape[1]
     held = min(count, 32)
-    out = jax.ShapeDtypeStruct((count // 2, width), table.dtype)
-    return pl.pallas_call(
-        functools.partial(pick_kernel, step),
-        out_shape=(out, out),
-        in_specs=[pl.BlockSpec(memory_space=pl.ANY)] * 3,
-        out_specs=(pl.BlockSpec(memory_space=pltpu.VMEM),) * 2,
-        scratch_shapes=[
+    out = (jax.ShapeDtypeStruct((count // 2, width), table.dtype),) * 2
+    heat = []
+    if places:
+        out += (jax.ShapeDtypeStruct((1, len(places)), jnp.float32),)
+        others = [in_hbm(other) for other in others]
+        heat = [pltpu.SMEM(other.shape, other.dtype) for other in others]
+        heat += [pltpu.SemaphoreType.DMA((2,))]
+    anywhere, vmem = pl.BlockSpec(memory_space=pl.ANY), pl.BlockSpec(memory_space=pltpu.VMEM)
+    return pl.pallas_call(
+        functools.partial(pick_kernel, step, places),
+        out_shape=out,
+        in_specs=[anywhere] * (2 + len(others)),
+        out_specs=(vmem,) * len(out),
+        scratch_shapes=heat
+        + [
             pltpu.SMEM(ids.shape, jnp.int32),
             pltpu.SMEM((count + 1,), jnp.int32),
             pltpu.VMEM((held, BLOCK, width), table.dtype),
@@ -110,7 +138,7 @@
         ],
         compiler_params=pltpu.CompilerParams(vmem_limit_bytes=16 * MIB),
         name="pick",
-    )(in_hbm(ids), in_hbm(table), after)
+    )(in_hbm(ids), in_hbm(table), *others)
 
 
 def in_hbm(array):
@@ -188,21 +216,9 @@
     return lax.ppermute(rows, "vocab", pairs)
 
 
-def load_kernel(places, table_ref, class_ref, heat_ref, after_ref, out_ref, temps_ref, sems):
-    copies = part_copies(table_ref, out_ref, sems, 0)
-    for copy in copies:
-        copy.start()
-    temps = jnp.ones(temps_ref.shape, jnp.float32)
-    lane = lax.broadcasted_iota(jnp.int32, temps.shape, 1)
-    for place, (step, row) in enumerate(places):
-        temps = jnp.where(lane == place, heat_ref[class_ref[step, row]], temps)
-    temps_ref[...] = temps
-    for copy in copies:
-        copy.wait()
-
-
-def more_kernel(table_ref, held_ref, after_ref, out_ref, token_ref, sems):
-    copies = part_copies(table_ref, out_ref, sems, table_ref.shape[0] // 2)
+def load_kernel(part, table_ref, *refs):
+    out_ref, token_ref, sems = refs[-3:]
+    copies = part_copies(table_ref, out_ref, sems, table_ref.shape[0] // 2 * part)
     for copy in copies:
         copy.start()
     token_ref[...] = jnp.zeros_like(token_ref)
@@ -220,42 +236,25 @@
     ]
 
 
-def loaded(table, classes, lookup, places, after):
-    hbm, smem, vmem = (pl.BlockSpec(memory_space=m) for m in (pl.ANY, pltpu.SMEM, pltpu.VMEM))
-    return pl.pallas_call(
-        functools.partial(load_kernel, places),
-        out_shape=(
-            jax.ShapeDtypeStruct(table.shape, table.dtype),
-            jax.ShapeDtypeStruct((1, len(places)), jnp.float32),
-        ),
-        in_specs=[hbm, smem, smem, hbm],
-        out_specs=(vmem, vmem),
-        scratch_shapes=[pltpu.SemaphoreType.DMA((4,))],
-        compiler_params=pltpu.CompilerParams(vmem_limit_bytes=4 * MIB),
-        name="load",
-    )(in_hbm(table), classes, lookup, after)
-
-
-def loaded_more(table, held, after):
+def loaded(table, after, held=None):
     anywhere, vmem = pl.BlockSpec(memory_space=pl.ANY), pl.BlockSpec(memory_space=pltpu.VMEM)
-    return pl.pallas_call(
-        more_kernel,
+    part = 0 if held is None else 1
+    return pl.pallas_call(
+        functools.partial(load_kernel, part),
         out_shape=(
             jax.ShapeDtypeStruct(table.shape, table.dtype),
             jax.ShapeDtypeStruct((8, 128), jnp.float32),
         ),
-        in_specs=[anywhere, vmem, anywhere],
+        in_specs=[anywhere] * 2 + [vmem] * part,
         out_specs=(vmem, vmem),
-        input_output_aliases={1: 0},
+        input_output_aliases={2: 0} if part else {},
         scratch_shapes=[pltpu.SemaphoreType.DMA((4,))],
         compiler_params=pltpu.CompilerParams(vmem_limit_bytes=4 * MIB),
-        name="more",
-    )(in_hbm(table), held, after)
-
-
-def norm_kernel(
-    first_ref, own_ref, got_ref, delta_ref, gain_ref, after_ref, also_ref, out_ref
-):
+        name="load",
+    )(in_hbm(table), after, *([held] if part else []))
+
+
+def norm_kernel(first_ref, own_ref, got_ref, delta_ref, gain_ref, after_ref, out_ref):
     width = first_ref.shape[1]
     gain = gain_ref[...]
 
@@ -285,17 +284,17 @@
     out_ref[...] = jnp.concatenate([one, two], axis=0).astype(out_ref.dtype)
 
 
-def normed(first, own, got, delta, gain, after, also):
+def normed(first, own, got, delta, gain, after):
     rows, width = first.shape
     vmem = pl.BlockSpec(memory_space=pltpu.VMEM)
     return pl.pallas_call(
         norm_kernel,
         out_shape=jax.ShapeDtypeStruct((2 * rows, width), jnp.bfloat16),
-        in_specs=[vmem] * 5 + [pl.BlockSpec(memory_space=pl.ANY)] * 2,
+        in_specs=[vmem] * 5 + [pl.BlockSpec(memory_space=pl.ANY)],
         out_specs=vmem,
         compiler_params=pltpu.CompilerParams(vmem_limit_bytes=12 * MIB),
         name="norm",
-    )(first, own, got, delta, gain.reshape(1, width), after, also)
+    )(first, own, got, delta, gain.reshape(1, width), after)
 
 
 def head_kernel(own_ref, got_ref, table_ref, temps_ref, scaled_ref, stats_ref):
@@ -391,12 +390,11 @@
         for k in range(quarter)
     ]
 
-    keep, send = picked_rows(ids, table, 0, ids)
+    keep, send, temps = picked_rows(ids, table, 0, places, classes, lookup)
     own, send, beside = folded(keep, swapped(send, 1), first, deltas)
     own = own + swapped(send, 2)
-    keep, send = picked_rows(ids, table, 1, own)
+    keep, send = picked_rows(ids, table, 1, (), own)
     keep = keep + swapped(send, 1)
-    following = keep[:quarter] + swapped(keep[quarter:], 2)
     for k, bit in enumerate(high):
         held = beside.shape[0] // 2
         moved = swapped(beside, bit)
@@ -406,24 +404,24 @@
             own = paired(plus_kernel, own, got, quarter, "plus", send)
     state = jnp.concatenate([beside[:held], moved[:held]], axis=0)
     delta = jnp.concatenate([beside[held:], moved[held:]], axis=0)
-    held_table, temps = loaded(table, classes, lookup, places, own)
-    states = normed(state, own, got, delta, gain, temps, following)
-    held_table, token = loaded_more(table, held_table, states)
-    half = quarter // 2
-    away = swapped(following[half:], high[0])
-    states = paired(chips_kernel, states, swapped(states, 2), rows, "chips", token, away)
+    head_table, token = loaded(table, own)
+    states = normed(state, own, got, delta, gain, token)
+    head_table, token = loaded(table, states, head_table)
+    states = paired(chips_kernel, states, swapped(states, 2), rows, "chips", token, keep)
     others = swapped(states, 1)
-    scaled, stats = head(states, others, held_table, temps)
-    following = paired(plus_kernel, following[:half], away, half, "plus", stats)
+    scaled, stats = head(states, others, head_table, temps)
     scaled = turned(scaled, places, steps)
-    for bit in high[1:]:
-        half = following.shape[0] // 2
-        following = following[:half] + swapped(following[half:], bit)
+    following = paired(plus_kernel, keep[:quarter], swapped(keep[quarter:], 2), quarter, "plus", stats)
+    if len(high) < 3:
+        parts = [following[k * rows_dev : (k + 1) * rows_dev] for k in range(shards // 4)]
+        following = sum((swapped(parts[k], 4 * k) for k in range(1, shards // 4)), parts[0])
+    for bit in high:
+        if following.shape[0] > rows_dev:
+            half = following.shape[0] // 2
+            following = following[:half] + swapped(following[half:], bit)
+        stats = merged(stats, swapped(stats, bit))
     embedded = (following.astype(jnp.float32) * math.sqrt(width)).astype(jnp.bfloat16)
-    for bit in high[:-1]:
-        stats = merged(stats, swapped(stats, bit))
-    stats = paired(merge_kernel, stats, swapped(stats, high[-1]), 2, "merge", following)
-    stats = merged(stats, swapped(stats, 2))
+    stats = paired(merge_kernel, stats, swapped(stats, 2), 2, "merge", following)
     logprobs = finished(scaled, stats, swapped(stats, 1), places)
     return logprobs, embedded
 

time: 49.8 us -> 50.7 us (1.018)
  starting transfers between devices: 21.3 us -> 22.5 us
  Pallas kernels: 15.4 us -> 14.7 us
    ppermute x16 -> x17, starting transfers between devices: 21.3 us -> 22.5 us  [swapped(): return lax.ppermute(rows, 'vocab', pairs)]
    pallas_call x4, Pallas kernels: 10.6 us -> 9.95 us  [the longest x2 5.24 us: loaded(): pl.pallas_call(functools.partial(load_kernel, part), out_shape=(jax.Shape...]
    ppermute x16 -> x17, waiting for transfers between devices: 10.9 us -> 11.4 us  [swapped(): return lax.ppermute(rows, 'vocab', pairs)]
  transfers between devices with their start and end apart: 16 -> 17, of which waited for: 9 -> 9; matrix products, arithmetic and copies ran while one was open for 2% -> 2% of each run, Pallas kernels for 17% -> 22%
where the time goes in v6:
time: 50.7 us; the launch traced here: 50.4 us
  starting transfers between devices  22.5 us (44%)
  Pallas kernels  14.7 us (29%)
  waiting for transfers between devices  11.4 us (22%)
  other arithmetic  0.86 us (2%)
  between operations  0.84 us (2%)
    ppermute x17, starting transfers between devices, swapped(): return lax.ppermute(rows, 'vocab', pairs)  22.5 us
    ppermute x17, waiting for transfers between devices, swapped(): return lax.ppermute(rows, 'vocab', pairs)  11.4 us
    pallas_call x2, Pallas kernels, loaded(): pl.pallas_call(functools.partial(load_kernel, part), out_shape=(jax.Shape...  5.24 us
    pallas_call x2, Pallas kernels, picked_rows(): pl.pallas_call(functools.partial(pick_kernel, step, places), out_shape=ou...  4.71 us
    pallas_call x1, Pallas kernels, head(): pl.pallas_call(head_kernel, out_shape=(jax.ShapeDtypeStruct((voc_dev, row...  3.14 us
  transfers between devices with their start and end apart: 17, of which 9 were waited for; matrix products, arithmetic and copies ran while one was open for 2% of the time, Pallas kernels for 22%

profile of v6, /device:TPU:0, one launch (start us, length us, event | category | flops | bytes accessed | tf_op | source)
XLA Modules:
  0.0 50.4 jit_solution(11628526580631970374)
XLA Ops:
  0.7 2.6 %pick.2 = (bf16[16,5376]{1,0:T(8,128)(2,1)S(1)}, bf16[16,5376]{1,0:T(8,128)(2,1)S(1)}, f32[1,64]{1,0:T(1,128)S(1)}) custom-call(s32[2,32]{1,0:T(2,128)} %ids_ref.3, bf16[1024,5376]{1,0:T(8,128)(2,1)} %table_ref.7, s32[2,32]{1,0:T(2,128)} %refs_0_.1, f32[8]{0:T(128)} %refs_1_.1), custom_call_target="tpu_custom_call" | custom-call | tf_op jit(solution)/shard_map/pick/pallas_call | solution.py:125
  3.2 0.5 %collective-permute-start = (bf16[16,5376]{1,0:T(8,128)(2,1)S(1)}, bf16[16,5376]{1,0:T(8,128)(2,1)S(1)}, u32[]{:S(2)}, u32[]{:S(2)}) collective-permute-start(bf16[16,5376]{1,0:T(8,128)(2,1)S(1)} %get-tuple-element.17), channel_id=1, source_target_pairs={{0,1},{1,0},{2,3},{3,2},{4,5},{5,4},{6,7},{7,6},{8,9},{9,8},{10,11... | collective-permute-start | bytes 516104 | tf_op jit(solution)/shard_map/ppermute | solution.py:216
  3.8 1.0 %collective-permute-done.got_ref = bf16[16,5376]{1,0:T(8,128)(2,1)S(1)} collective-permute-done((bf16[16,5376]{1,0:T(8,128)(2,1)S(1)}, bf16[16,5376]{1,0:T(8,128)(2,1)S(1)}, u32[]{:S(2)}, u32[]{:S(2)}) %collective-permute-start) | collective-permute-done | bytes 172064 | tf_op jit(solution)/shard_map/ppermute | solution.py:216
  4.8 0.0 copy-done.1
  4.8 0.1 fold.1
  4.9 2.9 %collective-permute-start.2 = (bf16[8,5376]{1,0:T(8,128)(2,1)S(1)}, bf16[8,5376]{1,0:T(8,128)(2,1)S(1)}, u32[]{:S(2)}, u32[]{:S(2)}) collective-permute-start(bf16[8,5376]{1,0:T(8,128)(2,1)S(1)} %get-tuple-element.20), channel_id=1, source_target_pairs={{0,2},{1,3},{2,0},{3,1},{4,6},{5,7},{6,4},{7,5},{8,10},{9,11},{10,... | collective-permute-start | bytes 258056 | tf_op jit(solution)/shard_map/ppermute | solution.py:216
  7.8 2.5 %collective-permute-start.1 = (bf16[4,5376]{1,0:T(4,128)(2,1)S(1)}, bf16[4,5376]{1,0:T(4,128)(2,1)S(1)}, u32[]{:S(2)}, u32[]{:S(2)}) collective-permute-start(bf16[4,5376]{1,0:T(4,128)(2,1)S(1)} %get-tuple-element.18.own_ref), channel_id=1, source_target_pairs={{0,8},{1,9},{2,10},{3,11},{4,12},{5,13},{6,14},{7,15},{8,0},{9,1},... | collective-permute-start | bytes 129032 | tf_op jit(solution)/shard_map/ppermute | solution.py:216
  10.3 0.0 copy-done.2
  10.3 0.3 collective-permute-done.2
  10.7 2.9 %collective-permute-start.4 = (bf16[8,5376]{1,0:T(8,128)(2,1)S(1)}, bf16[8,5376]{1,0:T(8,128)(2,1)S(1)}, u32[]{:S(2)}, u32[]{:S(2)}) collective-permute-start(bf16[8,5376]{1,0:T(8,128)(2,1)S(1)} %add.24.refs_0_.own_ref), channel_id=1, source_target_pairs={{0,8},{1,9},{2,10},{3,11},{4,12},{5,13},{6,14},{7,15},{8,0},{9,1},... | collective-permute-start | bytes 258056 | tf_op jit(solution)/shard_map/ppermute | solution.py:216
  13.6 0.0 collective-permute-done.1.got_ref
  13.6 1.5 %collective-permute-start.3 = (bf16[8,5376]{1,0:T(8,128)(2,1)S(1)}, bf16[8,5376]{1,0:T(8,128)(2,1)S(1)}, u32[]{:S(2)}, u32[]{:S(2)}) collective-permute-start(bf16[8,5376]{1,0:T(8,128)(2,1)S(1)} %join.1), channel_id=1, source_target_pairs={{0,4},{1,5},{2,6},{3,7},{4,0},{5,1},{6,2},{7,3},{8,12},{9,13},{10,... | collective-permute-start | bytes 258056 | tf_op jit(solution)/shard_map/ppermute | solution.py:216
  15.1 2.1 %pick.3 = (bf16[16,5376]{1,0:T(8,128)(2,1)S(1)}, bf16[16,5376]{1,0:T(8,128)(2,1)S(1)}) custom-call(s32[2,32]{1,0:T(2,128)} %ids_ref.3, bf16[1024,5376]{1,0:T(8,128)(2,1)} %table_ref.7, bf16[8,5376]{1,0:T(8,128)(2,1)S(1)} %add.24.refs_0_.own_ref), custom_call_target="tpu_custom_call" | custom-call | tf_op jit(solution)/shard_map/pick/pallas_call | solution.py:125
  17.3 0.1 collective-permute-start.7
  17.3 0.0 collective-permute-done.4.got_ref
  17.4 1.1 %collective-permute-start.5 = (bf16[8,5376]{1,0:T(8,128)(2,1)S(1)}, bf16[8,5376]{1,0:T(8,128)(2,1)S(1)}, u32[]{:S(2)}, u32[]{:S(2)}) collective-permute-start(bf16[8,5376]{1,0:T(8,128)(2,1)S(1)} %plus.2.refs_0_.own_ref), channel_id=1, source_target_pairs={{0,4},{1,5},{2,6},{3,7},{4,0},{5,1},{6,2},{7,3},{8,12},{9,13},{10,... | collective-permute-start | bytes 258056 | tf_op jit(solution)/shard_map/ppermute | solution.py:216
  18.5 0.0 collective-permute-done.3
  18.6 0.1 pad_maximum_fusion
  18.6 2.6 %load.2 = (bf16[1024,5376]{1,0:T(8,128)(2,1)S(1)}, f32[8,128]{1,0:T(8,128)S(1)}) custom-call(bf16[1024,5376]{1,0:T(8,128)(2,1)} %table_ref.7, bf16[8,5376]{1,0:T(8,128)(2,1)S(1)} %plus.2.refs_0_.own_ref), custom_call_target="tpu_custom_call" | custom-call | tf_op jit(solution)/shard_map/load/pallas_call | solution.py:242
  21.3 1.1 %collective-permute-done.5.got_ref = bf16[8,5376]{1,0:T(8,128)(2,1)S(1)} collective-permute-done((bf16[8,5376]{1,0:T(8,128)(2,1)S(1)}, bf16[8,5376]{1,0:T(8,128)(2,1)S(1)}, u32[]{:S(2)}, u32[]{:S(2)}) %collective-permute-start.5) | collective-permute-done | bytes 86048 | tf_op jit(solution)/shard_map/ppermute | solution.py:216
  22.4 0.3 norm.1.refs_0_.own_ref
  22.7 1.6 %collective-permute-start.6 = (bf16[16,5376]{1,0:T(8,128)(2,1)S(1)}, bf16[16,5376]{1,0:T(8,128)(2,1)S(1)}, u32[]{:S(2)}, u32[]{:S(2)}) collective-permute-start(bf16[16,5376]{1,0:T(8,128)(2,1)S(1)} %norm.1.refs_0_.own_ref), channel_id=1, source_target_pairs={{0,2},{1,3},{2,0},{3,1},{4,6},{5,7},{6,4},{7,5},{8,10},{9,11},{10,... | collective-permute-start | bytes 516104 | tf_op jit(solution)/shard_map/ppermute | solution.py:216
  24.3 2.6 %load.3 = (bf16[1024,5376]{1,0:T(8,128)(2,1)S(1)}, f32[8,128]{1,0:T(8,128)S(1)}) custom-call(bf16[1024,5376]{1,0:T(8,128)(2,1)} %table_ref.7, bf16[16,5376]{1,0:T(8,128)(2,1)S(1)} %norm.1.refs_0_.own_ref, bf16[1024,5376]{1,0:T(8,128)(2,1)S(1)} %get-tuple-element.23.refs_1_), custom_call_target="tpu_custom_call", output_to_operand_aliasing={{0}: (2, {})} | custom-call | tf_op jit(solution)/shard_map/load/pallas_call | solution.py:242
  26.9 0.0 collective-permute-done.7
  27.0 1.7 %collective-permute-done.6.got_ref = bf16[16,5376]{1,0:T(8,128)(2,1)S(1)} collective-permute-done((bf16[16,5376]{1,0:T(8,128)(2,1)S(1)}, bf16[16,5376]{1,0:T(8,128)(2,1)S(1)}, u32[]{:S(2)}, u32[]{:S(2)}) %collective-permute-start.6) | collective-permute-done | bytes 172064 | tf_op jit(solution)/shard_map/ppermute | solution.py:216
  28.8 0.1 collective-permute-start.8
  28.9 1.4 %collective-permute-start.12 = (bf16[8,5376]{1,0:T(8,128)(2,1)S(1)}, bf16[8,5376]{1,0:T(8,128)(2,1)S(1)}, u32[]{:S(2)}, u32[]{:S(2)}) collective-permute-start(bf16[8,5376]{1,0:T(8,128)(2,1)S(1)} %get-tuple-element.34), channel_id=1, source_target_pairs={{0,2},{1,3},{2,0},{3,1},{4,6},{5,7},{6,4},{7,5},{8,10},{9,11},{10,... | collective-permute-start | bytes 258056 | tf_op jit(solution)/shard_map/ppermute | solution.py:216
  30.3 0.2 collective-permute-done.8.got_ref
  30.5 3.1 %head.1 = (f32[1024,64]{1,0:T(8,128)S(1)}, f32[2,64]{1,0:T(2,128)S(1)}) custom-call(bf16[32,5376]{1,0:T(8,128)(2,1)S(1)} %chips.1.own_ref, bf16[32,5376]{1,0:T(8,128)(2,1)S(1)} %collective-permute-done.8.got_ref, bf16[1024,5376]{1,0:T(8,128)(2,1)S(1)} %get-tuple-element.26.table_ref, f32[1,64]{1,0:T(1,128)S(1)} %get-tuple-element.27.temps_ref), custom_call_target="tpu_custom_call" | custom-call | tf_op jit(solution)/shard_map/head/pallas_call | solution.py:318
  33.6 1.5 %collective-permute-start.9 = (f32[2,64]{1,0:T(2,128)S(1)}, f32[2,64]{1,0:T(2,128)S(1)}, u32[]{:S(2)}, u32[]{:S(2)}) collective-permute-start(f32[2,64]{1,0:T(2,128)S(1)} %get-tuple-element.29.refs_0_), channel_id=1, source_target_pairs={{0,8},{1,9},{2,10},{3,11},{4,12},{5,13},{6,14},{7,15},{8,0},{9,1},... | collective-permute-start | bytes 1544 | tf_op jit(solution)/shard_map/ppermute | solution.py:216
  35.1 0.0 collective-permute-done.12.got_ref
  35.2 3.0 %collective-permute-done.9 = f32[2,64]{1,0:T(2,128)S(1)} collective-permute-done((f32[2,64]{1,0:T(2,128)S(1)}, f32[2,64]{1,0:T(2,128)S(1)}, u32[]{:S(2)}, u32[]{:S(2)}) %collective-permute-start.9) | collective-permute-done | bytes 544 | tf_op jit(solution)/shard_map/ppermute | solution.py:216
  38.2 0.6 %collective-permute-start.10 = (f32[2,64]{1,0:T(2,128)S(1)}, f32[2,64]{1,0:T(2,128)S(1)}, u32[]{:S(2)}, u32[]{:S(2)}) collective-permute-start(f32[2,64]{1,0:T(2,128)S(1)} %pad_maximum_fusion.2), channel_id=1, source_target_pairs={{0,4},{1,5},{2,6},{3,7},{4,0},{5,1},{6,2},{7,3},{8,12},{9,13},{10,... | collective-permute-start | bytes 1544 | tf_op jit(solution)/shard_map/ppermute | solution.py:216
  38.8 0.1 fusion.4
  38.9 1.5 %collective-permute-start.13 = (bf16[2,5376]{1,0:T(2,128)(2,1)S(1)}, bf16[2,5376]{1,0:T(2,128)(2,1)S(1)}, u32[]{:S(2)}, u32[]{:S(2)}) collective-permute-start(bf16[2,5376]{1,0:T(2,128)(2,1)S(1)} %get-tuple-element.36), channel_id=1, source_target_pairs={{0,4},{1,5},{2,6},{3,7},{4,0},{5,1},{6,2},{7,3},{8,12},{9,13},{10,... | collective-permute-start | bytes 64520 | tf_op jit(solution)/shard_map/ppermute | solution.py:216
  40.4 2.6 %collective-permute-start.15 = (bf16[2,5376]{1,0:T(2,128)(2,1)S(1)}, bf16[2,5376]{1,0:T(2,128)(2,1)S(1)}, u32[]{:S(2)}, u32[]{:S(2)}) collective-permute-start(bf16[2,5376]{1,0:T(2,128)(2,1)S(1)} %get-tuple-element.37), channel_id=1, source_target_pairs={{0,12},{1,13},{2,14},{3,15},{4,8},{5,9},{6,10},{7,11},{8,4},{9,5},... | collective-permute-start | bytes 64520 | tf_op jit(solution)/shard_map/ppermute | solution.py:216
  43.0 0.0 collective-permute-start.14
  43.0 0.0 collective-permute-done.10
  43.0 1.6 %collective-permute-start.11 = (f32[2,64]{1,0:T(2,128)S(1)}, f32[2,64]{1,0:T(2,128)S(1)}, u32[]{:S(2)}, u32[]{:S(2)}) collective-permute-start(f32[2,64]{1,0:T(2,128)S(1)} %pad_maximum_fusion.3.own_ref), channel_id=1, source_target_pairs={{0,2},{1,3},{2,0},{3,1},{4,6},{5,7},{6,4},{7,5},{8,10},{9,11},{10,... | collective-permute-start | bytes 1544 | tf_op jit(solution)/shard_map/ppermute | solution.py:216
  44.6 0.0 collective-permute-done.13
  44.6 1.4 %collective-permute-done.15 = bf16[2,5376]{1,0:T(2,128)(2,1)S(1)} collective-permute-done((bf16[2,5376]{1,0:T(2,128)(2,1)S(1)}, bf16[2,5376]{1,0:T(2,128)(2,1)S(1)}, u32[]{:S(2)}, u32[]{:S(2)}) %collective-permute-start.15) | collective-permute-done | bytes 21536 | tf_op jit(solution)/shard_map/ppermute | solution.py:216
  46.0 1.7 %collective-permute-done.14 = bf16[2,5376]{1,0:T(2,128)(2,1)S(1)} collective-permute-done((bf16[2,5376]{1,0:T(2,128)(2,1)S(1)}, bf16[2,5376]{1,0:T(2,128)(2,1)S(1)}, u32[]{:S(2)}, u32[]{:S(2)}) %collective-permute-start.14) | collective-permute-done | bytes 21536 | tf_op jit(solution)/shard_map/ppermute | solution.py:216
  47.7 0.7 %multiply_convert_fusion = (bf16[2,5376]{1,0:T(2,128)(2,1)}, bf16[2,5376]{1,0:T(2,128)(2,1)S(1)}) fusion(bf16[2,5376]{1,0:T(2,128)(2,1)S(1)} %collective-permute-done.15, bf16[2,5376]{1,0:T(2,128)(2,1)S(1)} %collective-permute-done.14, bf16[2,5376]{1,0:T(2,128)(2,1)S(1)} %collective-permute-done.13, bf16[8,5376]{1,0:T(8,128)(2,1)S(1)} %plus.3), kind=kLoop, calls=%fused_computation.2 | loop fusion | flops 64512 | bytes 129024 | tf_op jit(solution)/shard_map/convert_element_type | solution.py:423
  48.3 0.0 collective-permute-done.11.got_ref
  48.4 0.1 collective-permute-start.16
  48.4 0.2 turn.1.scaled_ref
  48.6 0.9 %collective-permute-done.16.got_ref = f32[2,64]{1,0:T(2,128)S(1)} collective-permute-done((f32[2,64]{1,0:T(2,128)S(1)}, f32[2,64]{1,0:T(2,128)S(1)}, u32[]{:S(2)}, u32[]{:S(2)}) %collective-permute-start.16) | collective-permute-done | bytes 544 | tf_op jit(solution)/shard_map/ppermute | solution.py:216
  49.6 0.9 %finish.1 = f32[2,32,1024]{2,1,0:T(8,128)} custom-call(f32[2,32,1024]{2,1,0:T(8,128)S(1)} %turn.1.scaled_ref, f32[2,64]{1,0:T(2,128)S(1)} %merge.1.own_ref, f32[2,64]{1,0:T(2,128)S(1)} %collective-permute-done.16.got_ref), custom_call_target="tpu_custom_call" | custom-call | tf_op jit(solution)/shard_map/finish/pallas_call | solution.py:364
  (19 shorter events, 0.3 us)
Async XLA Ops:
  0.6 4.2 %copy-start.1 = (bf16[2,5376]{1,0:T(2,128)(2,1)S(1)}, bf16[2,5376]{1,0:T(2,128)(2,1)}, u32[]{:S(2)}) copy-start(bf16[2,5376]{1,0:T(2,128)(2,1)} %delta_ref.1) | copy-start | bytes 64516
  0.6 4.2 %copy-start = (bf16[2,5376]{1,0:T(2,128)(2,1)S(1)}, bf16[2,5376]{1,0:T(2,128)(2,1)}, u32[]{:S(2)}) copy-start(bf16[2,5376]{1,0:T(2,128)(2,1)} %first_ref.1) | copy-start | bytes 64516
  0.7 9.7 %copy-start.2 = (f32[5376]{0:T(1024)S(1)}, f32[5376]{0:T(1024)}, u32[]{:S(2)}) copy-start(f32[5376]{0:T(1024)} %param.9) | copy-start | bytes 64516
  3.2 1.6 %collective-permute-start = (bf16[16,5376]{1,0:T(8,128)(2,1)S(1)}, bf16[16,5376]{1,0:T(8,128)(2,1)S(1)}, u32[]{:S(2)}, u32[]{:S(2)}) collective-permute-start(bf16[16,5376]{1,0:T(8,128)(2,1)S(1)} %get-tuple-element.17), channel_id=1, source_target_pairs={{0,1},{1,0},{2,3},{3,2},{4,5},{5,4},{6,7},{7,6},{8,9},{9,8},{10,11... | collective-permute-start | bytes 516104 | tf_op jit(solution)/shard_map/ppermute | solution.py:216
  4.9 5.8 %collective-permute-start.2 = (bf16[8,5376]{1,0:T(8,128)(2,1)S(1)}, bf16[8,5376]{1,0:T(8,128)(2,1)S(1)}, u32[]{:S(2)}, u32[]{:S(2)}) collective-permute-start(bf16[8,5376]{1,0:T(8,128)(2,1)S(1)} %get-tuple-element.20), channel_id=1, source_target_pairs={{0,2},{1,3},{2,0},{3,1},{4,6},{5,7},{6,4},{7,5},{8,10},{9,11},{10,... | collective-permute-start | bytes 258056 | tf_op jit(solution)/shard_map/ppermute | solution.py:216
  7.8 5.7 %collective-permute-start.1 = (bf16[4,5376]{1,0:T(4,128)(2,1)S(1)}, bf16[4,5376]{1,0:T(4,128)(2,1)S(1)}, u32[]{:S(2)}, u32[]{:S(2)}) collective-permute-start(bf16[4,5376]{1,0:T(4,128)(2,1)S(1)} %get-tuple-element.18.own_ref), channel_id=1, source_target_pairs={{0,8},{1,9},{2,10},{3,11},{4,12},{5,13},{6,14},{7,15},{8,0},{9,1},... | collective-permute-start | bytes 129032 | tf_op jit(solution)/shard_map/ppermute | solution.py:216
  10.7 6.7 %collective-permute-start.4 = (bf16[8,5376]{1,0:T(8,128)(2,1)S(1)}, bf16[8,5376]{1,0:T(8,128)(2,1)S(1)}, u32[]{:S(2)}, u32[]{:S(2)}) collective-permute-start(bf16[8,5376]{1,0:T(8,128)(2,1)S(1)} %add.24.refs_0_.own_ref), channel_id=1, source_target_pairs={{0,8},{1,9},{2,10},{3,11},{4,12},{5,13},{6,14},{7,15},{8,0},{9,1},... | collective-permute-start | bytes 258056 | tf_op jit(solution)/shard_map/ppermute | solution.py:216
  13.6 4.9 %collective-permute-start.3 = (bf16[8,5376]{1,0:T(8,128)(2,1)S(1)}, bf16[8,5376]{1,0:T(8,128)(2,1)S(1)}, u32[]{:S(2)}, u32[]{:S(2)}) collective-permute-start(bf16[8,5376]{1,0:T(8,128)(2,1)S(1)} %join.1), channel_id=1, source_target_pairs={{0,4},{1,5},{2,6},{3,7},{4,0},{5,1},{6,2},{7,3},{8,12},{9,13},{10,... | collective-permute-start | bytes 258056 | tf_op jit(solution)/shard_map/ppermute | solution.py:216
  17.3 9.7 %collective-permute-start.7 = (bf16[16,5376]{1,0:T(8,128)(2,1)S(1)}, bf16[16,5376]{1,0:T(8,128)(2,1)S(1)}, u32[]{:S(2)}, u32[]{:S(2)}) collective-permute-start(bf16[16,5376]{1,0:T(8,128)(2,1)S(1)} %get-tuple-element.21.refs_0_), channel_id=1, source_target_pairs={{0,1},{1,0},{2,3},{3,2},{4,5},{5,4},{6,7},{7,6},{8,9},{9,8},{10,11... | collective-permute-start | bytes 516104 | tf_op jit(solution)/shard_map/ppermute | solution.py:216
  17.4 5.0 %collective-permute-start.5 = (bf16[8,5376]{1,0:T(8,128)(2,1)S(1)}, bf16[8,5376]{1,0:T(8,128)(2,1)S(1)}, u32[]{:S(2)}, u32[]{:S(2)}) collective-permute-start(bf16[8,5376]{1,0:T(8,128)(2,1)S(1)} %plus.2.refs_0_.own_ref), channel_id=1, source_target_pairs={{0,4},{1,5},{2,6},{3,7},{4,0},{5,1},{6,2},{7,3},{8,12},{9,13},{10,... | collective-permute-start | bytes 258056 | tf_op jit(solution)/shard_map/ppermute | solution.py:216
  22.7 6.0 %collective-permute-start.6 = (bf16[16,5376]{1,0:T(8,128)(2,1)S(1)}, bf16[16,5376]{1,0:T(8,128)(2,1)S(1)}, u32[]{:S(2)}, u32[]{:S(2)}) collective-permute-start(bf16[16,5376]{1,0:T(8,128)(2,1)S(1)} %norm.1.refs_0_.own_ref), channel_id=1, source_target_pairs={{0,2},{1,3},{2,0},{3,1},{4,6},{5,7},{6,4},{7,5},{8,10},{9,11},{10,... | collective-permute-start | bytes 516104 | tf_op jit(solution)/shard_map/ppermute | solution.py:216
  28.8 1.7 %collective-permute-start.8 = (bf16[32,5376]{1,0:T(8,128)(2,1)S(1)}, bf16[32,5376]{1,0:T(8,128)(2,1)S(1)}, u32[]{:S(2)}, u32[]{:S(2)}) collective-permute-start(bf16[32,5376]{1,0:T(8,128)(2,1)S(1)} %chips.1.own_ref), channel_id=1, source_target_pairs={{0,1},{1,0},{2,3},{3,2},{4,5},{5,4},{6,7},{7,6},{8,9},{9,8},{10,11... | collective-permute-start | bytes 1032200 | tf_op jit(solution)/shard_map/ppermute | solution.py:216
  28.9 6.3 %collective-permute-start.12 = (bf16[8,5376]{1,0:T(8,128)(2,1)S(1)}, bf16[8,5376]{1,0:T(8,128)(2,1)S(1)}, u32[]{:S(2)}, u32[]{:S(2)}) collective-permute-start(bf16[8,5376]{1,0:T(8,128)(2,1)S(1)} %get-tuple-element.34), channel_id=1, source_target_pairs={{0,2},{1,3},{2,0},{3,1},{4,6},{5,7},{6,4},{7,5},{8,10},{9,11},{10,... | collective-permute-start | bytes 258056 | tf_op jit(solution)/shard_map/ppermute | solution.py:216
  33.6 4.5 %collective-permute-start.9 = (f32[2,64]{1,0:T(2,128)S(1)}, f32[2,64]{1,0:T(2,128)S(1)}, u32[]{:S(2)}, u32[]{:S(2)}) collective-permute-start(f32[2,64]{1,0:T(2,128)S(1)} %get-tuple-element.29.refs_0_), channel_id=1, source_target_pairs={{0,8},{1,9},{2,10},{3,11},{4,12},{5,13},{6,14},{7,15},{8,0},{9,1},... | collective-permute-start | bytes 1544 | tf_op jit(solution)/shard_map/ppermute | solution.py:216
  38.2 4.8 %collective-permute-start.10 = (f32[2,64]{1,0:T(2,128)S(1)}, f32[2,64]{1,0:T(2,128)S(1)}, u32[]{:S(2)}, u32[]{:S(2)}) collective-permute-start(f32[2,64]{1,0:T(2,128)S(1)} %pad_maximum_fusion.2), channel_id=1, source_target_pairs={{0,4},{1,5},{2,6},{3,7},{4,0},{5,1},{6,2},{7,3},{8,12},{9,13},{10,... | collective-permute-start | bytes 1544 | tf_op jit(solution)/shard_map/ppermute | solution.py:216
  38.9 5.7 %collective-permute-start.13 = (bf16[2,5376]{1,0:T(2,128)(2,1)S(1)}, bf16[2,5376]{1,0:T(2,128)(2,1)S(1)}, u32[]{:S(2)}, u32[]{:S(2)}) collective-permute-start(bf16[2,5376]{1,0:T(2,128)(2,1)S(1)} %get-tuple-element.36), channel_id=1, source_target_pairs={{0,4},{1,5},{2,6},{3,7},{4,0},{5,1},{6,2},{7,3},{8,12},{9,13},{10,... | collective-permute-start | bytes 64520 | tf_op jit(solution)/shard_map/ppermute | solution.py:216
  40.4 5.6 %collective-permute-start.15 = (bf16[2,5376]{1,0:T(2,128)(2,1)S(1)}, bf16[2,5376]{1,0:T(2,128)(2,1)S(1)}, u32[]{:S(2)}, u32[]{:S(2)}) collective-permute-start(bf16[2,5376]{1,0:T(2,128)(2,1)S(1)} %get-tuple-element.37), channel_id=1, source_target_pairs={{0,12},{1,13},{2,14},{3,15},{4,8},{5,9},{6,10},{7,11},{8,4},{9,5},... | collective-permute-start | bytes 64520 | tf_op jit(solution)/shard_map/ppermute | solution.py:216
  43.0 4.7 %collective-permute-start.14 = (bf16[2,5376]{1,0:T(2,128)(2,1)S(1)}, bf16[2,5376]{1,0:T(2,128)(2,1)S(1)}, u32[]{:S(2)}, u32[]{:S(2)}) collective-permute-start(bf16[2,5376]{1,0:T(2,128)(2,1)S(1)} %get-tuple-element.38), channel_id=1, source_target_pairs={{0,8},{1,9},{2,10},{3,11},{4,12},{5,13},{6,14},{7,15},{8,0},{9,1},... | collective-permute-start | bytes 64520 | tf_op jit(solution)/shard_map/ppermute | solution.py:216
  43.0 5.3 %collective-permute-start.11 = (f32[2,64]{1,0:T(2,128)S(1)}, f32[2,64]{1,0:T(2,128)S(1)}, u32[]{:S(2)}, u32[]{:S(2)}) collective-permute-start(f32[2,64]{1,0:T(2,128)S(1)} %pad_maximum_fusion.3.own_ref), channel_id=1, source_target_pairs={{0,2},{1,3},{2,0},{3,1},{4,6},{5,7},{6,4},{7,5},{8,10},{9,11},{10,... | collective-permute-start | bytes 1544 | tf_op jit(solution)/shard_map/ppermute | solution.py:216
  48.4 1.2 %collective-permute-start.16 = (f32[2,64]{1,0:T(2,128)S(1)}, f32[2,64]{1,0:T(2,128)S(1)}, u32[]{:S(2)}, u32[]{:S(2)}) collective-permute-start(f32[2,64]{1,0:T(2,128)S(1)} %merge.1.own_ref), channel_id=1, source_target_pairs={{0,1},{1,0},{2,3},{3,2},{4,5},{5,4},{6,7},{7,6},{8,9},{9,8},{10,11... | collective-permute-start | bytes 1544 | tf_op jit(solution)/shard_map/ppermute | solution.py:216

commit v7 on v6

--- a/solution.py
+++ b/solution.py
@@ -254,7 +254,8 @@
     )(in_hbm(table), after, *([held] if part else []))
 
 
-def norm_kernel(first_ref, own_ref, got_ref, delta_ref, gain_ref, after_ref, out_ref):
+def norm_kernel(first_ref, own_ref, got_ref, delta_ref, gain_ref, *refs):
+    out_ref = refs[-1]
     width = first_ref.shape[1]
     gain = gain_ref[...]
 
@@ -284,17 +285,17 @@
     out_ref[...] = jnp.concatenate([one, two], axis=0).astype(out_ref.dtype)
 
 
-def normed(first, own, got, delta, gain, after):
+def normed(first, own, got, delta, gain, *after):
     rows, width = first.shape
     vmem = pl.BlockSpec(memory_space=pltpu.VMEM)
     return pl.pallas_call(
         norm_kernel,
         out_shape=jax.ShapeDtypeStruct((2 * rows, width), jnp.bfloat16),
-        in_specs=[vmem] * 5 + [pl.BlockSpec(memory_space=pl.ANY)],
+        in_specs=[vmem] * 5 + [pl.BlockSpec(memory_space=pl.ANY)] * len(after),
         out_specs=vmem,
         compiler_params=pltpu.CompilerParams(vmem_limit_bytes=12 * MIB),
         name="norm",
-    )(first, own, got, delta, gain.reshape(1, width), after)
+    )(first, own, got, delta, gain.reshape(1, width), *after)
 
 
 def head_kernel(own_ref, got_ref, table_ref, temps_ref, scaled_ref, stats_ref):
@@ -395,6 +396,7 @@
     own = own + swapped(send, 2)
     keep, send = picked_rows(ids, table, 1, (), own)
     keep = keep + swapped(send, 1)
+    following = keep[:quarter] + swapped(keep[quarter:], 2)
     for k, bit in enumerate(high):
         held = beside.shape[0] // 2
         moved = swapped(beside, bit)
@@ -405,23 +407,20 @@
     state = jnp.concatenate([beside[:held], moved[:held]], axis=0)
     delta = jnp.concatenate([beside[held:], moved[held:]], axis=0)
     head_table, token = loaded(table, own)
-    states = normed(state, own, got, delta, gain, token)
+    states = normed(state, own, got, delta, gain, token, following)
     head_table, token = loaded(table, states, head_table)
-    states = paired(chips_kernel, states, swapped(states, 2), rows, "chips", token, keep)
+    states = paired(chips_kernel, states, swapped(states, 2), rows, "chips", token)
     others = swapped(states, 1)
     scaled, stats = head(states, others, head_table, temps)
     scaled = turned(scaled, places, steps)
-    following = paired(plus_kernel, keep[:quarter], swapped(keep[quarter:], 2), quarter, "plus", stats)
-    if len(high) < 3:
-        parts = [following[k * rows_dev : (k + 1) * rows_dev] for k in range(shards // 4)]
-        following = sum((swapped(parts[k], 4 * k) for k in range(1, shards // 4)), parts[0])
     for bit in high:
-        if following.shape[0] > rows_dev:
-            half = following.shape[0] // 2
-            following = following[:half] + swapped(following[half:], bit)
+        half = following.shape[0] // 2
+        following = following[:half] + swapped(following[half:], bit)
+    embedded = (following.astype(jnp.float32) * math.sqrt(width)).astype(jnp.bfloat16)
+    for bit in high[:-1]:
         stats = merged(stats, swapped(stats, bit))
-    embedded = (following.astype(jnp.float32) * math.sqrt(width)).astype(jnp.bfloat16)
-    stats = paired(merge_kernel, stats, swapped(stats, 2), 2, "merge", following)
+    stats = paired(merge_kernel, stats, swapped(stats, high[-1]), 2, "merge", following)
+    stats = merged(stats, swapped(stats, 2))
     logprobs = finished(scaled, stats, swapped(stats, 1), places)
     return logprobs, embedded
 

time: 50.7 us -> 49.6 us (0.978)
  Pallas kernels: 14.7 us -> 13.6 us
    pallas_call x2, Pallas kernels: 4.71 us -> 3.68 us  [picked_rows(): pl.pallas_call(functools.partial(pick_kernel, step, places), out_shape=ou...]
    ppermute x17 -> x16, waiting for transfers between devices: 11.4 us -> 11.9 us  [swapped(): return lax.ppermute(rows, 'vocab', pairs)]
    ppermute x17 -> x16, starting transfers between devices: 22.5 us -> 22 us  [swapped(): return lax.ppermute(rows, 'vocab', pairs)]
  transfers between devices with their start and end apart: 17 -> 16, of which waited for: 9 -> 10; matrix products, arithmetic and copies ran while one was open for 2% -> 2% of each run, Pallas kernels for 22% -> 22%
where the time goes in v7:
time: 49.6 us; the launch traced here: 49.4 us
  starting transfers between devices  22 us (44%)
  Pallas kernels  13.6 us (27%)
  waiting for transfers between devices  11.9 us (24%)
  other arithmetic  0.87 us (2%)
  between operations  0.84 us (2%)
    ppermute x16, starting transfers between devices, swapped(): return lax.ppermute(rows, 'vocab', pairs)  22 us
    ppermute x16, waiting for transfers between devices, swapped(): return lax.ppermute(rows, 'vocab', pairs)  11.9 us
    pallas_call x2, Pallas kernels, loaded(): pl.pallas_call(functools.partial(load_kernel, part), out_shape=(jax.Shape...  5.24 us
    pallas_call x2, Pallas kernels, picked_rows(): pl.pallas_call(functools.partial(pick_kernel, step, places), out_shape=ou...  3.68 us
    pallas_call x1, Pallas kernels, head(): pl.pallas_call(head_kernel, out_shape=(jax.ShapeDtypeStruct((voc_dev, row...  3.14 us
  transfers between devices with their start and end apart: 16, of which 10 were waited for; matrix products, arithmetic and copies ran while one was open for 2% of the time, Pallas kernels for 22%

profile of v7, /device:TPU:0, one launch (start us, length us, event | category | flops | bytes accessed | tf_op | source)
XLA Modules:
  0.0 49.4 jit_solution(14838224673965374957)
XLA Ops:
  0.6 0.0 copy-start.1
  0.6 0.0 copy-start
  0.7 0.0 copy-start.2
  0.7 1.4 %pick.2 = (bf16[16,5376]{1,0:T(8,128)(2,1)S(1)}, bf16[16,5376]{1,0:T(8,128)(2,1)S(1)}, f32[1,64]{1,0:T(1,128)S(1)}) custom-call(s32[2,32]{1,0:T(2,128)} %ids_ref.3, bf16[1024,5376]{1,0:T(8,128)(2,1)} %table_ref.7, s32[2,32]{1,0:T(2,128)} %refs_0_.1, f32[8]{0:T(128)} %refs_1_.1), custom_call_target="tpu_custom_call" | custom-call | tf_op jit(solution)/shard_map/pick/pallas_call | solution.py:125
  2.0 1.6 %collective-permute-start = (bf16[16,5376]{1,0:T(8,128)(2,1)S(1)}, bf16[16,5376]{1,0:T(8,128)(2,1)S(1)}, u32[]{:S(2)}, u32[]{:S(2)}) collective-permute-start(bf16[16,5376]{1,0:T(8,128)(2,1)S(1)} %get-tuple-element.17), channel_id=1, source_target_pairs={{0,1},{1,0},{2,3},{3,2},{4,5},{5,4},{6,7},{7,6},{8,9},{9,8},{10,11... | collective-permute-start | bytes 516104 | tf_op jit(solution)/shard_map/ppermute | solution.py:216
  3.7 1.0 %collective-permute-done.got_ref = bf16[16,5376]{1,0:T(8,128)(2,1)S(1)} collective-permute-done((bf16[16,5376]{1,0:T(8,128)(2,1)S(1)}, bf16[16,5376]{1,0:T(8,128)(2,1)S(1)}, u32[]{:S(2)}, u32[]{:S(2)}) %collective-permute-start) | collective-permute-done | bytes 172064 | tf_op jit(solution)/shard_map/ppermute | solution.py:216
  4.7 0.0 copy-done.1
  4.7 0.0 copy-done
  4.7 0.1 fold.1
  4.8 2.8 %collective-permute-start.2 = (bf16[8,5376]{1,0:T(8,128)(2,1)S(1)}, bf16[8,5376]{1,0:T(8,128)(2,1)S(1)}, u32[]{:S(2)}, u32[]{:S(2)}) collective-permute-start(bf16[8,5376]{1,0:T(8,128)(2,1)S(1)} %get-tuple-element.20), channel_id=1, source_target_pairs={{0,2},{1,3},{2,0},{3,1},{4,6},{5,7},{6,4},{7,5},{8,10},{9,11},{10,... | collective-permute-start | bytes 258056 | tf_op jit(solution)/shard_map/ppermute | solution.py:216
  7.6 2.7 %collective-permute-start.1 = (bf16[4,5376]{1,0:T(4,128)(2,1)S(1)}, bf16[4,5376]{1,0:T(4,128)(2,1)S(1)}, u32[]{:S(2)}, u32[]{:S(2)}) collective-permute-start(bf16[4,5376]{1,0:T(4,128)(2,1)S(1)} %get-tuple-element.18.own_ref), channel_id=1, source_target_pairs={{0,8},{1,9},{2,10},{3,11},{4,12},{5,13},{6,14},{7,15},{8,0},{9,1},... | collective-permute-start | bytes 129032 | tf_op jit(solution)/shard_map/ppermute | solution.py:216
  10.3 0.1 collective-permute-done.2
  10.4 3.1 %collective-permute-start.4 = (bf16[8,5376]{1,0:T(8,128)(2,1)S(1)}, bf16[8,5376]{1,0:T(8,128)(2,1)S(1)}, u32[]{:S(2)}, u32[]{:S(2)}) collective-permute-start(bf16[8,5376]{1,0:T(8,128)(2,1)S(1)} %add.23.refs_0_.own_ref), channel_id=1, source_target_pairs={{0,8},{1,9},{2,10},{3,11},{4,12},{5,13},{6,14},{7,15},{8,0},{9,1},... | collective-permute-start | bytes 258056 | tf_op jit(solution)/shard_map/ppermute | solution.py:216
  13.6 0.0 collective-permute-done.1.got_ref
  13.6 1.7 %collective-permute-start.3 = (bf16[8,5376]{1,0:T(8,128)(2,1)S(1)}, bf16[8,5376]{1,0:T(8,128)(2,1)S(1)}, u32[]{:S(2)}, u32[]{:S(2)}) collective-permute-start(bf16[8,5376]{1,0:T(8,128)(2,1)S(1)} %join.1), channel_id=1, source_target_pairs={{0,4},{1,5},{2,6},{3,7},{4,0},{5,1},{6,2},{7,3},{8,12},{9,13},{10,... | collective-permute-start | bytes 258056 | tf_op jit(solution)/shard_map/ppermute | solution.py:216
  15.4 2.3 %pick.3 = (bf16[16,5376]{1,0:T(8,128)(2,1)S(1)}, bf16[16,5376]{1,0:T(8,128)(2,1)S(1)}) custom-call(s32[2,32]{1,0:T(2,128)} %ids_ref.3, bf16[1024,5376]{1,0:T(8,128)(2,1)} %table_ref.7, bf16[8,5376]{1,0:T(8,128)(2,1)S(1)} %add.23.refs_0_.own_ref), custom_call_target="tpu_custom_call" | custom-call | tf_op jit(solution)/shard_map/pick/pallas_call | solution.py:125
  17.7 0.1 collective-permute-start.6
  17.8 0.0 collective-permute-done.4.got_ref
  17.8 0.9 %collective-permute-start.5 = (bf16[8,5376]{1,0:T(8,128)(2,1)S(1)}, bf16[8,5376]{1,0:T(8,128)(2,1)S(1)}, u32[]{:S(2)}, u32[]{:S(2)}) collective-permute-start(bf16[8,5376]{1,0:T(8,128)(2,1)S(1)} %plus.1.refs_0_.own_ref), channel_id=1, source_target_pairs={{0,4},{1,5},{2,6},{3,7},{4,0},{5,1},{6,2},{7,3},{8,12},{9,13},{10,... | collective-permute-start | bytes 258056 | tf_op jit(solution)/shard_map/ppermute | solution.py:216
  18.7 0.0 collective-permute-done.3
  18.7 0.5 collective-permute-done.6
  19.2 1.2 %collective-permute-start.7 = (bf16[8,5376]{1,0:T(8,128)(2,1)S(1)}, bf16[8,5376]{1,0:T(8,128)(2,1)S(1)}, u32[]{:S(2)}, u32[]{:S(2)}) collective-permute-start(bf16[8,5376]{1,0:T(8,128)(2,1)S(1)} %slice.81), channel_id=1, source_target_pairs={{0,2},{1,3},{2,0},{3,1},{4,6},{5,7},{6,4},{7,5},{8,10},{9,11},{10,... | collective-permute-start | bytes 258056 | tf_op jit(solution)/shard_map/ppermute | solution.py:216
  20.5 0.1 pad_maximum_fusion
  20.6 2.6 %load.2 = (bf16[1024,5376]{1,0:T(8,128)(2,1)S(1)}, f32[8,128]{1,0:T(8,128)S(1)}) custom-call(bf16[1024,5376]{1,0:T(8,128)(2,1)} %table_ref.7, bf16[8,5376]{1,0:T(8,128)(2,1)S(1)} %plus.1.refs_0_.own_ref), custom_call_target="tpu_custom_call" | custom-call | tf_op jit(solution)/shard_map/load/pallas_call | solution.py:242
  23.2 0.7 %collective-permute-done.7 = bf16[8,5376]{1,0:T(8,128)(2,1)S(1)} collective-permute-done((bf16[8,5376]{1,0:T(8,128)(2,1)S(1)}, bf16[8,5376]{1,0:T(8,128)(2,1)S(1)}, u32[]{:S(2)}, u32[]{:S(2)}) %collective-permute-start.7) | collective-permute-done | bytes 86048 | tf_op jit(solution)/shard_map/ppermute | solution.py:216
  23.9 0.0 collective-permute-done.5.got_ref
  23.9 0.3 norm.1.refs_0_.own_ref
  24.2 1.2 %collective-permute-start.8 = (bf16[16,5376]{1,0:T(8,128)(2,1)S(1)}, bf16[16,5376]{1,0:T(8,128)(2,1)S(1)}, u32[]{:S(2)}, u32[]{:S(2)}) collective-permute-start(bf16[16,5376]{1,0:T(8,128)(2,1)S(1)} %norm.1.refs_0_.own_ref), channel_id=1, source_target_pairs={{0,2},{1,3},{2,0},{3,1},{4,6},{5,7},{6,4},{7,5},{8,10},{9,11},{10,... | collective-permute-start | bytes 516104 | tf_op jit(solution)/shard_map/ppermute | solution.py:216
  25.5 2.6 %load.3 = (bf16[1024,5376]{1,0:T(8,128)(2,1)S(1)}, f32[8,128]{1,0:T(8,128)S(1)}) custom-call(bf16[1024,5376]{1,0:T(8,128)(2,1)} %table_ref.7, bf16[16,5376]{1,0:T(8,128)(2,1)S(1)} %norm.1.refs_0_.own_ref, bf16[1024,5376]{1,0:T(8,128)(2,1)S(1)} %get-tuple-element.24.refs_1_), custom_call_target="tpu_custom_call", output_to_operand_aliasing={{0}: (2, {})} | custom-call | tf_op jit(solution)/shard_map/load/pallas_call | solution.py:242
  28.1 1.8 %collective-permute-done.8.got_ref = bf16[16,5376]{1,0:T(8,128)(2,1)S(1)} collective-permute-done((bf16[16,5376]{1,0:T(8,128)(2,1)S(1)}, bf16[16,5376]{1,0:T(8,128)(2,1)S(1)}, u32[]{:S(2)}, u32[]{:S(2)}) %collective-permute-start.8) | collective-permute-done | bytes 172064 | tf_op jit(solution)/shard_map/ppermute | solution.py:216
  29.9 0.1 collective-permute-start.9
  30.1 2.3 %collective-permute-start.12 = (bf16[4,5376]{1,0:T(4,128)(2,1)S(1)}, bf16[4,5376]{1,0:T(4,128)(2,1)S(1)}, u32[]{:S(2)}, u32[]{:S(2)}) collective-permute-start(bf16[4,5376]{1,0:T(4,128)(2,1)S(1)} %slice.83), channel_id=1, source_target_pairs={{0,8},{1,9},{2,10},{3,11},{4,12},{5,13},{6,14},{7,15},{8,0},{9,1},... | collective-permute-start | bytes 129032 | tf_op jit(solution)/shard_map/ppermute | solution.py:216
  32.3 0.0 collective-permute-done.9.got_ref
  32.3 3.1 %head.1 = (f32[1024,64]{1,0:T(8,128)S(1)}, f32[2,64]{1,0:T(2,128)S(1)}) custom-call(bf16[32,5376]{1,0:T(8,128)(2,1)S(1)} %chips.1.own_ref, bf16[32,5376]{1,0:T(8,128)(2,1)S(1)} %collective-permute-done.9.got_ref, bf16[1024,5376]{1,0:T(8,128)(2,1)S(1)} %get-tuple-element.26.table_ref, f32[1,64]{1,0:T(1,128)S(1)} %get-tuple-element.27.temps_ref), custom_call_target="tpu_custom_call" | custom-call | tf_op jit(solution)/shard_map/head/pallas_call | solution.py:319
  35.5 1.6 %collective-permute-start.10 = (f32[2,64]{1,0:T(2,128)S(1)}, f32[2,64]{1,0:T(2,128)S(1)}, u32[]{:S(2)}, u32[]{:S(2)}) collective-permute-start(f32[2,64]{1,0:T(2,128)S(1)} %get-tuple-element.29), channel_id=1, source_target_pairs={{0,8},{1,9},{2,10},{3,11},{4,12},{5,13},{6,14},{7,15},{8,0},{9,1},... | collective-permute-start | bytes 1544 | tf_op jit(solution)/shard_map/ppermute | solution.py:216
  37.1 0.0 collective-permute-done.12
  37.1 0.6 %collective-permute-start.13 = (bf16[2,5376]{1,0:T(2,128)(2,1)S(1)}, bf16[2,5376]{1,0:T(2,128)(2,1)S(1)}, u32[]{:S(2)}, u32[]{:S(2)}) collective-permute-start(bf16[2,5376]{1,0:T(2,128)(2,1)S(1)} %slice.85), channel_id=1, source_target_pairs={{0,4},{1,5},{2,6},{3,7},{4,0},{5,1},{6,2},{7,3},{8,12},{9,13},{10,... | collective-permute-start | bytes 64520 | tf_op jit(solution)/shard_map/ppermute | solution.py:216
  37.7 2.3 %collective-permute-done.10 = f32[2,64]{1,0:T(2,128)S(1)} collective-permute-done((f32[2,64]{1,0:T(2,128)S(1)}, f32[2,64]{1,0:T(2,128)S(1)}, u32[]{:S(2)}, u32[]{:S(2)}) %collective-permute-start.10) | collective-permute-done | bytes 544 | tf_op jit(solution)/shard_map/ppermute | solution.py:216
  40.0 0.6 %collective-permute-start.11 = (f32[2,64]{1,0:T(2,128)S(1)}, f32[2,64]{1,0:T(2,128)S(1)}, u32[]{:S(2)}, u32[]{:S(2)}) collective-permute-start(f32[2,64]{1,0:T(2,128)S(1)} %pad_maximum_fusion.2.own_ref), channel_id=1, source_target_pairs={{0,4},{1,5},{2,6},{3,7},{4,0},{5,1},{6,2},{7,3},{8,12},{9,13},{10,... | collective-permute-start | bytes 1544 | tf_op jit(solution)/shard_map/ppermute | solution.py:216
  40.6 0.4 collective-permute-done.13
  41.0 0.6 %multiply_convert_fusion = (bf16[2,5376]{1,0:T(2,128)(2,1)}, bf16[2,5376]{1,0:T(2,128)(2,1)S(1)}) fusion(bf16[2,5376]{1,0:T(2,128)(2,1)S(1)} %collective-permute-done.13, bf16[4,5376]{1,0:T(4,128)(2,1)S(1)} %slice_add_fusion.1), kind=kLoop, calls=%fused_computation.4 | loop fusion | flops 43008 | bytes 86016 | tf_op jit(solution)/shard_map/convert_element_type | solution.py:419
  41.7 2.0 %collective-permute-done.11.got_ref = f32[2,64]{1,0:T(2,128)S(1)} collective-permute-done((f32[2,64]{1,0:T(2,128)S(1)}, f32[2,64]{1,0:T(2,128)S(1)}, u32[]{:S(2)}, u32[]{:S(2)}) %collective-permute-start.11) | collective-permute-done | bytes 544 | tf_op jit(solution)/shard_map/ppermute | solution.py:216
  43.7 1.4 %collective-permute-start.14 = (f32[2,64]{1,0:T(2,128)S(1)}, f32[2,64]{1,0:T(2,128)S(1)}, u32[]{:S(2)}, u32[]{:S(2)}) collective-permute-start(f32[2,64]{1,0:T(2,128)S(1)} %merge.1), channel_id=1, source_target_pairs={{0,2},{1,3},{2,0},{3,1},{4,6},{5,7},{6,4},{7,5},{8,10},{9,11},{10,... | collective-permute-start | bytes 1544 | tf_op jit(solution)/shard_map/ppermute | solution.py:216
  45.1 2.2 %collective-permute-done.14 = f32[2,64]{1,0:T(2,128)S(1)} collective-permute-done((f32[2,64]{1,0:T(2,128)S(1)}, f32[2,64]{1,0:T(2,128)S(1)}, u32[]{:S(2)}, u32[]{:S(2)}) %collective-permute-start.14) | collective-permute-done | bytes 544 | tf_op jit(solution)/shard_map/ppermute | solution.py:216
  47.3 0.1 collective-permute-start.15
  47.4 0.2 turn.1.scaled_ref
  47.6 0.9 %collective-permute-done.15.got_ref = f32[2,64]{1,0:T(2,128)S(1)} collective-permute-done((f32[2,64]{1,0:T(2,128)S(1)}, f32[2,64]{1,0:T(2,128)S(1)}, u32[]{:S(2)}, u32[]{:S(2)}) %collective-permute-start.15) | collective-permute-done | bytes 544 | tf_op jit(solution)/shard_map/ppermute | solution.py:216
  48.5 0.9 %finish.1 = f32[2,32,1024]{2,1,0:T(8,128)} custom-call(f32[2,32,1024]{2,1,0:T(8,128)S(1)} %turn.1.scaled_ref, f32[2,64]{1,0:T(2,128)S(1)} %pad_maximum_fusion.3.own_ref, f32[2,64]{1,0:T(2,128)S(1)} %collective-permute-done.15.got_ref), custom_call_target="tpu_custom_call" | custom-call | tf_op jit(solution)/shard_map/finish/pallas_call | solution.py:365
  (19 shorter events, 0.4 us)
Async XLA Ops:
  0.6 4.1 %copy-start.1 = (bf16[2,5376]{1,0:T(2,128)(2,1)S(1)}, bf16[2,5376]{1,0:T(2,128)(2,1)}, u32[]{:S(2)}) copy-start(bf16[2,5376]{1,0:T(2,128)(2,1)} %delta_ref.1) | copy-start | bytes 64516
  0.6 4.1 %copy-start = (bf16[2,5376]{1,0:T(2,128)(2,1)S(1)}, bf16[2,5376]{1,0:T(2,128)(2,1)}, u32[]{:S(2)}) copy-start(bf16[2,5376]{1,0:T(2,128)(2,1)} %first_ref.1) | copy-start | bytes 64516
  0.7 9.6 %copy-start.2 = (f32[5376]{0:T(1024)S(1)}, f32[5376]{0:T(1024)}, u32[]{:S(2)}) copy-start(f32[5376]{0:T(1024)} %param.9) | copy-start | bytes 64516
  2.0 2.7 %collective-permute-start = (bf16[16,5376]{1,0:T(8,128)(2,1)S(1)}, bf16[16,5376]{1,0:T(8,128)(2,1)S(1)}, u32[]{:S(2)}, u32[]{:S(2)}) collective-permute-start(bf16[16,5376]{1,0:T(8,128)(2,1)S(1)} %get-tuple-element.17), channel_id=1, source_target_pairs={{0,1},{1,0},{2,3},{3,2},{4,5},{5,4},{6,7},{7,6},{8,9},{9,8},{10,11... | collective-permute-start | bytes 516104 | tf_op jit(solution)/shard_map/ppermute | solution.py:216
  4.8 5.6 %collective-permute-start.2 = (bf16[8,5376]{1,0:T(8,128)(2,1)S(1)}, bf16[8,5376]{1,0:T(8,128)(2,1)S(1)}, u32[]{:S(2)}, u32[]{:S(2)}) collective-permute-start(bf16[8,5376]{1,0:T(8,128)(2,1)S(1)} %get-tuple-element.20), channel_id=1, source_target_pairs={{0,2},{1,3},{2,0},{3,1},{4,6},{5,7},{6,4},{7,5},{8,10},{9,11},{10,... | collective-permute-start | bytes 258056 | tf_op jit(solution)/shard_map/ppermute | solution.py:216
  7.6 6.0 %collective-permute-start.1 = (bf16[4,5376]{1,0:T(4,128)(2,1)S(1)}, bf16[4,5376]{1,0:T(4,128)(2,1)S(1)}, u32[]{:S(2)}, u32[]{:S(2)}) collective-permute-start(bf16[4,5376]{1,0:T(4,128)(2,1)S(1)} %get-tuple-element.18.own_ref), channel_id=1, source_target_pairs={{0,8},{1,9},{2,10},{3,11},{4,12},{5,13},{6,14},{7,15},{8,0},{9,1},... | collective-permute-start | bytes 129032 | tf_op jit(solution)/shard_map/ppermute | solution.py:216
  10.4 7.4 %collective-permute-start.4 = (bf16[8,5376]{1,0:T(8,128)(2,1)S(1)}, bf16[8,5376]{1,0:T(8,128)(2,1)S(1)}, u32[]{:S(2)}, u32[]{:S(2)}) collective-permute-start(bf16[8,5376]{1,0:T(8,128)(2,1)S(1)} %add.23.refs_0_.own_ref), channel_id=1, source_target_pairs={{0,8},{1,9},{2,10},{3,11},{4,12},{5,13},{6,14},{7,15},{8,0},{9,1},... | collective-permute-start | bytes 258056 | tf_op jit(solution)/shard_map/ppermute | solution.py:216
  13.6 5.1 %collective-permute-start.3 = (bf16[8,5376]{1,0:T(8,128)(2,1)S(1)}, bf16[8,5376]{1,0:T(8,128)(2,1)S(1)}, u32[]{:S(2)}, u32[]{:S(2)}) collective-permute-start(bf16[8,5376]{1,0:T(8,128)(2,1)S(1)} %join.1), channel_id=1, source_target_pairs={{0,4},{1,5},{2,6},{3,7},{4,0},{5,1},{6,2},{7,3},{8,12},{9,13},{10,... | collective-permute-start | bytes 258056 | tf_op jit(solution)/shard_map/ppermute | solution.py:216
  17.7 1.5 %collective-permute-start.6 = (bf16[16,5376]{1,0:T(8,128)(2,1)S(1)}, bf16[16,5376]{1,0:T(8,128)(2,1)S(1)}, u32[]{:S(2)}, u32[]{:S(2)}) collective-permute-start(bf16[16,5376]{1,0:T(8,128)(2,1)S(1)} %get-tuple-element.21.refs_0_), channel_id=1, source_target_pairs={{0,1},{1,0},{2,3},{3,2},{4,5},{5,4},{6,7},{7,6},{8,9},{9,8},{10,11... | collective-permute-start | bytes 516104 | tf_op jit(solution)/shard_map/ppermute | solution.py:216
  17.8 6.1 %collective-permute-start.5 = (bf16[8,5376]{1,0:T(8,128)(2,1)S(1)}, bf16[8,5376]{1,0:T(8,128)(2,1)S(1)}, u32[]{:S(2)}, u32[]{:S(2)}) collective-permute-start(bf16[8,5376]{1,0:T(8,128)(2,1)S(1)} %plus.1.refs_0_.own_ref), channel_id=1, source_target_pairs={{0,4},{1,5},{2,6},{3,7},{4,0},{5,1},{6,2},{7,3},{8,12},{9,13},{10,... | collective-permute-start | bytes 258056 | tf_op jit(solution)/shard_map/ppermute | solution.py:216
  19.2 4.6 %collective-permute-start.7 = (bf16[8,5376]{1,0:T(8,128)(2,1)S(1)}, bf16[8,5376]{1,0:T(8,128)(2,1)S(1)}, u32[]{:S(2)}, u32[]{:S(2)}) collective-permute-start(bf16[8,5376]{1,0:T(8,128)(2,1)S(1)} %slice.81), channel_id=1, source_target_pairs={{0,2},{1,3},{2,0},{3,1},{4,6},{5,7},{6,4},{7,5},{8,10},{9,11},{10,... | collective-permute-start | bytes 258056 | tf_op jit(solution)/shard_map/ppermute | solution.py:216
  24.2 5.7 %collective-permute-start.8 = (bf16[16,5376]{1,0:T(8,128)(2,1)S(1)}, bf16[16,5376]{1,0:T(8,128)(2,1)S(1)}, u32[]{:S(2)}, u32[]{:S(2)}) collective-permute-start(bf16[16,5376]{1,0:T(8,128)(2,1)S(1)} %norm.1.refs_0_.own_ref), channel_id=1, source_target_pairs={{0,2},{1,3},{2,0},{3,1},{4,6},{5,7},{6,4},{7,5},{8,10},{9,11},{10,... | collective-permute-start | bytes 516104 | tf_op jit(solution)/shard_map/ppermute | solution.py:216
  29.9 2.4 %collective-permute-start.9 = (bf16[32,5376]{1,0:T(8,128)(2,1)S(1)}, bf16[32,5376]{1,0:T(8,128)(2,1)S(1)}, u32[]{:S(2)}, u32[]{:S(2)}) collective-permute-start(bf16[32,5376]{1,0:T(8,128)(2,1)S(1)} %chips.1.own_ref), channel_id=1, source_target_pairs={{0,1},{1,0},{2,3},{3,2},{4,5},{5,4},{6,7},{7,6},{8,9},{9,8},{10,11... | collective-permute-start | bytes 1032200 | tf_op jit(solution)/shard_map/ppermute | solution.py:216
  30.1 7.0 %collective-permute-start.12 = (bf16[4,5376]{1,0:T(4,128)(2,1)S(1)}, bf16[4,5376]{1,0:T(4,128)(2,1)S(1)}, u32[]{:S(2)}, u32[]{:S(2)}) collective-permute-start(bf16[4,5376]{1,0:T(4,128)(2,1)S(1)} %slice.83), channel_id=1, source_target_pairs={{0,8},{1,9},{2,10},{3,11},{4,12},{5,13},{6,14},{7,15},{8,0},{9,1},... | collective-permute-start | bytes 129032 | tf_op jit(solution)/shard_map/ppermute | solution.py:216
  35.5 4.5 %collective-permute-start.10 = (f32[2,64]{1,0:T(2,128)S(1)}, f32[2,64]{1,0:T(2,128)S(1)}, u32[]{:S(2)}, u32[]{:S(2)}) collective-permute-start(f32[2,64]{1,0:T(2,128)S(1)} %get-tuple-element.29), channel_id=1, source_target_pairs={{0,8},{1,9},{2,10},{3,11},{4,12},{5,13},{6,14},{7,15},{8,0},{9,1},... | collective-permute-start | bytes 1544 | tf_op jit(solution)/shard_map/ppermute | solution.py:216
  37.1 3.9 %collective-permute-start.13 = (bf16[2,5376]{1,0:T(2,128)(2,1)S(1)}, bf16[2,5376]{1,0:T(2,128)(2,1)S(1)}, u32[]{:S(2)}, u32[]{:S(2)}) collective-permute-start(bf16[2,5376]{1,0:T(2,128)(2,1)S(1)} %slice.85), channel_id=1, source_target_pairs={{0,4},{1,5},{2,6},{3,7},{4,0},{5,1},{6,2},{7,3},{8,12},{9,13},{10,... | collective-permute-start | bytes 64520 | tf_op jit(solution)/shard_map/ppermute | solution.py:216
  40.0 3.6 %collective-permute-start.11 = (f32[2,64]{1,0:T(2,128)S(1)}, f32[2,64]{1,0:T(2,128)S(1)}, u32[]{:S(2)}, u32[]{:S(2)}) collective-permute-start(f32[2,64]{1,0:T(2,128)S(1)} %pad_maximum_fusion.2.own_ref), channel_id=1, source_target_pairs={{0,4},{1,5},{2,6},{3,7},{4,0},{5,1},{6,2},{7,3},{8,12},{9,13},{10,... | collective-permute-start | bytes 1544 | tf_op jit(solution)/shard_map/ppermute | solution.py:216
  43.7 3.6 %collective-permute-start.14 = (f32[2,64]{1,0:T(2,128)S(1)}, f32[2,64]{1,0:T(2,128)S(1)}, u32[]{:S(2)}, u32[]{:S(2)}) collective-permute-start(f32[2,64]{1,0:T(2,128)S(1)} %merge.1), channel_id=1, source_target_pairs={{0,2},{1,3},{2,0},{3,1},{4,6},{5,7},{6,4},{7,5},{8,10},{9,11},{10,... | collective-permute-start | bytes 1544 | tf_op jit(solution)/shard_map/ppermute | solution.py:216
  47.3 1.2 %collective-permute-start.15 = (f32[2,64]{1,0:T(2,128)S(1)}, f32[2,64]{1,0:T(2,128)S(1)}, u32[]{:S(2)}, u32[]{:S(2)}) collective-permute-start(f32[2,64]{1,0:T(2,128)S(1)} %pad_maximum_fusion.3.own_ref), channel_id=1, source_target_pairs={{0,1},{1,0},{2,3},{3,2},{4,5},{5,4},{6,7},{7,6},{8,9},{9,8},{10,11... | collective-permute-start | bytes 1544 | tf_op jit(solution)/shard_map/ppermute | solution.py:216

commit v8 on v7

--- a/solution.py
+++ b/solution.py
@@ -40,7 +40,8 @@
             pltpu.make_async_copy(heat_ref, heat, heat_sems.at[1]),
         ]
     else:
-        outs = refs[-2:]
+        after_ref, *outs, head_ref, head_sems = refs
+        head_copies = part_copies(table_ref, head_ref, head_sems, 0)
     count = ids_ref.shape[1]
     held = slots.shape[0]
     voc_dev = table_ref.shape[0]
@@ -78,6 +79,9 @@
         def _(n):
             copy(n).start()
 
+        if not places and first == 0:
+            for part in head_copies:
+                part.start()
         if places and first == 0:
             for fetched in heat_copies:
                 fetched.wait()
@@ -108,6 +112,9 @@
     half = count // 2
     for part, out in enumerate(outs):
         out[...] = rows[part * half : (part + 1) * half].astype(out.dtype)
+    if not places:
+        for part in head_copies:
+            part.wait()
 
 
 def picked_rows(ids, table, step, places, *others):
@@ -121,6 +128,9 @@
         others = [in_hbm(other) for other in others]
         heat = [pltpu.SMEM(other.shape, other.dtype) for other in others]
         heat += [pltpu.SemaphoreType.DMA((2,))]
+    else:
+        out += (jax.ShapeDtypeStruct(table.shape, table.dtype),)
+        heat = [pltpu.SemaphoreType.DMA((4,))]
     anywhere, vmem = pl.BlockSpec(memory_space=pl.ANY), pl.BlockSpec(memory_space=pltpu.VMEM)
     return pl.pallas_call(
         functools.partial(pick_kernel, step, places),
@@ -216,9 +226,8 @@
     return lax.ppermute(rows, "vocab", pairs)
 
 
-def load_kernel(part, table_ref, *refs):
-    out_ref, token_ref, sems = refs[-3:]
-    copies = part_copies(table_ref, out_ref, sems, table_ref.shape[0] // 2 * part)
+def load_kernel(table_ref, after_ref, held_ref, out_ref, token_ref, sems):
+    copies = part_copies(table_ref, out_ref, sems, table_ref.shape[0] // 2)
     for copy in copies:
         copy.start()
     token_ref[...] = jnp.zeros_like(token_ref)
@@ -236,22 +245,21 @@
     ]
 
 
-def loaded(table, after, held=None):
+def loaded(table, held, after):
     anywhere, vmem = pl.BlockSpec(memory_space=pl.ANY), pl.BlockSpec(memory_space=pltpu.VMEM)
-    part = 0 if held is None else 1
-    return pl.pallas_call(
-        functools.partial(load_kernel, part),
+    return pl.pallas_call(
+        load_kernel,
         out_shape=(
             jax.ShapeDtypeStruct(table.shape, table.dtype),
             jax.ShapeDtypeStruct((8, 128), jnp.float32),
         ),
-        in_specs=[anywhere] * 2 + [vmem] * part,
+        in_specs=[anywhere, anywhere, vmem],
         out_specs=(vmem, vmem),
-        input_output_aliases={2: 0} if part else {},
+        input_output_aliases={2: 0},
         scratch_shapes=[pltpu.SemaphoreType.DMA((4,))],
         compiler_params=pltpu.CompilerParams(vmem_limit_bytes=4 * MIB),
         name="load",
-    )(in_hbm(table), after, *([held] if part else []))
+    )(in_hbm(table), after, held)
 
 
 def norm_kernel(first_ref, own_ref, got_ref, delta_ref, gain_ref, *refs):
@@ -394,7 +402,7 @@
     keep, send, temps = picked_rows(ids, table, 0, places, classes, lookup)
     own, send, beside = folded(keep, swapped(send, 1), first, deltas)
     own = own + swapped(send, 2)
-    keep, send = picked_rows(ids, table, 1, (), own)
+    keep, send, head_table = picked_rows(ids, table, 1, (), own)
     keep = keep + swapped(send, 1)
     following = keep[:quarter] + swapped(keep[quarter:], 2)
     for k, bit in enumerate(high):
@@ -406,9 +414,8 @@
             own = paired(plus_kernel, own, got, quarter, "plus", send)
     state = jnp.concatenate([beside[:held], moved[:held]], axis=0)
     delta = jnp.concatenate([beside[held:], moved[held:]], axis=0)
-    head_table, token = loaded(table, own)
-    states = normed(state, own, got, delta, gain, token, following)
-    head_table, token = loaded(table, states, head_table)
+    states = normed(state, own, got, delta, gain, following)
+    head_table, token = loaded(table, head_table, states)
     states = paired(chips_kernel, states, swapped(states, 2), rows, "chips", token)
     others = swapped(states, 1)
     scaled, stats = head(states, others, head_table, temps)

time: 49.6 us -> 51 us (1.028)
  waiting for transfers between devices: 11.9 us -> 14.2 us
  starting transfers between devices: 22 us -> 21.2 us
    pallas_call x2, Pallas kernels: 3.68 us -> 6.48 us  [picked_rows(): pl.pallas_call(functools.partial(pick_kernel, step, places), out_shape=ou...]
    pallas_call x2 -> x1, Pallas kernels: 5.24 us -> 2.62 us  [loaded(): pl.pallas_call(load_kernel, out_shape=(jax.ShapeDtypeStruct(table.shape,...]
    ppermute x16, waiting for transfers between devices: 11.9 us -> 14.2 us  [swapped(): return lax.ppermute(rows, 'vocab', pairs)]
    ppermute x16, starting transfers between devices: 22 us -> 21.2 us  [swapped(): return lax.ppermute(rows, 'vocab', pairs)]
  transfers between devices with their start and end apart: 16 -> 16, of which waited for: 10 -> 9; matrix products, arithmetic and copies ran while one was open for 2% -> 2% of each run, Pallas kernels for 22% -> 20%
where the time goes in v8:
time: 51 us
  starting transfers between devices  21.2 us (42%)
  waiting for transfers between devices  14.2 us (28%)
  Pallas kernels  13.8 us (27%)
  other arithmetic  0.88 us (2%)
  between operations  0.84 us (2%)
    ppermute x16, starting transfers between devices, swapped(): return lax.ppermute(rows, 'vocab', pairs)  21.2 us
    ppermute x16, waiting for transfers between devices, swapped(): return lax.ppermute(rows, 'vocab', pairs)  14.2 us
    pallas_call x2, Pallas kernels, picked_rows(): pl.pallas_call(functools.partial(pick_kernel, step, places), out_shape=ou...  6.48 us
    pallas_call x1, Pallas kernels, head(): pl.pallas_call(head_kernel, out_shape=(jax.ShapeDtypeStruct((voc_dev, row...  3.15 us
    pallas_call x1, Pallas kernels, loaded(): pl.pallas_call(load_kernel, out_shape=(jax.ShapeDtypeStruct(table.shape,...  2.62 us
  transfers between devices with their start and end apart: 16, of which 9 were waited for; matrix products, arithmetic and copies ran while one was open for 2% of the time, Pallas kernels for 20%

profile of v8, /device:TPU:0, one launch (start us, length us, event | category | flops | bytes accessed | tf_op | source)
XLA Modules:
  0.0 51.0 jit_solution(5268104873274730571)
XLA Ops:
  0.6 0.0 copy-start
  0.6 0.0 copy-start.1
  0.7 0.0 copy-start.2
  0.7 2.5 %pick.2 = (bf16[16,5376]{1,0:T(8,128)(2,1)S(1)}, bf16[16,5376]{1,0:T(8,128)(2,1)S(1)}, f32[1,64]{1,0:T(1,128)S(1)}) custom-call(s32[2,32]{1,0:T(2,128)} %ids_ref.3, bf16[1024,5376]{1,0:T(8,128)(2,1)} %table_ref.5, s32[2,32]{1,0:T(2,128)} %refs_0_.1, f32[8]{0:T(128)} %refs_1_.1), custom_call_target="tpu_custom_call" | custom-call | tf_op jit(solution)/shard_map/pick/pallas_call | solution.py:135
  3.1 0.3 collective-permute-start
  3.5 1.1 %collective-permute-done.got_ref = bf16[16,5376]{1,0:T(8,128)(2,1)S(1)} collective-permute-done((bf16[16,5376]{1,0:T(8,128)(2,1)S(1)}, bf16[16,5376]{1,0:T(8,128)(2,1)S(1)}, u32[]{:S(2)}, u32[]{:S(2)}) %collective-permute-start) | collective-permute-done | bytes 172064 | tf_op jit(solution)/shard_map/ppermute | solution.py:226
  4.6 0.0 copy-done
  4.6 0.0 copy-done.1
  4.6 0.1 fold.1
  4.7 3.0 %collective-permute-start.2 = (bf16[8,5376]{1,0:T(8,128)(2,1)S(1)}, bf16[8,5376]{1,0:T(8,128)(2,1)S(1)}, u32[]{:S(2)}, u32[]{:S(2)}) collective-permute-start(bf16[8,5376]{1,0:T(8,128)(2,1)S(1)} %get-tuple-element.19), channel_id=1, source_target_pairs={{0,2},{1,3},{2,0},{3,1},{4,6},{5,7},{6,4},{7,5},{8,10},{9,11},{10,... | collective-permute-start | bytes 258056 | tf_op jit(solution)/shard_map/ppermute | solution.py:226
  7.7 2.7 %collective-permute-start.1 = (bf16[4,5376]{1,0:T(4,128)(2,1)S(1)}, bf16[4,5376]{1,0:T(4,128)(2,1)S(1)}, u32[]{:S(2)}, u32[]{:S(2)}) collective-permute-start(bf16[4,5376]{1,0:T(4,128)(2,1)S(1)} %get-tuple-element.17.own_ref), channel_id=1, source_target_pairs={{0,8},{1,9},{2,10},{3,11},{4,12},{5,13},{6,14},{7,15},{8,0},{9,1},... | collective-permute-start | bytes 129032 | tf_op jit(solution)/shard_map/ppermute | solution.py:226
  10.4 0.0 copy-done.2
  10.4 0.1 collective-permute-done.2
  10.6 2.7 %collective-permute-start.4 = (bf16[8,5376]{1,0:T(8,128)(2,1)S(1)}, bf16[8,5376]{1,0:T(8,128)(2,1)S(1)}, u32[]{:S(2)}, u32[]{:S(2)}) collective-permute-start(bf16[8,5376]{1,0:T(8,128)(2,1)S(1)} %add.23.refs_0_.own_ref), channel_id=1, source_target_pairs={{0,8},{1,9},{2,10},{3,11},{4,12},{5,13},{6,14},{7,15},{8,0},{9,1},... | collective-permute-start | bytes 258056 | tf_op jit(solution)/shard_map/ppermute | solution.py:226
  13.3 0.0 collective-permute-done.1.got_ref
  13.4 1.6 %collective-permute-start.3 = (bf16[8,5376]{1,0:T(8,128)(2,1)S(1)}, bf16[8,5376]{1,0:T(8,128)(2,1)S(1)}, u32[]{:S(2)}, u32[]{:S(2)}) collective-permute-start(bf16[8,5376]{1,0:T(8,128)(2,1)S(1)} %join.1), channel_id=1, source_target_pairs={{0,4},{1,5},{2,6},{3,7},{4,0},{5,1},{6,2},{7,3},{8,12},{9,13},{10,... | collective-permute-start | bytes 258056 | tf_op jit(solution)/shard_map/ppermute | solution.py:226
  15.0 4.0 %pick.3 = (bf16[16,5376]{1,0:T(8,128)(2,1)S(1)}, bf16[16,5376]{1,0:T(8,128)(2,1)S(1)}, bf16[1024,5376]{1,0:T(8,128)(2,1)S(1)}) custom-call(s32[2,32]{1,0:T(2,128)} %ids_ref.3, bf16[1024,5376]{1,0:T(8,128)(2,1)} %table_ref.5, bf16[8,5376]{1,0:T(8,128)(2,1)S(1)} %add.23.refs_0_.own_ref), custom_call_target="tpu_custom_call" | custom-call | tf_op jit(solution)/shard_map/pick/pallas_call | solution.py:135
  19.0 0.1 collective-permute-start.6
  19.1 0.0 collective-permute-done.4.got_ref
  19.1 0.3 collective-permute-start.5
  19.4 0.0 collective-permute-done.3
  19.5 1.0 %collective-permute-done.6 = bf16[16,5376]{1,0:T(8,128)(2,1)S(1)} collective-permute-done((bf16[16,5376]{1,0:T(8,128)(2,1)S(1)}, bf16[16,5376]{1,0:T(8,128)(2,1)S(1)}, u32[]{:S(2)}, u32[]{:S(2)}) %collective-permute-start.6) | collective-permute-done | bytes 172064 | tf_op jit(solution)/shard_map/ppermute | solution.py:226
  20.5 1.7 %collective-permute-start.7 = (bf16[8,5376]{1,0:T(8,128)(2,1)S(1)}, bf16[8,5376]{1,0:T(8,128)(2,1)S(1)}, u32[]{:S(2)}, u32[]{:S(2)}) collective-permute-start(bf16[8,5376]{1,0:T(8,128)(2,1)S(1)} %slice.81), channel_id=1, source_target_pairs={{0,2},{1,3},{2,0},{3,1},{4,6},{5,7},{6,4},{7,5},{8,10},{9,11},{10,... | collective-permute-start | bytes 258056 | tf_op jit(solution)/shard_map/ppermute | solution.py:226
  22.3 0.1 pad_maximum_fusion
  22.3 2.8 %collective-permute-done.7 = bf16[8,5376]{1,0:T(8,128)(2,1)S(1)} collective-permute-done((bf16[8,5376]{1,0:T(8,128)(2,1)S(1)}, bf16[8,5376]{1,0:T(8,128)(2,1)S(1)}, u32[]{:S(2)}, u32[]{:S(2)}) %collective-permute-start.7) | collective-permute-done | bytes 86048 | tf_op jit(solution)/shard_map/ppermute | solution.py:226
  25.2 0.0 collective-permute-done.5.got_ref
  25.2 0.3 norm.1.after_ref.own_ref
  25.5 1.7 %collective-permute-start.8 = (bf16[16,5376]{1,0:T(8,128)(2,1)S(1)}, bf16[16,5376]{1,0:T(8,128)(2,1)S(1)}, u32[]{:S(2)}, u32[]{:S(2)}) collective-permute-start(bf16[16,5376]{1,0:T(8,128)(2,1)S(1)} %norm.1.after_ref.own_ref), channel_id=1, source_target_pairs={{0,2},{1,3},{2,0},{3,1},{4,6},{5,7},{6,4},{7,5},{8,10},{9,11},{10,... | collective-permute-start | bytes 516104 | tf_op jit(solution)/shard_map/ppermute | solution.py:226
  27.2 2.6 %load.1 = (bf16[1024,5376]{1,0:T(8,128)(2,1)S(1)}, f32[8,128]{1,0:T(8,128)S(1)}) custom-call(bf16[1024,5376]{1,0:T(8,128)(2,1)} %table_ref.5, bf16[16,5376]{1,0:T(8,128)(2,1)S(1)} %norm.1.after_ref.own_ref, bf16[1024,5376]{1,0:T(8,128)(2,1)S(1)} %get-tuple-element.22.held_ref), custom_call_target="tpu_custom_call", output_to_operand_aliasing={{0}: (2, {})} | custom-call | tf_op jit(solution)/shard_map/load/pallas_call | solution.py:250
  29.9 1.3 %collective-permute-done.8.got_ref = bf16[16,5376]{1,0:T(8,128)(2,1)S(1)} collective-permute-done((bf16[16,5376]{1,0:T(8,128)(2,1)S(1)}, bf16[16,5376]{1,0:T(8,128)(2,1)S(1)}, u32[]{:S(2)}, u32[]{:S(2)}) %collective-permute-start.8) | collective-permute-done | bytes 172064 | tf_op jit(solution)/shard_map/ppermute | solution.py:226
  31.2 0.1 collective-permute-start.9
  31.3 2.6 %collective-permute-start.12 = (bf16[4,5376]{1,0:T(4,128)(2,1)S(1)}, bf16[4,5376]{1,0:T(4,128)(2,1)S(1)}, u32[]{:S(2)}, u32[]{:S(2)}) collective-permute-start(bf16[4,5376]{1,0:T(4,128)(2,1)S(1)} %slice.83), channel_id=1, source_target_pairs={{0,8},{1,9},{2,10},{3,11},{4,12},{5,13},{6,14},{7,15},{8,0},{9,1},... | collective-permute-start | bytes 129032 | tf_op jit(solution)/shard_map/ppermute | solution.py:226
  33.9 0.0 collective-permute-done.9.got_ref
  33.9 3.2 %head.1 = (f32[1024,64]{1,0:T(8,128)S(1)}, f32[2,64]{1,0:T(2,128)S(1)}) custom-call(bf16[32,5376]{1,0:T(8,128)(2,1)S(1)} %chips.1.own_ref, bf16[32,5376]{1,0:T(8,128)(2,1)S(1)} %collective-permute-done.9.got_ref, bf16[1024,5376]{1,0:T(8,128)(2,1)S(1)} %get-tuple-element.24.table_ref, f32[1,64]{1,0:T(1,128)S(1)} %get-tuple-element.25.temps_ref), custom_call_target="tpu_custom_call" | custom-call | tf_op jit(solution)/shard_map/head/pallas_call | solution.py:327
  37.1 1.6 %collective-permute-start.10 = (f32[2,64]{1,0:T(2,128)S(1)}, f32[2,64]{1,0:T(2,128)S(1)}, u32[]{:S(2)}, u32[]{:S(2)}) collective-permute-start(f32[2,64]{1,0:T(2,128)S(1)} %get-tuple-element.27), channel_id=1, source_target_pairs={{0,8},{1,9},{2,10},{3,11},{4,12},{5,13},{6,14},{7,15},{8,0},{9,1},... | collective-permute-start | bytes 1544 | tf_op jit(solution)/shard_map/ppermute | solution.py:226
  38.7 0.0 collective-permute-done.12
  38.7 1.0 %collective-permute-start.13 = (bf16[2,5376]{1,0:T(2,128)(2,1)S(1)}, bf16[2,5376]{1,0:T(2,128)(2,1)S(1)}, u32[]{:S(2)}, u32[]{:S(2)}) collective-permute-start(bf16[2,5376]{1,0:T(2,128)(2,1)S(1)} %slice.85), channel_id=1, source_target_pairs={{0,4},{1,5},{2,6},{3,7},{4,0},{5,1},{6,2},{7,3},{8,12},{9,13},{10,... | collective-permute-start | bytes 64520 | tf_op jit(solution)/shard_map/ppermute | solution.py:226
  39.7 1.9 %collective-permute-done.10 = f32[2,64]{1,0:T(2,128)S(1)} collective-permute-done((f32[2,64]{1,0:T(2,128)S(1)}, f32[2,64]{1,0:T(2,128)S(1)}, u32[]{:S(2)}, u32[]{:S(2)}) %collective-permute-start.10) | collective-permute-done | bytes 544 | tf_op jit(solution)/shard_map/ppermute | solution.py:226
  41.6 1.0 %collective-permute-start.11 = (f32[2,64]{1,0:T(2,128)S(1)}, f32[2,64]{1,0:T(2,128)S(1)}, u32[]{:S(2)}, u32[]{:S(2)}) collective-permute-start(f32[2,64]{1,0:T(2,128)S(1)} %pad_maximum_fusion.2.own_ref), channel_id=1, source_target_pairs={{0,4},{1,5},{2,6},{3,7},{4,0},{5,1},{6,2},{7,3},{8,12},{9,13},{10,... | collective-permute-start | bytes 1544 | tf_op jit(solution)/shard_map/ppermute | solution.py:226
  42.6 0.0 collective-permute-done.13
  42.6 0.6 %multiply_convert_fusion = (bf16[2,5376]{1,0:T(2,128)(2,1)}, bf16[2,5376]{1,0:T(2,128)(2,1)S(1)}) fusion(bf16[2,5376]{1,0:T(2,128)(2,1)S(1)} %collective-permute-done.13, bf16[4,5376]{1,0:T(4,128)(2,1)S(1)} %slice_add_fusion.1), kind=kLoop, calls=%fused_computation.4 | loop fusion | flops 43008 | bytes 86016 | tf_op jit(solution)/shard_map/convert_element_type | solution.py:426
  43.3 2.0 %collective-permute-done.11.got_ref = f32[2,64]{1,0:T(2,128)S(1)} collective-permute-done((f32[2,64]{1,0:T(2,128)S(1)}, f32[2,64]{1,0:T(2,128)S(1)}, u32[]{:S(2)}, u32[]{:S(2)}) %collective-permute-start.11) | collective-permute-done | bytes 544 | tf_op jit(solution)/shard_map/ppermute | solution.py:226
  45.3 0.7 %collective-permute-start.14 = (f32[2,64]{1,0:T(2,128)S(1)}, f32[2,64]{1,0:T(2,128)S(1)}, u32[]{:S(2)}, u32[]{:S(2)}) collective-permute-start(f32[2,64]{1,0:T(2,128)S(1)} %merge.1), channel_id=1, source_target_pairs={{0,2},{1,3},{2,0},{3,1},{4,6},{5,7},{6,4},{7,5},{8,10},{9,11},{10,... | collective-permute-start | bytes 1544 | tf_op jit(solution)/shard_map/ppermute | solution.py:226
  46.0 2.9 %collective-permute-done.14 = f32[2,64]{1,0:T(2,128)S(1)} collective-permute-done((f32[2,64]{1,0:T(2,128)S(1)}, f32[2,64]{1,0:T(2,128)S(1)}, u32[]{:S(2)}, u32[]{:S(2)}) %collective-permute-start.14) | collective-permute-done | bytes 544 | tf_op jit(solution)/shard_map/ppermute | solution.py:226
  48.9 0.1 collective-permute-start.15
  49.0 0.2 turn.1.scaled_ref
  49.2 0.9 %collective-permute-done.15.got_ref = f32[2,64]{1,0:T(2,128)S(1)} collective-permute-done((f32[2,64]{1,0:T(2,128)S(1)}, f32[2,64]{1,0:T(2,128)S(1)}, u32[]{:S(2)}, u32[]{:S(2)}) %collective-permute-start.15) | collective-permute-done | bytes 544 | tf_op jit(solution)/shard_map/ppermute | solution.py:226
  50.1 0.9 %finish.1 = f32[2,32,1024]{2,1,0:T(8,128)} custom-call(f32[2,32,1024]{2,1,0:T(8,128)S(1)} %turn.1.scaled_ref, f32[2,64]{1,0:T(2,128)S(1)} %pad_maximum_fusion.3.own_ref, f32[2,64]{1,0:T(2,128)S(1)} %collective-permute-done.15.got_ref), custom_call_target="tpu_custom_call" | custom-call | tf_op jit(solution)/shard_map/finish/pallas_call | solution.py:373
  (18 shorter events, 0.4 us)
Async XLA Ops:
  0.6 4.0 %copy-start = (bf16[2,5376]{1,0:T(2,128)(2,1)S(1)}, bf16[2,5376]{1,0:T(2,128)(2,1)}, u32[]{:S(2)}) copy-start(bf16[2,5376]{1,0:T(2,128)(2,1)} %first_ref.1) | copy-start | bytes 64516
  0.6 4.0 %copy-start.1 = (bf16[2,5376]{1,0:T(2,128)(2,1)S(1)}, bf16[2,5376]{1,0:T(2,128)(2,1)}, u32[]{:S(2)}) copy-start(bf16[2,5376]{1,0:T(2,128)(2,1)} %delta_ref.1) | copy-start | bytes 64516
  0.7 9.8 %copy-start.2 = (f32[5376]{0:T(1024)S(1)}, f32[5376]{0:T(1024)}, u32[]{:S(2)}) copy-start(f32[5376]{0:T(1024)} %param.9) | copy-start | bytes 64516
  3.1 1.5 %collective-permute-start = (bf16[16,5376]{1,0:T(8,128)(2,1)S(1)}, bf16[16,5376]{1,0:T(8,128)(2,1)S(1)}, u32[]{:S(2)}, u32[]{:S(2)}) collective-permute-start(bf16[16,5376]{1,0:T(8,128)(2,1)S(1)} %get-tuple-element.16), channel_id=1, source_target_pairs={{0,1},{1,0},{2,3},{3,2},{4,5},{5,4},{6,7},{7,6},{8,9},{9,8},{10,11... | collective-permute-start | bytes 516104 | tf_op jit(solution)/shard_map/ppermute | solution.py:226
  4.7 5.9 %collective-permute-start.2 = (bf16[8,5376]{1,0:T(8,128)(2,1)S(1)}, bf16[8,5376]{1,0:T(8,128)(2,1)S(1)}, u32[]{:S(2)}, u32[]{:S(2)}) collective-permute-start(bf16[8,5376]{1,0:T(8,128)(2,1)S(1)} %get-tuple-element.19), channel_id=1, source_target_pairs={{0,2},{1,3},{2,0},{3,1},{4,6},{5,7},{6,4},{7,5},{8,10},{9,11},{10,... | collective-permute-start | bytes 258056 | tf_op jit(solution)/shard_map/ppermute | solution.py:226
  7.7 5.6 %collective-permute-start.1 = (bf16[4,5376]{1,0:T(4,128)(2,1)S(1)}, bf16[4,5376]{1,0:T(4,128)(2,1)S(1)}, u32[]{:S(2)}, u32[]{:S(2)}) collective-permute-start(bf16[4,5376]{1,0:T(4,128)(2,1)S(1)} %get-tuple-element.17.own_ref), channel_id=1, source_target_pairs={{0,8},{1,9},{2,10},{3,11},{4,12},{5,13},{6,14},{7,15},{8,0},{9,1},... | collective-permute-start | bytes 129032 | tf_op jit(solution)/shard_map/ppermute | solution.py:226
  10.6 8.5 %collective-permute-start.4 = (bf16[8,5376]{1,0:T(8,128)(2,1)S(1)}, bf16[8,5376]{1,0:T(8,128)(2,1)S(1)}, u32[]{:S(2)}, u32[]{:S(2)}) collective-permute-start(bf16[8,5376]{1,0:T(8,128)(2,1)S(1)} %add.23.refs_0_.own_ref), channel_id=1, source_target_pairs={{0,8},{1,9},{2,10},{3,11},{4,12},{5,13},{6,14},{7,15},{8,0},{9,1},... | collective-permute-start | bytes 258056 | tf_op jit(solution)/shard_map/ppermute | solution.py:226
  13.4 6.0 %collective-permute-start.3 = (bf16[8,5376]{1,0:T(8,128)(2,1)S(1)}, bf16[8,5376]{1,0:T(8,128)(2,1)S(1)}, u32[]{:S(2)}, u32[]{:S(2)}) collective-permute-start(bf16[8,5376]{1,0:T(8,128)(2,1)S(1)} %join.1), channel_id=1, source_target_pairs={{0,4},{1,5},{2,6},{3,7},{4,0},{5,1},{6,2},{7,3},{8,12},{9,13},{10,... | collective-permute-start | bytes 258056 | tf_op jit(solution)/shard_map/ppermute | solution.py:226
  19.0 1.5 %collective-permute-start.6 = (bf16[16,5376]{1,0:T(8,128)(2,1)S(1)}, bf16[16,5376]{1,0:T(8,128)(2,1)S(1)}, u32[]{:S(2)}, u32[]{:S(2)}) collective-permute-start(bf16[16,5376]{1,0:T(8,128)(2,1)S(1)} %get-tuple-element.20.refs_0_), channel_id=1, source_target_pairs={{0,1},{1,0},{2,3},{3,2},{4,5},{5,4},{6,7},{7,6},{8,9},{9,8},{10,11... | collective-permute-start | bytes 516104 | tf_op jit(solution)/shard_map/ppermute | solution.py:226
  19.1 6.1 %collective-permute-start.5 = (bf16[8,5376]{1,0:T(8,128)(2,1)S(1)}, bf16[8,5376]{1,0:T(8,128)(2,1)S(1)}, u32[]{:S(2)}, u32[]{:S(2)}) collective-permute-start(bf16[8,5376]{1,0:T(8,128)(2,1)S(1)} %plus.1.own_ref), channel_id=1, source_target_pairs={{0,4},{1,5},{2,6},{3,7},{4,0},{5,1},{6,2},{7,3},{8,12},{9,13},{10,... | collective-permute-start | bytes 258056 | tf_op jit(solution)/shard_map/ppermute | solution.py:226
  20.5 4.6 %collective-permute-start.7 = (bf16[8,5376]{1,0:T(8,128)(2,1)S(1)}, bf16[8,5376]{1,0:T(8,128)(2,1)S(1)}, u32[]{:S(2)}, u32[]{:S(2)}) collective-permute-start(bf16[8,5376]{1,0:T(8,128)(2,1)S(1)} %slice.81), channel_id=1, source_target_pairs={{0,2},{1,3},{2,0},{3,1},{4,6},{5,7},{6,4},{7,5},{8,10},{9,11},{10,... | collective-permute-start | bytes 258056 | tf_op jit(solution)/shard_map/ppermute | solution.py:226
  25.5 5.7 %collective-permute-start.8 = (bf16[16,5376]{1,0:T(8,128)(2,1)S(1)}, bf16[16,5376]{1,0:T(8,128)(2,1)S(1)}, u32[]{:S(2)}, u32[]{:S(2)}) collective-permute-start(bf16[16,5376]{1,0:T(8,128)(2,1)S(1)} %norm.1.after_ref.own_ref), channel_id=1, source_target_pairs={{0,2},{1,3},{2,0},{3,1},{4,6},{5,7},{6,4},{7,5},{8,10},{9,11},{10,... | collective-permute-start | bytes 516104 | tf_op jit(solution)/shard_map/ppermute | solution.py:226
  31.2 2.7 %collective-permute-start.9 = (bf16[32,5376]{1,0:T(8,128)(2,1)S(1)}, bf16[32,5376]{1,0:T(8,128)(2,1)S(1)}, u32[]{:S(2)}, u32[]{:S(2)}) collective-permute-start(bf16[32,5376]{1,0:T(8,128)(2,1)S(1)} %chips.1.own_ref), channel_id=1, source_target_pairs={{0,1},{1,0},{2,3},{3,2},{4,5},{5,4},{6,7},{7,6},{8,9},{9,8},{10,11... | collective-permute-start | bytes 1032200 | tf_op jit(solution)/shard_map/ppermute | solution.py:226
  31.3 7.3 %collective-permute-start.12 = (bf16[4,5376]{1,0:T(4,128)(2,1)S(1)}, bf16[4,5376]{1,0:T(4,128)(2,1)S(1)}, u32[]{:S(2)}, u32[]{:S(2)}) collective-permute-start(bf16[4,5376]{1,0:T(4,128)(2,1)S(1)} %slice.83), channel_id=1, source_target_pairs={{0,8},{1,9},{2,10},{3,11},{4,12},{5,13},{6,14},{7,15},{8,0},{9,1},... | collective-permute-start | bytes 129032 | tf_op jit(solution)/shard_map/ppermute | solution.py:226
  37.1 4.5 %collective-permute-start.10 = (f32[2,64]{1,0:T(2,128)S(1)}, f32[2,64]{1,0:T(2,128)S(1)}, u32[]{:S(2)}, u32[]{:S(2)}) collective-permute-start(f32[2,64]{1,0:T(2,128)S(1)} %get-tuple-element.27), channel_id=1, source_target_pairs={{0,8},{1,9},{2,10},{3,11},{4,12},{5,13},{6,14},{7,15},{8,0},{9,1},... | collective-permute-start | bytes 1544 | tf_op jit(solution)/shard_map/ppermute | solution.py:226
  38.7 3.9 %collective-permute-start.13 = (bf16[2,5376]{1,0:T(2,128)(2,1)S(1)}, bf16[2,5376]{1,0:T(2,128)(2,1)S(1)}, u32[]{:S(2)}, u32[]{:S(2)}) collective-permute-start(bf16[2,5376]{1,0:T(2,128)(2,1)S(1)} %slice.85), channel_id=1, source_target_pairs={{0,4},{1,5},{2,6},{3,7},{4,0},{5,1},{6,2},{7,3},{8,12},{9,13},{10,... | collective-permute-start | bytes 64520 | tf_op jit(solution)/shard_map/ppermute | solution.py:226
  41.6 3.6 %collective-permute-start.11 = (f32[2,64]{1,0:T(2,128)S(1)}, f32[2,64]{1,0:T(2,128)S(1)}, u32[]{:S(2)}, u32[]{:S(2)}) collective-permute-start(f32[2,64]{1,0:T(2,128)S(1)} %pad_maximum_fusion.2.own_ref), channel_id=1, source_target_pairs={{0,4},{1,5},{2,6},{3,7},{4,0},{5,1},{6,2},{7,3},{8,12},{9,13},{10,... | collective-permute-start | bytes 1544 | tf_op jit(solution)/shard_map/ppermute | solution.py:226
  45.3 3.6 %collective-permute-start.14 = (f32[2,64]{1,0:T(2,128)S(1)}, f32[2,64]{1,0:T(2,128)S(1)}, u32[]{:S(2)}, u32[]{:S(2)}) collective-permute-start(f32[2,64]{1,0:T(2,128)S(1)} %merge.1), channel_id=1, source_target_pairs={{0,2},{1,3},{2,0},{3,1},{4,6},{5,7},{6,4},{7,5},{8,10},{9,11},{10,... | collective-permute-start | bytes 1544 | tf_op jit(solution)/shard_map/ppermute | solution.py:226
  48.9 1.2 %collective-permute-start.15 = (f32[2,64]{1,0:T(2,128)S(1)}, f32[2,64]{1,0:T(2,128)S(1)}, u32[]{:S(2)}, u32[]{:S(2)}) collective-permute-start(f32[2,64]{1,0:T(2,128)S(1)} %pad_maximum_fusion.3.own_ref), channel_id=1, source_target_pairs={{0,1},{1,0},{2,3},{3,2},{4,5},{5,4},{6,7},{7,6},{8,9},{9,8},{10,11... | collective-permute-start | bytes 1544 | tf_op jit(solution)/shard_map/ppermute | solution.py:226

commit v9 on v7

--- a/solution.py
+++ b/solution.py
@@ -216,9 +216,15 @@
     return lax.ppermute(rows, "vocab", pairs)
 
 
-def load_kernel(part, table_ref, *refs):
+def load_kernel(first, last, table_ref, *refs):
     out_ref, token_ref, sems = refs[-3:]
-    copies = part_copies(table_ref, out_ref, sems, table_ref.shape[0] // 2 * part)
+    parts = sems.shape[0]
+    part = (last - first) // parts
+    rows = [pl.ds(first + k * part, part) for k in range(parts)]
+    copies = [
+        pltpu.make_async_copy(table_ref.at[at], out_ref.at[at], sems.at[k])
+        for k, at in enumerate(rows)
+    ]
     for copy in copies:
         copy.start()
     token_ref[...] = jnp.zeros_like(token_ref)
@@ -226,32 +232,22 @@
         copy.wait()
 
 
-def part_copies(table_ref, out_ref, sems, first):
-    parts = sems.shape[0]
-    part = table_ref.shape[0] // 2 // parts
-    rows = [pl.ds(first + k * part, part) for k in range(parts)]
-    return [
-        pltpu.make_async_copy(table_ref.at[at], out_ref.at[at], sems.at[k])
-        for k, at in enumerate(rows)
-    ]
-
-
-def loaded(table, after, held=None):
+def loaded(table, first, last, held, *after):
     anywhere, vmem = pl.BlockSpec(memory_space=pl.ANY), pl.BlockSpec(memory_space=pltpu.VMEM)
-    part = 0 if held is None else 1
-    return pl.pallas_call(
-        functools.partial(load_kernel, part),
+    held = [] if held is None else [held]
+    return pl.pallas_call(
+        functools.partial(load_kernel, first, last),
         out_shape=(
             jax.ShapeDtypeStruct(table.shape, table.dtype),
             jax.ShapeDtypeStruct((8, 128), jnp.float32),
         ),
-        in_specs=[anywhere] * 2 + [vmem] * part,
+        in_specs=[anywhere] * (1 + len(after)) + [vmem] * len(held),
         out_specs=(vmem, vmem),
-        input_output_aliases={2: 0} if part else {},
+        input_output_aliases={1 + len(after): 0} if held else {},
         scratch_shapes=[pltpu.SemaphoreType.DMA((4,))],
         compiler_params=pltpu.CompilerParams(vmem_limit_bytes=4 * MIB),
         name="load",
-    )(in_hbm(table), after, *([held] if part else []))
+    )(in_hbm(table), *after, *held)
 
 
 def norm_kernel(first_ref, own_ref, got_ref, delta_ref, gain_ref, *refs):
@@ -406,9 +402,10 @@
             own = paired(plus_kernel, own, got, quarter, "plus", send)
     state = jnp.concatenate([beside[:held], moved[:held]], axis=0)
     delta = jnp.concatenate([beside[held:], moved[held:]], axis=0)
-    head_table, token = loaded(table, own)
-    states = normed(state, own, got, delta, gain, token, following)
-    head_table, token = loaded(table, states, head_table)
+    voc_dev = table.shape[0]
+    head_table, token = loaded(table, 0, voc_dev // 4, None, own)
+    states = normed(state, own, got, delta, gain, token)
+    head_table, token = loaded(table, voc_dev // 4, voc_dev, head_table, states, following)
     states = paired(chips_kernel, states, swapped(states, 2), rows, "chips", token)
     others = swapped(states, 1)
     scaled, stats = head(states, others, head_table, temps)

time: 49.6 us -> 48.6 us (0.980)
  starting transfers between devices: 22 us -> 20.5 us
  Pallas kernels: 13.6 us -> 14.9 us
  waiting for transfers between devices: 11.9 us -> 11 us
    ppermute x16, starting transfers between devices: 22 us -> 20.5 us  [swapped(): return lax.ppermute(rows, 'vocab', pairs)]
    pallas_call x2, Pallas kernels: 3.68 us -> 4.98 us  [picked_rows(): pl.pallas_call(functools.partial(pick_kernel, step, places), out_shape=ou...]
    ppermute x16, waiting for transfers between devices: 11.9 us -> 11 us  [swapped(): return lax.ppermute(rows, 'vocab', pairs)]
  transfers between devices with their start and end apart: 16 -> 16, of which waited for: 10 -> 9; matrix products, arithmetic and copies ran while one was open for 2% -> 2% of each run, Pallas kernels for 22% -> 24%
where the time goes in v9:
time: 48.6 us; the launch traced here: 48.3 us
  starting transfers between devices  20.5 us (42%)
  Pallas kernels  14.9 us (31%)
  waiting for transfers between devices  11 us (23%)
  other arithmetic  0.87 us (2%)
  between operations  0.84 us (2%)
    ppermute x16, starting transfers between devices, swapped(): return lax.ppermute(rows, 'vocab', pairs)  20.5 us
    ppermute x16, waiting for transfers between devices, swapped(): return lax.ppermute(rows, 'vocab', pairs)  11 us
    pallas_call x2, Pallas kernels, loaded(): pl.pallas_call(functools.partial(load_kernel, first, last), out_shape=(ja...  5.23 us
    pallas_call x2, Pallas kernels, picked_rows(): pl.pallas_call(functools.partial(pick_kernel, step, places), out_shape=ou...  4.98 us
    pallas_call x1, Pallas kernels, head(): pl.pallas_call(head_kernel, out_shape=(jax.ShapeDtypeStruct((voc_dev, row...  3.14 us
  transfers between devices with their start and end apart: 16, of which 9 were waited for; matrix products, arithmetic and copies ran while one was open for 2% of the time, Pallas kernels for 24%

profile of v9, /device:TPU:0, one launch (start us, length us, event | category | flops | bytes accessed | tf_op | source)
XLA Modules:
  0.0 48.3 jit_solution(16435258710589706085)
XLA Ops:
  0.6 0.0 copy-start
  0.6 0.0 copy-start.1
  0.7 0.0 copy-start.2
  0.7 2.5 %pick.2 = (bf16[16,5376]{1,0:T(8,128)(2,1)S(1)}, bf16[16,5376]{1,0:T(8,128)(2,1)S(1)}, f32[1,64]{1,0:T(1,128)S(1)}) custom-call(s32[2,32]{1,0:T(2,128)} %ids_ref.3, bf16[1024,5376]{1,0:T(8,128)(2,1)} %table_ref.7, s32[2,32]{1,0:T(2,128)} %refs_0_.1, f32[8]{0:T(128)} %refs_1_.1), custom_call_target="tpu_custom_call" | custom-call | tf_op jit(solution)/shard_map/pick/pallas_call | solution.py:125
  3.1 0.4 collective-permute-start
  3.6 1.0 %collective-permute-done.got_ref = bf16[16,5376]{1,0:T(8,128)(2,1)S(1)} collective-permute-done((bf16[16,5376]{1,0:T(8,128)(2,1)S(1)}, bf16[16,5376]{1,0:T(8,128)(2,1)S(1)}, u32[]{:S(2)}, u32[]{:S(2)}) %collective-permute-start) | collective-permute-done | bytes 172064 | tf_op jit(solution)/shard_map/ppermute | solution.py:216
  4.6 0.0 copy-done
  4.6 0.0 copy-done.1
  4.6 0.1 fold.1
  4.7 2.9 %collective-permute-start.2 = (bf16[8,5376]{1,0:T(8,128)(2,1)S(1)}, bf16[8,5376]{1,0:T(8,128)(2,1)S(1)}, u32[]{:S(2)}, u32[]{:S(2)}) collective-permute-start(bf16[8,5376]{1,0:T(8,128)(2,1)S(1)} %get-tuple-element.20), channel_id=1, source_target_pairs={{0,2},{1,3},{2,0},{3,1},{4,6},{5,7},{6,4},{7,5},{8,10},{9,11},{10,... | collective-permute-start | bytes 258056 | tf_op jit(solution)/shard_map/ppermute | solution.py:216
  7.6 2.8 %collective-permute-start.1 = (bf16[4,5376]{1,0:T(4,128)(2,1)S(1)}, bf16[4,5376]{1,0:T(4,128)(2,1)S(1)}, u32[]{:S(2)}, u32[]{:S(2)}) collective-permute-start(bf16[4,5376]{1,0:T(4,128)(2,1)S(1)} %get-tuple-element.18.own_ref), channel_id=1, source_target_pairs={{0,8},{1,9},{2,10},{3,11},{4,12},{5,13},{6,14},{7,15},{8,0},{9,1},... | collective-permute-start | bytes 129032 | tf_op jit(solution)/shard_map/ppermute | solution.py:216
  10.4 0.0 collective-permute-done.2
  10.5 2.9 %collective-permute-start.4 = (bf16[8,5376]{1,0:T(8,128)(2,1)S(1)}, bf16[8,5376]{1,0:T(8,128)(2,1)S(1)}, u32[]{:S(2)}, u32[]{:S(2)}) collective-permute-start(bf16[8,5376]{1,0:T(8,128)(2,1)S(1)} %add.23.refs_0_.own_ref), channel_id=1, source_target_pairs={{0,8},{1,9},{2,10},{3,11},{4,12},{5,13},{6,14},{7,15},{8,0},{9,1},... | collective-permute-start | bytes 258056 | tf_op jit(solution)/shard_map/ppermute | solution.py:216
  13.4 0.0 collective-permute-done.1.got_ref
  13.4 1.6 %collective-permute-start.3 = (bf16[8,5376]{1,0:T(8,128)(2,1)S(1)}, bf16[8,5376]{1,0:T(8,128)(2,1)S(1)}, u32[]{:S(2)}, u32[]{:S(2)}) collective-permute-start(bf16[8,5376]{1,0:T(8,128)(2,1)S(1)} %join.1), channel_id=1, source_target_pairs={{0,4},{1,5},{2,6},{3,7},{4,0},{5,1},{6,2},{7,3},{8,12},{9,13},{10,... | collective-permute-start | bytes 258056 | tf_op jit(solution)/shard_map/ppermute | solution.py:216
  15.0 2.5 %pick.3 = (bf16[16,5376]{1,0:T(8,128)(2,1)S(1)}, bf16[16,5376]{1,0:T(8,128)(2,1)S(1)}) custom-call(s32[2,32]{1,0:T(2,128)} %ids_ref.3, bf16[1024,5376]{1,0:T(8,128)(2,1)} %table_ref.7, bf16[8,5376]{1,0:T(8,128)(2,1)S(1)} %add.23.refs_0_.own_ref), custom_call_target="tpu_custom_call" | custom-call | tf_op jit(solution)/shard_map/pick/pallas_call | solution.py:125
  17.5 0.1 collective-permute-start.7
  17.6 0.0 collective-permute-done.4.got_ref
  17.6 1.2 %collective-permute-start.5 = (bf16[8,5376]{1,0:T(8,128)(2,1)S(1)}, bf16[8,5376]{1,0:T(8,128)(2,1)S(1)}, u32[]{:S(2)}, u32[]{:S(2)}) collective-permute-start(bf16[8,5376]{1,0:T(8,128)(2,1)S(1)} %plus.1.refs_0_.own_ref), channel_id=1, source_target_pairs={{0,4},{1,5},{2,6},{3,7},{4,0},{5,1},{6,2},{7,3},{8,12},{9,13},{10,... | collective-permute-start | bytes 258056 | tf_op jit(solution)/shard_map/ppermute | solution.py:216
  18.8 0.0 collective-permute-done.3
  18.8 0.2 collective-permute-done.7
  19.1 1.3 %collective-permute-start.8 = (bf16[8,5376]{1,0:T(8,128)(2,1)S(1)}, bf16[8,5376]{1,0:T(8,128)(2,1)S(1)}, u32[]{:S(2)}, u32[]{:S(2)}) collective-permute-start(bf16[8,5376]{1,0:T(8,128)(2,1)S(1)} %slice.81), channel_id=1, source_target_pairs={{0,2},{1,3},{2,0},{3,1},{4,6},{5,7},{6,4},{7,5},{8,10},{9,11},{10,... | collective-permute-start | bytes 258056 | tf_op jit(solution)/shard_map/ppermute | solution.py:216
  20.4 0.1 pad_maximum_fusion
  20.5 1.8 %load.2 = (bf16[1024,5376]{1,0:T(8,128)(2,1)S(1)}, f32[8,128]{1,0:T(8,128)S(1)}) custom-call(bf16[1024,5376]{1,0:T(8,128)(2,1)} %table_ref.7, bf16[8,5376]{1,0:T(8,128)(2,1)S(1)} %plus.1.refs_0_.own_ref), custom_call_target="tpu_custom_call" | custom-call | tf_op jit(solution)/shard_map/load/pallas_call | solution.py:238
  22.2 0.4 collective-permute-done.5.got_ref
  22.6 0.3 norm.1.refs_0_.own_ref
  22.9 1.3 %collective-permute-start.6 = (bf16[16,5376]{1,0:T(8,128)(2,1)S(1)}, bf16[16,5376]{1,0:T(8,128)(2,1)S(1)}, u32[]{:S(2)}, u32[]{:S(2)}) collective-permute-start(bf16[16,5376]{1,0:T(8,128)(2,1)S(1)} %norm.1.refs_0_.own_ref), channel_id=1, source_target_pairs={{0,2},{1,3},{2,0},{3,1},{4,6},{5,7},{6,4},{7,5},{8,10},{9,11},{10,... | collective-permute-start | bytes 516104 | tf_op jit(solution)/shard_map/ppermute | solution.py:216
  24.3 0.0 collective-permute-done.8
  24.3 3.5 %load.3 = (bf16[1024,5376]{1,0:T(8,128)(2,1)S(1)}, f32[8,128]{1,0:T(8,128)S(1)}) custom-call(bf16[1024,5376]{1,0:T(8,128)(2,1)} %table_ref.7, bf16[16,5376]{1,0:T(8,128)(2,1)S(1)} %norm.1.refs_0_.own_ref, bf16[8,5376]{1,0:T(8,128)(2,1)S(1)} %slice_add_fusion.refs_1_, bf16[1024,5376]{1,0:T(8,128)(2,1)S(1)} %get-tuple-element.24.refs_2_), custom_call_target="tpu_custom_call", output_to_operand_aliasing={{0}: (3, {})} | custom-call | tf_op jit(solution)/shard_map/load/pallas_call | solution.py:238
  27.8 1.2 %collective-permute-done.6.got_ref = bf16[16,5376]{1,0:T(8,128)(2,1)S(1)} collective-permute-done((bf16[16,5376]{1,0:T(8,128)(2,1)S(1)}, bf16[16,5376]{1,0:T(8,128)(2,1)S(1)}, u32[]{:S(2)}, u32[]{:S(2)}) %collective-permute-start.6) | collective-permute-done | bytes 172064 | tf_op jit(solution)/shard_map/ppermute | solution.py:216
  29.0 0.1 collective-permute-start.9
  29.2 2.1 %collective-permute-start.12 = (bf16[4,5376]{1,0:T(4,128)(2,1)S(1)}, bf16[4,5376]{1,0:T(4,128)(2,1)S(1)}, u32[]{:S(2)}, u32[]{:S(2)}) collective-permute-start(bf16[4,5376]{1,0:T(4,128)(2,1)S(1)} %slice.83), channel_id=1, source_target_pairs={{0,8},{1,9},{2,10},{3,11},{4,12},{5,13},{6,14},{7,15},{8,0},{9,1},... | collective-permute-start | bytes 129032 | tf_op jit(solution)/shard_map/ppermute | solution.py:216
  31.2 0.0 collective-permute-done.9.got_ref
  31.2 3.1 %head.1 = (f32[1024,64]{1,0:T(8,128)S(1)}, f32[2,64]{1,0:T(2,128)S(1)}) custom-call(bf16[32,5376]{1,0:T(8,128)(2,1)S(1)} %chips.1.own_ref, bf16[32,5376]{1,0:T(8,128)(2,1)S(1)} %collective-permute-done.9.got_ref, bf16[1024,5376]{1,0:T(8,128)(2,1)S(1)} %get-tuple-element.26.table_ref, f32[1,64]{1,0:T(1,128)S(1)} %get-tuple-element.27.temps_ref), custom_call_target="tpu_custom_call" | custom-call | tf_op jit(solution)/shard_map/head/pallas_call | solution.py:315
  34.4 1.6 %collective-permute-start.10 = (f32[2,64]{1,0:T(2,128)S(1)}, f32[2,64]{1,0:T(2,128)S(1)}, u32[]{:S(2)}, u32[]{:S(2)}) collective-permute-start(f32[2,64]{1,0:T(2,128)S(1)} %get-tuple-element.29), channel_id=1, source_target_pairs={{0,8},{1,9},{2,10},{3,11},{4,12},{5,13},{6,14},{7,15},{8,0},{9,1},... | collective-permute-start | bytes 1544 | tf_op jit(solution)/shard_map/ppermute | solution.py:216
  36.0 0.0 collective-permute-done.12
  36.0 0.8 %collective-permute-start.13 = (bf16[2,5376]{1,0:T(2,128)(2,1)S(1)}, bf16[2,5376]{1,0:T(2,128)(2,1)S(1)}, u32[]{:S(2)}, u32[]{:S(2)}) collective-permute-start(bf16[2,5376]{1,0:T(2,128)(2,1)S(1)} %slice.85), channel_id=1, source_target_pairs={{0,4},{1,5},{2,6},{3,7},{4,0},{5,1},{6,2},{7,3},{8,12},{9,13},{10,... | collective-permute-start | bytes 64520 | tf_op jit(solution)/shard_map/ppermute | solution.py:216
  36.8 2.1 %collective-permute-done.10 = f32[2,64]{1,0:T(2,128)S(1)} collective-permute-done((f32[2,64]{1,0:T(2,128)S(1)}, f32[2,64]{1,0:T(2,128)S(1)}, u32[]{:S(2)}, u32[]{:S(2)}) %collective-permute-start.10) | collective-permute-done | bytes 544 | tf_op jit(solution)/shard_map/ppermute | solution.py:216
  38.9 0.8 %collective-permute-start.11 = (f32[2,64]{1,0:T(2,128)S(1)}, f32[2,64]{1,0:T(2,128)S(1)}, u32[]{:S(2)}, u32[]{:S(2)}) collective-permute-start(f32[2,64]{1,0:T(2,128)S(1)} %pad_maximum_fusion.2.own_ref), channel_id=1, source_target_pairs={{0,4},{1,5},{2,6},{3,7},{4,0},{5,1},{6,2},{7,3},{8,12},{9,13},{10,... | collective-permute-start | bytes 1544 | tf_op jit(solution)/shard_map/ppermute | solution.py:216
  39.7 0.2 collective-permute-done.13
  39.9 0.6 %multiply_convert_fusion = (bf16[2,5376]{1,0:T(2,128)(2,1)}, bf16[2,5376]{1,0:T(2,128)(2,1)S(1)}) fusion(bf16[2,5376]{1,0:T(2,128)(2,1)S(1)} %collective-permute-done.13, bf16[4,5376]{1,0:T(4,128)(2,1)S(1)} %slice_add_fusion.1), kind=kLoop, calls=%fused_computation.4 | loop fusion | flops 43008 | bytes 86016 | tf_op jit(solution)/shard_map/convert_element_type | solution.py:416
  40.6 2.0 %collective-permute-done.11.got_ref = f32[2,64]{1,0:T(2,128)S(1)} collective-permute-done((f32[2,64]{1,0:T(2,128)S(1)}, f32[2,64]{1,0:T(2,128)S(1)}, u32[]{:S(2)}, u32[]{:S(2)}) %collective-permute-start.11) | collective-permute-done | bytes 544 | tf_op jit(solution)/shard_map/ppermute | solution.py:216
  42.6 0.7 %collective-permute-start.14 = (f32[2,64]{1,0:T(2,128)S(1)}, f32[2,64]{1,0:T(2,128)S(1)}, u32[]{:S(2)}, u32[]{:S(2)}) collective-permute-start(f32[2,64]{1,0:T(2,128)S(1)} %merge.1), channel_id=1, source_target_pairs={{0,2},{1,3},{2,0},{3,1},{4,6},{5,7},{6,4},{7,5},{8,10},{9,11},{10,... | collective-permute-start | bytes 1544 | tf_op jit(solution)/shard_map/ppermute | solution.py:216
  43.2 3.0 %collective-permute-done.14 = f32[2,64]{1,0:T(2,128)S(1)} collective-permute-done((f32[2,64]{1,0:T(2,128)S(1)}, f32[2,64]{1,0:T(2,128)S(1)}, u32[]{:S(2)}, u32[]{:S(2)}) %collective-permute-start.14) | collective-permute-done | bytes 544 | tf_op jit(solution)/shard_map/ppermute | solution.py:216
  46.2 0.1 collective-permute-start.15
  46.3 0.2 turn.1.scaled_ref
  46.5 0.9 %collective-permute-done.15.got_ref = f32[2,64]{1,0:T(2,128)S(1)} collective-permute-done((f32[2,64]{1,0:T(2,128)S(1)}, f32[2,64]{1,0:T(2,128)S(1)}, u32[]{:S(2)}, u32[]{:S(2)}) %collective-permute-start.15) | collective-permute-done | bytes 544 | tf_op jit(solution)/shard_map/ppermute | solution.py:216
  47.4 0.9 %finish.1 = f32[2,32,1024]{2,1,0:T(8,128)} custom-call(f32[2,32,1024]{2,1,0:T(8,128)S(1)} %turn.1.scaled_ref, f32[2,64]{1,0:T(2,128)S(1)} %pad_maximum_fusion.3.own_ref, f32[2,64]{1,0:T(2,128)S(1)} %collective-permute-done.15.got_ref), custom_call_target="tpu_custom_call" | custom-call | tf_op jit(solution)/shard_map/finish/pallas_call | solution.py:361
  (19 shorter events, 0.4 us)
Async XLA Ops:
  0.6 4.0 %copy-start = (bf16[2,5376]{1,0:T(2,128)(2,1)S(1)}, bf16[2,5376]{1,0:T(2,128)(2,1)}, u32[]{:S(2)}) copy-start(bf16[2,5376]{1,0:T(2,128)(2,1)} %first_ref.1) | copy-start | bytes 64516
  0.6 4.0 %copy-start.1 = (bf16[2,5376]{1,0:T(2,128)(2,1)S(1)}, bf16[2,5376]{1,0:T(2,128)(2,1)}, u32[]{:S(2)}) copy-start(bf16[2,5376]{1,0:T(2,128)(2,1)} %delta_ref.1) | copy-start | bytes 64516
  0.7 9.8 %copy-start.2 = (f32[5376]{0:T(1024)S(1)}, f32[5376]{0:T(1024)}, u32[]{:S(2)}) copy-start(f32[5376]{0:T(1024)} %param.9) | copy-start | bytes 64516
  3.1 1.5 %collective-permute-start = (bf16[16,5376]{1,0:T(8,128)(2,1)S(1)}, bf16[16,5376]{1,0:T(8,128)(2,1)S(1)}, u32[]{:S(2)}, u32[]{:S(2)}) collective-permute-start(bf16[16,5376]{1,0:T(8,128)(2,1)S(1)} %get-tuple-element.17), channel_id=1, source_target_pairs={{0,1},{1,0},{2,3},{3,2},{4,5},{5,4},{6,7},{7,6},{8,9},{9,8},{10,11... | collective-permute-start | bytes 516104 | tf_op jit(solution)/shard_map/ppermute | solution.py:216
  4.7 5.8 %collective-permute-start.2 = (bf16[8,5376]{1,0:T(8,128)(2,1)S(1)}, bf16[8,5376]{1,0:T(8,128)(2,1)S(1)}, u32[]{:S(2)}, u32[]{:S(2)}) collective-permute-start(bf16[8,5376]{1,0:T(8,128)(2,1)S(1)} %get-tuple-element.20), channel_id=1, source_target_pairs={{0,2},{1,3},{2,0},{3,1},{4,6},{5,7},{6,4},{7,5},{8,10},{9,11},{10,... | collective-permute-start | bytes 258056 | tf_op jit(solution)/shard_map/ppermute | solution.py:216
  7.6 5.7 %collective-permute-start.1 = (bf16[4,5376]{1,0:T(4,128)(2,1)S(1)}, bf16[4,5376]{1,0:T(4,128)(2,1)S(1)}, u32[]{:S(2)}, u32[]{:S(2)}) collective-permute-start(bf16[4,5376]{1,0:T(4,128)(2,1)S(1)} %get-tuple-element.18.own_ref), channel_id=1, source_target_pairs={{0,8},{1,9},{2,10},{3,11},{4,12},{5,13},{6,14},{7,15},{8,0},{9,1},... | collective-permute-start | bytes 129032 | tf_op jit(solution)/shard_map/ppermute | solution.py:216
  10.5 7.1 %collective-permute-start.4 = (bf16[8,5376]{1,0:T(8,128)(2,1)S(1)}, bf16[8,5376]{1,0:T(8,128)(2,1)S(1)}, u32[]{:S(2)}, u32[]{:S(2)}) collective-permute-start(bf16[8,5376]{1,0:T(8,128)(2,1)S(1)} %add.23.refs_0_.own_ref), channel_id=1, source_target_pairs={{0,8},{1,9},{2,10},{3,11},{4,12},{5,13},{6,14},{7,15},{8,0},{9,1},... | collective-permute-start | bytes 258056 | tf_op jit(solution)/shard_map/ppermute | solution.py:216
  13.4 5.4 %collective-permute-start.3 = (bf16[8,5376]{1,0:T(8,128)(2,1)S(1)}, bf16[8,5376]{1,0:T(8,128)(2,1)S(1)}, u32[]{:S(2)}, u32[]{:S(2)}) collective-permute-start(bf16[8,5376]{1,0:T(8,128)(2,1)S(1)} %join.1), channel_id=1, source_target_pairs={{0,4},{1,5},{2,6},{3,7},{4,0},{5,1},{6,2},{7,3},{8,12},{9,13},{10,... | collective-permute-start | bytes 258056 | tf_op jit(solution)/shard_map/ppermute | solution.py:216
  17.5 1.5 %collective-permute-start.7 = (bf16[16,5376]{1,0:T(8,128)(2,1)S(1)}, bf16[16,5376]{1,0:T(8,128)(2,1)S(1)}, u32[]{:S(2)}, u32[]{:S(2)}) collective-permute-start(bf16[16,5376]{1,0:T(8,128)(2,1)S(1)} %get-tuple-element.21.refs_0_), channel_id=1, source_target_pairs={{0,1},{1,0},{2,3},{3,2},{4,5},{5,4},{6,7},{7,6},{8,9},{9,8},{10,11... | collective-permute-start | bytes 516104 | tf_op jit(solution)/shard_map/ppermute | solution.py:216
  17.6 5.0 %collective-permute-start.5 = (bf16[8,5376]{1,0:T(8,128)(2,1)S(1)}, bf16[8,5376]{1,0:T(8,128)(2,1)S(1)}, u32[]{:S(2)}, u32[]{:S(2)}) collective-permute-start(bf16[8,5376]{1,0:T(8,128)(2,1)S(1)} %plus.1.refs_0_.own_ref), channel_id=1, source_target_pairs={{0,4},{1,5},{2,6},{3,7},{4,0},{5,1},{6,2},{7,3},{8,12},{9,13},{10,... | collective-permute-start | bytes 258056 | tf_op jit(solution)/shard_map/ppermute | solution.py:216
  19.1 5.2 %collective-permute-start.8 = (bf16[8,5376]{1,0:T(8,128)(2,1)S(1)}, bf16[8,5376]{1,0:T(8,128)(2,1)S(1)}, u32[]{:S(2)}, u32[]{:S(2)}) collective-permute-start(bf16[8,5376]{1,0:T(8,128)(2,1)S(1)} %slice.81), channel_id=1, source_target_pairs={{0,2},{1,3},{2,0},{3,1},{4,6},{5,7},{6,4},{7,5},{8,10},{9,11},{10,... | collective-permute-start | bytes 258056 | tf_op jit(solution)/shard_map/ppermute | solution.py:216
  22.9 6.0 %collective-permute-start.6 = (bf16[16,5376]{1,0:T(8,128)(2,1)S(1)}, bf16[16,5376]{1,0:T(8,128)(2,1)S(1)}, u32[]{:S(2)}, u32[]{:S(2)}) collective-permute-start(bf16[16,5376]{1,0:T(8,128)(2,1)S(1)} %norm.1.refs_0_.own_ref), channel_id=1, source_target_pairs={{0,2},{1,3},{2,0},{3,1},{4,6},{5,7},{6,4},{7,5},{8,10},{9,11},{10,... | collective-permute-start | bytes 516104 | tf_op jit(solution)/shard_map/ppermute | solution.py:216
  29.0 2.2 %collective-permute-start.9 = (bf16[32,5376]{1,0:T(8,128)(2,1)S(1)}, bf16[32,5376]{1,0:T(8,128)(2,1)S(1)}, u32[]{:S(2)}, u32[]{:S(2)}) collective-permute-start(bf16[32,5376]{1,0:T(8,128)(2,1)S(1)} %chips.1.own_ref), channel_id=1, source_target_pairs={{0,1},{1,0},{2,3},{3,2},{4,5},{5,4},{6,7},{7,6},{8,9},{9,8},{10,11... | collective-permute-start | bytes 1032200 | tf_op jit(solution)/shard_map/ppermute | solution.py:216
  29.2 6.8 %collective-permute-start.12 = (bf16[4,5376]{1,0:T(4,128)(2,1)S(1)}, bf16[4,5376]{1,0:T(4,128)(2,1)S(1)}, u32[]{:S(2)}, u32[]{:S(2)}) collective-permute-start(bf16[4,5376]{1,0:T(4,128)(2,1)S(1)} %slice.83), channel_id=1, source_target_pairs={{0,8},{1,9},{2,10},{3,11},{4,12},{5,13},{6,14},{7,15},{8,0},{9,1},... | collective-permute-start | bytes 129032 | tf_op jit(solution)/shard_map/ppermute | solution.py:216
  34.4 4.5 %collective-permute-start.10 = (f32[2,64]{1,0:T(2,128)S(1)}, f32[2,64]{1,0:T(2,128)S(1)}, u32[]{:S(2)}, u32[]{:S(2)}) collective-permute-start(f32[2,64]{1,0:T(2,128)S(1)} %get-tuple-element.29), channel_id=1, source_target_pairs={{0,8},{1,9},{2,10},{3,11},{4,12},{5,13},{6,14},{7,15},{8,0},{9,1},... | collective-permute-start | bytes 1544 | tf_op jit(solution)/shard_map/ppermute | solution.py:216
  36.0 3.9 %collective-permute-start.13 = (bf16[2,5376]{1,0:T(2,128)(2,1)S(1)}, bf16[2,5376]{1,0:T(2,128)(2,1)S(1)}, u32[]{:S(2)}, u32[]{:S(2)}) collective-permute-start(bf16[2,5376]{1,0:T(2,128)(2,1)S(1)} %slice.85), channel_id=1, source_target_pairs={{0,4},{1,5},{2,6},{3,7},{4,0},{5,1},{6,2},{7,3},{8,12},{9,13},{10,... | collective-permute-start | bytes 64520 | tf_op jit(solution)/shard_map/ppermute | solution.py:216
  38.9 3.6 %collective-permute-start.11 = (f32[2,64]{1,0:T(2,128)S(1)}, f32[2,64]{1,0:T(2,128)S(1)}, u32[]{:S(2)}, u32[]{:S(2)}) collective-permute-start(f32[2,64]{1,0:T(2,128)S(1)} %pad_maximum_fusion.2.own_ref), channel_id=1, source_target_pairs={{0,4},{1,5},{2,6},{3,7},{4,0},{5,1},{6,2},{7,3},{8,12},{9,13},{10,... | collective-permute-start | bytes 1544 | tf_op jit(solution)/shard_map/ppermute | solution.py:216
  42.6 3.6 %collective-permute-start.14 = (f32[2,64]{1,0:T(2,128)S(1)}, f32[2,64]{1,0:T(2,128)S(1)}, u32[]{:S(2)}, u32[]{:S(2)}) collective-permute-start(f32[2,64]{1,0:T(2,128)S(1)} %merge.1), channel_id=1, source_target_pairs={{0,2},{1,3},{2,0},{3,1},{4,6},{5,7},{6,4},{7,5},{8,10},{9,11},{10,... | collective-permute-start | bytes 1544 | tf_op jit(solution)/shard_map/ppermute | solution.py:216
  46.2 1.2 %collective-permute-start.15 = (f32[2,64]{1,0:T(2,128)S(1)}, f32[2,64]{1,0:T(2,128)S(1)}, u32[]{:S(2)}, u32[]{:S(2)}) collective-permute-start(f32[2,64]{1,0:T(2,128)S(1)} %pad_maximum_fusion.3.own_ref), channel_id=1, source_target_pairs={{0,1},{1,0},{2,3},{3,2},{4,5},{5,4},{6,7},{7,6},{8,9},{9,8},{10,11... | collective-permute-start | bytes 1544 | tf_op jit(solution)/shard_map/ppermute | solution.py:216

commit v10 on v9

--- a/solution.py
+++ b/solution.py
@@ -12,18 +12,10 @@
 MIB = 2**20
 
 
-def reversed_bits(value, bits):
-    out = 0
-    for k in range(bits):
-        out = out * 2 + (value >> k & 1)
-    return out
-
-
 def table_rows(rows, shards):
-    bits = shards.bit_length() - 3
     dev = rows // shards
     return [
-        (reversed_bits(q, bits) * 4 + y * 2 + c) * dev + j
+        (q * 4 + y * 2 + c) * dev + j
         for c in range(2)
         for y in range(2)
         for q in range(shards // 4)
@@ -99,9 +91,10 @@
             )
             owner = r // rows_dev
             way = owner % 4 ^ low
-            order = owner // 4 ^ me // 4
-            if step == 0:
-                order = sum((owner // 4 >> k) % 2 << (bits - 1 - k) for k in range(bits))
+            order = owner // 4
+            if step > 0:
+                chip = order ^ me // 4
+                order = sum((chip >> k) % 2 << (bits - 1 - k) for k in range(bits))
             place = (way % 2 * 2 + way // 2) * (shards // 4) + order
             rows[pl.ds(place * rows_dev + r % rows_dev, 1), :] = picked
 
@@ -268,7 +261,7 @@
             parts = [rows[i * size : (i + 1) * size] for i in range(2 << k)]
             other = [parts[i ^ 1] for i in range(2 << k)]
             rows = jnp.where(
-                me // 4 >> k & 1 != 0, jnp.concatenate(other), jnp.concatenate(parts)
+                me // 4 >> bits - 1 - k & 1 != 0, jnp.concatenate(other), jnp.concatenate(parts)
             )
         return rows
 
@@ -395,7 +388,7 @@
     following = keep[:quarter] + swapped(keep[quarter:], 2)
     for k, bit in enumerate(high):
         held = beside.shape[0] // 2
-        moved = swapped(beside, bit)
+        moved = swapped(beside, high[-1 - k])
         got = swapped(own, bit)
         if k < len(high) - 1:
             beside = paired(join_kernel, beside, moved, 4 * held, "join", own)
@@ -410,7 +403,7 @@
     others = swapped(states, 1)
     scaled, stats = head(states, others, head_table, temps)
     scaled = turned(scaled, places, steps)
-    for bit in high:
+    for bit in reversed(high):
         half = following.shape[0] // 2
         following = following[:half] + swapped(following[half:], bit)
     embedded = (following.astype(jnp.float32) * math.sqrt(width)).astype(jnp.bfloat16)

time: 48.6 us -> 50.1 us (1.031)
  waiting for transfers between devices: 11 us -> 14.8 us
  starting transfers between devices: 20.5 us -> 18.5 us
    ppermute x16, waiting for transfers between devices: 11 us -> 14.8 us  [swapped(): return lax.ppermute(rows, 'vocab', pairs)]
    ppermute x16, starting transfers between devices: 20.5 us -> 18.5 us  [swapped(): return lax.ppermute(rows, 'vocab', pairs)]
  transfers between devices with their start and end apart: 16 -> 16, of which waited for: 9 -> 11; matrix products, arithmetic and copies ran while one was open for 2% -> 2% of each run, Pallas kernels for 24% -> 23%
where the time goes in v10:
time: 50.1 us; the launch traced here: 49.7 us
  starting transfers between devices  18.5 us (37%)
  waiting for transfers between devices  14.8 us (30%)
  Pallas kernels  14.7 us (29%)
  other arithmetic  0.88 us (2%)
  between operations  0.84 us (2%)
    ppermute x16, starting transfers between devices, swapped(): return lax.ppermute(rows, 'vocab', pairs)  18.5 us
    ppermute x16, waiting for transfers between devices, swapped(): return lax.ppermute(rows, 'vocab', pairs)  14.8 us
    pallas_call x2, Pallas kernels, loaded(): pl.pallas_call(functools.partial(load_kernel, first, last), out_shape=(ja...  5.23 us
    pallas_call x2, Pallas kernels, picked_rows(): pl.pallas_call(functools.partial(pick_kernel, step, places), out_shape=ou...  4.71 us
    pallas_call x1, Pallas kernels, head(): pl.pallas_call(head_kernel, out_shape=(jax.ShapeDtypeStruct((voc_dev, row...  3.15 us
  transfers between devices with their start and end apart: 16, of which 11 were waited for; matrix products, arithmetic and copies ran while one was open for 2% of the time, Pallas kernels for 23%

profile of v10, /device:TPU:0, one launch (start us, length us, event | category | flops | bytes accessed | tf_op | source)
XLA Modules:
  0.0 49.7 jit_solution(12943190462822581878)
XLA Ops:
  0.6 0.0 copy-start
  0.6 0.0 copy-start.1
  0.7 0.0 copy-start.2
  0.7 2.4 %pick.2 = (bf16[16,5376]{1,0:T(8,128)(2,1)S(1)}, bf16[16,5376]{1,0:T(8,128)(2,1)S(1)}, f32[1,64]{1,0:T(1,128)S(1)}) custom-call(s32[2,32]{1,0:T(2,128)} %ids_ref.3, bf16[1024,5376]{1,0:T(8,128)(2,1)} %table_ref.7, s32[2,32]{1,0:T(2,128)} %refs_0_.1, f32[8]{0:T(128)} %refs_1_.1), custom_call_target="tpu_custom_call" | custom-call | tf_op jit(solution)/shard_map/pick/pallas_call | solution.py:118
  3.1 0.5 %collective-permute-start = (bf16[16,5376]{1,0:T(8,128)(2,1)S(1)}, bf16[16,5376]{1,0:T(8,128)(2,1)S(1)}, u32[]{:S(2)}, u32[]{:S(2)}) collective-permute-start(bf16[16,5376]{1,0:T(8,128)(2,1)S(1)} %get-tuple-element.17), channel_id=1, source_target_pairs={{0,1},{1,0},{2,3},{3,2},{4,5},{5,4},{6,7},{7,6},{8,9},{9,8},{10,11... | collective-permute-start | bytes 516104 | tf_op jit(solution)/shard_map/ppermute | solution.py:209
  3.6 1.0 %collective-permute-done.got_ref = bf16[16,5376]{1,0:T(8,128)(2,1)S(1)} collective-permute-done((bf16[16,5376]{1,0:T(8,128)(2,1)S(1)}, bf16[16,5376]{1,0:T(8,128)(2,1)S(1)}, u32[]{:S(2)}, u32[]{:S(2)}) %collective-permute-start) | collective-permute-done | bytes 172064 | tf_op jit(solution)/shard_map/ppermute | solution.py:209
  4.6 0.0 copy-done
  4.6 0.0 copy-done.1
  4.6 0.1 fold.1
  4.7 2.4 %collective-permute-start.2 = (bf16[8,5376]{1,0:T(8,128)(2,1)S(1)}, bf16[8,5376]{1,0:T(8,128)(2,1)S(1)}, u32[]{:S(2)}, u32[]{:S(2)}) collective-permute-start(bf16[8,5376]{1,0:T(8,128)(2,1)S(1)} %get-tuple-element.20), channel_id=1, source_target_pairs={{0,2},{1,3},{2,0},{3,1},{4,6},{5,7},{6,4},{7,5},{8,10},{9,11},{10,... | collective-permute-start | bytes 258056 | tf_op jit(solution)/shard_map/ppermute | solution.py:209
  7.1 2.1 %collective-permute-start.1 = (bf16[4,5376]{1,0:T(4,128)(2,1)S(1)}, bf16[4,5376]{1,0:T(4,128)(2,1)S(1)}, u32[]{:S(2)}, u32[]{:S(2)}) collective-permute-start(bf16[4,5376]{1,0:T(4,128)(2,1)S(1)} %get-tuple-element.18.own_ref), channel_id=1, source_target_pairs={{0,4},{1,5},{2,6},{3,7},{4,0},{5,1},{6,2},{7,3},{8,12},{9,13},{10,... | collective-permute-start | bytes 129032 | tf_op jit(solution)/shard_map/ppermute | solution.py:209
  9.2 0.9 %collective-permute-done.2 = bf16[8,5376]{1,0:T(8,128)(2,1)S(1)} collective-permute-done((bf16[8,5376]{1,0:T(8,128)(2,1)S(1)}, bf16[8,5376]{1,0:T(8,128)(2,1)S(1)}, u32[]{:S(2)}, u32[]{:S(2)}) %collective-permute-start.2) | collective-permute-done | bytes 86048 | tf_op jit(solution)/shard_map/ppermute | solution.py:209
  10.2 3.1 %collective-permute-start.4 = (bf16[8,5376]{1,0:T(8,128)(2,1)S(1)}, bf16[8,5376]{1,0:T(8,128)(2,1)S(1)}, u32[]{:S(2)}, u32[]{:S(2)}) collective-permute-start(bf16[8,5376]{1,0:T(8,128)(2,1)S(1)} %add.23.refs_0_.own_ref), channel_id=1, source_target_pairs={{0,8},{1,9},{2,10},{3,11},{4,12},{5,13},{6,14},{7,15},{8,0},{9,1},... | collective-permute-start | bytes 258056 | tf_op jit(solution)/shard_map/ppermute | solution.py:209
  13.3 0.0 collective-permute-done.1.got_ref
  13.4 1.0 %collective-permute-start.3 = (bf16[8,5376]{1,0:T(8,128)(2,1)S(1)}, bf16[8,5376]{1,0:T(8,128)(2,1)S(1)}, u32[]{:S(2)}, u32[]{:S(2)}) collective-permute-start(bf16[8,5376]{1,0:T(8,128)(2,1)S(1)} %join.1), channel_id=1, source_target_pairs={{0,8},{1,9},{2,10},{3,11},{4,12},{5,13},{6,14},{7,15},{8,0},{9,1},... | collective-permute-start | bytes 258056 | tf_op jit(solution)/shard_map/ppermute | solution.py:209
  14.4 2.3 %pick.3 = (bf16[16,5376]{1,0:T(8,128)(2,1)S(1)}, bf16[16,5376]{1,0:T(8,128)(2,1)S(1)}) custom-call(s32[2,32]{1,0:T(2,128)} %ids_ref.3, bf16[1024,5376]{1,0:T(8,128)(2,1)} %table_ref.7, bf16[8,5376]{1,0:T(8,128)(2,1)S(1)} %add.23.refs_0_.own_ref), custom_call_target="tpu_custom_call" | custom-call | tf_op jit(solution)/shard_map/pick/pallas_call | solution.py:118
  16.7 0.1 collective-permute-start.7
  16.8 2.1 %collective-permute-done.4.got_ref = bf16[8,5376]{1,0:T(8,128)(2,1)S(1)} collective-permute-done((bf16[8,5376]{1,0:T(8,128)(2,1)S(1)}, bf16[8,5376]{1,0:T(8,128)(2,1)S(1)}, u32[]{:S(2)}, u32[]{:S(2)}) %collective-permute-start.4) | collective-permute-done | bytes 86048 | tf_op jit(solution)/shard_map/ppermute | solution.py:209
  18.9 1.0 %collective-permute-start.5 = (bf16[8,5376]{1,0:T(8,128)(2,1)S(1)}, bf16[8,5376]{1,0:T(8,128)(2,1)S(1)}, u32[]{:S(2)}, u32[]{:S(2)}) collective-permute-start(bf16[8,5376]{1,0:T(8,128)(2,1)S(1)} %plus.1.refs_0_.own_ref), channel_id=1, source_target_pairs={{0,4},{1,5},{2,6},{3,7},{4,0},{5,1},{6,2},{7,3},{8,12},{9,13},{10,... | collective-permute-start | bytes 258056 | tf_op jit(solution)/shard_map/ppermute | solution.py:209
  19.9 1.3 %collective-permute-done.3 = bf16[8,5376]{1,0:T(8,128)(2,1)S(1)} collective-permute-done((bf16[8,5376]{1,0:T(8,128)(2,1)S(1)}, bf16[8,5376]{1,0:T(8,128)(2,1)S(1)}, u32[]{:S(2)}, u32[]{:S(2)}) %collective-permute-start.3) | collective-permute-done | bytes 86048 | tf_op jit(solution)/shard_map/ppermute | solution.py:209
  21.2 0.0 collective-permute-done.7
  21.3 1.6 %collective-permute-start.8 = (bf16[8,5376]{1,0:T(8,128)(2,1)S(1)}, bf16[8,5376]{1,0:T(8,128)(2,1)S(1)}, u32[]{:S(2)}, u32[]{:S(2)}) collective-permute-start(bf16[8,5376]{1,0:T(8,128)(2,1)S(1)} %slice.81), channel_id=1, source_target_pairs={{0,2},{1,3},{2,0},{3,1},{4,6},{5,7},{6,4},{7,5},{8,10},{9,11},{10,... | collective-permute-start | bytes 258056 | tf_op jit(solution)/shard_map/ppermute | solution.py:209
  22.8 0.1 pad_maximum_fusion
  22.9 1.8 %load.2 = (bf16[1024,5376]{1,0:T(8,128)(2,1)S(1)}, f32[8,128]{1,0:T(8,128)S(1)}) custom-call(bf16[1024,5376]{1,0:T(8,128)(2,1)} %table_ref.7, bf16[8,5376]{1,0:T(8,128)(2,1)S(1)} %plus.1.refs_0_.own_ref), custom_call_target="tpu_custom_call" | custom-call | tf_op jit(solution)/shard_map/load/pallas_call | solution.py:231
  24.7 0.0 collective-permute-done.5.got_ref
  24.7 0.3 norm.1.refs_0_.own_ref
  25.0 0.6 %collective-permute-start.6 = (bf16[16,5376]{1,0:T(8,128)(2,1)S(1)}, bf16[16,5376]{1,0:T(8,128)(2,1)S(1)}, u32[]{:S(2)}, u32[]{:S(2)}) collective-permute-start(bf16[16,5376]{1,0:T(8,128)(2,1)S(1)} %norm.1.refs_0_.own_ref), channel_id=1, source_target_pairs={{0,2},{1,3},{2,0},{3,1},{4,6},{5,7},{6,4},{7,5},{8,10},{9,11},{10,... | collective-permute-start | bytes 516104 | tf_op jit(solution)/shard_map/ppermute | solution.py:209
  25.6 0.2 collective-permute-done.8
  25.8 3.5 %load.3 = (bf16[1024,5376]{1,0:T(8,128)(2,1)S(1)}, f32[8,128]{1,0:T(8,128)S(1)}) custom-call(bf16[1024,5376]{1,0:T(8,128)(2,1)} %table_ref.7, bf16[16,5376]{1,0:T(8,128)(2,1)S(1)} %norm.1.refs_0_.own_ref, bf16[8,5376]{1,0:T(8,128)(2,1)S(1)} %slice_add_fusion.refs_1_, bf16[1024,5376]{1,0:T(8,128)(2,1)S(1)} %get-tuple-element.24.refs_2_), custom_call_target="tpu_custom_call", output_to_operand_aliasing={{0}: (3, {})} | custom-call | tf_op jit(solution)/shard_map/load/pallas_call | solution.py:231
  29.3 1.4 %collective-permute-done.6.got_ref = bf16[16,5376]{1,0:T(8,128)(2,1)S(1)} collective-permute-done((bf16[16,5376]{1,0:T(8,128)(2,1)S(1)}, bf16[16,5376]{1,0:T(8,128)(2,1)S(1)}, u32[]{:S(2)}, u32[]{:S(2)}) %collective-permute-start.6) | collective-permute-done | bytes 172064 | tf_op jit(solution)/shard_map/ppermute | solution.py:209
  30.8 0.1 collective-permute-start.9
  30.9 1.0 %collective-permute-start.12 = (bf16[4,5376]{1,0:T(4,128)(2,1)S(1)}, bf16[4,5376]{1,0:T(4,128)(2,1)S(1)}, u32[]{:S(2)}, u32[]{:S(2)}) collective-permute-start(bf16[4,5376]{1,0:T(4,128)(2,1)S(1)} %slice.83), channel_id=1, source_target_pairs={{0,4},{1,5},{2,6},{3,7},{4,0},{5,1},{6,2},{7,3},{8,12},{9,13},{10,... | collective-permute-start | bytes 129032 | tf_op jit(solution)/shard_map/ppermute | solution.py:209
  31.8 0.6 %collective-permute-done.9.got_ref = bf16[32,5376]{1,0:T(8,128)(2,1)S(1)} collective-permute-done((bf16[32,5376]{1,0:T(8,128)(2,1)S(1)}, bf16[32,5376]{1,0:T(8,128)(2,1)S(1)}, u32[]{:S(2)}, u32[]{:S(2)}) %collective-permute-start.9) | collective-permute-done | bytes 344096 | tf_op jit(solution)/shard_map/ppermute | solution.py:209
  32.5 3.2 %head.1 = (f32[1024,64]{1,0:T(8,128)S(1)}, f32[2,64]{1,0:T(2,128)S(1)}) custom-call(bf16[32,5376]{1,0:T(8,128)(2,1)S(1)} %chips.1.own_ref, bf16[32,5376]{1,0:T(8,128)(2,1)S(1)} %collective-permute-done.9.got_ref, bf16[1024,5376]{1,0:T(8,128)(2,1)S(1)} %get-tuple-element.26.table_ref, f32[1,64]{1,0:T(1,128)S(1)} %get-tuple-element.27.temps_ref), custom_call_target="tpu_custom_call" | custom-call | tf_op jit(solution)/shard_map/head/pallas_call | solution.py:308
  35.6 2.8 %collective-permute-start.10 = (f32[2,64]{1,0:T(2,128)S(1)}, f32[2,64]{1,0:T(2,128)S(1)}, u32[]{:S(2)}, u32[]{:S(2)}) collective-permute-start(f32[2,64]{1,0:T(2,128)S(1)} %get-tuple-element.29), channel_id=1, source_target_pairs={{0,8},{1,9},{2,10},{3,11},{4,12},{5,13},{6,14},{7,15},{8,0},{9,1},... | collective-permute-start | bytes 1544 | tf_op jit(solution)/shard_map/ppermute | solution.py:209
  38.5 0.0 collective-permute-done.12
  38.5 0.2 collective-permute-start.13
  38.8 1.4 %collective-permute-done.10 = f32[2,64]{1,0:T(2,128)S(1)} collective-permute-done((f32[2,64]{1,0:T(2,128)S(1)}, f32[2,64]{1,0:T(2,128)S(1)}, u32[]{:S(2)}, u32[]{:S(2)}) %collective-permute-start.10) | collective-permute-done | bytes 544 | tf_op jit(solution)/shard_map/ppermute | solution.py:209
  40.2 1.4 %collective-permute-start.11 = (f32[2,64]{1,0:T(2,128)S(1)}, f32[2,64]{1,0:T(2,128)S(1)}, u32[]{:S(2)}, u32[]{:S(2)}) collective-permute-start(f32[2,64]{1,0:T(2,128)S(1)} %pad_maximum_fusion.2.own_ref), channel_id=1, source_target_pairs={{0,4},{1,5},{2,6},{3,7},{4,0},{5,1},{6,2},{7,3},{8,12},{9,13},{10,... | collective-permute-start | bytes 1544 | tf_op jit(solution)/shard_map/ppermute | solution.py:209
  41.6 1.7 %collective-permute-done.13 = bf16[2,5376]{1,0:T(2,128)(2,1)S(1)} collective-permute-done((bf16[2,5376]{1,0:T(2,128)(2,1)S(1)}, bf16[2,5376]{1,0:T(2,128)(2,1)S(1)}, u32[]{:S(2)}, u32[]{:S(2)}) %collective-permute-start.13) | collective-permute-done | bytes 21536 | tf_op jit(solution)/shard_map/ppermute | solution.py:209
  43.3 0.6 %multiply_convert_fusion = (bf16[2,5376]{1,0:T(2,128)(2,1)}, bf16[2,5376]{1,0:T(2,128)(2,1)S(1)}) fusion(bf16[2,5376]{1,0:T(2,128)(2,1)S(1)} %collective-permute-done.13, bf16[4,5376]{1,0:T(4,128)(2,1)S(1)} %slice_add_fusion.1), kind=kLoop, calls=%fused_computation.4 | loop fusion | flops 43008 | bytes 86016 | tf_op jit(solution)/shard_map/convert_element_type | solution.py:409
  44.0 0.0 collective-permute-done.11.got_ref
  44.0 0.5 collective-permute-start.14
  44.5 3.1 %collective-permute-done.14 = f32[2,64]{1,0:T(2,128)S(1)} collective-permute-done((f32[2,64]{1,0:T(2,128)S(1)}, f32[2,64]{1,0:T(2,128)S(1)}, u32[]{:S(2)}, u32[]{:S(2)}) %collective-permute-start.14) | collective-permute-done | bytes 544 | tf_op jit(solution)/shard_map/ppermute | solution.py:209
  47.7 0.1 collective-permute-start.15
  47.7 0.2 turn.1.scaled_ref
  48.0 0.9 %collective-permute-done.15.got_ref = f32[2,64]{1,0:T(2,128)S(1)} collective-permute-done((f32[2,64]{1,0:T(2,128)S(1)}, f32[2,64]{1,0:T(2,128)S(1)}, u32[]{:S(2)}, u32[]{:S(2)}) %collective-permute-start.15) | collective-permute-done | bytes 544 | tf_op jit(solution)/shard_map/ppermute | solution.py:209
  48.9 0.9 %finish.1 = f32[2,32,1024]{2,1,0:T(8,128)} custom-call(f32[2,32,1024]{2,1,0:T(8,128)S(1)} %turn.1.scaled_ref, f32[2,64]{1,0:T(2,128)S(1)} %pad_maximum_fusion.3.own_ref, f32[2,64]{1,0:T(2,128)S(1)} %collective-permute-done.15.got_ref), custom_call_target="tpu_custom_call" | custom-call | tf_op jit(solution)/shard_map/finish/pallas_call | solution.py:354
  (19 shorter events, 0.4 us)
Async XLA Ops:
  0.6 4.0 %copy-start = (bf16[2,5376]{1,0:T(2,128)(2,1)S(1)}, bf16[2,5376]{1,0:T(2,128)(2,1)}, u32[]{:S(2)}) copy-start(bf16[2,5376]{1,0:T(2,128)(2,1)} %first_ref.1) | copy-start | bytes 64516
  0.6 4.0 %copy-start.1 = (bf16[2,5376]{1,0:T(2,128)(2,1)S(1)}, bf16[2,5376]{1,0:T(2,128)(2,1)}, u32[]{:S(2)}) copy-start(bf16[2,5376]{1,0:T(2,128)(2,1)} %delta_ref.1) | copy-start | bytes 64516
  0.7 8.6 %copy-start.2 = (f32[5376]{0:T(1024)S(1)}, f32[5376]{0:T(1024)}, u32[]{:S(2)}) copy-start(f32[5376]{0:T(1024)} %param.9) | copy-start | bytes 64516
  3.1 1.6 %collective-permute-start = (bf16[16,5376]{1,0:T(8,128)(2,1)S(1)}, bf16[16,5376]{1,0:T(8,128)(2,1)S(1)}, u32[]{:S(2)}, u32[]{:S(2)}) collective-permute-start(bf16[16,5376]{1,0:T(8,128)(2,1)S(1)} %get-tuple-element.17), channel_id=1, source_target_pairs={{0,1},{1,0},{2,3},{3,2},{4,5},{5,4},{6,7},{7,6},{8,9},{9,8},{10,11... | collective-permute-start | bytes 516104 | tf_op jit(solution)/shard_map/ppermute | solution.py:209
  4.7 5.5 %collective-permute-start.2 = (bf16[8,5376]{1,0:T(8,128)(2,1)S(1)}, bf16[8,5376]{1,0:T(8,128)(2,1)S(1)}, u32[]{:S(2)}, u32[]{:S(2)}) collective-permute-start(bf16[8,5376]{1,0:T(8,128)(2,1)S(1)} %get-tuple-element.20), channel_id=1, source_target_pairs={{0,2},{1,3},{2,0},{3,1},{4,6},{5,7},{6,4},{7,5},{8,10},{9,11},{10,... | collective-permute-start | bytes 258056 | tf_op jit(solution)/shard_map/ppermute | solution.py:209
  7.1 6.2 %collective-permute-start.1 = (bf16[4,5376]{1,0:T(4,128)(2,1)S(1)}, bf16[4,5376]{1,0:T(4,128)(2,1)S(1)}, u32[]{:S(2)}, u32[]{:S(2)}) collective-permute-start(bf16[4,5376]{1,0:T(4,128)(2,1)S(1)} %get-tuple-element.18.own_ref), channel_id=1, source_target_pairs={{0,4},{1,5},{2,6},{3,7},{4,0},{5,1},{6,2},{7,3},{8,12},{9,13},{10,... | collective-permute-start | bytes 129032 | tf_op jit(solution)/shard_map/ppermute | solution.py:209
  10.2 8.7 %collective-permute-start.4 = (bf16[8,5376]{1,0:T(8,128)(2,1)S(1)}, bf16[8,5376]{1,0:T(8,128)(2,1)S(1)}, u32[]{:S(2)}, u32[]{:S(2)}) collective-permute-start(bf16[8,5376]{1,0:T(8,128)(2,1)S(1)} %add.23.refs_0_.own_ref), channel_id=1, source_target_pairs={{0,8},{1,9},{2,10},{3,11},{4,12},{5,13},{6,14},{7,15},{8,0},{9,1},... | collective-permute-start | bytes 258056 | tf_op jit(solution)/shard_map/ppermute | solution.py:209
  13.4 7.8 %collective-permute-start.3 = (bf16[8,5376]{1,0:T(8,128)(2,1)S(1)}, bf16[8,5376]{1,0:T(8,128)(2,1)S(1)}, u32[]{:S(2)}, u32[]{:S(2)}) collective-permute-start(bf16[8,5376]{1,0:T(8,128)(2,1)S(1)} %join.1), channel_id=1, source_target_pairs={{0,8},{1,9},{2,10},{3,11},{4,12},{5,13},{6,14},{7,15},{8,0},{9,1},... | collective-permute-start | bytes 258056 | tf_op jit(solution)/shard_map/ppermute | solution.py:209
  16.7 4.5 %collective-permute-start.7 = (bf16[16,5376]{1,0:T(8,128)(2,1)S(1)}, bf16[16,5376]{1,0:T(8,128)(2,1)S(1)}, u32[]{:S(2)}, u32[]{:S(2)}) collective-permute-start(bf16[16,5376]{1,0:T(8,128)(2,1)S(1)} %get-tuple-element.21.refs_0_), channel_id=1, source_target_pairs={{0,1},{1,0},{2,3},{3,2},{4,5},{5,4},{6,7},{7,6},{8,9},{9,8},{10,11... | collective-permute-start | bytes 516104 | tf_op jit(solution)/shard_map/ppermute | solution.py:209
  18.9 5.8 %collective-permute-start.5 = (bf16[8,5376]{1,0:T(8,128)(2,1)S(1)}, bf16[8,5376]{1,0:T(8,128)(2,1)S(1)}, u32[]{:S(2)}, u32[]{:S(2)}) collective-permute-start(bf16[8,5376]{1,0:T(8,128)(2,1)S(1)} %plus.1.refs_0_.own_ref), channel_id=1, source_target_pairs={{0,4},{1,5},{2,6},{3,7},{4,0},{5,1},{6,2},{7,3},{8,12},{9,13},{10,... | collective-permute-start | bytes 258056 | tf_op jit(solution)/shard_map/ppermute | solution.py:209
  21.3 4.6 %collective-permute-start.8 = (bf16[8,5376]{1,0:T(8,128)(2,1)S(1)}, bf16[8,5376]{1,0:T(8,128)(2,1)S(1)}, u32[]{:S(2)}, u32[]{:S(2)}) collective-permute-start(bf16[8,5376]{1,0:T(8,128)(2,1)S(1)} %slice.81), channel_id=1, source_target_pairs={{0,2},{1,3},{2,0},{3,1},{4,6},{5,7},{6,4},{7,5},{8,10},{9,11},{10,... | collective-permute-start | bytes 258056 | tf_op jit(solution)/shard_map/ppermute | solution.py:209
  25.0 5.7 %collective-permute-start.6 = (bf16[16,5376]{1,0:T(8,128)(2,1)S(1)}, bf16[16,5376]{1,0:T(8,128)(2,1)S(1)}, u32[]{:S(2)}, u32[]{:S(2)}) collective-permute-start(bf16[16,5376]{1,0:T(8,128)(2,1)S(1)} %norm.1.refs_0_.own_ref), channel_id=1, source_target_pairs={{0,2},{1,3},{2,0},{3,1},{4,6},{5,7},{6,4},{7,5},{8,10},{9,11},{10,... | collective-permute-start | bytes 516104 | tf_op jit(solution)/shard_map/ppermute | solution.py:209
  30.8 1.7 %collective-permute-start.9 = (bf16[32,5376]{1,0:T(8,128)(2,1)S(1)}, bf16[32,5376]{1,0:T(8,128)(2,1)S(1)}, u32[]{:S(2)}, u32[]{:S(2)}) collective-permute-start(bf16[32,5376]{1,0:T(8,128)(2,1)S(1)} %chips.1.own_ref), channel_id=1, source_target_pairs={{0,1},{1,0},{2,3},{3,2},{4,5},{5,4},{6,7},{7,6},{8,9},{9,8},{10,11... | collective-permute-start | bytes 1032200 | tf_op jit(solution)/shard_map/ppermute | solution.py:209
  30.9 7.6 %collective-permute-start.12 = (bf16[4,5376]{1,0:T(4,128)(2,1)S(1)}, bf16[4,5376]{1,0:T(4,128)(2,1)S(1)}, u32[]{:S(2)}, u32[]{:S(2)}) collective-permute-start(bf16[4,5376]{1,0:T(4,128)(2,1)S(1)} %slice.83), channel_id=1, source_target_pairs={{0,4},{1,5},{2,6},{3,7},{4,0},{5,1},{6,2},{7,3},{8,12},{9,13},{10,... | collective-permute-start | bytes 129032 | tf_op jit(solution)/shard_map/ppermute | solution.py:209
  35.6 4.5 %collective-permute-start.10 = (f32[2,64]{1,0:T(2,128)S(1)}, f32[2,64]{1,0:T(2,128)S(1)}, u32[]{:S(2)}, u32[]{:S(2)}) collective-permute-start(f32[2,64]{1,0:T(2,128)S(1)} %get-tuple-element.29), channel_id=1, source_target_pairs={{0,8},{1,9},{2,10},{3,11},{4,12},{5,13},{6,14},{7,15},{8,0},{9,1},... | collective-permute-start | bytes 1544 | tf_op jit(solution)/shard_map/ppermute | solution.py:209
  38.5 4.8 %collective-permute-start.13 = (bf16[2,5376]{1,0:T(2,128)(2,1)S(1)}, bf16[2,5376]{1,0:T(2,128)(2,1)S(1)}, u32[]{:S(2)}, u32[]{:S(2)}) collective-permute-start(bf16[2,5376]{1,0:T(2,128)(2,1)S(1)} %slice.85), channel_id=1, source_target_pairs={{0,8},{1,9},{2,10},{3,11},{4,12},{5,13},{6,14},{7,15},{8,0},{9,1},... | collective-permute-start | bytes 64520 | tf_op jit(solution)/shard_map/ppermute | solution.py:209
  40.2 3.8 %collective-permute-start.11 = (f32[2,64]{1,0:T(2,128)S(1)}, f32[2,64]{1,0:T(2,128)S(1)}, u32[]{:S(2)}, u32[]{:S(2)}) collective-permute-start(f32[2,64]{1,0:T(2,128)S(1)} %pad_maximum_fusion.2.own_ref), channel_id=1, source_target_pairs={{0,4},{1,5},{2,6},{3,7},{4,0},{5,1},{6,2},{7,3},{8,12},{9,13},{10,... | collective-permute-start | bytes 1544 | tf_op jit(solution)/shard_map/ppermute | solution.py:209
  44.0 3.6 %collective-permute-start.14 = (f32[2,64]{1,0:T(2,128)S(1)}, f32[2,64]{1,0:T(2,128)S(1)}, u32[]{:S(2)}, u32[]{:S(2)}) collective-permute-start(f32[2,64]{1,0:T(2,128)S(1)} %merge.1), channel_id=1, source_target_pairs={{0,2},{1,3},{2,0},{3,1},{4,6},{5,7},{6,4},{7,5},{8,10},{9,11},{10,... | collective-permute-start | bytes 1544 | tf_op jit(solution)/shard_map/ppermute | solution.py:209
  47.7 1.2 %collective-permute-start.15 = (f32[2,64]{1,0:T(2,128)S(1)}, f32[2,64]{1,0:T(2,128)S(1)}, u32[]{:S(2)}, u32[]{:S(2)}) collective-permute-start(f32[2,64]{1,0:T(2,128)S(1)} %pad_maximum_fusion.3.own_ref), channel_id=1, source_target_pairs={{0,1},{1,0},{2,3},{3,2},{4,5},{5,4},{6,7},{7,6},{8,9},{9,8},{10,11... | collective-permute-start | bytes 1544 | tf_op jit(solution)/shard_map/ppermute | solution.py:209

commit v11 on v9

--- a/solution.py
+++ b/solution.py
@@ -99,9 +99,8 @@
             )
             owner = r // rows_dev
             way = owner % 4 ^ low
-            order = owner // 4 ^ me // 4
-            if step == 0:
-                order = sum((owner // 4 >> k) % 2 << (bits - 1 - k) for k in range(bits))
+            chip = owner // 4 if step == 0 else owner // 4 ^ me // 4
+            order = sum((chip >> k) % 2 << (bits - 1 - k) for k in range(bits))
             place = (way % 2 * 2 + way // 2) * (shards // 4) + order
             rows[pl.ds(place * rows_dev + r % rows_dev, 1), :] = picked
 
@@ -403,14 +402,13 @@
     state = jnp.concatenate([beside[:held], moved[:held]], axis=0)
     delta = jnp.concatenate([beside[held:], moved[held:]], axis=0)
     voc_dev = table.shape[0]
-    head_table, token = loaded(table, 0, voc_dev // 4, None, own)
-    states = normed(state, own, got, delta, gain, token)
-    head_table, token = loaded(table, voc_dev // 4, voc_dev, head_table, states, following)
+    states = normed(state, own, got, delta, gain)
+    head_table, token = loaded(table, 0, voc_dev, None, states, following)
     states = paired(chips_kernel, states, swapped(states, 2), rows, "chips", token)
     others = swapped(states, 1)
     scaled, stats = head(states, others, head_table, temps)
     scaled = turned(scaled, places, steps)
-    for bit in high:
+    for bit in reversed(high):
         half = following.shape[0] // 2
         following = following[:half] + swapped(following[half:], bit)
     embedded = (following.astype(jnp.float32) * math.sqrt(width)).astype(jnp.bfloat16)

time: 48.6 us -> 47.7 us (0.981)
  Pallas kernels: 14.9 us -> 13.5 us
  starting transfers between devices: 20.5 us -> 21.7 us
  waiting for transfers between devices: 11 us -> 10.4 us
    ppermute x16, starting transfers between devices: 20.5 us -> 21.7 us  [swapped(): return lax.ppermute(rows, 'vocab', pairs)]
    pallas_call x2 -> x1, Pallas kernels: 5.23 us -> 4.25 us  [loaded(): pl.pallas_call(functools.partial(load_kernel, first, last), out_shape=(ja...]
    ppermute x16, waiting for transfers between devices: 11 us -> 10.4 us  [swapped(): return lax.ppermute(rows, 'vocab', pairs)]
  transfers between devices with their start and end apart: 16 -> 16, of which waited for: 9 -> 10; matrix products, arithmetic and copies ran while one was open for 2% -> 2% of each run, Pallas kernels for 24% -> 21%
where the time goes in v11:
time: 47.7 us; the launch traced here: 47.5 us
  starting transfers between devices  21.7 us (45%)
  Pallas kernels  13.5 us (28%)
  waiting for transfers between devices  10.4 us (22%)
  other arithmetic  0.88 us (2%)
  between operations  0.84 us (2%)
    ppermute x16, starting transfers between devices, swapped(): return lax.ppermute(rows, 'vocab', pairs)  21.7 us
    ppermute x16, waiting for transfers between devices, swapped(): return lax.ppermute(rows, 'vocab', pairs)  10.4 us
    pallas_call x2, Pallas kernels, picked_rows(): pl.pallas_call(functools.partial(pick_kernel, step, places), out_shape=ou...  4.53 us
    pallas_call x1, Pallas kernels, loaded(): pl.pallas_call(functools.partial(load_kernel, first, last), out_shape=(ja...  4.25 us
    pallas_call x1, Pallas kernels, head(): pl.pallas_call(head_kernel, out_shape=(jax.ShapeDtypeStruct((voc_dev, row...  3.15 us
  transfers between devices with their start and end apart: 16, of which 10 were waited for; matrix products, arithmetic and copies ran while one was open for 2% of the time, Pallas kernels for 21%

profile of v11, /device:TPU:0, one launch (start us, length us, event | category | flops | bytes accessed | tf_op | source)
XLA Modules:
  0.0 47.5 jit_solution(10866832440662497267)
XLA Ops:
  0.6 0.0 copy-start.1
  0.6 0.0 copy-start
  0.7 0.0 copy-start.2
  0.7 2.4 %pick.2 = (bf16[16,5376]{1,0:T(8,128)(2,1)S(1)}, bf16[16,5376]{1,0:T(8,128)(2,1)S(1)}, f32[1,64]{1,0:T(1,128)S(1)}) custom-call(s32[2,32]{1,0:T(2,128)} %ids_ref.3, bf16[1024,5376]{1,0:T(8,128)(2,1)} %table_ref.5, s32[2,32]{1,0:T(2,128)} %refs_0_.1, f32[8]{0:T(128)} %refs_1_.1), custom_call_target="tpu_custom_call" | custom-call | tf_op jit(solution)/shard_map/pick/pallas_call | solution.py:124
  3.1 0.4 collective-permute-start
  3.5 1.0 %collective-permute-done.got_ref = bf16[16,5376]{1,0:T(8,128)(2,1)S(1)} collective-permute-done((bf16[16,5376]{1,0:T(8,128)(2,1)S(1)}, bf16[16,5376]{1,0:T(8,128)(2,1)S(1)}, u32[]{:S(2)}, u32[]{:S(2)}) %collective-permute-start) | collective-permute-done | bytes 172064 | tf_op jit(solution)/shard_map/ppermute | solution.py:215
  4.5 0.0 copy-done.1
  4.5 0.0 copy-done
  4.5 0.1 fold.1
  4.6 3.0 %collective-permute-start.2 = (bf16[8,5376]{1,0:T(8,128)(2,1)S(1)}, bf16[8,5376]{1,0:T(8,128)(2,1)S(1)}, u32[]{:S(2)}, u32[]{:S(2)}) collective-permute-start(bf16[8,5376]{1,0:T(8,128)(2,1)S(1)} %get-tuple-element.18), channel_id=1, source_target_pairs={{0,2},{1,3},{2,0},{3,1},{4,6},{5,7},{6,4},{7,5},{8,10},{9,11},{10,... | collective-permute-start | bytes 258056 | tf_op jit(solution)/shard_map/ppermute | solution.py:215
  7.6 2.7 %collective-permute-start.1 = (bf16[4,5376]{1,0:T(4,128)(2,1)S(1)}, bf16[4,5376]{1,0:T(4,128)(2,1)S(1)}, u32[]{:S(2)}, u32[]{:S(2)}) collective-permute-start(bf16[4,5376]{1,0:T(4,128)(2,1)S(1)} %get-tuple-element.16.own_ref), channel_id=1, source_target_pairs={{0,8},{1,9},{2,10},{3,11},{4,12},{5,13},{6,14},{7,15},{8,0},{9,1},... | collective-permute-start | bytes 129032 | tf_op jit(solution)/shard_map/ppermute | solution.py:215
  10.3 0.0 copy-done.2
  10.3 0.1 collective-permute-done.2
  10.5 2.9 %collective-permute-start.4 = (bf16[8,5376]{1,0:T(8,128)(2,1)S(1)}, bf16[8,5376]{1,0:T(8,128)(2,1)S(1)}, u32[]{:S(2)}, u32[]{:S(2)}) collective-permute-start(bf16[8,5376]{1,0:T(8,128)(2,1)S(1)} %add.23.refs_0_.own_ref), channel_id=1, source_target_pairs={{0,8},{1,9},{2,10},{3,11},{4,12},{5,13},{6,14},{7,15},{8,0},{9,1},... | collective-permute-start | bytes 258056 | tf_op jit(solution)/shard_map/ppermute | solution.py:215
  13.4 0.0 collective-permute-done.1.got_ref
  13.4 1.6 %collective-permute-start.3 = (bf16[8,5376]{1,0:T(8,128)(2,1)S(1)}, bf16[8,5376]{1,0:T(8,128)(2,1)S(1)}, u32[]{:S(2)}, u32[]{:S(2)}) collective-permute-start(bf16[8,5376]{1,0:T(8,128)(2,1)S(1)} %join.1), channel_id=1, source_target_pairs={{0,4},{1,5},{2,6},{3,7},{4,0},{5,1},{6,2},{7,3},{8,12},{9,13},{10,... | collective-permute-start | bytes 258056 | tf_op jit(solution)/shard_map/ppermute | solution.py:215
  15.0 2.1 %pick.3 = (bf16[16,5376]{1,0:T(8,128)(2,1)S(1)}, bf16[16,5376]{1,0:T(8,128)(2,1)S(1)}) custom-call(s32[2,32]{1,0:T(2,128)} %ids_ref.3, bf16[1024,5376]{1,0:T(8,128)(2,1)} %table_ref.5, bf16[8,5376]{1,0:T(8,128)(2,1)S(1)} %add.23.refs_0_.own_ref), custom_call_target="tpu_custom_call" | custom-call | tf_op jit(solution)/shard_map/pick/pallas_call | solution.py:124
  17.2 0.1 collective-permute-start.7
  17.3 0.0 collective-permute-done.4.got_ref
  17.3 1.4 %collective-permute-start.5 = (bf16[8,5376]{1,0:T(8,128)(2,1)S(1)}, bf16[8,5376]{1,0:T(8,128)(2,1)S(1)}, u32[]{:S(2)}, u32[]{:S(2)}) collective-permute-start(bf16[8,5376]{1,0:T(8,128)(2,1)S(1)} %plus.1.own_ref), channel_id=1, source_target_pairs={{0,4},{1,5},{2,6},{3,7},{4,0},{5,1},{6,2},{7,3},{8,12},{9,13},{10,... | collective-permute-start | bytes 258056 | tf_op jit(solution)/shard_map/ppermute | solution.py:215
  18.7 0.0 collective-permute-done.3
  18.8 0.0 collective-permute-done.7
  18.8 1.6 %collective-permute-start.8 = (bf16[8,5376]{1,0:T(8,128)(2,1)S(1)}, bf16[8,5376]{1,0:T(8,128)(2,1)S(1)}, u32[]{:S(2)}, u32[]{:S(2)}) collective-permute-start(bf16[8,5376]{1,0:T(8,128)(2,1)S(1)} %slice.81), channel_id=1, source_target_pairs={{0,2},{1,3},{2,0},{3,1},{4,6},{5,7},{6,4},{7,5},{8,10},{9,11},{10,... | collective-permute-start | bytes 258056 | tf_op jit(solution)/shard_map/ppermute | solution.py:215
  20.4 0.1 pad_maximum_fusion
  20.5 1.8 %collective-permute-done.5.got_ref = bf16[8,5376]{1,0:T(8,128)(2,1)S(1)} collective-permute-done((bf16[8,5376]{1,0:T(8,128)(2,1)S(1)}, bf16[8,5376]{1,0:T(8,128)(2,1)S(1)}, u32[]{:S(2)}, u32[]{:S(2)}) %collective-permute-start.5) | collective-permute-done | bytes 86048 | tf_op jit(solution)/shard_map/ppermute | solution.py:215
  22.3 0.3 norm.1.refs_0_.own_ref
  22.6 1.7 %collective-permute-start.6 = (bf16[16,5376]{1,0:T(8,128)(2,1)S(1)}, bf16[16,5376]{1,0:T(8,128)(2,1)S(1)}, u32[]{:S(2)}, u32[]{:S(2)}) collective-permute-start(bf16[16,5376]{1,0:T(8,128)(2,1)S(1)} %norm.1.refs_0_.own_ref), channel_id=1, source_target_pairs={{0,2},{1,3},{2,0},{3,1},{4,6},{5,7},{6,4},{7,5},{8,10},{9,11},{10,... | collective-permute-start | bytes 516104 | tf_op jit(solution)/shard_map/ppermute | solution.py:215
  24.3 0.0 collective-permute-done.8
  24.3 4.2 %load.1 = (bf16[1024,5376]{1,0:T(8,128)(2,1)S(1)}, f32[8,128]{1,0:T(8,128)S(1)}) custom-call(bf16[1024,5376]{1,0:T(8,128)(2,1)} %table_ref.5, bf16[16,5376]{1,0:T(8,128)(2,1)S(1)} %norm.1.refs_0_.own_ref, bf16[8,5376]{1,0:T(8,128)(2,1)S(1)} %slice_add_fusion.refs_1_), custom_call_target="tpu_custom_call" | custom-call | tf_op jit(solution)/shard_map/load/pallas_call | solution.py:237
  28.5 0.1 collective-permute-done.6.got_ref
  28.7 0.1 collective-permute-start.9
  28.8 0.8 %collective-permute-start.12 = (bf16[4,5376]{1,0:T(4,128)(2,1)S(1)}, bf16[4,5376]{1,0:T(4,128)(2,1)S(1)}, u32[]{:S(2)}, u32[]{:S(2)}) collective-permute-start(bf16[4,5376]{1,0:T(4,128)(2,1)S(1)} %slice.83), channel_id=1, source_target_pairs={{0,4},{1,5},{2,6},{3,7},{4,0},{5,1},{6,2},{7,3},{8,12},{9,13},{10,... | collective-permute-start | bytes 129032 | tf_op jit(solution)/shard_map/ppermute | solution.py:215
  29.6 0.8 %collective-permute-done.9.got_ref = bf16[32,5376]{1,0:T(8,128)(2,1)S(1)} collective-permute-done((bf16[32,5376]{1,0:T(8,128)(2,1)S(1)}, bf16[32,5376]{1,0:T(8,128)(2,1)S(1)}, u32[]{:S(2)}, u32[]{:S(2)}) %collective-permute-start.9) | collective-permute-done | bytes 344096 | tf_op jit(solution)/shard_map/ppermute | solution.py:215
  30.4 3.2 %head.1 = (f32[1024,64]{1,0:T(8,128)S(1)}, f32[2,64]{1,0:T(2,128)S(1)}) custom-call(bf16[32,5376]{1,0:T(8,128)(2,1)S(1)} %chips.1.own_ref, bf16[32,5376]{1,0:T(8,128)(2,1)S(1)} %collective-permute-done.9.got_ref, bf16[1024,5376]{1,0:T(8,128)(2,1)S(1)} %get-tuple-element.22.table_ref, f32[1,64]{1,0:T(1,128)S(1)} %get-tuple-element.23.temps_ref), custom_call_target="tpu_custom_call" | custom-call | tf_op jit(solution)/shard_map/head/pallas_call | solution.py:314
  33.6 2.7 %collective-permute-start.10 = (f32[2,64]{1,0:T(2,128)S(1)}, f32[2,64]{1,0:T(2,128)S(1)}, u32[]{:S(2)}, u32[]{:S(2)}) collective-permute-start(f32[2,64]{1,0:T(2,128)S(1)} %get-tuple-element.25), channel_id=1, source_target_pairs={{0,8},{1,9},{2,10},{3,11},{4,12},{5,13},{6,14},{7,15},{8,0},{9,1},... | collective-permute-start | bytes 1544 | tf_op jit(solution)/shard_map/ppermute | solution.py:215
  36.2 0.0 collective-permute-done.12
  36.3 0.4 collective-permute-start.13
  36.7 1.4 %collective-permute-done.10 = f32[2,64]{1,0:T(2,128)S(1)} collective-permute-done((f32[2,64]{1,0:T(2,128)S(1)}, f32[2,64]{1,0:T(2,128)S(1)}, u32[]{:S(2)}, u32[]{:S(2)}) %collective-permute-start.10) | collective-permute-done | bytes 544 | tf_op jit(solution)/shard_map/ppermute | solution.py:215
  38.1 0.8 %collective-permute-start.11 = (f32[2,64]{1,0:T(2,128)S(1)}, f32[2,64]{1,0:T(2,128)S(1)}, u32[]{:S(2)}, u32[]{:S(2)}) collective-permute-start(f32[2,64]{1,0:T(2,128)S(1)} %pad_maximum_fusion.2.own_ref), channel_id=1, source_target_pairs={{0,4},{1,5},{2,6},{3,7},{4,0},{5,1},{6,2},{7,3},{8,12},{9,13},{10,... | collective-permute-start | bytes 1544 | tf_op jit(solution)/shard_map/ppermute | solution.py:215
  38.9 2.1 %collective-permute-done.13 = bf16[2,5376]{1,0:T(2,128)(2,1)S(1)} collective-permute-done((bf16[2,5376]{1,0:T(2,128)(2,1)S(1)}, bf16[2,5376]{1,0:T(2,128)(2,1)S(1)}, u32[]{:S(2)}, u32[]{:S(2)}) %collective-permute-start.13) | collective-permute-done | bytes 21536 | tf_op jit(solution)/shard_map/ppermute | solution.py:215
  41.0 0.6 %multiply_convert_fusion = (bf16[2,5376]{1,0:T(2,128)(2,1)}, bf16[2,5376]{1,0:T(2,128)(2,1)S(1)}) fusion(bf16[2,5376]{1,0:T(2,128)(2,1)S(1)} %collective-permute-done.13, bf16[4,5376]{1,0:T(4,128)(2,1)S(1)} %slice_add_fusion.1), kind=kLoop, calls=%fused_computation.4 | loop fusion | flops 43008 | bytes 86016 | tf_op jit(solution)/shard_map/convert_element_type | solution.py:414
  41.7 0.1 collective-permute-done.11.got_ref
  41.8 1.7 %collective-permute-start.14 = (f32[2,64]{1,0:T(2,128)S(1)}, f32[2,64]{1,0:T(2,128)S(1)}, u32[]{:S(2)}, u32[]{:S(2)}) collective-permute-start(f32[2,64]{1,0:T(2,128)S(1)} %merge.1), channel_id=1, source_target_pairs={{0,2},{1,3},{2,0},{3,1},{4,6},{5,7},{6,4},{7,5},{8,10},{9,11},{10,... | collective-permute-start | bytes 1544 | tf_op jit(solution)/shard_map/ppermute | solution.py:215
  43.4 2.0 %collective-permute-done.14 = f32[2,64]{1,0:T(2,128)S(1)} collective-permute-done((f32[2,64]{1,0:T(2,128)S(1)}, f32[2,64]{1,0:T(2,128)S(1)}, u32[]{:S(2)}, u32[]{:S(2)}) %collective-permute-start.14) | collective-permute-done | bytes 544 | tf_op jit(solution)/shard_map/ppermute | solution.py:215
  45.4 0.1 collective-permute-start.15
  45.5 0.2 turn.1.scaled_ref
  45.7 0.9 %collective-permute-done.15.got_ref = f32[2,64]{1,0:T(2,128)S(1)} collective-permute-done((f32[2,64]{1,0:T(2,128)S(1)}, f32[2,64]{1,0:T(2,128)S(1)}, u32[]{:S(2)}, u32[]{:S(2)}) %collective-permute-start.15) | collective-permute-done | bytes 544 | tf_op jit(solution)/shard_map/ppermute | solution.py:215
  46.6 0.9 %finish.1 = f32[2,32,1024]{2,1,0:T(8,128)} custom-call(f32[2,32,1024]{2,1,0:T(8,128)S(1)} %turn.1.scaled_ref, f32[2,64]{1,0:T(2,128)S(1)} %pad_maximum_fusion.3.own_ref, f32[2,64]{1,0:T(2,128)S(1)} %collective-permute-done.15.got_ref), custom_call_target="tpu_custom_call" | custom-call | tf_op jit(solution)/shard_map/finish/pallas_call | solution.py:360
  (18 shorter events, 0.4 us)
Async XLA Ops:
  0.6 3.9 %copy-start.1 = (bf16[2,5376]{1,0:T(2,128)(2,1)S(1)}, bf16[2,5376]{1,0:T(2,128)(2,1)}, u32[]{:S(2)}) copy-start(bf16[2,5376]{1,0:T(2,128)(2,1)} %delta_ref.1) | copy-start | bytes 64516
  0.6 3.9 %copy-start = (bf16[2,5376]{1,0:T(2,128)(2,1)S(1)}, bf16[2,5376]{1,0:T(2,128)(2,1)}, u32[]{:S(2)}) copy-start(bf16[2,5376]{1,0:T(2,128)(2,1)} %first_ref.1) | copy-start | bytes 64516
  0.7 9.7 %copy-start.2 = (f32[5376]{0:T(1024)S(1)}, f32[5376]{0:T(1024)}, u32[]{:S(2)}) copy-start(f32[5376]{0:T(1024)} %param.9) | copy-start | bytes 64516
  3.1 1.5 %collective-permute-start = (bf16[16,5376]{1,0:T(8,128)(2,1)S(1)}, bf16[16,5376]{1,0:T(8,128)(2,1)S(1)}, u32[]{:S(2)}, u32[]{:S(2)}) collective-permute-start(bf16[16,5376]{1,0:T(8,128)(2,1)S(1)} %get-tuple-element.15), channel_id=1, source_target_pairs={{0,1},{1,0},{2,3},{3,2},{4,5},{5,4},{6,7},{7,6},{8,9},{9,8},{10,11... | collective-permute-start | bytes 516104 | tf_op jit(solution)/shard_map/ppermute | solution.py:215
  4.6 5.9 %collective-permute-start.2 = (bf16[8,5376]{1,0:T(8,128)(2,1)S(1)}, bf16[8,5376]{1,0:T(8,128)(2,1)S(1)}, u32[]{:S(2)}, u32[]{:S(2)}) collective-permute-start(bf16[8,5376]{1,0:T(8,128)(2,1)S(1)} %get-tuple-element.18), channel_id=1, source_target_pairs={{0,2},{1,3},{2,0},{3,1},{4,6},{5,7},{6,4},{7,5},{8,10},{9,11},{10,... | collective-permute-start | bytes 258056 | tf_op jit(solution)/shard_map/ppermute | solution.py:215
  7.6 5.7 %collective-permute-start.1 = (bf16[4,5376]{1,0:T(4,128)(2,1)S(1)}, bf16[4,5376]{1,0:T(4,128)(2,1)S(1)}, u32[]{:S(2)}, u32[]{:S(2)}) collective-permute-start(bf16[4,5376]{1,0:T(4,128)(2,1)S(1)} %get-tuple-element.16.own_ref), channel_id=1, source_target_pairs={{0,8},{1,9},{2,10},{3,11},{4,12},{5,13},{6,14},{7,15},{8,0},{9,1},... | collective-permute-start | bytes 129032 | tf_op jit(solution)/shard_map/ppermute | solution.py:215
  10.5 6.7 %collective-permute-start.4 = (bf16[8,5376]{1,0:T(8,128)(2,1)S(1)}, bf16[8,5376]{1,0:T(8,128)(2,1)S(1)}, u32[]{:S(2)}, u32[]{:S(2)}) collective-permute-start(bf16[8,5376]{1,0:T(8,128)(2,1)S(1)} %add.23.refs_0_.own_ref), channel_id=1, source_target_pairs={{0,8},{1,9},{2,10},{3,11},{4,12},{5,13},{6,14},{7,15},{8,0},{9,1},... | collective-permute-start | bytes 258056 | tf_op jit(solution)/shard_map/ppermute | solution.py:215
  13.4 5.3 %collective-permute-start.3 = (bf16[8,5376]{1,0:T(8,128)(2,1)S(1)}, bf16[8,5376]{1,0:T(8,128)(2,1)S(1)}, u32[]{:S(2)}, u32[]{:S(2)}) collective-permute-start(bf16[8,5376]{1,0:T(8,128)(2,1)S(1)} %join.1), channel_id=1, source_target_pairs={{0,4},{1,5},{2,6},{3,7},{4,0},{5,1},{6,2},{7,3},{8,12},{9,13},{10,... | collective-permute-start | bytes 258056 | tf_op jit(solution)/shard_map/ppermute | solution.py:215
  17.2 1.6 %collective-permute-start.7 = (bf16[16,5376]{1,0:T(8,128)(2,1)S(1)}, bf16[16,5376]{1,0:T(8,128)(2,1)S(1)}, u32[]{:S(2)}, u32[]{:S(2)}) collective-permute-start(bf16[16,5376]{1,0:T(8,128)(2,1)S(1)} %get-tuple-element.19.refs_0_), channel_id=1, source_target_pairs={{0,1},{1,0},{2,3},{3,2},{4,5},{5,4},{6,7},{7,6},{8,9},{9,8},{10,11... | collective-permute-start | bytes 516104 | tf_op jit(solution)/shard_map/ppermute | solution.py:215
  17.3 5.0 %collective-permute-start.5 = (bf16[8,5376]{1,0:T(8,128)(2,1)S(1)}, bf16[8,5376]{1,0:T(8,128)(2,1)S(1)}, u32[]{:S(2)}, u32[]{:S(2)}) collective-permute-start(bf16[8,5376]{1,0:T(8,128)(2,1)S(1)} %plus.1.own_ref), channel_id=1, source_target_pairs={{0,4},{1,5},{2,6},{3,7},{4,0},{5,1},{6,2},{7,3},{8,12},{9,13},{10,... | collective-permute-start | bytes 258056 | tf_op jit(solution)/shard_map/ppermute | solution.py:215
  18.8 5.4 %collective-permute-start.8 = (bf16[8,5376]{1,0:T(8,128)(2,1)S(1)}, bf16[8,5376]{1,0:T(8,128)(2,1)S(1)}, u32[]{:S(2)}, u32[]{:S(2)}) collective-permute-start(bf16[8,5376]{1,0:T(8,128)(2,1)S(1)} %slice.81), channel_id=1, source_target_pairs={{0,2},{1,3},{2,0},{3,1},{4,6},{5,7},{6,4},{7,5},{8,10},{9,11},{10,... | collective-permute-start | bytes 258056 | tf_op jit(solution)/shard_map/ppermute | solution.py:215
  22.6 6.0 %collective-permute-start.6 = (bf16[16,5376]{1,0:T(8,128)(2,1)S(1)}, bf16[16,5376]{1,0:T(8,128)(2,1)S(1)}, u32[]{:S(2)}, u32[]{:S(2)}) collective-permute-start(bf16[16,5376]{1,0:T(8,128)(2,1)S(1)} %norm.1.refs_0_.own_ref), channel_id=1, source_target_pairs={{0,2},{1,3},{2,0},{3,1},{4,6},{5,7},{6,4},{7,5},{8,10},{9,11},{10,... | collective-permute-start | bytes 516104 | tf_op jit(solution)/shard_map/ppermute | solution.py:215
  28.7 1.7 %collective-permute-start.9 = (bf16[32,5376]{1,0:T(8,128)(2,1)S(1)}, bf16[32,5376]{1,0:T(8,128)(2,1)S(1)}, u32[]{:S(2)}, u32[]{:S(2)}) collective-permute-start(bf16[32,5376]{1,0:T(8,128)(2,1)S(1)} %chips.1.own_ref), channel_id=1, source_target_pairs={{0,1},{1,0},{2,3},{3,2},{4,5},{5,4},{6,7},{7,6},{8,9},{9,8},{10,11... | collective-permute-start | bytes 1032200 | tf_op jit(solution)/shard_map/ppermute | solution.py:215
  28.8 7.4 %collective-permute-start.12 = (bf16[4,5376]{1,0:T(4,128)(2,1)S(1)}, bf16[4,5376]{1,0:T(4,128)(2,1)S(1)}, u32[]{:S(2)}, u32[]{:S(2)}) collective-permute-start(bf16[4,5376]{1,0:T(4,128)(2,1)S(1)} %slice.83), channel_id=1, source_target_pairs={{0,4},{1,5},{2,6},{3,7},{4,0},{5,1},{6,2},{7,3},{8,12},{9,13},{10,... | collective-permute-start | bytes 129032 | tf_op jit(solution)/shard_map/ppermute | solution.py:215
  33.6 4.5 %collective-permute-start.10 = (f32[2,64]{1,0:T(2,128)S(1)}, f32[2,64]{1,0:T(2,128)S(1)}, u32[]{:S(2)}, u32[]{:S(2)}) collective-permute-start(f32[2,64]{1,0:T(2,128)S(1)} %get-tuple-element.25), channel_id=1, source_target_pairs={{0,8},{1,9},{2,10},{3,11},{4,12},{5,13},{6,14},{7,15},{8,0},{9,1},... | collective-permute-start | bytes 1544 | tf_op jit(solution)/shard_map/ppermute | solution.py:215
  36.3 4.8 %collective-permute-start.13 = (bf16[2,5376]{1,0:T(2,128)(2,1)S(1)}, bf16[2,5376]{1,0:T(2,128)(2,1)S(1)}, u32[]{:S(2)}, u32[]{:S(2)}) collective-permute-start(bf16[2,5376]{1,0:T(2,128)(2,1)S(1)} %slice.85), channel_id=1, source_target_pairs={{0,8},{1,9},{2,10},{3,11},{4,12},{5,13},{6,14},{7,15},{8,0},{9,1},... | collective-permute-start | bytes 64520 | tf_op jit(solution)/shard_map/ppermute | solution.py:215
  38.1 3.6 %collective-permute-start.11 = (f32[2,64]{1,0:T(2,128)S(1)}, f32[2,64]{1,0:T(2,128)S(1)}, u32[]{:S(2)}, u32[]{:S(2)}) collective-permute-start(f32[2,64]{1,0:T(2,128)S(1)} %pad_maximum_fusion.2.own_ref), channel_id=1, source_target_pairs={{0,4},{1,5},{2,6},{3,7},{4,0},{5,1},{6,2},{7,3},{8,12},{9,13},{10,... | collective-permute-start | bytes 1544 | tf_op jit(solution)/shard_map/ppermute | solution.py:215
  41.8 3.6 %collective-permute-start.14 = (f32[2,64]{1,0:T(2,128)S(1)}, f32[2,64]{1,0:T(2,128)S(1)}, u32[]{:S(2)}, u32[]{:S(2)}) collective-permute-start(f32[2,64]{1,0:T(2,128)S(1)} %merge.1), channel_id=1, source_target_pairs={{0,2},{1,3},{2,0},{3,1},{4,6},{5,7},{6,4},{7,5},{8,10},{9,11},{10,... | collective-permute-start | bytes 1544 | tf_op jit(solution)/shard_map/ppermute | solution.py:215
  45.4 1.2 %collective-permute-start.15 = (f32[2,64]{1,0:T(2,128)S(1)}, f32[2,64]{1,0:T(2,128)S(1)}, u32[]{:S(2)}, u32[]{:S(2)}) collective-permute-start(f32[2,64]{1,0:T(2,128)S(1)} %pad_maximum_fusion.3.own_ref), channel_id=1, source_target_pairs={{0,1},{1,0},{2,3},{3,2},{4,5},{5,4},{6,7},{7,6},{8,9},{9,8},{10,11... | collective-permute-start | bytes 1544 | tf_op jit(solution)/shard_map/ppermute | solution.py:215

commit v12 on v11

--- a/solution.py
+++ b/solution.py
@@ -144,7 +144,8 @@
     return pltpu.with_memory_space_constraint(array, pltpu.HBM)
 
 
-def fold_kernel(keep_ref, got_ref, first_ref, delta_ref, own_ref, send_ref, beside_ref):
+def fold_kernel(keep_ref, got_ref, first_ref, delta_ref, after_ref, *outs):
+    own_ref, send_ref, beside_ref = outs
     total = keep_ref[...].astype(jnp.float32) + got_ref[...].astype(jnp.float32)
     half = own_ref.shape[0]
     own_ref[...] = total[:half].astype(own_ref.dtype)
@@ -154,18 +155,18 @@
     ).astype(beside_ref.dtype)
 
 
-def folded(keep, got, first, deltas):
+def folded(keep, got, first, deltas, after):
     rows, width = keep.shape
     vmem = pl.BlockSpec(memory_space=pltpu.VMEM)
     part = jax.ShapeDtypeStruct((rows // 2, width), keep.dtype)
     return pl.pallas_call(
         fold_kernel,
         out_shape=(part, part, jax.ShapeDtypeStruct((2 * first.shape[0], width), keep.dtype)),
-        in_specs=[vmem] * 4,
+        in_specs=[vmem] * 4 + [pl.BlockSpec(memory_space=pl.ANY)],
         out_specs=(vmem,) * 3,
         compiler_params=pltpu.CompilerParams(vmem_limit_bytes=12 * MIB),
         name="fold",
-    )(keep, got, first, deltas)
+    )(keep, got, first, deltas, after)
 
 
 def plus_kernel(own_ref, got_ref, *refs):
@@ -181,13 +182,27 @@
     out_ref[...] = jnp.concatenate(parts, axis=0).astype(out_ref.dtype)
 
 
-def chips_kernel(own_ref, got_ref, *refs):
-    out_ref = refs[-1]
-    own, got = own_ref[...], got_ref[...]
+def chips_kernel(one_ref, one_got_ref, two_ref, two_got_ref, after_ref, out_ref):
+    own = [ref[...].astype(jnp.float32) for ref in (one_ref, two_ref)]
+    got = [ref[...].astype(jnp.float32) for ref in (one_got_ref, two_got_ref)]
+    own, got = jnp.concatenate(own, axis=0), jnp.concatenate(got, axis=0)
     upper = lax.axis_index("vocab") // 2 % 2 == 1
     rows = own.shape[0]
-    out_ref[:rows, :] = jnp.where(upper, got, own)
-    out_ref[rows:, :] = jnp.where(upper, own, got)
+    out_ref[:rows, :] = jnp.where(upper, got, own).astype(out_ref.dtype)
+    out_ref[rows:, :] = jnp.where(upper, own, got).astype(out_ref.dtype)
+
+
+def chips(one, one_got, two, two_got, after):
+    rows, width = one.shape
+    vmem = pl.BlockSpec(memory_space=pltpu.VMEM)
+    return pl.pallas_call(
+        chips_kernel,
+        out_shape=jax.ShapeDtypeStruct((4 * rows, width), one.dtype),
+        in_specs=[vmem] * 4 + [pl.BlockSpec(memory_space=pl.ANY)],
+        out_specs=vmem,
+        compiler_params=pltpu.CompilerParams(vmem_limit_bytes=12 * MIB),
+        name="chips",
+    )(one, one_got, two, two_got, after)
 
 
 def merge_kernel(own_ref, got_ref, *refs):
@@ -249,48 +264,46 @@
     )(in_hbm(table), *after, *held)
 
 
-def norm_kernel(first_ref, own_ref, got_ref, delta_ref, gain_ref, *refs):
-    out_ref = refs[-1]
-    width = first_ref.shape[1]
-    gain = gain_ref[...]
-
-    def rescaled(hidden):
-        squares = jnp.mean(hidden * hidden, axis=-1, keepdims=True)
-        return hidden * lax.rsqrt(squares + 1e-06) * gain
-
+def rescaled(hidden, gain):
+    squares = jnp.mean(hidden * hidden, axis=-1, keepdims=True)
+    return hidden * lax.rsqrt(squares + 1e-06) * gain
+
+
+def in_order(rows):
     me = lax.axis_index("vocab")
     bits = lax.axis_size("vocab").bit_length() - 3
-
-    def in_order(rows):
-        for k in range(bits):
-            size = rows.shape[0] >> k + 1
-            parts = [rows[i * size : (i + 1) * size] for i in range(2 << k)]
-            other = [parts[i ^ 1] for i in range(2 << k)]
-            rows = jnp.where(
-                me // 4 >> k & 1 != 0, jnp.concatenate(other), jnp.concatenate(parts)
-            )
-        return rows
-
-    one = rescaled(in_order(first_ref[...].astype(jnp.float32)))
+    for k in range(bits):
+        size = rows.shape[0] >> k + 1
+        parts = [rows[i * size : (i + 1) * size] for i in range(2 << k)]
+        other = [parts[i ^ 1] for i in range(2 << k)]
+        rows = jnp.where(me // 4 >> k & 1 != 0, jnp.concatenate(other), jnp.concatenate(parts))
+    return rows
+
+
+def first_kernel(hidden_ref, gain_ref, out_ref):
+    hidden = in_order(hidden_ref[...].astype(jnp.float32))
+    out_ref[...] = rescaled(hidden, gain_ref[...]).astype(out_ref.dtype)
+
+
+def second_kernel(delta_ref, gain_ref, own_ref, got_ref, out_ref):
+    width = out_ref.shape[1]
     picked = own_ref[...].astype(jnp.float32) + got_ref[...].astype(jnp.float32)
     embedded = (picked * math.sqrt(width)).astype(jnp.bfloat16)
-    two = rescaled(
-        embedded.astype(jnp.float32) + in_order(delta_ref[...].astype(jnp.float32))
-    )
-    out_ref[...] = jnp.concatenate([one, two], axis=0).astype(out_ref.dtype)
-
-
-def normed(first, own, got, delta, gain, *after):
-    rows, width = first.shape
+    hidden = embedded.astype(jnp.float32) + in_order(delta_ref[...].astype(jnp.float32))
+    out_ref[...] = rescaled(hidden, gain_ref[...]).astype(out_ref.dtype)
+
+
+def normed(kernel, hidden, gain, *picked):
+    rows, width = hidden.shape
     vmem = pl.BlockSpec(memory_space=pltpu.VMEM)
     return pl.pallas_call(
-        norm_kernel,
-        out_shape=jax.ShapeDtypeStruct((2 * rows, width), jnp.bfloat16),
-        in_specs=[vmem] * 5 + [pl.BlockSpec(memory_space=pl.ANY)] * len(after),
+        kernel,
+        out_shape=jax.ShapeDtypeStruct((rows, width), jnp.bfloat16),
+        in_specs=[vmem] * (2 + len(picked)),
         out_specs=vmem,
         compiler_params=pltpu.CompilerParams(vmem_limit_bytes=12 * MIB),
         name="norm",
-    )(first, own, got, delta, gain.reshape(1, width), *after)
+    )(hidden, gain.reshape(1, width), *picked)
 
 
 def head_kernel(own_ref, got_ref, table_ref, temps_ref, scaled_ref, stats_ref):
@@ -387,7 +400,9 @@
     ]
 
     keep, send, temps = picked_rows(ids, table, 0, places, classes, lookup)
-    own, send, beside = folded(keep, swapped(send, 1), first, deltas)
+    voc_dev = table.shape[0]
+    head_table, token = loaded(table, 0, voc_dev // 8, None, send)
+    own, send, beside = folded(keep, swapped(send, 1), first, deltas, token)
     own = own + swapped(send, 2)
     keep, send = picked_rows(ids, table, 1, (), own)
     keep = keep + swapped(send, 1)
@@ -401,10 +416,13 @@
             own = paired(plus_kernel, own, got, quarter, "plus", send)
     state = jnp.concatenate([beside[:held], moved[:held]], axis=0)
     delta = jnp.concatenate([beside[held:], moved[held:]], axis=0)
-    voc_dev = table.shape[0]
-    states = normed(state, own, got, delta, gain)
-    head_table, token = loaded(table, 0, voc_dev, None, states, following)
-    states = paired(chips_kernel, states, swapped(states, 2), rows, "chips", token)
+    one = normed(first_kernel, state, gain)
+    one_got = swapped(one, 2)
+    two = normed(second_kernel, delta, gain, own, got)
+    last = voc_dev // 8 * 7
+    head_table, token = loaded(table, voc_dev // 8, last, head_table, two, following, one_got)
+    states = chips(one, one_got, two, swapped(two, 2), token)
+    head_table, token = loaded(table, last, voc_dev, head_table, states)
     others = swapped(states, 1)
     scaled, stats = head(states, others, head_table, temps)
     scaled = turned(scaled, places, steps)

time: 47.7 us -> 50.9 us (1.067)
  Pallas kernels: 13.5 us -> 16.5 us
  waiting for transfers between devices: 10.4 us -> 11.2 us
  starting transfers between devices: 21.7 us -> 21.1 us
    pallas_call x1 -> x3, Pallas kernels: 4.25 us -> 6.7 us  [loaded(): pl.pallas_call(functools.partial(load_kernel, first, last), out_shape=(ja...]
    ppermute x16 -> x17, waiting for transfers between devices: 10.4 us -> 11.2 us  [swapped(): return lax.ppermute(rows, 'vocab', pairs)]
    ppermute x16 -> x17, starting transfers between devices: 21.7 us -> 21.1 us  [swapped(): return lax.ppermute(rows, 'vocab', pairs)]
  transfers between devices with their start and end apart: 16 -> 17, of which waited for: 10 -> 9; matrix products, arithmetic and copies ran while one was open for 2% -> 2% of each run, Pallas kernels for 21% -> 25%
where the time goes in v12:
time: 50.9 us; the launch traced here: 50.7 us
  starting transfers between devices  21.1 us (41%)
  Pallas kernels  16.5 us (32%)
  waiting for transfers between devices  11.2 us (22%)
  between operations  0.89 us (2%)
  other arithmetic  0.88 us (2%)
    ppermute x17, starting transfers between devices, swapped(): return lax.ppermute(rows, 'vocab', pairs)  21.1 us
    ppermute x17, waiting for transfers between devices, swapped(): return lax.ppermute(rows, 'vocab', pairs)  11.2 us
    pallas_call x3, Pallas kernels, loaded(): pl.pallas_call(functools.partial(load_kernel, first, last), out_shape=(ja...  6.7 us
    pallas_call x2, Pallas kernels, picked_rows(): pl.pallas_call(functools.partial(pick_kernel, step, places), out_shape=ou...  4.89 us
    pallas_call x1, Pallas kernels, head(): pl.pallas_call(head_kernel, out_shape=(jax.ShapeDtypeStruct((voc_dev, row...  3.16 us
  transfers between devices with their start and end apart: 17, of which 9 were waited for; matrix products, arithmetic and copies ran while one was open for 2% of the time, Pallas kernels for 25%

profile of v12, /device:TPU:0, one launch (start us, length us, event | category | flops | bytes accessed | tf_op | source)
XLA Modules:
  0.0 50.7 jit_solution(14122136160005567157)
XLA Ops:
  0.7 2.6 %pick.2 = (bf16[16,5376]{1,0:T(8,128)(2,1)S(1)}, bf16[16,5376]{1,0:T(8,128)(2,1)S(1)}, f32[1,64]{1,0:T(1,128)S(1)}) custom-call(s32[2,32]{1,0:T(2,128)} %ids_ref.3, bf16[1024,5376]{1,0:T(8,128)(2,1)} %table_ref.9, s32[2,32]{1,0:T(2,128)} %refs_0_.1, f32[8]{0:T(128)} %refs_1_.1), custom_call_target="tpu_custom_call" | custom-call | tf_op jit(solution)/shard_map/pick/pallas_call | solution.py:124
  3.2 0.2 collective-permute-start
  3.5 1.3 %load.3 = (bf16[1024,5376]{1,0:T(8,128)(2,1)S(1)}, f32[8,128]{1,0:T(8,128)S(1)}) custom-call(bf16[1024,5376]{1,0:T(8,128)(2,1)} %table_ref.9, bf16[16,5376]{1,0:T(8,128)(2,1)S(1)} %get-tuple-element.18.refs_0_), custom_call_target="tpu_custom_call" | custom-call | tf_op jit(solution)/shard_map/load/pallas_call | solution.py:252
  4.8 0.0 collective-permute-done.got_ref
  4.8 0.0 copy-done
  4.9 0.1 fold.1
  4.9 2.8 %collective-permute-start.2 = (bf16[8,5376]{1,0:T(8,128)(2,1)S(1)}, bf16[8,5376]{1,0:T(8,128)(2,1)S(1)}, u32[]{:S(2)}, u32[]{:S(2)}) collective-permute-start(bf16[8,5376]{1,0:T(8,128)(2,1)S(1)} %get-tuple-element.22), channel_id=1, source_target_pairs={{0,2},{1,3},{2,0},{3,1},{4,6},{5,7},{6,4},{7,5},{8,10},{9,11},{10,... | collective-permute-start | bytes 258056 | tf_op jit(solution)/shard_map/ppermute | solution.py:230
  7.7 2.6 %collective-permute-start.1 = (bf16[4,5376]{1,0:T(4,128)(2,1)S(1)}, bf16[4,5376]{1,0:T(4,128)(2,1)S(1)}, u32[]{:S(2)}, u32[]{:S(2)}) collective-permute-start(bf16[4,5376]{1,0:T(4,128)(2,1)S(1)} %get-tuple-element.20.own_ref), channel_id=1, source_target_pairs={{0,8},{1,9},{2,10},{3,11},{4,12},{5,13},{6,14},{7,15},{8,0},{9,1},... | collective-permute-start | bytes 129032 | tf_op jit(solution)/shard_map/ppermute | solution.py:230
  10.3 0.5 %collective-permute-done.2 = bf16[8,5376]{1,0:T(8,128)(2,1)S(1)} collective-permute-done((bf16[8,5376]{1,0:T(8,128)(2,1)S(1)}, bf16[8,5376]{1,0:T(8,128)(2,1)S(1)}, u32[]{:S(2)}, u32[]{:S(2)}) %collective-permute-start.2) | collective-permute-done | bytes 86048 | tf_op jit(solution)/shard_map/ppermute | solution.py:230
  10.9 2.8 %collective-permute-start.5 = (bf16[8,5376]{1,0:T(8,128)(2,1)S(1)}, bf16[8,5376]{1,0:T(8,128)(2,1)S(1)}, u32[]{:S(2)}, u32[]{:S(2)}) collective-permute-start(bf16[8,5376]{1,0:T(8,128)(2,1)S(1)} %add.23.refs_0_.own_ref), channel_id=1, source_target_pairs={{0,8},{1,9},{2,10},{3,11},{4,12},{5,13},{6,14},{7,15},{8,0},{9,1},... | collective-permute-start | bytes 258056 | tf_op jit(solution)/shard_map/ppermute | solution.py:230
  13.7 0.0 collective-permute-done.1.got_ref
  13.8 1.6 %collective-permute-start.3 = (bf16[8,5376]{1,0:T(8,128)(2,1)S(1)}, bf16[8,5376]{1,0:T(8,128)(2,1)S(1)}, u32[]{:S(2)}, u32[]{:S(2)}) collective-permute-start(bf16[8,5376]{1,0:T(8,128)(2,1)S(1)} %join.1), channel_id=1, source_target_pairs={{0,4},{1,5},{2,6},{3,7},{4,0},{5,1},{6,2},{7,3},{8,12},{9,13},{10,... | collective-permute-start | bytes 258056 | tf_op jit(solution)/shard_map/ppermute | solution.py:230
  15.4 2.3 %pick.3 = (bf16[16,5376]{1,0:T(8,128)(2,1)S(1)}, bf16[16,5376]{1,0:T(8,128)(2,1)S(1)}) custom-call(s32[2,32]{1,0:T(2,128)} %ids_ref.3, bf16[1024,5376]{1,0:T(8,128)(2,1)} %table_ref.9, bf16[8,5376]{1,0:T(8,128)(2,1)S(1)} %add.23.refs_0_.own_ref), custom_call_target="tpu_custom_call" | custom-call | tf_op jit(solution)/shard_map/pick/pallas_call | solution.py:124
  17.7 0.1 collective-permute-start.8
  17.8 0.5 collective-permute-done.5.got_ref
  18.2 0.6 %collective-permute-start.6 = (bf16[8,5376]{1,0:T(8,128)(2,1)S(1)}, bf16[8,5376]{1,0:T(8,128)(2,1)S(1)}, u32[]{:S(2)}, u32[]{:S(2)}) collective-permute-start(bf16[8,5376]{1,0:T(8,128)(2,1)S(1)} %plus.1.own_ref), channel_id=1, source_target_pairs={{0,4},{1,5},{2,6},{3,7},{4,0},{5,1},{6,2},{7,3},{8,12},{9,13},{10,... | collective-permute-start | bytes 258056 | tf_op jit(solution)/shard_map/ppermute | solution.py:230
  18.8 0.0 collective-permute-done.3
  18.9 0.2 norm.2.one_ref
  19.1 1.6 %collective-permute-start.4 = (bf16[8,5376]{1,0:T(8,128)(2,1)S(1)}, bf16[8,5376]{1,0:T(8,128)(2,1)S(1)}, u32[]{:S(2)}, u32[]{:S(2)}) collective-permute-start(bf16[8,5376]{1,0:T(8,128)(2,1)S(1)} %norm.2.one_ref), channel_id=1, source_target_pairs={{0,2},{1,3},{2,0},{3,1},{4,6},{5,7},{6,4},{7,5},{8,10},{9,11},{10,... | collective-permute-start | bytes 258056 | tf_op jit(solution)/shard_map/ppermute | solution.py:230
  20.8 0.0 collective-permute-done.8
  20.8 0.5 %collective-permute-start.9 = (bf16[8,5376]{1,0:T(8,128)(2,1)S(1)}, bf16[8,5376]{1,0:T(8,128)(2,1)S(1)}, u32[]{:S(2)}, u32[]{:S(2)}) collective-permute-start(bf16[8,5376]{1,0:T(8,128)(2,1)S(1)} %slice.81), channel_id=1, source_target_pairs={{0,2},{1,3},{2,0},{3,1},{4,6},{5,7},{6,4},{7,5},{8,10},{9,11},{10,... | collective-permute-start | bytes 258056 | tf_op jit(solution)/shard_map/ppermute | solution.py:230
  21.4 1.4 %collective-permute-done.6.got_ref = bf16[8,5376]{1,0:T(8,128)(2,1)S(1)} collective-permute-done((bf16[8,5376]{1,0:T(8,128)(2,1)S(1)}, bf16[8,5376]{1,0:T(8,128)(2,1)S(1)}, u32[]{:S(2)}, u32[]{:S(2)}) %collective-permute-start.6) | collective-permute-done | bytes 86048 | tf_op jit(solution)/shard_map/ppermute | solution.py:230
  22.8 0.2 norm.3.refs_0_.two_ref
  23.0 1.4 %collective-permute-start.7 = (bf16[8,5376]{1,0:T(8,128)(2,1)S(1)}, bf16[8,5376]{1,0:T(8,128)(2,1)S(1)}, u32[]{:S(2)}, u32[]{:S(2)}) collective-permute-start(bf16[8,5376]{1,0:T(8,128)(2,1)S(1)} %norm.3.refs_0_.two_ref), channel_id=1, source_target_pairs={{0,2},{1,3},{2,0},{3,1},{4,6},{5,7},{6,4},{7,5},{8,10},{9,11},{10,... | collective-permute-start | bytes 258056 | tf_op jit(solution)/shard_map/ppermute | solution.py:230
  24.4 1.8 %collective-permute-done.9 = bf16[8,5376]{1,0:T(8,128)(2,1)S(1)} collective-permute-done((bf16[8,5376]{1,0:T(8,128)(2,1)S(1)}, bf16[8,5376]{1,0:T(8,128)(2,1)S(1)}, u32[]{:S(2)}, u32[]{:S(2)}) %collective-permute-start.9) | collective-permute-done | bytes 86048 | tf_op jit(solution)/shard_map/ppermute | solution.py:230
  26.2 0.0 collective-permute-done.4.refs_2_.one_got_ref
  26.2 3.5 %load.4 = (bf16[1024,5376]{1,0:T(8,128)(2,1)S(1)}, f32[8,128]{1,0:T(8,128)S(1)}) custom-call(bf16[1024,5376]{1,0:T(8,128)(2,1)} %table_ref.9, bf16[8,5376]{1,0:T(8,128)(2,1)S(1)} %norm.3.refs_0_.two_ref, bf16[8,5376]{1,0:T(8,128)(2,1)S(1)} %slice_add_fusion.refs_1_, ...), custom_call_target="tpu_custom_call", output_to_operand_aliasing={{0}: (4, {})} | custom-call | tf_op jit(solution)/shard_map/load/pallas_call | solution.py:252
  29.7 0.0 collective-permute-done.7.two_got_ref
  29.7 0.1 chips.1.refs_0_.own_ref
  29.8 0.1 collective-permute-start.10
  30.0 1.8 %collective-permute-start.13 = (bf16[4,5376]{1,0:T(4,128)(2,1)S(1)}, bf16[4,5376]{1,0:T(4,128)(2,1)S(1)}, u32[]{:S(2)}, u32[]{:S(2)}) collective-permute-start(bf16[4,5376]{1,0:T(4,128)(2,1)S(1)} %slice.83), channel_id=1, source_target_pairs={{0,4},{1,5},{2,6},{3,7},{4,0},{5,1},{6,2},{7,3},{8,12},{9,13},{10,... | collective-permute-start | bytes 129032 | tf_op jit(solution)/shard_map/ppermute | solution.py:230
  31.7 1.9 %load.5 = (bf16[1024,5376]{1,0:T(8,128)(2,1)S(1)}, f32[8,128]{1,0:T(8,128)}) custom-call(bf16[1024,5376]{1,0:T(8,128)(2,1)} %table_ref.9, bf16[32,5376]{1,0:T(8,128)(2,1)S(1)} %chips.1.refs_0_.own_ref, bf16[1024,5376]{1,0:T(8,128)(2,1)S(1)} %get-tuple-element.27.refs_1_), custom_call_target="tpu_custom_call", output_to_operand_aliasing={{0}: (2, {})} | custom-call | tf_op jit(solution)/shard_map/load/pallas_call | solution.py:252
  33.6 0.0 collective-permute-done.10.got_ref
  33.6 3.2 %head.1 = (f32[1024,64]{1,0:T(8,128)S(1)}, f32[2,64]{1,0:T(2,128)S(1)}) custom-call(bf16[32,5376]{1,0:T(8,128)(2,1)S(1)} %chips.1.refs_0_.own_ref, bf16[32,5376]{1,0:T(8,128)(2,1)S(1)} %collective-permute-done.10.got_ref, bf16[1024,5376]{1,0:T(8,128)(2,1)S(1)} %get-tuple-element.28.table_ref, f32[1,64]{1,0:T(1,128)S(1)} %get-tuple-element.29.temps_ref), custom_call_target="tpu_custom_call" | custom-call | tf_op jit(solution)/shard_map/head/pallas_call | solution.py:327
  36.8 2.2 %collective-permute-start.11 = (f32[2,64]{1,0:T(2,128)S(1)}, f32[2,64]{1,0:T(2,128)S(1)}, u32[]{:S(2)}, u32[]{:S(2)}) collective-permute-start(f32[2,64]{1,0:T(2,128)S(1)} %get-tuple-element.31), channel_id=1, source_target_pairs={{0,8},{1,9},{2,10},{3,11},{4,12},{5,13},{6,14},{7,15},{8,0},{9,1},... | collective-permute-start | bytes 1544 | tf_op jit(solution)/shard_map/ppermute | solution.py:230
  39.0 0.0 collective-permute-done.13
  39.1 0.8 %collective-permute-start.14 = (bf16[2,5376]{1,0:T(2,128)(2,1)S(1)}, bf16[2,5376]{1,0:T(2,128)(2,1)S(1)}, u32[]{:S(2)}, u32[]{:S(2)}) collective-permute-start(bf16[2,5376]{1,0:T(2,128)(2,1)S(1)} %slice.85), channel_id=1, source_target_pairs={{0,8},{1,9},{2,10},{3,11},{4,12},{5,13},{6,14},{7,15},{8,0},{9,1},... | collective-permute-start | bytes 64520 | tf_op jit(solution)/shard_map/ppermute | solution.py:230
  39.9 1.4 %collective-permute-done.11 = f32[2,64]{1,0:T(2,128)S(1)} collective-permute-done((f32[2,64]{1,0:T(2,128)S(1)}, f32[2,64]{1,0:T(2,128)S(1)}, u32[]{:S(2)}, u32[]{:S(2)}) %collective-permute-start.11) | collective-permute-done | bytes 544 | tf_op jit(solution)/shard_map/ppermute | solution.py:230
  41.4 0.8 %collective-permute-start.12 = (f32[2,64]{1,0:T(2,128)S(1)}, f32[2,64]{1,0:T(2,128)S(1)}, u32[]{:S(2)}, u32[]{:S(2)}) collective-permute-start(f32[2,64]{1,0:T(2,128)S(1)} %pad_maximum_fusion.2.own_ref), channel_id=1, source_target_pairs={{0,4},{1,5},{2,6},{3,7},{4,0},{5,1},{6,2},{7,3},{8,12},{9,13},{10,... | collective-permute-start | bytes 1544 | tf_op jit(solution)/shard_map/ppermute | solution.py:230
  42.2 1.8 %collective-permute-done.14 = bf16[2,5376]{1,0:T(2,128)(2,1)S(1)} collective-permute-done((bf16[2,5376]{1,0:T(2,128)(2,1)S(1)}, bf16[2,5376]{1,0:T(2,128)(2,1)S(1)}, u32[]{:S(2)}, u32[]{:S(2)}) %collective-permute-start.14) | collective-permute-done | bytes 21536 | tf_op jit(solution)/shard_map/ppermute | solution.py:230
  44.0 0.6 %multiply_convert_fusion = (bf16[2,5376]{1,0:T(2,128)(2,1)}, bf16[2,5376]{1,0:T(2,128)(2,1)S(1)}) fusion(bf16[2,5376]{1,0:T(2,128)(2,1)S(1)} %collective-permute-done.14, bf16[4,5376]{1,0:T(4,128)(2,1)S(1)} %slice_add_fusion.1), kind=kLoop, calls=%fused_computation.4 | loop fusion | flops 43008 | bytes 86016 | tf_op jit(solution)/shard_map/convert_element_type | solution.py:432
  44.6 0.4 collective-permute-done.12.got_ref
  45.0 1.1 %collective-permute-start.15 = (f32[2,64]{1,0:T(2,128)S(1)}, f32[2,64]{1,0:T(2,128)S(1)}, u32[]{:S(2)}, u32[]{:S(2)}) collective-permute-start(f32[2,64]{1,0:T(2,128)S(1)} %merge.1), channel_id=1, source_target_pairs={{0,2},{1,3},{2,0},{3,1},{4,6},{5,7},{6,4},{7,5},{8,10},{9,11},{10,... | collective-permute-start | bytes 1544 | tf_op jit(solution)/shard_map/ppermute | solution.py:230
  46.1 2.5 %collective-permute-done.15 = f32[2,64]{1,0:T(2,128)S(1)} collective-permute-done((f32[2,64]{1,0:T(2,128)S(1)}, f32[2,64]{1,0:T(2,128)S(1)}, u32[]{:S(2)}, u32[]{:S(2)}) %collective-permute-start.15) | collective-permute-done | bytes 544 | tf_op jit(solution)/shard_map/ppermute | solution.py:230
  48.7 0.1 collective-permute-start.16
  48.7 0.2 turn.1.scaled_ref
  49.0 0.9 %collective-permute-done.16.got_ref = f32[2,64]{1,0:T(2,128)S(1)} collective-permute-done((f32[2,64]{1,0:T(2,128)S(1)}, f32[2,64]{1,0:T(2,128)S(1)}, u32[]{:S(2)}, u32[]{:S(2)}) %collective-permute-start.16) | collective-permute-done | bytes 544 | tf_op jit(solution)/shard_map/ppermute | solution.py:230
  49.9 0.9 %finish.1 = f32[2,32,1024]{2,1,0:T(8,128)} custom-call(f32[2,32,1024]{2,1,0:T(8,128)S(1)} %turn.1.scaled_ref, f32[2,64]{1,0:T(2,128)S(1)} %pad_maximum_fusion.3.own_ref, f32[2,64]{1,0:T(2,128)S(1)} %collective-permute-done.16.got_ref), custom_call_target="tpu_custom_call" | custom-call | tf_op jit(solution)/shard_map/finish/pallas_call | solution.py:373
  (24 shorter events, 0.5 us)
Async XLA Ops:
  0.6 4.2 %copy-start = (bf16[2,5376]{1,0:T(2,128)(2,1)S(1)}, bf16[2,5376]{1,0:T(2,128)(2,1)}, u32[]{:S(2)}) copy-start(bf16[2,5376]{1,0:T(2,128)(2,1)} %first_ref.1) | copy-start | bytes 64516
  0.6 4.2 %copy-start.1 = (bf16[2,5376]{1,0:T(2,128)(2,1)S(1)}, bf16[2,5376]{1,0:T(2,128)(2,1)}, u32[]{:S(2)}) copy-start(bf16[2,5376]{1,0:T(2,128)(2,1)} %delta_ref.1) | copy-start | bytes 64516
  0.7 9.7 %copy-start.2 = (f32[5376]{0:T(1024)S(1)}, f32[5376]{0:T(1024)}, u32[]{:S(2)}) copy-start(f32[5376]{0:T(1024)} %param.9) | copy-start | bytes 64516
  3.2 1.6 %collective-permute-start = (bf16[16,5376]{1,0:T(8,128)(2,1)S(1)}, bf16[16,5376]{1,0:T(8,128)(2,1)S(1)}, u32[]{:S(2)}, u32[]{:S(2)}) collective-permute-start(bf16[16,5376]{1,0:T(8,128)(2,1)S(1)} %get-tuple-element.18.refs_0_), channel_id=1, source_target_pairs={{0,1},{1,0},{2,3},{3,2},{4,5},{5,4},{6,7},{7,6},{8,9},{9,8},{10,11... | collective-permute-start | bytes 516104 | tf_op jit(solution)/shard_map/ppermute | solution.py:230
  4.9 6.0 %collective-permute-start.2 = (bf16[8,5376]{1,0:T(8,128)(2,1)S(1)}, bf16[8,5376]{1,0:T(8,128)(2,1)S(1)}, u32[]{:S(2)}, u32[]{:S(2)}) collective-permute-start(bf16[8,5376]{1,0:T(8,128)(2,1)S(1)} %get-tuple-element.22), channel_id=1, source_target_pairs={{0,2},{1,3},{2,0},{3,1},{4,6},{5,7},{6,4},{7,5},{8,10},{9,11},{10,... | collective-permute-start | bytes 258056 | tf_op jit(solution)/shard_map/ppermute | solution.py:230
  7.7 6.0 %collective-permute-start.1 = (bf16[4,5376]{1,0:T(4,128)(2,1)S(1)}, bf16[4,5376]{1,0:T(4,128)(2,1)S(1)}, u32[]{:S(2)}, u32[]{:S(2)}) collective-permute-start(bf16[4,5376]{1,0:T(4,128)(2,1)S(1)} %get-tuple-element.20.own_ref), channel_id=1, source_target_pairs={{0,8},{1,9},{2,10},{3,11},{4,12},{5,13},{6,14},{7,15},{8,0},{9,1},... | collective-permute-start | bytes 129032 | tf_op jit(solution)/shard_map/ppermute | solution.py:230
  10.9 7.3 %collective-permute-start.5 = (bf16[8,5376]{1,0:T(8,128)(2,1)S(1)}, bf16[8,5376]{1,0:T(8,128)(2,1)S(1)}, u32[]{:S(2)}, u32[]{:S(2)}) collective-permute-start(bf16[8,5376]{1,0:T(8,128)(2,1)S(1)} %add.23.refs_0_.own_ref), channel_id=1, source_target_pairs={{0,8},{1,9},{2,10},{3,11},{4,12},{5,13},{6,14},{7,15},{8,0},{9,1},... | collective-permute-start | bytes 258056 | tf_op jit(solution)/shard_map/ppermute | solution.py:230
  13.8 5.1 %collective-permute-start.3 = (bf16[8,5376]{1,0:T(8,128)(2,1)S(1)}, bf16[8,5376]{1,0:T(8,128)(2,1)S(1)}, u32[]{:S(2)}, u32[]{:S(2)}) collective-permute-start(bf16[8,5376]{1,0:T(8,128)(2,1)S(1)} %join.1), channel_id=1, source_target_pairs={{0,4},{1,5},{2,6},{3,7},{4,0},{5,1},{6,2},{7,3},{8,12},{9,13},{10,... | collective-permute-start | bytes 258056 | tf_op jit(solution)/shard_map/ppermute | solution.py:230
  17.7 3.1 %collective-permute-start.8 = (bf16[16,5376]{1,0:T(8,128)(2,1)S(1)}, bf16[16,5376]{1,0:T(8,128)(2,1)S(1)}, u32[]{:S(2)}, u32[]{:S(2)}) collective-permute-start(bf16[16,5376]{1,0:T(8,128)(2,1)S(1)} %get-tuple-element.23.refs_0_), channel_id=1, source_target_pairs={{0,1},{1,0},{2,3},{3,2},{4,5},{5,4},{6,7},{7,6},{8,9},{9,8},{10,11... | collective-permute-start | bytes 516104 | tf_op jit(solution)/shard_map/ppermute | solution.py:230
  18.2 4.6 %collective-permute-start.6 = (bf16[8,5376]{1,0:T(8,128)(2,1)S(1)}, bf16[8,5376]{1,0:T(8,128)(2,1)S(1)}, u32[]{:S(2)}, u32[]{:S(2)}) collective-permute-start(bf16[8,5376]{1,0:T(8,128)(2,1)S(1)} %plus.1.own_ref), channel_id=1, source_target_pairs={{0,4},{1,5},{2,6},{3,7},{4,0},{5,1},{6,2},{7,3},{8,12},{9,13},{10,... | collective-permute-start | bytes 258056 | tf_op jit(solution)/shard_map/ppermute | solution.py:230
  19.1 7.1 %collective-permute-start.4 = (bf16[8,5376]{1,0:T(8,128)(2,1)S(1)}, bf16[8,5376]{1,0:T(8,128)(2,1)S(1)}, u32[]{:S(2)}, u32[]{:S(2)}) collective-permute-start(bf16[8,5376]{1,0:T(8,128)(2,1)S(1)} %norm.2.one_ref), channel_id=1, source_target_pairs={{0,2},{1,3},{2,0},{3,1},{4,6},{5,7},{6,4},{7,5},{8,10},{9,11},{10,... | collective-permute-start | bytes 258056 | tf_op jit(solution)/shard_map/ppermute | solution.py:230
  20.8 5.4 %collective-permute-start.9 = (bf16[8,5376]{1,0:T(8,128)(2,1)S(1)}, bf16[8,5376]{1,0:T(8,128)(2,1)S(1)}, u32[]{:S(2)}, u32[]{:S(2)}) collective-permute-start(bf16[8,5376]{1,0:T(8,128)(2,1)S(1)} %slice.81), channel_id=1, source_target_pairs={{0,2},{1,3},{2,0},{3,1},{4,6},{5,7},{6,4},{7,5},{8,10},{9,11},{10,... | collective-permute-start | bytes 258056 | tf_op jit(solution)/shard_map/ppermute | solution.py:230
  23.0 6.7 %collective-permute-start.7 = (bf16[8,5376]{1,0:T(8,128)(2,1)S(1)}, bf16[8,5376]{1,0:T(8,128)(2,1)S(1)}, u32[]{:S(2)}, u32[]{:S(2)}) collective-permute-start(bf16[8,5376]{1,0:T(8,128)(2,1)S(1)} %norm.3.refs_0_.two_ref), channel_id=1, source_target_pairs={{0,2},{1,3},{2,0},{3,1},{4,6},{5,7},{6,4},{7,5},{8,10},{9,11},{10,... | collective-permute-start | bytes 258056 | tf_op jit(solution)/shard_map/ppermute | solution.py:230
  29.8 3.8 %collective-permute-start.10 = (bf16[32,5376]{1,0:T(8,128)(2,1)S(1)}, bf16[32,5376]{1,0:T(8,128)(2,1)S(1)}, u32[]{:S(2)}, u32[]{:S(2)}) collective-permute-start(bf16[32,5376]{1,0:T(8,128)(2,1)S(1)} %chips.1.refs_0_.own_ref), channel_id=1, source_target_pairs={{0,1},{1,0},{2,3},{3,2},{4,5},{5,4},{6,7},{7,6},{8,9},{9,8},{10,11... | collective-permute-start | bytes 1032200 | tf_op jit(solution)/shard_map/ppermute | solution.py:230
  30.0 9.1 %collective-permute-start.13 = (bf16[4,5376]{1,0:T(4,128)(2,1)S(1)}, bf16[4,5376]{1,0:T(4,128)(2,1)S(1)}, u32[]{:S(2)}, u32[]{:S(2)}) collective-permute-start(bf16[4,5376]{1,0:T(4,128)(2,1)S(1)} %slice.83), channel_id=1, source_target_pairs={{0,4},{1,5},{2,6},{3,7},{4,0},{5,1},{6,2},{7,3},{8,12},{9,13},{10,... | collective-permute-start | bytes 129032 | tf_op jit(solution)/shard_map/ppermute | solution.py:230
  36.8 4.5 %collective-permute-start.11 = (f32[2,64]{1,0:T(2,128)S(1)}, f32[2,64]{1,0:T(2,128)S(1)}, u32[]{:S(2)}, u32[]{:S(2)}) collective-permute-start(f32[2,64]{1,0:T(2,128)S(1)} %get-tuple-element.31), channel_id=1, source_target_pairs={{0,8},{1,9},{2,10},{3,11},{4,12},{5,13},{6,14},{7,15},{8,0},{9,1},... | collective-permute-start | bytes 1544 | tf_op jit(solution)/shard_map/ppermute | solution.py:230
  39.1 4.9 %collective-permute-start.14 = (bf16[2,5376]{1,0:T(2,128)(2,1)S(1)}, bf16[2,5376]{1,0:T(2,128)(2,1)S(1)}, u32[]{:S(2)}, u32[]{:S(2)}) collective-permute-start(bf16[2,5376]{1,0:T(2,128)(2,1)S(1)} %slice.85), channel_id=1, source_target_pairs={{0,8},{1,9},{2,10},{3,11},{4,12},{5,13},{6,14},{7,15},{8,0},{9,1},... | collective-permute-start | bytes 64520 | tf_op jit(solution)/shard_map/ppermute | solution.py:230
  41.4 3.6 %collective-permute-start.12 = (f32[2,64]{1,0:T(2,128)S(1)}, f32[2,64]{1,0:T(2,128)S(1)}, u32[]{:S(2)}, u32[]{:S(2)}) collective-permute-start(f32[2,64]{1,0:T(2,128)S(1)} %pad_maximum_fusion.2.own_ref), channel_id=1, source_target_pairs={{0,4},{1,5},{2,6},{3,7},{4,0},{5,1},{6,2},{7,3},{8,12},{9,13},{10,... | collective-permute-start | bytes 1544 | tf_op jit(solution)/shard_map/ppermute | solution.py:230
  45.0 3.6 %collective-permute-start.15 = (f32[2,64]{1,0:T(2,128)S(1)}, f32[2,64]{1,0:T(2,128)S(1)}, u32[]{:S(2)}, u32[]{:S(2)}) collective-permute-start(f32[2,64]{1,0:T(2,128)S(1)} %merge.1), channel_id=1, source_target_pairs={{0,2},{1,3},{2,0},{3,1},{4,6},{5,7},{6,4},{7,5},{8,10},{9,11},{10,... | collective-permute-start | bytes 1544 | tf_op jit(solution)/shard_map/ppermute | solution.py:230
  48.7 1.2 %collective-permute-start.16 = (f32[2,64]{1,0:T(2,128)S(1)}, f32[2,64]{1,0:T(2,128)S(1)}, u32[]{:S(2)}, u32[]{:S(2)}) collective-permute-start(f32[2,64]{1,0:T(2,128)S(1)} %pad_maximum_fusion.3.own_ref), channel_id=1, source_target_pairs={{0,1},{1,0},{2,3},{3,2},{4,5},{5,4},{6,7},{7,6},{8,9},{9,8},{10,11... | collective-permute-start | bytes 1544 | tf_op jit(solution)/shard_map/ppermute | solution.py:230

commit v13 on v12

--- a/solution.py
+++ b/solution.py
@@ -419,10 +419,10 @@
     one = normed(first_kernel, state, gain)
     one_got = swapped(one, 2)
     two = normed(second_kernel, delta, gain, own, got)
-    last = voc_dev // 8 * 7
-    head_table, token = loaded(table, voc_dev // 8, last, head_table, two, following, one_got)
+    middle = voc_dev // 8 * 5
+    head_table, token = loaded(table, voc_dev // 8, middle, head_table, two)
+    head_table, token = loaded(table, middle, voc_dev, head_table, following, one_got)
     states = chips(one, one_got, two, swapped(two, 2), token)
-    head_table, token = loaded(table, last, voc_dev, head_table, states)
     others = swapped(states, 1)
     scaled, stats = head(states, others, head_table, temps)
     scaled = turned(scaled, places, steps)

time: 50.9 us -> 49.4 us (0.971)
  starting transfers between devices: 21.1 us -> 19.4 us
  waiting for transfers between devices: 11.2 us -> 12.7 us
  Pallas kernels: 16.5 us -> 15.1 us
    ppermute x17, starting transfers between devices: 21.1 us -> 19.4 us  [swapped(): return lax.ppermute(rows, 'vocab', pairs)]
    ppermute x17, waiting for transfers between devices: 11.2 us -> 12.7 us  [swapped(): return lax.ppermute(rows, 'vocab', pairs)]
    pallas_call x2, Pallas kernels: 4.89 us -> 3.52 us  [picked_rows(): pl.pallas_call(functools.partial(pick_kernel, step, places), out_shape=ou...]
  transfers between devices with their start and end apart: 17 -> 17, of which waited for: 9 -> 10; matrix products, arithmetic and copies ran while one was open for 2% -> 2% of each run, Pallas kernels for 25% -> 24%
where the time goes in v13:
time: 49.4 us; the launch traced here: 49.2 us
  starting transfers between devices  19.4 us (39%)
  Pallas kernels  15.1 us (31%)
  waiting for transfers between devices  12.7 us (26%)
  other arithmetic  0.89 us (2%)
  between operations  0.89 us (2%)
    ppermute x17, starting transfers between devices, swapped(): return lax.ppermute(rows, 'vocab', pairs)  19.4 us
    ppermute x17, waiting for transfers between devices, swapped(): return lax.ppermute(rows, 'vocab', pairs)  12.7 us
    pallas_call x3, Pallas kernels, loaded(): pl.pallas_call(functools.partial(load_kernel, first, last), out_shape=(ja...  6.72 us
    pallas_call x2, Pallas kernels, picked_rows(): pl.pallas_call(functools.partial(pick_kernel, step, places), out_shape=ou...  3.52 us
    pallas_call x1, Pallas kernels, head(): pl.pallas_call(head_kernel, out_shape=(jax.ShapeDtypeStruct((voc_dev, row...  3.14 us
  transfers between devices with their start and end apart: 17, of which 10 were waited for; matrix products, arithmetic and copies ran while one was open for 2% of the time, Pallas kernels for 24%

profile of v13, /device:TPU:0, one launch (start us, length us, event | category | flops | bytes accessed | tf_op | source)
XLA Modules:
  0.0 49.2 jit_solution(4117305596867775537)
XLA Ops:
  0.6 0.0 copy-start
  0.7 2.4 %pick.2 = (bf16[16,5376]{1,0:T(8,128)(2,1)S(1)}, bf16[16,5376]{1,0:T(8,128)(2,1)S(1)}, f32[1,64]{1,0:T(1,128)S(1)}) custom-call(s32[2,32]{1,0:T(2,128)} %ids_ref.3, bf16[1024,5376]{1,0:T(8,128)(2,1)} %table_ref.9, s32[2,32]{1,0:T(2,128)} %refs_0_.1, f32[8]{0:T(128)} %refs_1_.1), custom_call_target="tpu_custom_call" | custom-call | tf_op jit(solution)/shard_map/pick/pallas_call | solution.py:124
  3.1 0.7 %collective-permute-start = (bf16[16,5376]{1,0:T(8,128)(2,1)S(1)}, bf16[16,5376]{1,0:T(8,128)(2,1)S(1)}, u32[]{:S(2)}, u32[]{:S(2)}) collective-permute-start(bf16[16,5376]{1,0:T(8,128)(2,1)S(1)} %get-tuple-element.18.refs_0_), channel_id=1, source_target_pairs={{0,1},{1,0},{2,3},{3,2},{4,5},{5,4},{6,7},{7,6},{8,9},{9,8},{10,11... | collective-permute-start | bytes 516104 | tf_op jit(solution)/shard_map/ppermute | solution.py:230
  3.8 1.3 %load.3 = (bf16[1024,5376]{1,0:T(8,128)(2,1)S(1)}, f32[8,128]{1,0:T(8,128)S(1)}) custom-call(bf16[1024,5376]{1,0:T(8,128)(2,1)} %table_ref.9, bf16[16,5376]{1,0:T(8,128)(2,1)S(1)} %get-tuple-element.18.refs_0_), custom_call_target="tpu_custom_call" | custom-call | tf_op jit(solution)/shard_map/load/pallas_call | solution.py:252
  5.1 0.0 collective-permute-done.got_ref
  5.1 0.1 fold.1
  5.2 2.5 %collective-permute-start.2 = (bf16[8,5376]{1,0:T(8,128)(2,1)S(1)}, bf16[8,5376]{1,0:T(8,128)(2,1)S(1)}, u32[]{:S(2)}, u32[]{:S(2)}) collective-permute-start(bf16[8,5376]{1,0:T(8,128)(2,1)S(1)} %get-tuple-element.22), channel_id=1, source_target_pairs={{0,2},{1,3},{2,0},{3,1},{4,6},{5,7},{6,4},{7,5},{8,10},{9,11},{10,... | collective-permute-start | bytes 258056 | tf_op jit(solution)/shard_map/ppermute | solution.py:230
  7.7 2.5 %collective-permute-start.1 = (bf16[4,5376]{1,0:T(4,128)(2,1)S(1)}, bf16[4,5376]{1,0:T(4,128)(2,1)S(1)}, u32[]{:S(2)}, u32[]{:S(2)}) collective-permute-start(bf16[4,5376]{1,0:T(4,128)(2,1)S(1)} %get-tuple-element.20.own_ref), channel_id=1, source_target_pairs={{0,8},{1,9},{2,10},{3,11},{4,12},{5,13},{6,14},{7,15},{8,0},{9,1},... | collective-permute-start | bytes 129032 | tf_op jit(solution)/shard_map/ppermute | solution.py:230
  10.2 0.7 %collective-permute-done.2 = bf16[8,5376]{1,0:T(8,128)(2,1)S(1)} collective-permute-done((bf16[8,5376]{1,0:T(8,128)(2,1)S(1)}, bf16[8,5376]{1,0:T(8,128)(2,1)S(1)}, u32[]{:S(2)}, u32[]{:S(2)}) %collective-permute-start.2) | collective-permute-done | bytes 86048 | tf_op jit(solution)/shard_map/ppermute | solution.py:230
  10.9 2.7 %collective-permute-start.5 = (bf16[8,5376]{1,0:T(8,128)(2,1)S(1)}, bf16[8,5376]{1,0:T(8,128)(2,1)S(1)}, u32[]{:S(2)}, u32[]{:S(2)}) collective-permute-start(bf16[8,5376]{1,0:T(8,128)(2,1)S(1)} %add.23.refs_0_.own_ref), channel_id=1, source_target_pairs={{0,8},{1,9},{2,10},{3,11},{4,12},{5,13},{6,14},{7,15},{8,0},{9,1},... | collective-permute-start | bytes 258056 | tf_op jit(solution)/shard_map/ppermute | solution.py:230
  13.6 0.0 collective-permute-done.1.got_ref
  13.7 1.8 %collective-permute-start.3 = (bf16[8,5376]{1,0:T(8,128)(2,1)S(1)}, bf16[8,5376]{1,0:T(8,128)(2,1)S(1)}, u32[]{:S(2)}, u32[]{:S(2)}) collective-permute-start(bf16[8,5376]{1,0:T(8,128)(2,1)S(1)} %join.1), channel_id=1, source_target_pairs={{0,4},{1,5},{2,6},{3,7},{4,0},{5,1},{6,2},{7,3},{8,12},{9,13},{10,... | collective-permute-start | bytes 258056 | tf_op jit(solution)/shard_map/ppermute | solution.py:230
  15.5 1.1 %pick.3 = (bf16[16,5376]{1,0:T(8,128)(2,1)S(1)}, bf16[16,5376]{1,0:T(8,128)(2,1)S(1)}) custom-call(s32[2,32]{1,0:T(2,128)} %ids_ref.3, bf16[1024,5376]{1,0:T(8,128)(2,1)} %table_ref.9, bf16[8,5376]{1,0:T(8,128)(2,1)S(1)} %add.23.refs_0_.own_ref), custom_call_target="tpu_custom_call" | custom-call | tf_op jit(solution)/shard_map/pick/pallas_call | solution.py:124
  16.7 0.1 collective-permute-start.8
  16.7 1.4 %collective-permute-done.5.got_ref = bf16[8,5376]{1,0:T(8,128)(2,1)S(1)} collective-permute-done((bf16[8,5376]{1,0:T(8,128)(2,1)S(1)}, bf16[8,5376]{1,0:T(8,128)(2,1)S(1)}, u32[]{:S(2)}, u32[]{:S(2)}) %collective-permute-start.5) | collective-permute-done | bytes 86048 | tf_op jit(solution)/shard_map/ppermute | solution.py:230
  18.2 0.5 collective-permute-start.6
  18.6 0.3 collective-permute-done.3
  19.0 0.2 norm.2.one_ref
  19.2 1.5 %collective-permute-start.4 = (bf16[8,5376]{1,0:T(8,128)(2,1)S(1)}, bf16[8,5376]{1,0:T(8,128)(2,1)S(1)}, u32[]{:S(2)}, u32[]{:S(2)}) collective-permute-start(bf16[8,5376]{1,0:T(8,128)(2,1)S(1)} %norm.2.one_ref), channel_id=1, source_target_pairs={{0,2},{1,3},{2,0},{3,1},{4,6},{5,7},{6,4},{7,5},{8,10},{9,11},{10,... | collective-permute-start | bytes 258056 | tf_op jit(solution)/shard_map/ppermute | solution.py:230
  20.7 0.0 collective-permute-done.8
  20.7 0.7 %collective-permute-start.9 = (bf16[8,5376]{1,0:T(8,128)(2,1)S(1)}, bf16[8,5376]{1,0:T(8,128)(2,1)S(1)}, u32[]{:S(2)}, u32[]{:S(2)}) collective-permute-start(bf16[8,5376]{1,0:T(8,128)(2,1)S(1)} %slice.81), channel_id=1, source_target_pairs={{0,2},{1,3},{2,0},{3,1},{4,6},{5,7},{6,4},{7,5},{8,10},{9,11},{10,... | collective-permute-start | bytes 258056 | tf_op jit(solution)/shard_map/ppermute | solution.py:230
  21.5 1.3 %collective-permute-done.6.got_ref = bf16[8,5376]{1,0:T(8,128)(2,1)S(1)} collective-permute-done((bf16[8,5376]{1,0:T(8,128)(2,1)S(1)}, bf16[8,5376]{1,0:T(8,128)(2,1)S(1)}, u32[]{:S(2)}, u32[]{:S(2)}) %collective-permute-start.6) | collective-permute-done | bytes 86048 | tf_op jit(solution)/shard_map/ppermute | solution.py:230
  22.7 0.2 norm.3.refs_0_.two_ref
  23.0 1.8 %collective-permute-start.7 = (bf16[8,5376]{1,0:T(8,128)(2,1)S(1)}, bf16[8,5376]{1,0:T(8,128)(2,1)S(1)}, u32[]{:S(2)}, u32[]{:S(2)}) collective-permute-start(bf16[8,5376]{1,0:T(8,128)(2,1)S(1)} %norm.3.refs_0_.two_ref), channel_id=1, source_target_pairs={{0,2},{1,3},{2,0},{3,1},{4,6},{5,7},{6,4},{7,5},{8,10},{9,11},{10,... | collective-permute-start | bytes 258056 | tf_op jit(solution)/shard_map/ppermute | solution.py:230
  24.8 3.2 %load.4 = (bf16[1024,5376]{1,0:T(8,128)(2,1)S(1)}, f32[8,128]{1,0:T(8,128)}) custom-call(bf16[1024,5376]{1,0:T(8,128)(2,1)} %table_ref.9, bf16[8,5376]{1,0:T(8,128)(2,1)S(1)} %norm.3.refs_0_.two_ref, bf16[1024,5376]{1,0:T(8,128)(2,1)S(1)} %get-tuple-element.25.refs_1_), custom_call_target="tpu_custom_call", output_to_operand_aliasing={{0}: (2, {})} | custom-call | tf_op jit(solution)/shard_map/load/pallas_call | solution.py:252
  28.0 0.0 collective-permute-done.9
  28.0 0.0 collective-permute-done.4.refs_1_.one_got_ref
  28.0 2.2 %load.5 = (bf16[1024,5376]{1,0:T(8,128)(2,1)S(1)}, f32[8,128]{1,0:T(8,128)S(1)}) custom-call(bf16[1024,5376]{1,0:T(8,128)(2,1)} %table_ref.9, bf16[8,5376]{1,0:T(8,128)(2,1)S(1)} %slice_add_fusion.refs_0_, bf16[8,5376]{1,0:T(8,128)(2,1)S(1)} %collective-permute-done.4.refs_1_.one_got_ref, ...), custom_call_target="tpu_custom_call", output_to_operand_aliasing={{0}: (3, {})} | custom-call | tf_op jit(solution)/shard_map/load/pallas_call | solution.py:252
  30.2 0.0 collective-permute-done.7.two_got_ref
  30.2 0.1 chips.1.own_ref
  30.4 0.1 collective-permute-start.10
  30.5 0.4 collective-permute-start.13
  30.9 1.2 %collective-permute-done.10.got_ref = bf16[32,5376]{1,0:T(8,128)(2,1)S(1)} collective-permute-done((bf16[32,5376]{1,0:T(8,128)(2,1)S(1)}, bf16[32,5376]{1,0:T(8,128)(2,1)S(1)}, u32[]{:S(2)}, u32[]{:S(2)}) %collective-permute-start.10) | collective-permute-done | bytes 344096 | tf_op jit(solution)/shard_map/ppermute | solution.py:230
  32.1 3.1 %head.1 = (f32[1024,64]{1,0:T(8,128)S(1)}, f32[2,64]{1,0:T(2,128)S(1)}) custom-call(bf16[32,5376]{1,0:T(8,128)(2,1)S(1)} %chips.1.own_ref, bf16[32,5376]{1,0:T(8,128)(2,1)S(1)} %collective-permute-done.10.got_ref, bf16[1024,5376]{1,0:T(8,128)(2,1)S(1)} %get-tuple-element.28.table_ref, f32[1,64]{1,0:T(1,128)S(1)} %get-tuple-element.29.temps_ref), custom_call_target="tpu_custom_call" | custom-call | tf_op jit(solution)/shard_map/head/pallas_call | solution.py:327
  35.2 2.1 %collective-permute-start.11 = (f32[2,64]{1,0:T(2,128)S(1)}, f32[2,64]{1,0:T(2,128)S(1)}, u32[]{:S(2)}, u32[]{:S(2)}) collective-permute-start(f32[2,64]{1,0:T(2,128)S(1)} %get-tuple-element.31), channel_id=1, source_target_pairs={{0,8},{1,9},{2,10},{3,11},{4,12},{5,13},{6,14},{7,15},{8,0},{9,1},... | collective-permute-start | bytes 1544 | tf_op jit(solution)/shard_map/ppermute | solution.py:230
  37.3 0.0 collective-permute-done.13
  37.4 0.9 %collective-permute-start.14 = (bf16[2,5376]{1,0:T(2,128)(2,1)S(1)}, bf16[2,5376]{1,0:T(2,128)(2,1)S(1)}, u32[]{:S(2)}, u32[]{:S(2)}) collective-permute-start(bf16[2,5376]{1,0:T(2,128)(2,1)S(1)} %slice.85), channel_id=1, source_target_pairs={{0,8},{1,9},{2,10},{3,11},{4,12},{5,13},{6,14},{7,15},{8,0},{9,1},... | collective-permute-start | bytes 64520 | tf_op jit(solution)/shard_map/ppermute | solution.py:230
  38.3 1.4 %collective-permute-done.11 = f32[2,64]{1,0:T(2,128)S(1)} collective-permute-done((f32[2,64]{1,0:T(2,128)S(1)}, f32[2,64]{1,0:T(2,128)S(1)}, u32[]{:S(2)}, u32[]{:S(2)}) %collective-permute-start.11) | collective-permute-done | bytes 544 | tf_op jit(solution)/shard_map/ppermute | solution.py:230
  39.8 0.7 %collective-permute-start.12 = (f32[2,64]{1,0:T(2,128)S(1)}, f32[2,64]{1,0:T(2,128)S(1)}, u32[]{:S(2)}, u32[]{:S(2)}) collective-permute-start(f32[2,64]{1,0:T(2,128)S(1)} %pad_maximum_fusion.2.own_ref), channel_id=1, source_target_pairs={{0,4},{1,5},{2,6},{3,7},{4,0},{5,1},{6,2},{7,3},{8,12},{9,13},{10,... | collective-permute-start | bytes 1544 | tf_op jit(solution)/shard_map/ppermute | solution.py:230
  40.5 1.7 %collective-permute-done.14 = bf16[2,5376]{1,0:T(2,128)(2,1)S(1)} collective-permute-done((bf16[2,5376]{1,0:T(2,128)(2,1)S(1)}, bf16[2,5376]{1,0:T(2,128)(2,1)S(1)}, u32[]{:S(2)}, u32[]{:S(2)}) %collective-permute-start.14) | collective-permute-done | bytes 21536 | tf_op jit(solution)/shard_map/ppermute | solution.py:230
  42.3 0.6 %multiply_convert_fusion = (bf16[2,5376]{1,0:T(2,128)(2,1)}, bf16[2,5376]{1,0:T(2,128)(2,1)S(1)}) fusion(bf16[2,5376]{1,0:T(2,128)(2,1)S(1)} %collective-permute-done.14, bf16[4,5376]{1,0:T(4,128)(2,1)S(1)} %slice_add_fusion.1), kind=kLoop, calls=%fused_computation.4 | loop fusion | flops 43008 | bytes 86016 | tf_op jit(solution)/shard_map/convert_element_type | solution.py:432
  42.9 0.5 %collective-permute-done.12.got_ref = f32[2,64]{1,0:T(2,128)S(1)} collective-permute-done((f32[2,64]{1,0:T(2,128)S(1)}, f32[2,64]{1,0:T(2,128)S(1)}, u32[]{:S(2)}, u32[]{:S(2)}) %collective-permute-start.12) | collective-permute-done | bytes 544 | tf_op jit(solution)/shard_map/ppermute | solution.py:230
  43.4 0.3 collective-permute-start.15
  43.8 3.3 %collective-permute-done.15 = f32[2,64]{1,0:T(2,128)S(1)} collective-permute-done((f32[2,64]{1,0:T(2,128)S(1)}, f32[2,64]{1,0:T(2,128)S(1)}, u32[]{:S(2)}, u32[]{:S(2)}) %collective-permute-start.15) | collective-permute-done | bytes 544 | tf_op jit(solution)/shard_map/ppermute | solution.py:230
  47.1 0.1 collective-permute-start.16
  47.2 0.2 turn.1.scaled_ref
  47.4 0.9 %collective-permute-done.16.got_ref = f32[2,64]{1,0:T(2,128)S(1)} collective-permute-done((f32[2,64]{1,0:T(2,128)S(1)}, f32[2,64]{1,0:T(2,128)S(1)}, u32[]{:S(2)}, u32[]{:S(2)}) %collective-permute-start.16) | collective-permute-done | bytes 544 | tf_op jit(solution)/shard_map/ppermute | solution.py:230
  48.3 0.9 %finish.1 = f32[2,32,1024]{2,1,0:T(8,128)} custom-call(f32[2,32,1024]{2,1,0:T(8,128)S(1)} %turn.1.scaled_ref, f32[2,64]{1,0:T(2,128)S(1)} %pad_maximum_fusion.3.own_ref, f32[2,64]{1,0:T(2,128)S(1)} %collective-permute-done.16.got_ref), custom_call_target="tpu_custom_call" | custom-call | tf_op jit(solution)/shard_map/finish/pallas_call | solution.py:373
  (24 shorter events, 0.5 us)
Async XLA Ops:
  0.6 4.5 %copy-start = (bf16[2,5376]{1,0:T(2,128)(2,1)S(1)}, bf16[2,5376]{1,0:T(2,128)(2,1)}, u32[]{:S(2)}) copy-start(bf16[2,5376]{1,0:T(2,128)(2,1)} %first_ref.1) | copy-start | bytes 64516
  0.6 4.5 %copy-start.1 = (bf16[2,5376]{1,0:T(2,128)(2,1)S(1)}, bf16[2,5376]{1,0:T(2,128)(2,1)}, u32[]{:S(2)}) copy-start(bf16[2,5376]{1,0:T(2,128)(2,1)} %delta_ref.1) | copy-start | bytes 64516
  0.7 9.6 %copy-start.2 = (f32[5376]{0:T(1024)S(1)}, f32[5376]{0:T(1024)}, u32[]{:S(2)}) copy-start(f32[5376]{0:T(1024)} %param.9) | copy-start | bytes 64516
  3.1 2.0 %collective-permute-start = (bf16[16,5376]{1,0:T(8,128)(2,1)S(1)}, bf16[16,5376]{1,0:T(8,128)(2,1)S(1)}, u32[]{:S(2)}, u32[]{:S(2)}) collective-permute-start(bf16[16,5376]{1,0:T(8,128)(2,1)S(1)} %get-tuple-element.18.refs_0_), channel_id=1, source_target_pairs={{0,1},{1,0},{2,3},{3,2},{4,5},{5,4},{6,7},{7,6},{8,9},{9,8},{10,11... | collective-permute-start | bytes 516104 | tf_op jit(solution)/shard_map/ppermute | solution.py:230
  5.2 5.7 %collective-permute-start.2 = (bf16[8,5376]{1,0:T(8,128)(2,1)S(1)}, bf16[8,5376]{1,0:T(8,128)(2,1)S(1)}, u32[]{:S(2)}, u32[]{:S(2)}) collective-permute-start(bf16[8,5376]{1,0:T(8,128)(2,1)S(1)} %get-tuple-element.22), channel_id=1, source_target_pairs={{0,2},{1,3},{2,0},{3,1},{4,6},{5,7},{6,4},{7,5},{8,10},{9,11},{10,... | collective-permute-start | bytes 258056 | tf_op jit(solution)/shard_map/ppermute | solution.py:230
  7.7 5.9 %collective-permute-start.1 = (bf16[4,5376]{1,0:T(4,128)(2,1)S(1)}, bf16[4,5376]{1,0:T(4,128)(2,1)S(1)}, u32[]{:S(2)}, u32[]{:S(2)}) collective-permute-start(bf16[4,5376]{1,0:T(4,128)(2,1)S(1)} %get-tuple-element.20.own_ref), channel_id=1, source_target_pairs={{0,8},{1,9},{2,10},{3,11},{4,12},{5,13},{6,14},{7,15},{8,0},{9,1},... | collective-permute-start | bytes 129032 | tf_op jit(solution)/shard_map/ppermute | solution.py:230
  10.9 7.2 %collective-permute-start.5 = (bf16[8,5376]{1,0:T(8,128)(2,1)S(1)}, bf16[8,5376]{1,0:T(8,128)(2,1)S(1)}, u32[]{:S(2)}, u32[]{:S(2)}) collective-permute-start(bf16[8,5376]{1,0:T(8,128)(2,1)S(1)} %add.23.refs_0_.own_ref), channel_id=1, source_target_pairs={{0,8},{1,9},{2,10},{3,11},{4,12},{5,13},{6,14},{7,15},{8,0},{9,1},... | collective-permute-start | bytes 258056 | tf_op jit(solution)/shard_map/ppermute | solution.py:230
  13.7 5.2 %collective-permute-start.3 = (bf16[8,5376]{1,0:T(8,128)(2,1)S(1)}, bf16[8,5376]{1,0:T(8,128)(2,1)S(1)}, u32[]{:S(2)}, u32[]{:S(2)}) collective-permute-start(bf16[8,5376]{1,0:T(8,128)(2,1)S(1)} %join.1), channel_id=1, source_target_pairs={{0,4},{1,5},{2,6},{3,7},{4,0},{5,1},{6,2},{7,3},{8,12},{9,13},{10,... | collective-permute-start | bytes 258056 | tf_op jit(solution)/shard_map/ppermute | solution.py:230
  16.7 4.0 %collective-permute-start.8 = (bf16[16,5376]{1,0:T(8,128)(2,1)S(1)}, bf16[16,5376]{1,0:T(8,128)(2,1)S(1)}, u32[]{:S(2)}, u32[]{:S(2)}) collective-permute-start(bf16[16,5376]{1,0:T(8,128)(2,1)S(1)} %get-tuple-element.23.refs_0_), channel_id=1, source_target_pairs={{0,1},{1,0},{2,3},{3,2},{4,5},{5,4},{6,7},{7,6},{8,9},{9,8},{10,11... | collective-permute-start | bytes 516104 | tf_op jit(solution)/shard_map/ppermute | solution.py:230
  18.2 4.6 %collective-permute-start.6 = (bf16[8,5376]{1,0:T(8,128)(2,1)S(1)}, bf16[8,5376]{1,0:T(8,128)(2,1)S(1)}, u32[]{:S(2)}, u32[]{:S(2)}) collective-permute-start(bf16[8,5376]{1,0:T(8,128)(2,1)S(1)} %plus.1.own_ref), channel_id=1, source_target_pairs={{0,4},{1,5},{2,6},{3,7},{4,0},{5,1},{6,2},{7,3},{8,12},{9,13},{10,... | collective-permute-start | bytes 258056 | tf_op jit(solution)/shard_map/ppermute | solution.py:230
  19.2 8.8 %collective-permute-start.4 = (bf16[8,5376]{1,0:T(8,128)(2,1)S(1)}, bf16[8,5376]{1,0:T(8,128)(2,1)S(1)}, u32[]{:S(2)}, u32[]{:S(2)}) collective-permute-start(bf16[8,5376]{1,0:T(8,128)(2,1)S(1)} %norm.2.one_ref), channel_id=1, source_target_pairs={{0,2},{1,3},{2,0},{3,1},{4,6},{5,7},{6,4},{7,5},{8,10},{9,11},{10,... | collective-permute-start | bytes 258056 | tf_op jit(solution)/shard_map/ppermute | solution.py:230
  20.7 7.3 %collective-permute-start.9 = (bf16[8,5376]{1,0:T(8,128)(2,1)S(1)}, bf16[8,5376]{1,0:T(8,128)(2,1)S(1)}, u32[]{:S(2)}, u32[]{:S(2)}) collective-permute-start(bf16[8,5376]{1,0:T(8,128)(2,1)S(1)} %slice.81), channel_id=1, source_target_pairs={{0,2},{1,3},{2,0},{3,1},{4,6},{5,7},{6,4},{7,5},{8,10},{9,11},{10,... | collective-permute-start | bytes 258056 | tf_op jit(solution)/shard_map/ppermute | solution.py:230
  23.0 7.3 %collective-permute-start.7 = (bf16[8,5376]{1,0:T(8,128)(2,1)S(1)}, bf16[8,5376]{1,0:T(8,128)(2,1)S(1)}, u32[]{:S(2)}, u32[]{:S(2)}) collective-permute-start(bf16[8,5376]{1,0:T(8,128)(2,1)S(1)} %norm.3.refs_0_.two_ref), channel_id=1, source_target_pairs={{0,2},{1,3},{2,0},{3,1},{4,6},{5,7},{6,4},{7,5},{8,10},{9,11},{10,... | collective-permute-start | bytes 258056 | tf_op jit(solution)/shard_map/ppermute | solution.py:230
  30.4 1.7 %collective-permute-start.10 = (bf16[32,5376]{1,0:T(8,128)(2,1)S(1)}, bf16[32,5376]{1,0:T(8,128)(2,1)S(1)}, u32[]{:S(2)}, u32[]{:S(2)}) collective-permute-start(bf16[32,5376]{1,0:T(8,128)(2,1)S(1)} %chips.1.own_ref), channel_id=1, source_target_pairs={{0,1},{1,0},{2,3},{3,2},{4,5},{5,4},{6,7},{7,6},{8,9},{9,8},{10,11... | collective-permute-start | bytes 1032200 | tf_op jit(solution)/shard_map/ppermute | solution.py:230
  30.5 6.9 %collective-permute-start.13 = (bf16[4,5376]{1,0:T(4,128)(2,1)S(1)}, bf16[4,5376]{1,0:T(4,128)(2,1)S(1)}, u32[]{:S(2)}, u32[]{:S(2)}) collective-permute-start(bf16[4,5376]{1,0:T(4,128)(2,1)S(1)} %slice.83), channel_id=1, source_target_pairs={{0,4},{1,5},{2,6},{3,7},{4,0},{5,1},{6,2},{7,3},{8,12},{9,13},{10,... | collective-permute-start | bytes 129032 | tf_op jit(solution)/shard_map/ppermute | solution.py:230
  35.2 4.5 %collective-permute-start.11 = (f32[2,64]{1,0:T(2,128)S(1)}, f32[2,64]{1,0:T(2,128)S(1)}, u32[]{:S(2)}, u32[]{:S(2)}) collective-permute-start(f32[2,64]{1,0:T(2,128)S(1)} %get-tuple-element.31), channel_id=1, source_target_pairs={{0,8},{1,9},{2,10},{3,11},{4,12},{5,13},{6,14},{7,15},{8,0},{9,1},... | collective-permute-start | bytes 1544 | tf_op jit(solution)/shard_map/ppermute | solution.py:230
  37.4 4.9 %collective-permute-start.14 = (bf16[2,5376]{1,0:T(2,128)(2,1)S(1)}, bf16[2,5376]{1,0:T(2,128)(2,1)S(1)}, u32[]{:S(2)}, u32[]{:S(2)}) collective-permute-start(bf16[2,5376]{1,0:T(2,128)(2,1)S(1)} %slice.85), channel_id=1, source_target_pairs={{0,8},{1,9},{2,10},{3,11},{4,12},{5,13},{6,14},{7,15},{8,0},{9,1},... | collective-permute-start | bytes 64520 | tf_op jit(solution)/shard_map/ppermute | solution.py:230
  39.8 3.6 %collective-permute-start.12 = (f32[2,64]{1,0:T(2,128)S(1)}, f32[2,64]{1,0:T(2,128)S(1)}, u32[]{:S(2)}, u32[]{:S(2)}) collective-permute-start(f32[2,64]{1,0:T(2,128)S(1)} %pad_maximum_fusion.2.own_ref), channel_id=1, source_target_pairs={{0,4},{1,5},{2,6},{3,7},{4,0},{5,1},{6,2},{7,3},{8,12},{9,13},{10,... | collective-permute-start | bytes 1544 | tf_op jit(solution)/shard_map/ppermute | solution.py:230
  43.4 3.6 %collective-permute-start.15 = (f32[2,64]{1,0:T(2,128)S(1)}, f32[2,64]{1,0:T(2,128)S(1)}, u32[]{:S(2)}, u32[]{:S(2)}) collective-permute-start(f32[2,64]{1,0:T(2,128)S(1)} %merge.1), channel_id=1, source_target_pairs={{0,2},{1,3},{2,0},{3,1},{4,6},{5,7},{6,4},{7,5},{8,10},{9,11},{10,... | collective-permute-start | bytes 1544 | tf_op jit(solution)/shard_map/ppermute | solution.py:230
  47.1 1.2 %collective-permute-start.16 = (f32[2,64]{1,0:T(2,128)S(1)}, f32[2,64]{1,0:T(2,128)S(1)}, u32[]{:S(2)}, u32[]{:S(2)}) collective-permute-start(f32[2,64]{1,0:T(2,128)S(1)} %pad_maximum_fusion.3.own_ref), channel_id=1, source_target_pairs={{0,1},{1,0},{2,3},{3,2},{4,5},{5,4},{6,7},{7,6},{8,9},{9,8},{10,11... | collective-permute-start | bytes 1544 | tf_op jit(solution)/shard_map/ppermute | solution.py:230

commit v14 on v13

--- a/solution.py
+++ b/solution.py
@@ -182,7 +182,8 @@
     out_ref[...] = jnp.concatenate(parts, axis=0).astype(out_ref.dtype)
 
 
-def chips_kernel(one_ref, one_got_ref, two_ref, two_got_ref, after_ref, out_ref):
+def chips_kernel(one_ref, one_got_ref, two_ref, two_got_ref, *refs):
+    out_ref = refs[-1]
     own = [ref[...].astype(jnp.float32) for ref in (one_ref, two_ref)]
     got = [ref[...].astype(jnp.float32) for ref in (one_got_ref, two_got_ref)]
     own, got = jnp.concatenate(own, axis=0), jnp.concatenate(got, axis=0)
@@ -192,17 +193,17 @@
     out_ref[rows:, :] = jnp.where(upper, own, got).astype(out_ref.dtype)
 
 
-def chips(one, one_got, two, two_got, after):
+def chips(one, one_got, two, two_got, *after):
     rows, width = one.shape
     vmem = pl.BlockSpec(memory_space=pltpu.VMEM)
     return pl.pallas_call(
         chips_kernel,
         out_shape=jax.ShapeDtypeStruct((4 * rows, width), one.dtype),
-        in_specs=[vmem] * 4 + [pl.BlockSpec(memory_space=pl.ANY)],
+        in_specs=[vmem] * 4 + [pl.BlockSpec(memory_space=pl.ANY)] * len(after),
         out_specs=vmem,
         compiler_params=pltpu.CompilerParams(vmem_limit_bytes=12 * MIB),
         name="chips",
-    )(one, one_got, two, two_got, after)
+    )(one, one_got, two, two_got, *after)
 
 
 def merge_kernel(own_ref, got_ref, *refs):
@@ -419,10 +420,8 @@
     one = normed(first_kernel, state, gain)
     one_got = swapped(one, 2)
     two = normed(second_kernel, delta, gain, own, got)
-    middle = voc_dev // 8 * 5
-    head_table, token = loaded(table, voc_dev // 8, middle, head_table, two)
-    head_table, token = loaded(table, middle, voc_dev, head_table, following, one_got)
-    states = chips(one, one_got, two, swapped(two, 2), token)
+    head_table, token = loaded(table, voc_dev // 8, voc_dev, head_table, two)
+    states = chips(one, one_got, two, swapped(two, 2), token, following)
     others = swapped(states, 1)
     scaled, stats = head(states, others, head_table, temps)
     scaled = turned(scaled, places, steps)

time: 49.4 us -> 47.6 us (0.964)
  waiting for transfers between devices: 12.7 us -> 10.5 us
  starting transfers between devices: 19.4 us -> 19.9 us
    ppermute x17, waiting for transfers between devices: 12.7 us -> 10.5 us  [swapped(): return lax.ppermute(rows, 'vocab', pairs)]
    pallas_call x3 -> x2, Pallas kernels: 6.72 us -> 5.18 us  [loaded(): pl.pallas_call(functools.partial(load_kernel, first, last), out_shape=(ja...]
    pallas_call x2, Pallas kernels: 3.52 us -> 4.8 us  [picked_rows(): pl.pallas_call(functools.partial(pick_kernel, step, places), out_shape=ou...]
    ppermute x17, starting transfers between devices: 19.4 us -> 19.9 us  [swapped(): return lax.ppermute(rows, 'vocab', pairs)]
  transfers between devices with their start and end apart: 17 -> 17, of which waited for: 10 -> 9; matrix products, arithmetic and copies ran while one was open for 2% -> 2% of each run, Pallas kernels for 24% -> 24%
where the time goes in v14:
time: 47.6 us; the launch traced here: 47.3 us
  starting transfers between devices  19.9 us (42%)
  Pallas kernels  14.9 us (31%)
  waiting for transfers between devices  10.5 us (22%)
  other arithmetic  0.89 us (2%)
  between operations  0.89 us (2%)
    ppermute x17, starting transfers between devices, swapped(): return lax.ppermute(rows, 'vocab', pairs)  19.9 us
    ppermute x17, waiting for transfers between devices, swapped(): return lax.ppermute(rows, 'vocab', pairs)  10.5 us
    pallas_call x2, Pallas kernels, loaded(): pl.pallas_call(functools.partial(load_kernel, first, last), out_shape=(ja...  5.18 us
    pallas_call x2, Pallas kernels, picked_rows(): pl.pallas_call(functools.partial(pick_kernel, step, places), out_shape=ou...  4.8 us
    pallas_call x1, Pallas kernels, head(): pl.pallas_call(head_kernel, out_shape=(jax.ShapeDtypeStruct((voc_dev, row...  3.15 us
  transfers between devices with their start and end apart: 17, of which 9 were waited for; matrix products, arithmetic and copies ran while one was open for 2% of the time, Pallas kernels for 24%

profile of v14, /device:TPU:0, one launch (start us, length us, event | category | flops | bytes accessed | tf_op | source)
XLA Modules:
  0.0 47.3 jit_solution(1019448935410381257)
XLA Ops:
  0.7 2.6 %pick.2 = (bf16[16,5376]{1,0:T(8,128)(2,1)S(1)}, bf16[16,5376]{1,0:T(8,128)(2,1)S(1)}, f32[1,64]{1,0:T(1,128)S(1)}) custom-call(s32[2,32]{1,0:T(2,128)} %ids_ref.3, bf16[1024,5376]{1,0:T(8,128)(2,1)} %table_ref.7, s32[2,32]{1,0:T(2,128)} %refs_0_.1, f32[8]{0:T(128)} %refs_1_.1), custom_call_target="tpu_custom_call" | custom-call | tf_op jit(solution)/shard_map/pick/pallas_call | solution.py:124
  3.2 0.4 collective-permute-start
  3.7 1.3 %load.2 = (bf16[1024,5376]{1,0:T(8,128)(2,1)S(1)}, f32[8,128]{1,0:T(8,128)S(1)}) custom-call(bf16[1024,5376]{1,0:T(8,128)(2,1)} %table_ref.7, bf16[16,5376]{1,0:T(8,128)(2,1)S(1)} %get-tuple-element.17.refs_0_), custom_call_target="tpu_custom_call" | custom-call | tf_op jit(solution)/shard_map/load/pallas_call | solution.py:253
  5.0 0.0 collective-permute-done.got_ref
  5.0 0.0 copy-done
  5.0 0.0 copy-done.1
  5.0 0.1 fold.1
  5.1 2.5 %collective-permute-start.2 = (bf16[8,5376]{1,0:T(8,128)(2,1)S(1)}, bf16[8,5376]{1,0:T(8,128)(2,1)S(1)}, u32[]{:S(2)}, u32[]{:S(2)}) collective-permute-start(bf16[8,5376]{1,0:T(8,128)(2,1)S(1)} %get-tuple-element.21), channel_id=1, source_target_pairs={{0,2},{1,3},{2,0},{3,1},{4,6},{5,7},{6,4},{7,5},{8,10},{9,11},{10,... | collective-permute-start | bytes 258056 | tf_op jit(solution)/shard_map/ppermute | solution.py:231
  7.6 2.5 %collective-permute-start.1 = (bf16[4,5376]{1,0:T(4,128)(2,1)S(1)}, bf16[4,5376]{1,0:T(4,128)(2,1)S(1)}, u32[]{:S(2)}, u32[]{:S(2)}) collective-permute-start(bf16[4,5376]{1,0:T(4,128)(2,1)S(1)} %get-tuple-element.19.own_ref), channel_id=1, source_target_pairs={{0,8},{1,9},{2,10},{3,11},{4,12},{5,13},{6,14},{7,15},{8,0},{9,1},... | collective-permute-start | bytes 129032 | tf_op jit(solution)/shard_map/ppermute | solution.py:231
  10.2 0.6 %collective-permute-done.2 = bf16[8,5376]{1,0:T(8,128)(2,1)S(1)} collective-permute-done((bf16[8,5376]{1,0:T(8,128)(2,1)S(1)}, bf16[8,5376]{1,0:T(8,128)(2,1)S(1)}, u32[]{:S(2)}, u32[]{:S(2)}) %collective-permute-start.2) | collective-permute-done | bytes 86048 | tf_op jit(solution)/shard_map/ppermute | solution.py:231
  10.8 3.1 %collective-permute-start.5 = (bf16[8,5376]{1,0:T(8,128)(2,1)S(1)}, bf16[8,5376]{1,0:T(8,128)(2,1)S(1)}, u32[]{:S(2)}, u32[]{:S(2)}) collective-permute-start(bf16[8,5376]{1,0:T(8,128)(2,1)S(1)} %add.23.refs_0_.own_ref), channel_id=1, source_target_pairs={{0,8},{1,9},{2,10},{3,11},{4,12},{5,13},{6,14},{7,15},{8,0},{9,1},... | collective-permute-start | bytes 258056 | tf_op jit(solution)/shard_map/ppermute | solution.py:231
  13.9 0.0 collective-permute-done.1.got_ref
  13.9 1.2 %collective-permute-start.3 = (bf16[8,5376]{1,0:T(8,128)(2,1)S(1)}, bf16[8,5376]{1,0:T(8,128)(2,1)S(1)}, u32[]{:S(2)}, u32[]{:S(2)}) collective-permute-start(bf16[8,5376]{1,0:T(8,128)(2,1)S(1)} %join.1), channel_id=1, source_target_pairs={{0,4},{1,5},{2,6},{3,7},{4,0},{5,1},{6,2},{7,3},{8,12},{9,13},{10,... | collective-permute-start | bytes 258056 | tf_op jit(solution)/shard_map/ppermute | solution.py:231
  15.1 2.2 %pick.3 = (bf16[16,5376]{1,0:T(8,128)(2,1)S(1)}, bf16[16,5376]{1,0:T(8,128)(2,1)S(1)}) custom-call(s32[2,32]{1,0:T(2,128)} %ids_ref.3, bf16[1024,5376]{1,0:T(8,128)(2,1)} %table_ref.7, bf16[8,5376]{1,0:T(8,128)(2,1)S(1)} %add.23.refs_0_.own_ref), custom_call_target="tpu_custom_call" | custom-call | tf_op jit(solution)/shard_map/pick/pallas_call | solution.py:124
  17.4 0.1 collective-permute-start.8
  17.4 0.6 %collective-permute-done.5.got_ref = bf16[8,5376]{1,0:T(8,128)(2,1)S(1)} collective-permute-done((bf16[8,5376]{1,0:T(8,128)(2,1)S(1)}, bf16[8,5376]{1,0:T(8,128)(2,1)S(1)}, u32[]{:S(2)}, u32[]{:S(2)}) %collective-permute-start.5) | collective-permute-done | bytes 86048 | tf_op jit(solution)/shard_map/ppermute | solution.py:231
  18.1 0.9 %collective-permute-start.6 = (bf16[8,5376]{1,0:T(8,128)(2,1)S(1)}, bf16[8,5376]{1,0:T(8,128)(2,1)S(1)}, u32[]{:S(2)}, u32[]{:S(2)}) collective-permute-start(bf16[8,5376]{1,0:T(8,128)(2,1)S(1)} %plus.1.own_ref), channel_id=1, source_target_pairs={{0,4},{1,5},{2,6},{3,7},{4,0},{5,1},{6,2},{7,3},{8,12},{9,13},{10,... | collective-permute-start | bytes 258056 | tf_op jit(solution)/shard_map/ppermute | solution.py:231
  19.0 0.0 collective-permute-done.3
  19.1 0.2 norm.2.one_ref
  19.3 1.3 %collective-permute-start.4 = (bf16[8,5376]{1,0:T(8,128)(2,1)S(1)}, bf16[8,5376]{1,0:T(8,128)(2,1)S(1)}, u32[]{:S(2)}, u32[]{:S(2)}) collective-permute-start(bf16[8,5376]{1,0:T(8,128)(2,1)S(1)} %norm.2.one_ref), channel_id=1, source_target_pairs={{0,2},{1,3},{2,0},{3,1},{4,6},{5,7},{6,4},{7,5},{8,10},{9,11},{10,... | collective-permute-start | bytes 258056 | tf_op jit(solution)/shard_map/ppermute | solution.py:231
  20.5 0.0 collective-permute-done.8
  20.6 0.9 %collective-permute-start.9 = (bf16[8,5376]{1,0:T(8,128)(2,1)S(1)}, bf16[8,5376]{1,0:T(8,128)(2,1)S(1)}, u32[]{:S(2)}, u32[]{:S(2)}) collective-permute-start(bf16[8,5376]{1,0:T(8,128)(2,1)S(1)} %slice.81), channel_id=1, source_target_pairs={{0,2},{1,3},{2,0},{3,1},{4,6},{5,7},{6,4},{7,5},{8,10},{9,11},{10,... | collective-permute-start | bytes 258056 | tf_op jit(solution)/shard_map/ppermute | solution.py:231
  21.5 1.1 %collective-permute-done.6.got_ref = bf16[8,5376]{1,0:T(8,128)(2,1)S(1)} collective-permute-done((bf16[8,5376]{1,0:T(8,128)(2,1)S(1)}, bf16[8,5376]{1,0:T(8,128)(2,1)S(1)}, u32[]{:S(2)}, u32[]{:S(2)}) %collective-permute-start.6) | collective-permute-done | bytes 86048 | tf_op jit(solution)/shard_map/ppermute | solution.py:231
  22.6 0.2 norm.3.refs_0_.two_ref
  22.9 1.6 %collective-permute-start.7 = (bf16[8,5376]{1,0:T(8,128)(2,1)S(1)}, bf16[8,5376]{1,0:T(8,128)(2,1)S(1)}, u32[]{:S(2)}, u32[]{:S(2)}) collective-permute-start(bf16[8,5376]{1,0:T(8,128)(2,1)S(1)} %norm.3.refs_0_.two_ref), channel_id=1, source_target_pairs={{0,2},{1,3},{2,0},{3,1},{4,6},{5,7},{6,4},{7,5},{8,10},{9,11},{10,... | collective-permute-start | bytes 258056 | tf_op jit(solution)/shard_map/ppermute | solution.py:231
  24.4 3.9 %load.3 = (bf16[1024,5376]{1,0:T(8,128)(2,1)S(1)}, f32[8,128]{1,0:T(8,128)S(1)}) custom-call(bf16[1024,5376]{1,0:T(8,128)(2,1)} %table_ref.7, bf16[8,5376]{1,0:T(8,128)(2,1)S(1)} %norm.3.refs_0_.two_ref, bf16[1024,5376]{1,0:T(8,128)(2,1)S(1)} %get-tuple-element.23.refs_1_), custom_call_target="tpu_custom_call", output_to_operand_aliasing={{0}: (2, {})} | custom-call | tf_op jit(solution)/shard_map/load/pallas_call | solution.py:253
  28.3 0.0 collective-permute-done.9
  28.3 0.0 collective-permute-done.4.one_got_ref
  28.3 0.0 collective-permute-done.7.two_got_ref
  28.3 0.1 chips.1.own_ref
  28.4 0.1 collective-permute-start.10
  28.6 0.6 %collective-permute-start.13 = (bf16[4,5376]{1,0:T(4,128)(2,1)S(1)}, bf16[4,5376]{1,0:T(4,128)(2,1)S(1)}, u32[]{:S(2)}, u32[]{:S(2)}) collective-permute-start(bf16[4,5376]{1,0:T(4,128)(2,1)S(1)} %slice.83), channel_id=1, source_target_pairs={{0,4},{1,5},{2,6},{3,7},{4,0},{5,1},{6,2},{7,3},{8,12},{9,13},{10,... | collective-permute-start | bytes 129032 | tf_op jit(solution)/shard_map/ppermute | solution.py:231
  29.2 1.0 %collective-permute-done.10.got_ref = bf16[32,5376]{1,0:T(8,128)(2,1)S(1)} collective-permute-done((bf16[32,5376]{1,0:T(8,128)(2,1)S(1)}, bf16[32,5376]{1,0:T(8,128)(2,1)S(1)}, u32[]{:S(2)}, u32[]{:S(2)}) %collective-permute-start.10) | collective-permute-done | bytes 344096 | tf_op jit(solution)/shard_map/ppermute | solution.py:231
  30.2 3.1 %head.1 = (f32[1024,64]{1,0:T(8,128)S(1)}, f32[2,64]{1,0:T(2,128)S(1)}) custom-call(bf16[32,5376]{1,0:T(8,128)(2,1)S(1)} %chips.1.own_ref, bf16[32,5376]{1,0:T(8,128)(2,1)S(1)} %collective-permute-done.10.got_ref, bf16[1024,5376]{1,0:T(8,128)(2,1)S(1)} %get-tuple-element.26.table_ref, f32[1,64]{1,0:T(1,128)S(1)} %get-tuple-element.27.temps_ref), custom_call_target="tpu_custom_call" | custom-call | tf_op jit(solution)/shard_map/head/pallas_call | solution.py:328
  33.3 2.5 %collective-permute-start.11 = (f32[2,64]{1,0:T(2,128)S(1)}, f32[2,64]{1,0:T(2,128)S(1)}, u32[]{:S(2)}, u32[]{:S(2)}) collective-permute-start(f32[2,64]{1,0:T(2,128)S(1)} %get-tuple-element.29), channel_id=1, source_target_pairs={{0,8},{1,9},{2,10},{3,11},{4,12},{5,13},{6,14},{7,15},{8,0},{9,1},... | collective-permute-start | bytes 1544 | tf_op jit(solution)/shard_map/ppermute | solution.py:231
  35.9 0.0 collective-permute-done.13
  35.9 0.5 %collective-permute-start.14 = (bf16[2,5376]{1,0:T(2,128)(2,1)S(1)}, bf16[2,5376]{1,0:T(2,128)(2,1)S(1)}, u32[]{:S(2)}, u32[]{:S(2)}) collective-permute-start(bf16[2,5376]{1,0:T(2,128)(2,1)S(1)} %slice.85), channel_id=1, source_target_pairs={{0,8},{1,9},{2,10},{3,11},{4,12},{5,13},{6,14},{7,15},{8,0},{9,1},... | collective-permute-start | bytes 64520 | tf_op jit(solution)/shard_map/ppermute | solution.py:231
  36.4 1.4 %collective-permute-done.11 = f32[2,64]{1,0:T(2,128)S(1)} collective-permute-done((f32[2,64]{1,0:T(2,128)S(1)}, f32[2,64]{1,0:T(2,128)S(1)}, u32[]{:S(2)}, u32[]{:S(2)}) %collective-permute-start.11) | collective-permute-done | bytes 544 | tf_op jit(solution)/shard_map/ppermute | solution.py:231
  37.9 1.2 %collective-permute-start.12 = (f32[2,64]{1,0:T(2,128)S(1)}, f32[2,64]{1,0:T(2,128)S(1)}, u32[]{:S(2)}, u32[]{:S(2)}) collective-permute-start(f32[2,64]{1,0:T(2,128)S(1)} %pad_maximum_fusion.2.own_ref), channel_id=1, source_target_pairs={{0,4},{1,5},{2,6},{3,7},{4,0},{5,1},{6,2},{7,3},{8,12},{9,13},{10,... | collective-permute-start | bytes 1544 | tf_op jit(solution)/shard_map/ppermute | solution.py:231
  39.0 1.7 %collective-permute-done.14 = bf16[2,5376]{1,0:T(2,128)(2,1)S(1)} collective-permute-done((bf16[2,5376]{1,0:T(2,128)(2,1)S(1)}, bf16[2,5376]{1,0:T(2,128)(2,1)S(1)}, u32[]{:S(2)}, u32[]{:S(2)}) %collective-permute-start.14) | collective-permute-done | bytes 21536 | tf_op jit(solution)/shard_map/ppermute | solution.py:231
  40.8 0.6 %multiply_convert_fusion = (bf16[2,5376]{1,0:T(2,128)(2,1)}, bf16[2,5376]{1,0:T(2,128)(2,1)S(1)}) fusion(bf16[2,5376]{1,0:T(2,128)(2,1)S(1)} %collective-permute-done.14, bf16[4,5376]{1,0:T(4,128)(2,1)S(1)} %slice_add_fusion.1), kind=kLoop, calls=%fused_computation.4 | loop fusion | flops 43008 | bytes 86016 | tf_op jit(solution)/shard_map/convert_element_type | solution.py:431
  41.4 0.1 collective-permute-done.12.got_ref
  41.5 0.6 %collective-permute-start.15 = (f32[2,64]{1,0:T(2,128)S(1)}, f32[2,64]{1,0:T(2,128)S(1)}, u32[]{:S(2)}, u32[]{:S(2)}) collective-permute-start(f32[2,64]{1,0:T(2,128)S(1)} %merge.1), channel_id=1, source_target_pairs={{0,2},{1,3},{2,0},{3,1},{4,6},{5,7},{6,4},{7,5},{8,10},{9,11},{10,... | collective-permute-start | bytes 1544 | tf_op jit(solution)/shard_map/ppermute | solution.py:231
  42.1 3.0 %collective-permute-done.15 = f32[2,64]{1,0:T(2,128)S(1)} collective-permute-done((f32[2,64]{1,0:T(2,128)S(1)}, f32[2,64]{1,0:T(2,128)S(1)}, u32[]{:S(2)}, u32[]{:S(2)}) %collective-permute-start.15) | collective-permute-done | bytes 544 | tf_op jit(solution)/shard_map/ppermute | solution.py:231
  45.2 0.1 collective-permute-start.16
  45.3 0.2 turn.1.scaled_ref
  45.5 0.9 %collective-permute-done.16.got_ref = f32[2,64]{1,0:T(2,128)S(1)} collective-permute-done((f32[2,64]{1,0:T(2,128)S(1)}, f32[2,64]{1,0:T(2,128)S(1)}, u32[]{:S(2)}, u32[]{:S(2)}) %collective-permute-start.16) | collective-permute-done | bytes 544 | tf_op jit(solution)/shard_map/ppermute | solution.py:231
  46.4 0.9 %finish.1 = f32[2,32,1024]{2,1,0:T(8,128)} custom-call(f32[2,32,1024]{2,1,0:T(8,128)S(1)} %turn.1.scaled_ref, f32[2,64]{1,0:T(2,128)S(1)} %pad_maximum_fusion.3.own_ref, f32[2,64]{1,0:T(2,128)S(1)} %collective-permute-done.16.got_ref), custom_call_target="tpu_custom_call" | custom-call | tf_op jit(solution)/shard_map/finish/pallas_call | solution.py:374
  (23 shorter events, 0.5 us)
Async XLA Ops:
  0.6 4.4 %copy-start = (bf16[2,5376]{1,0:T(2,128)(2,1)S(1)}, bf16[2,5376]{1,0:T(2,128)(2,1)}, u32[]{:S(2)}) copy-start(bf16[2,5376]{1,0:T(2,128)(2,1)} %first_ref.1) | copy-start | bytes 64516
  0.6 4.4 %copy-start.1 = (bf16[2,5376]{1,0:T(2,128)(2,1)S(1)}, bf16[2,5376]{1,0:T(2,128)(2,1)}, u32[]{:S(2)}) copy-start(bf16[2,5376]{1,0:T(2,128)(2,1)} %delta_ref.1) | copy-start | bytes 64516
  0.7 9.5 %copy-start.2 = (f32[5376]{0:T(1024)S(1)}, f32[5376]{0:T(1024)}, u32[]{:S(2)}) copy-start(f32[5376]{0:T(1024)} %param.9) | copy-start | bytes 64516
  3.2 1.8 %collective-permute-start = (bf16[16,5376]{1,0:T(8,128)(2,1)S(1)}, bf16[16,5376]{1,0:T(8,128)(2,1)S(1)}, u32[]{:S(2)}, u32[]{:S(2)}) collective-permute-start(bf16[16,5376]{1,0:T(8,128)(2,1)S(1)} %get-tuple-element.17.refs_0_), channel_id=1, source_target_pairs={{0,1},{1,0},{2,3},{3,2},{4,5},{5,4},{6,7},{7,6},{8,9},{9,8},{10,11... | collective-permute-start | bytes 516104 | tf_op jit(solution)/shard_map/ppermute | solution.py:231
  5.1 5.7 %collective-permute-start.2 = (bf16[8,5376]{1,0:T(8,128)(2,1)S(1)}, bf16[8,5376]{1,0:T(8,128)(2,1)S(1)}, u32[]{:S(2)}, u32[]{:S(2)}) collective-permute-start(bf16[8,5376]{1,0:T(8,128)(2,1)S(1)} %get-tuple-element.21), channel_id=1, source_target_pairs={{0,2},{1,3},{2,0},{3,1},{4,6},{5,7},{6,4},{7,5},{8,10},{9,11},{10,... | collective-permute-start | bytes 258056 | tf_op jit(solution)/shard_map/ppermute | solution.py:231
  7.6 6.2 %collective-permute-start.1 = (bf16[4,5376]{1,0:T(4,128)(2,1)S(1)}, bf16[4,5376]{1,0:T(4,128)(2,1)S(1)}, u32[]{:S(2)}, u32[]{:S(2)}) collective-permute-start(bf16[4,5376]{1,0:T(4,128)(2,1)S(1)} %get-tuple-element.19.own_ref), channel_id=1, source_target_pairs={{0,8},{1,9},{2,10},{3,11},{4,12},{5,13},{6,14},{7,15},{8,0},{9,1},... | collective-permute-start | bytes 129032 | tf_op jit(solution)/shard_map/ppermute | solution.py:231
  10.8 7.2 %collective-permute-start.5 = (bf16[8,5376]{1,0:T(8,128)(2,1)S(1)}, bf16[8,5376]{1,0:T(8,128)(2,1)S(1)}, u32[]{:S(2)}, u32[]{:S(2)}) collective-permute-start(bf16[8,5376]{1,0:T(8,128)(2,1)S(1)} %add.23.refs_0_.own_ref), channel_id=1, source_target_pairs={{0,8},{1,9},{2,10},{3,11},{4,12},{5,13},{6,14},{7,15},{8,0},{9,1},... | collective-permute-start | bytes 258056 | tf_op jit(solution)/shard_map/ppermute | solution.py:231
  13.9 5.0 %collective-permute-start.3 = (bf16[8,5376]{1,0:T(8,128)(2,1)S(1)}, bf16[8,5376]{1,0:T(8,128)(2,1)S(1)}, u32[]{:S(2)}, u32[]{:S(2)}) collective-permute-start(bf16[8,5376]{1,0:T(8,128)(2,1)S(1)} %join.1), channel_id=1, source_target_pairs={{0,4},{1,5},{2,6},{3,7},{4,0},{5,1},{6,2},{7,3},{8,12},{9,13},{10,... | collective-permute-start | bytes 258056 | tf_op jit(solution)/shard_map/ppermute | solution.py:231
  17.4 3.1 %collective-permute-start.8 = (bf16[16,5376]{1,0:T(8,128)(2,1)S(1)}, bf16[16,5376]{1,0:T(8,128)(2,1)S(1)}, u32[]{:S(2)}, u32[]{:S(2)}) collective-permute-start(bf16[16,5376]{1,0:T(8,128)(2,1)S(1)} %get-tuple-element.22.refs_0_), channel_id=1, source_target_pairs={{0,1},{1,0},{2,3},{3,2},{4,5},{5,4},{6,7},{7,6},{8,9},{9,8},{10,11... | collective-permute-start | bytes 516104 | tf_op jit(solution)/shard_map/ppermute | solution.py:231
  18.1 4.6 %collective-permute-start.6 = (bf16[8,5376]{1,0:T(8,128)(2,1)S(1)}, bf16[8,5376]{1,0:T(8,128)(2,1)S(1)}, u32[]{:S(2)}, u32[]{:S(2)}) collective-permute-start(bf16[8,5376]{1,0:T(8,128)(2,1)S(1)} %plus.1.own_ref), channel_id=1, source_target_pairs={{0,4},{1,5},{2,6},{3,7},{4,0},{5,1},{6,2},{7,3},{8,12},{9,13},{10,... | collective-permute-start | bytes 258056 | tf_op jit(solution)/shard_map/ppermute | solution.py:231
  19.3 9.1 %collective-permute-start.4 = (bf16[8,5376]{1,0:T(8,128)(2,1)S(1)}, bf16[8,5376]{1,0:T(8,128)(2,1)S(1)}, u32[]{:S(2)}, u32[]{:S(2)}) collective-permute-start(bf16[8,5376]{1,0:T(8,128)(2,1)S(1)} %norm.2.one_ref), channel_id=1, source_target_pairs={{0,2},{1,3},{2,0},{3,1},{4,6},{5,7},{6,4},{7,5},{8,10},{9,11},{10,... | collective-permute-start | bytes 258056 | tf_op jit(solution)/shard_map/ppermute | solution.py:231
  20.6 7.7 %collective-permute-start.9 = (bf16[8,5376]{1,0:T(8,128)(2,1)S(1)}, bf16[8,5376]{1,0:T(8,128)(2,1)S(1)}, u32[]{:S(2)}, u32[]{:S(2)}) collective-permute-start(bf16[8,5376]{1,0:T(8,128)(2,1)S(1)} %slice.81), channel_id=1, source_target_pairs={{0,2},{1,3},{2,0},{3,1},{4,6},{5,7},{6,4},{7,5},{8,10},{9,11},{10,... | collective-permute-start | bytes 258056 | tf_op jit(solution)/shard_map/ppermute | solution.py:231
  22.9 5.5 %collective-permute-start.7 = (bf16[8,5376]{1,0:T(8,128)(2,1)S(1)}, bf16[8,5376]{1,0:T(8,128)(2,1)S(1)}, u32[]{:S(2)}, u32[]{:S(2)}) collective-permute-start(bf16[8,5376]{1,0:T(8,128)(2,1)S(1)} %norm.3.refs_0_.two_ref), channel_id=1, source_target_pairs={{0,2},{1,3},{2,0},{3,1},{4,6},{5,7},{6,4},{7,5},{8,10},{9,11},{10,... | collective-permute-start | bytes 258056 | tf_op jit(solution)/shard_map/ppermute | solution.py:231
  28.4 1.7 %collective-permute-start.10 = (bf16[32,5376]{1,0:T(8,128)(2,1)S(1)}, bf16[32,5376]{1,0:T(8,128)(2,1)S(1)}, u32[]{:S(2)}, u32[]{:S(2)}) collective-permute-start(bf16[32,5376]{1,0:T(8,128)(2,1)S(1)} %chips.1.own_ref), channel_id=1, source_target_pairs={{0,1},{1,0},{2,3},{3,2},{4,5},{5,4},{6,7},{7,6},{8,9},{9,8},{10,11... | collective-permute-start | bytes 1032200 | tf_op jit(solution)/shard_map/ppermute | solution.py:231
  28.6 7.3 %collective-permute-start.13 = (bf16[4,5376]{1,0:T(4,128)(2,1)S(1)}, bf16[4,5376]{1,0:T(4,128)(2,1)S(1)}, u32[]{:S(2)}, u32[]{:S(2)}) collective-permute-start(bf16[4,5376]{1,0:T(4,128)(2,1)S(1)} %slice.83), channel_id=1, source_target_pairs={{0,4},{1,5},{2,6},{3,7},{4,0},{5,1},{6,2},{7,3},{8,12},{9,13},{10,... | collective-permute-start | bytes 129032 | tf_op jit(solution)/shard_map/ppermute | solution.py:231
  33.3 4.5 %collective-permute-start.11 = (f32[2,64]{1,0:T(2,128)S(1)}, f32[2,64]{1,0:T(2,128)S(1)}, u32[]{:S(2)}, u32[]{:S(2)}) collective-permute-start(f32[2,64]{1,0:T(2,128)S(1)} %get-tuple-element.29), channel_id=1, source_target_pairs={{0,8},{1,9},{2,10},{3,11},{4,12},{5,13},{6,14},{7,15},{8,0},{9,1},... | collective-permute-start | bytes 1544 | tf_op jit(solution)/shard_map/ppermute | solution.py:231
  35.9 4.8 %collective-permute-start.14 = (bf16[2,5376]{1,0:T(2,128)(2,1)S(1)}, bf16[2,5376]{1,0:T(2,128)(2,1)S(1)}, u32[]{:S(2)}, u32[]{:S(2)}) collective-permute-start(bf16[2,5376]{1,0:T(2,128)(2,1)S(1)} %slice.85), channel_id=1, source_target_pairs={{0,8},{1,9},{2,10},{3,11},{4,12},{5,13},{6,14},{7,15},{8,0},{9,1},... | collective-permute-start | bytes 64520 | tf_op jit(solution)/shard_map/ppermute | solution.py:231
  37.9 3.6 %collective-permute-start.12 = (f32[2,64]{1,0:T(2,128)S(1)}, f32[2,64]{1,0:T(2,128)S(1)}, u32[]{:S(2)}, u32[]{:S(2)}) collective-permute-start(f32[2,64]{1,0:T(2,128)S(1)} %pad_maximum_fusion.2.own_ref), channel_id=1, source_target_pairs={{0,4},{1,5},{2,6},{3,7},{4,0},{5,1},{6,2},{7,3},{8,12},{9,13},{10,... | collective-permute-start | bytes 1544 | tf_op jit(solution)/shard_map/ppermute | solution.py:231
  41.5 3.6 %collective-permute-start.15 = (f32[2,64]{1,0:T(2,128)S(1)}, f32[2,64]{1,0:T(2,128)S(1)}, u32[]{:S(2)}, u32[]{:S(2)}) collective-permute-start(f32[2,64]{1,0:T(2,128)S(1)} %merge.1), channel_id=1, source_target_pairs={{0,2},{1,3},{2,0},{3,1},{4,6},{5,7},{6,4},{7,5},{8,10},{9,11},{10,... | collective-permute-start | bytes 1544 | tf_op jit(solution)/shard_map/ppermute | solution.py:231
  45.2 1.2 %collective-permute-start.16 = (f32[2,64]{1,0:T(2,128)S(1)}, f32[2,64]{1,0:T(2,128)S(1)}, u32[]{:S(2)}, u32[]{:S(2)}) collective-permute-start(f32[2,64]{1,0:T(2,128)S(1)} %pad_maximum_fusion.3.own_ref), channel_id=1, source_target_pairs={{0,1},{1,0},{2,3},{3,2},{4,5},{5,4},{6,7},{7,6},{8,9},{9,8},{10,11... | collective-permute-start | bytes 1544 | tf_op jit(solution)/shard_map/ppermute | solution.py:231

commit v15 on v14

--- a/solution.py
+++ b/solution.py
@@ -259,7 +259,7 @@
         in_specs=[anywhere] * (1 + len(after)) + [vmem] * len(held),
         out_specs=(vmem, vmem),
         input_output_aliases={1 + len(after): 0} if held else {},
-        scratch_shapes=[pltpu.SemaphoreType.DMA((4,))],
+        scratch_shapes=[pltpu.SemaphoreType.DMA((8,))],
         compiler_params=pltpu.CompilerParams(vmem_limit_bytes=4 * MIB),
         name="load",
     )(in_hbm(table), *after, *held)

time: 47.6 us -> 48.2 us (1.013)
  waiting for transfers between devices: 10.5 us -> 11.2 us
    ppermute x17, waiting for transfers between devices: 10.5 us -> 11.2 us  [swapped(): return lax.ppermute(rows, 'vocab', pairs)]
  transfers between devices with their start and end apart: 17 -> 17, of which waited for: 9 -> 10; matrix products, arithmetic and copies ran while one was open for 2% -> 2% of each run, Pallas kernels for 24% -> 24%
where the time goes in v15:
time: 48.2 us; the launch traced here: 47.9 us
  starting transfers between devices  19.9 us (41%)
  Pallas kernels  14.9 us (31%)
  waiting for transfers between devices  11.2 us (23%)
  other arithmetic  0.89 us (2%)
  between operations  0.88 us (2%)
    ppermute x17, starting transfers between devices, swapped(): return lax.ppermute(rows, 'vocab', pairs)  19.9 us
    ppermute x17, waiting for transfers between devices, swapped(): return lax.ppermute(rows, 'vocab', pairs)  11.2 us
    pallas_call x2, Pallas kernels, loaded(): pl.pallas_call(functools.partial(load_kernel, first, last), out_shape=(ja...  5.32 us
    pallas_call x2, Pallas kernels, picked_rows(): pl.pallas_call(functools.partial(pick_kernel, step, places), out_shape=ou...  4.72 us
    pallas_call x1, Pallas kernels, head(): pl.pallas_call(head_kernel, out_shape=(jax.ShapeDtypeStruct((voc_dev, row...  3.15 us
  transfers between devices with their start and end apart: 17, of which 10 were waited for; matrix products, arithmetic and copies ran while one was open for 2% of the time, Pallas kernels for 24%

profile of v15, /device:TPU:0, one launch (start us, length us, event | category | flops | bytes accessed | tf_op | source)
XLA Modules:
  0.0 47.9 jit_solution(625995956398331132)
XLA Ops:
  0.6 0.0 copy-start
  0.6 0.0 copy-start.1
  0.7 2.3 %pick.2 = (bf16[16,5376]{1,0:T(8,128)(2,1)S(1)}, bf16[16,5376]{1,0:T(8,128)(2,1)S(1)}, f32[1,64]{1,0:T(1,128)S(1)}) custom-call(s32[2,32]{1,0:T(2,128)} %ids_ref.3, bf16[1024,5376]{1,0:T(8,128)(2,1)} %table_ref.7, s32[2,32]{1,0:T(2,128)} %refs_0_.1, f32[8]{0:T(128)} %refs_1_.1), custom_call_target="tpu_custom_call" | custom-call | tf_op jit(solution)/shard_map/pick/pallas_call | solution.py:124
  3.0 0.5 %collective-permute-start = (bf16[16,5376]{1,0:T(8,128)(2,1)S(1)}, bf16[16,5376]{1,0:T(8,128)(2,1)S(1)}, u32[]{:S(2)}, u32[]{:S(2)}) collective-permute-start(bf16[16,5376]{1,0:T(8,128)(2,1)S(1)} %get-tuple-element.17.refs_0_), channel_id=1, source_target_pairs={{0,1},{1,0},{2,3},{3,2},{4,5},{5,4},{6,7},{7,6},{8,9},{9,8},{10,11... | collective-permute-start | bytes 516104 | tf_op jit(solution)/shard_map/ppermute | solution.py:231
  3.5 1.5 %load.2 = (bf16[1024,5376]{1,0:T(8,128)(2,1)S(1)}, f32[8,128]{1,0:T(8,128)S(1)}) custom-call(bf16[1024,5376]{1,0:T(8,128)(2,1)} %table_ref.7, bf16[16,5376]{1,0:T(8,128)(2,1)S(1)} %get-tuple-element.17.refs_0_), custom_call_target="tpu_custom_call" | custom-call | tf_op jit(solution)/shard_map/load/pallas_call | solution.py:253
  5.0 0.0 collective-permute-done.got_ref
  5.0 0.1 fold.1
  5.1 2.7 %collective-permute-start.2 = (bf16[8,5376]{1,0:T(8,128)(2,1)S(1)}, bf16[8,5376]{1,0:T(8,128)(2,1)S(1)}, u32[]{:S(2)}, u32[]{:S(2)}) collective-permute-start(bf16[8,5376]{1,0:T(8,128)(2,1)S(1)} %get-tuple-element.21), channel_id=1, source_target_pairs={{0,2},{1,3},{2,0},{3,1},{4,6},{5,7},{6,4},{7,5},{8,10},{9,11},{10,... | collective-permute-start | bytes 258056 | tf_op jit(solution)/shard_map/ppermute | solution.py:231
  7.8 2.6 %collective-permute-start.1 = (bf16[4,5376]{1,0:T(4,128)(2,1)S(1)}, bf16[4,5376]{1,0:T(4,128)(2,1)S(1)}, u32[]{:S(2)}, u32[]{:S(2)}) collective-permute-start(bf16[4,5376]{1,0:T(4,128)(2,1)S(1)} %get-tuple-element.19.own_ref), channel_id=1, source_target_pairs={{0,8},{1,9},{2,10},{3,11},{4,12},{5,13},{6,14},{7,15},{8,0},{9,1},... | collective-permute-start | bytes 129032 | tf_op jit(solution)/shard_map/ppermute | solution.py:231
  10.4 0.6 %collective-permute-done.2 = bf16[8,5376]{1,0:T(8,128)(2,1)S(1)} collective-permute-done((bf16[8,5376]{1,0:T(8,128)(2,1)S(1)}, bf16[8,5376]{1,0:T(8,128)(2,1)S(1)}, u32[]{:S(2)}, u32[]{:S(2)}) %collective-permute-start.2) | collective-permute-done | bytes 86048 | tf_op jit(solution)/shard_map/ppermute | solution.py:231
  11.0 3.1 %collective-permute-start.5 = (bf16[8,5376]{1,0:T(8,128)(2,1)S(1)}, bf16[8,5376]{1,0:T(8,128)(2,1)S(1)}, u32[]{:S(2)}, u32[]{:S(2)}) collective-permute-start(bf16[8,5376]{1,0:T(8,128)(2,1)S(1)} %add.23.refs_0_.own_ref), channel_id=1, source_target_pairs={{0,8},{1,9},{2,10},{3,11},{4,12},{5,13},{6,14},{7,15},{8,0},{9,1},... | collective-permute-start | bytes 258056 | tf_op jit(solution)/shard_map/ppermute | solution.py:231
  14.1 0.0 collective-permute-done.1.got_ref
  14.2 1.4 %collective-permute-start.3 = (bf16[8,5376]{1,0:T(8,128)(2,1)S(1)}, bf16[8,5376]{1,0:T(8,128)(2,1)S(1)}, u32[]{:S(2)}, u32[]{:S(2)}) collective-permute-start(bf16[8,5376]{1,0:T(8,128)(2,1)S(1)} %join.1), channel_id=1, source_target_pairs={{0,4},{1,5},{2,6},{3,7},{4,0},{5,1},{6,2},{7,3},{8,12},{9,13},{10,... | collective-permute-start | bytes 258056 | tf_op jit(solution)/shard_map/ppermute | solution.py:231
  15.6 2.4 %pick.3 = (bf16[16,5376]{1,0:T(8,128)(2,1)S(1)}, bf16[16,5376]{1,0:T(8,128)(2,1)S(1)}) custom-call(s32[2,32]{1,0:T(2,128)} %ids_ref.3, bf16[1024,5376]{1,0:T(8,128)(2,1)} %table_ref.7, bf16[8,5376]{1,0:T(8,128)(2,1)S(1)} %add.23.refs_0_.own_ref), custom_call_target="tpu_custom_call" | custom-call | tf_op jit(solution)/shard_map/pick/pallas_call | solution.py:124
  18.1 0.1 collective-permute-start.8
  18.1 0.3 collective-permute-done.5.got_ref
  18.5 0.7 %collective-permute-start.6 = (bf16[8,5376]{1,0:T(8,128)(2,1)S(1)}, bf16[8,5376]{1,0:T(8,128)(2,1)S(1)}, u32[]{:S(2)}, u32[]{:S(2)}) collective-permute-start(bf16[8,5376]{1,0:T(8,128)(2,1)S(1)} %plus.1.own_ref), channel_id=1, source_target_pairs={{0,4},{1,5},{2,6},{3,7},{4,0},{5,1},{6,2},{7,3},{8,12},{9,13},{10,... | collective-permute-start | bytes 258056 | tf_op jit(solution)/shard_map/ppermute | solution.py:231
  19.2 0.1 collective-permute-done.3
  19.4 0.2 norm.2.one_ref
  19.6 1.3 %collective-permute-start.4 = (bf16[8,5376]{1,0:T(8,128)(2,1)S(1)}, bf16[8,5376]{1,0:T(8,128)(2,1)S(1)}, u32[]{:S(2)}, u32[]{:S(2)}) collective-permute-start(bf16[8,5376]{1,0:T(8,128)(2,1)S(1)} %norm.2.one_ref), channel_id=1, source_target_pairs={{0,2},{1,3},{2,0},{3,1},{4,6},{5,7},{6,4},{7,5},{8,10},{9,11},{10,... | collective-permute-start | bytes 258056 | tf_op jit(solution)/shard_map/ppermute | solution.py:231
  20.9 0.0 collective-permute-done.8
  21.0 0.8 %collective-permute-start.9 = (bf16[8,5376]{1,0:T(8,128)(2,1)S(1)}, bf16[8,5376]{1,0:T(8,128)(2,1)S(1)}, u32[]{:S(2)}, u32[]{:S(2)}) collective-permute-start(bf16[8,5376]{1,0:T(8,128)(2,1)S(1)} %slice.81), channel_id=1, source_target_pairs={{0,2},{1,3},{2,0},{3,1},{4,6},{5,7},{6,4},{7,5},{8,10},{9,11},{10,... | collective-permute-start | bytes 258056 | tf_op jit(solution)/shard_map/ppermute | solution.py:231
  21.9 1.3 %collective-permute-done.6.got_ref = bf16[8,5376]{1,0:T(8,128)(2,1)S(1)} collective-permute-done((bf16[8,5376]{1,0:T(8,128)(2,1)S(1)}, bf16[8,5376]{1,0:T(8,128)(2,1)S(1)}, u32[]{:S(2)}, u32[]{:S(2)}) %collective-permute-start.6) | collective-permute-done | bytes 86048 | tf_op jit(solution)/shard_map/ppermute | solution.py:231
  23.2 0.2 norm.3.refs_0_.two_ref
  23.4 1.7 %collective-permute-start.7 = (bf16[8,5376]{1,0:T(8,128)(2,1)S(1)}, bf16[8,5376]{1,0:T(8,128)(2,1)S(1)}, u32[]{:S(2)}, u32[]{:S(2)}) collective-permute-start(bf16[8,5376]{1,0:T(8,128)(2,1)S(1)} %norm.3.refs_0_.two_ref), channel_id=1, source_target_pairs={{0,2},{1,3},{2,0},{3,1},{4,6},{5,7},{6,4},{7,5},{8,10},{9,11},{10,... | collective-permute-start | bytes 258056 | tf_op jit(solution)/shard_map/ppermute | solution.py:231
  25.1 3.8 %load.3 = (bf16[1024,5376]{1,0:T(8,128)(2,1)S(1)}, f32[8,128]{1,0:T(8,128)S(1)}) custom-call(bf16[1024,5376]{1,0:T(8,128)(2,1)} %table_ref.7, bf16[8,5376]{1,0:T(8,128)(2,1)S(1)} %norm.3.refs_0_.two_ref, bf16[1024,5376]{1,0:T(8,128)(2,1)S(1)} %get-tuple-element.23.refs_1_), custom_call_target="tpu_custom_call", output_to_operand_aliasing={{0}: (2, {})} | custom-call | tf_op jit(solution)/shard_map/load/pallas_call | solution.py:253
  29.0 0.0 collective-permute-done.9
  29.0 0.0 collective-permute-done.4.one_got_ref
  29.0 0.0 collective-permute-done.7.two_got_ref
  29.0 0.1 chips.1.own_ref
  29.1 0.1 collective-permute-start.10
  29.2 0.4 collective-permute-start.13
  29.6 1.3 %collective-permute-done.10.got_ref = bf16[32,5376]{1,0:T(8,128)(2,1)S(1)} collective-permute-done((bf16[32,5376]{1,0:T(8,128)(2,1)S(1)}, bf16[32,5376]{1,0:T(8,128)(2,1)S(1)}, u32[]{:S(2)}, u32[]{:S(2)}) %collective-permute-start.10) | collective-permute-done | bytes 344096 | tf_op jit(solution)/shard_map/ppermute | solution.py:231
  30.8 3.1 %head.1 = (f32[1024,64]{1,0:T(8,128)S(1)}, f32[2,64]{1,0:T(2,128)S(1)}) custom-call(bf16[32,5376]{1,0:T(8,128)(2,1)S(1)} %chips.1.own_ref, bf16[32,5376]{1,0:T(8,128)(2,1)S(1)} %collective-permute-done.10.got_ref, bf16[1024,5376]{1,0:T(8,128)(2,1)S(1)} %get-tuple-element.26.table_ref, f32[1,64]{1,0:T(1,128)S(1)} %get-tuple-element.27.temps_ref), custom_call_target="tpu_custom_call" | custom-call | tf_op jit(solution)/shard_map/head/pallas_call | solution.py:328
  34.0 2.1 %collective-permute-start.11 = (f32[2,64]{1,0:T(2,128)S(1)}, f32[2,64]{1,0:T(2,128)S(1)}, u32[]{:S(2)}, u32[]{:S(2)}) collective-permute-start(f32[2,64]{1,0:T(2,128)S(1)} %get-tuple-element.29), channel_id=1, source_target_pairs={{0,8},{1,9},{2,10},{3,11},{4,12},{5,13},{6,14},{7,15},{8,0},{9,1},... | collective-permute-start | bytes 1544 | tf_op jit(solution)/shard_map/ppermute | solution.py:231
  36.1 0.0 collective-permute-done.13
  36.1 1.0 %collective-permute-start.14 = (bf16[2,5376]{1,0:T(2,128)(2,1)S(1)}, bf16[2,5376]{1,0:T(2,128)(2,1)S(1)}, u32[]{:S(2)}, u32[]{:S(2)}) collective-permute-start(bf16[2,5376]{1,0:T(2,128)(2,1)S(1)} %slice.85), channel_id=1, source_target_pairs={{0,8},{1,9},{2,10},{3,11},{4,12},{5,13},{6,14},{7,15},{8,0},{9,1},... | collective-permute-start | bytes 64520 | tf_op jit(solution)/shard_map/ppermute | solution.py:231
  37.1 1.4 %collective-permute-done.11 = f32[2,64]{1,0:T(2,128)S(1)} collective-permute-done((f32[2,64]{1,0:T(2,128)S(1)}, f32[2,64]{1,0:T(2,128)S(1)}, u32[]{:S(2)}, u32[]{:S(2)}) %collective-permute-start.11) | collective-permute-done | bytes 544 | tf_op jit(solution)/shard_map/ppermute | solution.py:231
  38.5 0.7 %collective-permute-start.12 = (f32[2,64]{1,0:T(2,128)S(1)}, f32[2,64]{1,0:T(2,128)S(1)}, u32[]{:S(2)}, u32[]{:S(2)}) collective-permute-start(f32[2,64]{1,0:T(2,128)S(1)} %pad_maximum_fusion.2.own_ref), channel_id=1, source_target_pairs={{0,4},{1,5},{2,6},{3,7},{4,0},{5,1},{6,2},{7,3},{8,12},{9,13},{10,... | collective-permute-start | bytes 1544 | tf_op jit(solution)/shard_map/ppermute | solution.py:231
  39.2 1.7 %collective-permute-done.14 = bf16[2,5376]{1,0:T(2,128)(2,1)S(1)} collective-permute-done((bf16[2,5376]{1,0:T(2,128)(2,1)S(1)}, bf16[2,5376]{1,0:T(2,128)(2,1)S(1)}, u32[]{:S(2)}, u32[]{:S(2)}) %collective-permute-start.14) | collective-permute-done | bytes 21536 | tf_op jit(solution)/shard_map/ppermute | solution.py:231
  41.0 0.6 %multiply_convert_fusion = (bf16[2,5376]{1,0:T(2,128)(2,1)}, bf16[2,5376]{1,0:T(2,128)(2,1)S(1)}) fusion(bf16[2,5376]{1,0:T(2,128)(2,1)S(1)} %collective-permute-done.14, bf16[4,5376]{1,0:T(4,128)(2,1)S(1)} %slice_add_fusion.1), kind=kLoop, calls=%fused_computation.4 | loop fusion | flops 43008 | bytes 86016 | tf_op jit(solution)/shard_map/convert_element_type | solution.py:431
  41.6 0.6 %collective-permute-done.12.got_ref = f32[2,64]{1,0:T(2,128)S(1)} collective-permute-done((f32[2,64]{1,0:T(2,128)S(1)}, f32[2,64]{1,0:T(2,128)S(1)}, u32[]{:S(2)}, u32[]{:S(2)}) %collective-permute-start.12) | collective-permute-done | bytes 544 | tf_op jit(solution)/shard_map/ppermute | solution.py:231
  42.2 0.6 %collective-permute-start.15 = (f32[2,64]{1,0:T(2,128)S(1)}, f32[2,64]{1,0:T(2,128)S(1)}, u32[]{:S(2)}, u32[]{:S(2)}) collective-permute-start(f32[2,64]{1,0:T(2,128)S(1)} %merge.1), channel_id=1, source_target_pairs={{0,2},{1,3},{2,0},{3,1},{4,6},{5,7},{6,4},{7,5},{8,10},{9,11},{10,... | collective-permute-start | bytes 1544 | tf_op jit(solution)/shard_map/ppermute | solution.py:231
  42.8 3.0 %collective-permute-done.15 = f32[2,64]{1,0:T(2,128)S(1)} collective-permute-done((f32[2,64]{1,0:T(2,128)S(1)}, f32[2,64]{1,0:T(2,128)S(1)}, u32[]{:S(2)}, u32[]{:S(2)}) %collective-permute-start.15) | collective-permute-done | bytes 544 | tf_op jit(solution)/shard_map/ppermute | solution.py:231
  45.9 0.1 collective-permute-start.16
  45.9 0.2 turn.1.scaled_ref
  46.1 0.9 %collective-permute-done.16.got_ref = f32[2,64]{1,0:T(2,128)S(1)} collective-permute-done((f32[2,64]{1,0:T(2,128)S(1)}, f32[2,64]{1,0:T(2,128)S(1)}, u32[]{:S(2)}, u32[]{:S(2)}) %collective-permute-start.16) | collective-permute-done | bytes 544 | tf_op jit(solution)/shard_map/ppermute | solution.py:231
  47.1 0.9 %finish.1 = f32[2,32,1024]{2,1,0:T(8,128)} custom-call(f32[2,32,1024]{2,1,0:T(8,128)S(1)} %turn.1.scaled_ref, f32[2,64]{1,0:T(2,128)S(1)} %pad_maximum_fusion.3.own_ref, f32[2,64]{1,0:T(2,128)S(1)} %collective-permute-done.16.got_ref), custom_call_target="tpu_custom_call" | custom-call | tf_op jit(solution)/shard_map/finish/pallas_call | solution.py:374
  (23 shorter events, 0.5 us)
Async XLA Ops:
  0.6 4.4 %copy-start = (bf16[2,5376]{1,0:T(2,128)(2,1)S(1)}, bf16[2,5376]{1,0:T(2,128)(2,1)}, u32[]{:S(2)}) copy-start(bf16[2,5376]{1,0:T(2,128)(2,1)} %first_ref.1) | copy-start | bytes 64516
  0.6 4.4 %copy-start.1 = (bf16[2,5376]{1,0:T(2,128)(2,1)S(1)}, bf16[2,5376]{1,0:T(2,128)(2,1)}, u32[]{:S(2)}) copy-start(bf16[2,5376]{1,0:T(2,128)(2,1)} %delta_ref.1) | copy-start | bytes 64516
  0.7 9.7 %copy-start.2 = (f32[5376]{0:T(1024)S(1)}, f32[5376]{0:T(1024)}, u32[]{:S(2)}) copy-start(f32[5376]{0:T(1024)} %param.9) | copy-start | bytes 64516
  3.0 2.0 %collective-permute-start = (bf16[16,5376]{1,0:T(8,128)(2,1)S(1)}, bf16[16,5376]{1,0:T(8,128)(2,1)S(1)}, u32[]{:S(2)}, u32[]{:S(2)}) collective-permute-start(bf16[16,5376]{1,0:T(8,128)(2,1)S(1)} %get-tuple-element.17.refs_0_), channel_id=1, source_target_pairs={{0,1},{1,0},{2,3},{3,2},{4,5},{5,4},{6,7},{7,6},{8,9},{9,8},{10,11... | collective-permute-start | bytes 516104 | tf_op jit(solution)/shard_map/ppermute | solution.py:231
  5.1 5.9 %collective-permute-start.2 = (bf16[8,5376]{1,0:T(8,128)(2,1)S(1)}, bf16[8,5376]{1,0:T(8,128)(2,1)S(1)}, u32[]{:S(2)}, u32[]{:S(2)}) collective-permute-start(bf16[8,5376]{1,0:T(8,128)(2,1)S(1)} %get-tuple-element.21), channel_id=1, source_target_pairs={{0,2},{1,3},{2,0},{3,1},{4,6},{5,7},{6,4},{7,5},{8,10},{9,11},{10,... | collective-permute-start | bytes 258056 | tf_op jit(solution)/shard_map/ppermute | solution.py:231
  7.8 6.4 %collective-permute-start.1 = (bf16[4,5376]{1,0:T(4,128)(2,1)S(1)}, bf16[4,5376]{1,0:T(4,128)(2,1)S(1)}, u32[]{:S(2)}, u32[]{:S(2)}) collective-permute-start(bf16[4,5376]{1,0:T(4,128)(2,1)S(1)} %get-tuple-element.19.own_ref), channel_id=1, source_target_pairs={{0,8},{1,9},{2,10},{3,11},{4,12},{5,13},{6,14},{7,15},{8,0},{9,1},... | collective-permute-start | bytes 129032 | tf_op jit(solution)/shard_map/ppermute | solution.py:231
  11.0 7.5 %collective-permute-start.5 = (bf16[8,5376]{1,0:T(8,128)(2,1)S(1)}, bf16[8,5376]{1,0:T(8,128)(2,1)S(1)}, u32[]{:S(2)}, u32[]{:S(2)}) collective-permute-start(bf16[8,5376]{1,0:T(8,128)(2,1)S(1)} %add.23.refs_0_.own_ref), channel_id=1, source_target_pairs={{0,8},{1,9},{2,10},{3,11},{4,12},{5,13},{6,14},{7,15},{8,0},{9,1},... | collective-permute-start | bytes 258056 | tf_op jit(solution)/shard_map/ppermute | solution.py:231
  14.2 5.1 %collective-permute-start.3 = (bf16[8,5376]{1,0:T(8,128)(2,1)S(1)}, bf16[8,5376]{1,0:T(8,128)(2,1)S(1)}, u32[]{:S(2)}, u32[]{:S(2)}) collective-permute-start(bf16[8,5376]{1,0:T(8,128)(2,1)S(1)} %join.1), channel_id=1, source_target_pairs={{0,4},{1,5},{2,6},{3,7},{4,0},{5,1},{6,2},{7,3},{8,12},{9,13},{10,... | collective-permute-start | bytes 258056 | tf_op jit(solution)/shard_map/ppermute | solution.py:231
  18.1 2.9 %collective-permute-start.8 = (bf16[16,5376]{1,0:T(8,128)(2,1)S(1)}, bf16[16,5376]{1,0:T(8,128)(2,1)S(1)}, u32[]{:S(2)}, u32[]{:S(2)}) collective-permute-start(bf16[16,5376]{1,0:T(8,128)(2,1)S(1)} %get-tuple-element.22.refs_0_), channel_id=1, source_target_pairs={{0,1},{1,0},{2,3},{3,2},{4,5},{5,4},{6,7},{7,6},{8,9},{9,8},{10,11... | collective-permute-start | bytes 516104 | tf_op jit(solution)/shard_map/ppermute | solution.py:231
  18.5 4.7 %collective-permute-start.6 = (bf16[8,5376]{1,0:T(8,128)(2,1)S(1)}, bf16[8,5376]{1,0:T(8,128)(2,1)S(1)}, u32[]{:S(2)}, u32[]{:S(2)}) collective-permute-start(bf16[8,5376]{1,0:T(8,128)(2,1)S(1)} %plus.1.own_ref), channel_id=1, source_target_pairs={{0,4},{1,5},{2,6},{3,7},{4,0},{5,1},{6,2},{7,3},{8,12},{9,13},{10,... | collective-permute-start | bytes 258056 | tf_op jit(solution)/shard_map/ppermute | solution.py:231
  19.6 9.4 %collective-permute-start.4 = (bf16[8,5376]{1,0:T(8,128)(2,1)S(1)}, bf16[8,5376]{1,0:T(8,128)(2,1)S(1)}, u32[]{:S(2)}, u32[]{:S(2)}) collective-permute-start(bf16[8,5376]{1,0:T(8,128)(2,1)S(1)} %norm.2.one_ref), channel_id=1, source_target_pairs={{0,2},{1,3},{2,0},{3,1},{4,6},{5,7},{6,4},{7,5},{8,10},{9,11},{10,... | collective-permute-start | bytes 258056 | tf_op jit(solution)/shard_map/ppermute | solution.py:231
  21.0 8.0 %collective-permute-start.9 = (bf16[8,5376]{1,0:T(8,128)(2,1)S(1)}, bf16[8,5376]{1,0:T(8,128)(2,1)S(1)}, u32[]{:S(2)}, u32[]{:S(2)}) collective-permute-start(bf16[8,5376]{1,0:T(8,128)(2,1)S(1)} %slice.81), channel_id=1, source_target_pairs={{0,2},{1,3},{2,0},{3,1},{4,6},{5,7},{6,4},{7,5},{8,10},{9,11},{10,... | collective-permute-start | bytes 258056 | tf_op jit(solution)/shard_map/ppermute | solution.py:231
  23.4 5.6 %collective-permute-start.7 = (bf16[8,5376]{1,0:T(8,128)(2,1)S(1)}, bf16[8,5376]{1,0:T(8,128)(2,1)S(1)}, u32[]{:S(2)}, u32[]{:S(2)}) collective-permute-start(bf16[8,5376]{1,0:T(8,128)(2,1)S(1)} %norm.3.refs_0_.two_ref), channel_id=1, source_target_pairs={{0,2},{1,3},{2,0},{3,1},{4,6},{5,7},{6,4},{7,5},{8,10},{9,11},{10,... | collective-permute-start | bytes 258056 | tf_op jit(solution)/shard_map/ppermute | solution.py:231
  29.1 1.7 %collective-permute-start.10 = (bf16[32,5376]{1,0:T(8,128)(2,1)S(1)}, bf16[32,5376]{1,0:T(8,128)(2,1)S(1)}, u32[]{:S(2)}, u32[]{:S(2)}) collective-permute-start(bf16[32,5376]{1,0:T(8,128)(2,1)S(1)} %chips.1.own_ref), channel_id=1, source_target_pairs={{0,1},{1,0},{2,3},{3,2},{4,5},{5,4},{6,7},{7,6},{8,9},{9,8},{10,11... | collective-permute-start | bytes 1032200 | tf_op jit(solution)/shard_map/ppermute | solution.py:231
  29.2 6.8 %collective-permute-start.13 = (bf16[4,5376]{1,0:T(4,128)(2,1)S(1)}, bf16[4,5376]{1,0:T(4,128)(2,1)S(1)}, u32[]{:S(2)}, u32[]{:S(2)}) collective-permute-start(bf16[4,5376]{1,0:T(4,128)(2,1)S(1)} %slice.83), channel_id=1, source_target_pairs={{0,4},{1,5},{2,6},{3,7},{4,0},{5,1},{6,2},{7,3},{8,12},{9,13},{10,... | collective-permute-start | bytes 129032 | tf_op jit(solution)/shard_map/ppermute | solution.py:231
  34.0 4.5 %collective-permute-start.11 = (f32[2,64]{1,0:T(2,128)S(1)}, f32[2,64]{1,0:T(2,128)S(1)}, u32[]{:S(2)}, u32[]{:S(2)}) collective-permute-start(f32[2,64]{1,0:T(2,128)S(1)} %get-tuple-element.29), channel_id=1, source_target_pairs={{0,8},{1,9},{2,10},{3,11},{4,12},{5,13},{6,14},{7,15},{8,0},{9,1},... | collective-permute-start | bytes 1544 | tf_op jit(solution)/shard_map/ppermute | solution.py:231
  36.1 4.9 %collective-permute-start.14 = (bf16[2,5376]{1,0:T(2,128)(2,1)S(1)}, bf16[2,5376]{1,0:T(2,128)(2,1)S(1)}, u32[]{:S(2)}, u32[]{:S(2)}) collective-permute-start(bf16[2,5376]{1,0:T(2,128)(2,1)S(1)} %slice.85), channel_id=1, source_target_pairs={{0,8},{1,9},{2,10},{3,11},{4,12},{5,13},{6,14},{7,15},{8,0},{9,1},... | collective-permute-start | bytes 64520 | tf_op jit(solution)/shard_map/ppermute | solution.py:231
  38.5 3.6 %collective-permute-start.12 = (f32[2,64]{1,0:T(2,128)S(1)}, f32[2,64]{1,0:T(2,128)S(1)}, u32[]{:S(2)}, u32[]{:S(2)}) collective-permute-start(f32[2,64]{1,0:T(2,128)S(1)} %pad_maximum_fusion.2.own_ref), channel_id=1, source_target_pairs={{0,4},{1,5},{2,6},{3,7},{4,0},{5,1},{6,2},{7,3},{8,12},{9,13},{10,... | collective-permute-start | bytes 1544 | tf_op jit(solution)/shard_map/ppermute | solution.py:231
  42.2 3.6 %collective-permute-start.15 = (f32[2,64]{1,0:T(2,128)S(1)}, f32[2,64]{1,0:T(2,128)S(1)}, u32[]{:S(2)}, u32[]{:S(2)}) collective-permute-start(f32[2,64]{1,0:T(2,128)S(1)} %merge.1), channel_id=1, source_target_pairs={{0,2},{1,3},{2,0},{3,1},{4,6},{5,7},{6,4},{7,5},{8,10},{9,11},{10,... | collective-permute-start | bytes 1544 | tf_op jit(solution)/shard_map/ppermute | solution.py:231
  45.9 1.2 %collective-permute-start.16 = (f32[2,64]{1,0:T(2,128)S(1)}, f32[2,64]{1,0:T(2,128)S(1)}, u32[]{:S(2)}, u32[]{:S(2)}) collective-permute-start(f32[2,64]{1,0:T(2,128)S(1)} %pad_maximum_fusion.3.own_ref), channel_id=1, source_target_pairs={{0,1},{1,0},{2,3},{3,2},{4,5},{5,4},{6,7},{7,6},{8,9},{9,8},{10,11... | collective-permute-start | bytes 1544 | tf_op jit(solution)/shard_map/ppermute | solution.py:231

commit v16 on v14

--- a/solution.py
+++ b/solution.py
@@ -354,7 +354,7 @@
     )(scaled)
 
 
-def finish_kernel(order, scaled_ref, own_ref, got_ref, out_ref):
+def finish_kernel(order, scaled_ref, own_ref, got_ref, out_ref, held, sems):
     own, got = own_ref[...], got_ref[...]
     peak = jnp.maximum(own[0:1], got[0:1])
     total = own[1:2] * jnp.exp(own[0:1] - peak) + got[1:2] * jnp.exp(got[0:1] - peak)
@@ -365,15 +365,28 @@
     voc_dev = out_ref.shape[2]
     peak = jnp.concatenate([peak] * (voc_dev // 128), axis=1)
     log = jnp.concatenate([log] * (voc_dev // 128), axis=1)
-    for place, (step, row) in enumerate(order):
-        at = slice(place, place + 1)
-        out_ref[step, row : row + 1, :] = scaled_ref[step, row : row + 1, :] - peak[at] - log[at]
+    copies = []
+    for now in range(held.shape[0]):
+        for place, (step, row) in enumerate(order):
+            if step == now:
+                at = slice(place, place + 1)
+                held[step, row : row + 1, :] = scaled_ref[step, row : row + 1, :] - peak[at] - log[at]
+        copies.append(pltpu.make_async_copy(held.at[now], out_ref.at[now], sems.at[now]))
+        copies[-1].start()
+    for copy in copies:
+        copy.wait()
 
 
 def finished(scaled, own, got, order):
     return pl.pallas_call(
         functools.partial(finish_kernel, order),
         out_shape=jax.ShapeDtypeStruct(scaled.shape, jnp.float32),
+        in_specs=[pl.BlockSpec(memory_space=pltpu.VMEM)] * 3,
+        out_specs=pl.BlockSpec(memory_space=pl.ANY),
+        scratch_shapes=[
+            pltpu.VMEM(scaled.shape, jnp.float32),
+            pltpu.SemaphoreType.DMA(scaled.shape[:1]),
+        ],
         compiler_params=pltpu.CompilerParams(vmem_limit_bytes=12 * MIB),
         name="finish",
     )(scaled, own, got)

time: 47.6 us -> 47.4 us (level)
  waiting for transfers between devices: 10.5 us -> 9.27 us
  starting transfers between devices: 19.9 us -> 21 us
    ppermute x17, waiting for transfers between devices: 10.5 us -> 9.27 us  [swapped(): return lax.ppermute(rows, 'vocab', pairs)]
    ppermute x17, starting transfers between devices: 19.9 us -> 21 us  [swapped(): return lax.ppermute(rows, 'vocab', pairs)]
where the time goes in v16:
time: 47.4 us; the launch traced here: 47 us
  starting transfers between devices  21 us (44%)
  Pallas kernels  14.8 us (31%)
  waiting for transfers between devices  9.27 us (20%)
  other arithmetic  0.89 us (2%)
  between operations  0.87 us (2%)
    ppermute x17, starting transfers between devices, swapped(): return lax.ppermute(rows, 'vocab', pairs)  21 us
    ppermute x17, waiting for transfers between devices, swapped(): return lax.ppermute(rows, 'vocab', pairs)  9.27 us
    pallas_call x2, Pallas kernels, loaded(): pl.pallas_call(functools.partial(load_kernel, first, last), out_shape=(ja...  5.18 us
    pallas_call x2, Pallas kernels, picked_rows(): pl.pallas_call(functools.partial(pick_kernel, step, places), out_shape=ou...  4.71 us
    pallas_call x1, Pallas kernels, head(): pl.pallas_call(head_kernel, out_shape=(jax.ShapeDtypeStruct((voc_dev, row...  3.15 us
  transfers between devices with their start and end apart: 17, of which 9 were waited for; matrix products, arithmetic and copies ran while one was open for 2% of the time, Pallas kernels for 24%

profile of v16, /device:TPU:0, one launch (start us, length us, event | category | flops | bytes accessed | tf_op | source)
XLA Modules:
  0.0 47.0 jit_solution(10969823129193269564)
XLA Ops:
  0.6 0.0 copy-start
  0.7 2.5 %pick.2 = (bf16[16,5376]{1,0:T(8,128)(2,1)S(1)}, bf16[16,5376]{1,0:T(8,128)(2,1)S(1)}, f32[1,64]{1,0:T(1,128)S(1)}) custom-call(s32[2,32]{1,0:T(2,128)} %ids_ref.3, bf16[1024,5376]{1,0:T(8,128)(2,1)} %table_ref.7, s32[2,32]{1,0:T(2,128)} %refs_0_.1, f32[8]{0:T(128)} %refs_1_.1), custom_call_target="tpu_custom_call" | custom-call | tf_op jit(solution)/shard_map/pick/pallas_call | solution.py:124
  3.1 0.1 collective-permute-start
  3.2 1.3 %load.2 = (bf16[1024,5376]{1,0:T(8,128)(2,1)S(1)}, f32[8,128]{1,0:T(8,128)S(1)}) custom-call(bf16[1024,5376]{1,0:T(8,128)(2,1)} %table_ref.7, bf16[16,5376]{1,0:T(8,128)(2,1)S(1)} %get-tuple-element.17.refs_0_), custom_call_target="tpu_custom_call" | custom-call | tf_op jit(solution)/shard_map/load/pallas_call | solution.py:253
  4.6 0.1 collective-permute-done.got_ref
  4.6 0.0 copy-done
  4.6 0.1 fold.1
  4.7 3.0 %collective-permute-start.2 = (bf16[8,5376]{1,0:T(8,128)(2,1)S(1)}, bf16[8,5376]{1,0:T(8,128)(2,1)S(1)}, u32[]{:S(2)}, u32[]{:S(2)}) collective-permute-start(bf16[8,5376]{1,0:T(8,128)(2,1)S(1)} %get-tuple-element.21), channel_id=1, source_target_pairs={{0,2},{1,3},{2,0},{3,1},{4,6},{5,7},{6,4},{7,5},{8,10},{9,11},{10,... | collective-permute-start | bytes 258056 | tf_op jit(solution)/shard_map/ppermute | solution.py:231
  7.7 2.4 %collective-permute-start.1 = (bf16[4,5376]{1,0:T(4,128)(2,1)S(1)}, bf16[4,5376]{1,0:T(4,128)(2,1)S(1)}, u32[]{:S(2)}, u32[]{:S(2)}) collective-permute-start(bf16[4,5376]{1,0:T(4,128)(2,1)S(1)} %get-tuple-element.19.own_ref), channel_id=1, source_target_pairs={{0,8},{1,9},{2,10},{3,11},{4,12},{5,13},{6,14},{7,15},{8,0},{9,1},... | collective-permute-start | bytes 129032 | tf_op jit(solution)/shard_map/ppermute | solution.py:231
  10.2 0.7 %collective-permute-done.2 = bf16[8,5376]{1,0:T(8,128)(2,1)S(1)} collective-permute-done((bf16[8,5376]{1,0:T(8,128)(2,1)S(1)}, bf16[8,5376]{1,0:T(8,128)(2,1)S(1)}, u32[]{:S(2)}, u32[]{:S(2)}) %collective-permute-start.2) | collective-permute-done | bytes 86048 | tf_op jit(solution)/shard_map/ppermute | solution.py:231
  10.9 3.0 %collective-permute-start.5 = (bf16[8,5376]{1,0:T(8,128)(2,1)S(1)}, bf16[8,5376]{1,0:T(8,128)(2,1)S(1)}, u32[]{:S(2)}, u32[]{:S(2)}) collective-permute-start(bf16[8,5376]{1,0:T(8,128)(2,1)S(1)} %add.23.refs_0_.own_ref), channel_id=1, source_target_pairs={{0,8},{1,9},{2,10},{3,11},{4,12},{5,13},{6,14},{7,15},{8,0},{9,1},... | collective-permute-start | bytes 258056 | tf_op jit(solution)/shard_map/ppermute | solution.py:231
  13.9 0.0 collective-permute-done.1.got_ref
  13.9 1.5 %collective-permute-start.3 = (bf16[8,5376]{1,0:T(8,128)(2,1)S(1)}, bf16[8,5376]{1,0:T(8,128)(2,1)S(1)}, u32[]{:S(2)}, u32[]{:S(2)}) collective-permute-start(bf16[8,5376]{1,0:T(8,128)(2,1)S(1)} %join.1), channel_id=1, source_target_pairs={{0,4},{1,5},{2,6},{3,7},{4,0},{5,1},{6,2},{7,3},{8,12},{9,13},{10,... | collective-permute-start | bytes 258056 | tf_op jit(solution)/shard_map/ppermute | solution.py:231
  15.4 2.2 %pick.3 = (bf16[16,5376]{1,0:T(8,128)(2,1)S(1)}, bf16[16,5376]{1,0:T(8,128)(2,1)S(1)}) custom-call(s32[2,32]{1,0:T(2,128)} %ids_ref.3, bf16[1024,5376]{1,0:T(8,128)(2,1)} %table_ref.7, bf16[8,5376]{1,0:T(8,128)(2,1)S(1)} %add.23.refs_0_.own_ref), custom_call_target="tpu_custom_call" | custom-call | tf_op jit(solution)/shard_map/pick/pallas_call | solution.py:124
  17.7 0.1 collective-permute-start.8
  17.8 0.0 collective-permute-done.5.got_ref
  17.8 1.1 %collective-permute-start.6 = (bf16[8,5376]{1,0:T(8,128)(2,1)S(1)}, bf16[8,5376]{1,0:T(8,128)(2,1)S(1)}, u32[]{:S(2)}, u32[]{:S(2)}) collective-permute-start(bf16[8,5376]{1,0:T(8,128)(2,1)S(1)} %plus.1.own_ref), channel_id=1, source_target_pairs={{0,4},{1,5},{2,6},{3,7},{4,0},{5,1},{6,2},{7,3},{8,12},{9,13},{10,... | collective-permute-start | bytes 258056 | tf_op jit(solution)/shard_map/ppermute | solution.py:231
  18.9 0.0 collective-permute-done.3
  19.0 0.2 norm.2.one_ref
  19.2 1.7 %collective-permute-start.4 = (bf16[8,5376]{1,0:T(8,128)(2,1)S(1)}, bf16[8,5376]{1,0:T(8,128)(2,1)S(1)}, u32[]{:S(2)}, u32[]{:S(2)}) collective-permute-start(bf16[8,5376]{1,0:T(8,128)(2,1)S(1)} %norm.2.one_ref), channel_id=1, source_target_pairs={{0,2},{1,3},{2,0},{3,1},{4,6},{5,7},{6,4},{7,5},{8,10},{9,11},{10,... | collective-permute-start | bytes 258056 | tf_op jit(solution)/shard_map/ppermute | solution.py:231
  20.9 0.0 collective-permute-done.8
  20.9 0.5 collective-permute-start.9
  21.5 1.3 %collective-permute-done.6.got_ref = bf16[8,5376]{1,0:T(8,128)(2,1)S(1)} collective-permute-done((bf16[8,5376]{1,0:T(8,128)(2,1)S(1)}, bf16[8,5376]{1,0:T(8,128)(2,1)S(1)}, u32[]{:S(2)}, u32[]{:S(2)}) %collective-permute-start.6) | collective-permute-done | bytes 86048 | tf_op jit(solution)/shard_map/ppermute | solution.py:231
  22.8 0.2 norm.3.refs_0_.two_ref
  23.0 1.2 %collective-permute-start.7 = (bf16[8,5376]{1,0:T(8,128)(2,1)S(1)}, bf16[8,5376]{1,0:T(8,128)(2,1)S(1)}, u32[]{:S(2)}, u32[]{:S(2)}) collective-permute-start(bf16[8,5376]{1,0:T(8,128)(2,1)S(1)} %norm.3.refs_0_.two_ref), channel_id=1, source_target_pairs={{0,2},{1,3},{2,0},{3,1},{4,6},{5,7},{6,4},{7,5},{8,10},{9,11},{10,... | collective-permute-start | bytes 258056 | tf_op jit(solution)/shard_map/ppermute | solution.py:231
  24.2 3.9 %load.3 = (bf16[1024,5376]{1,0:T(8,128)(2,1)S(1)}, f32[8,128]{1,0:T(8,128)S(1)}) custom-call(bf16[1024,5376]{1,0:T(8,128)(2,1)} %table_ref.7, bf16[8,5376]{1,0:T(8,128)(2,1)S(1)} %norm.3.refs_0_.two_ref, bf16[1024,5376]{1,0:T(8,128)(2,1)S(1)} %get-tuple-element.23.refs_1_), custom_call_target="tpu_custom_call", output_to_operand_aliasing={{0}: (2, {})} | custom-call | tf_op jit(solution)/shard_map/load/pallas_call | solution.py:253
  28.0 0.0 collective-permute-done.9
  28.1 0.0 collective-permute-done.4.one_got_ref
  28.1 0.0 collective-permute-done.7.two_got_ref
  28.1 0.1 chips.1.own_ref
  28.2 0.1 collective-permute-start.10
  28.3 1.2 %collective-permute-start.13 = (bf16[4,5376]{1,0:T(4,128)(2,1)S(1)}, bf16[4,5376]{1,0:T(4,128)(2,1)S(1)}, u32[]{:S(2)}, u32[]{:S(2)}) collective-permute-start(bf16[4,5376]{1,0:T(4,128)(2,1)S(1)} %slice.83), channel_id=1, source_target_pairs={{0,4},{1,5},{2,6},{3,7},{4,0},{5,1},{6,2},{7,3},{8,12},{9,13},{10,... | collective-permute-start | bytes 129032 | tf_op jit(solution)/shard_map/ppermute | solution.py:231
  29.5 0.4 collective-permute-done.10.got_ref
  29.9 3.1 %head.1 = (f32[1024,64]{1,0:T(8,128)S(1)}, f32[2,64]{1,0:T(2,128)S(1)}) custom-call(bf16[32,5376]{1,0:T(8,128)(2,1)S(1)} %chips.1.own_ref, bf16[32,5376]{1,0:T(8,128)(2,1)S(1)} %collective-permute-done.10.got_ref, bf16[1024,5376]{1,0:T(8,128)(2,1)S(1)} %get-tuple-element.26.table_ref, f32[1,64]{1,0:T(1,128)S(1)} %get-tuple-element.27.temps_ref), custom_call_target="tpu_custom_call" | custom-call | tf_op jit(solution)/shard_map/head/pallas_call | solution.py:328
  33.1 2.1 %collective-permute-start.11 = (f32[2,64]{1,0:T(2,128)S(1)}, f32[2,64]{1,0:T(2,128)S(1)}, u32[]{:S(2)}, u32[]{:S(2)}) collective-permute-start(f32[2,64]{1,0:T(2,128)S(1)} %get-tuple-element.29), channel_id=1, source_target_pairs={{0,8},{1,9},{2,10},{3,11},{4,12},{5,13},{6,14},{7,15},{8,0},{9,1},... | collective-permute-start | bytes 1544 | tf_op jit(solution)/shard_map/ppermute | solution.py:231
  35.2 0.0 collective-permute-done.13
  35.2 0.9 %collective-permute-start.14 = (bf16[2,5376]{1,0:T(2,128)(2,1)S(1)}, bf16[2,5376]{1,0:T(2,128)(2,1)S(1)}, u32[]{:S(2)}, u32[]{:S(2)}) collective-permute-start(bf16[2,5376]{1,0:T(2,128)(2,1)S(1)} %slice.85), channel_id=1, source_target_pairs={{0,8},{1,9},{2,10},{3,11},{4,12},{5,13},{6,14},{7,15},{8,0},{9,1},... | collective-permute-start | bytes 64520 | tf_op jit(solution)/shard_map/ppermute | solution.py:231
  36.2 1.4 %collective-permute-done.11 = f32[2,64]{1,0:T(2,128)S(1)} collective-permute-done((f32[2,64]{1,0:T(2,128)S(1)}, f32[2,64]{1,0:T(2,128)S(1)}, u32[]{:S(2)}, u32[]{:S(2)}) %collective-permute-start.11) | collective-permute-done | bytes 544 | tf_op jit(solution)/shard_map/ppermute | solution.py:231
  37.6 1.2 %collective-permute-start.12 = (f32[2,64]{1,0:T(2,128)S(1)}, f32[2,64]{1,0:T(2,128)S(1)}, u32[]{:S(2)}, u32[]{:S(2)}) collective-permute-start(f32[2,64]{1,0:T(2,128)S(1)} %pad_maximum_fusion.2.own_ref), channel_id=1, source_target_pairs={{0,4},{1,5},{2,6},{3,7},{4,0},{5,1},{6,2},{7,3},{8,12},{9,13},{10,... | collective-permute-start | bytes 1544 | tf_op jit(solution)/shard_map/ppermute | solution.py:231
  38.8 1.2 %collective-permute-done.14 = bf16[2,5376]{1,0:T(2,128)(2,1)S(1)} collective-permute-done((bf16[2,5376]{1,0:T(2,128)(2,1)S(1)}, bf16[2,5376]{1,0:T(2,128)(2,1)S(1)}, u32[]{:S(2)}, u32[]{:S(2)}) %collective-permute-start.14) | collective-permute-done | bytes 21536 | tf_op jit(solution)/shard_map/ppermute | solution.py:231
  40.0 0.6 %multiply_convert_fusion = (bf16[2,5376]{1,0:T(2,128)(2,1)}, bf16[2,5376]{1,0:T(2,128)(2,1)S(1)}) fusion(bf16[2,5376]{1,0:T(2,128)(2,1)S(1)} %collective-permute-done.14, bf16[4,5376]{1,0:T(4,128)(2,1)S(1)} %slice_add_fusion.1), kind=kLoop, calls=%fused_computation.4 | loop fusion | flops 43008 | bytes 86016 | tf_op jit(solution)/shard_map/convert_element_type | solution.py:444
  40.7 0.6 %collective-permute-done.12.got_ref = f32[2,64]{1,0:T(2,128)S(1)} collective-permute-done((f32[2,64]{1,0:T(2,128)S(1)}, f32[2,64]{1,0:T(2,128)S(1)}, u32[]{:S(2)}, u32[]{:S(2)}) %collective-permute-start.12) | collective-permute-done | bytes 544 | tf_op jit(solution)/shard_map/ppermute | solution.py:231
  41.3 1.0 %collective-permute-start.15 = (f32[2,64]{1,0:T(2,128)S(1)}, f32[2,64]{1,0:T(2,128)S(1)}, u32[]{:S(2)}, u32[]{:S(2)}) collective-permute-start(f32[2,64]{1,0:T(2,128)S(1)} %merge.1), channel_id=1, source_target_pairs={{0,2},{1,3},{2,0},{3,1},{4,6},{5,7},{6,4},{7,5},{8,10},{9,11},{10,... | collective-permute-start | bytes 1544 | tf_op jit(solution)/shard_map/ppermute | solution.py:231
  42.3 2.6 %collective-permute-done.15 = f32[2,64]{1,0:T(2,128)S(1)} collective-permute-done((f32[2,64]{1,0:T(2,128)S(1)}, f32[2,64]{1,0:T(2,128)S(1)}, u32[]{:S(2)}, u32[]{:S(2)}) %collective-permute-start.15) | collective-permute-done | bytes 544 | tf_op jit(solution)/shard_map/ppermute | solution.py:231
  44.9 0.1 collective-permute-start.16
  45.0 0.2 turn.1.scaled_ref
  45.2 0.9 %collective-permute-done.16.got_ref = f32[2,64]{1,0:T(2,128)S(1)} collective-permute-done((f32[2,64]{1,0:T(2,128)S(1)}, f32[2,64]{1,0:T(2,128)S(1)}, u32[]{:S(2)}, u32[]{:S(2)}) %collective-permute-start.16) | collective-permute-done | bytes 544 | tf_op jit(solution)/shard_map/ppermute | solution.py:231
  46.1 0.9 %finish.1 = f32[2,32,1024]{2,1,0:T(8,128)} custom-call(f32[2,32,1024]{2,1,0:T(8,128)S(1)} %turn.1.scaled_ref, f32[2,64]{1,0:T(2,128)S(1)} %pad_maximum_fusion.3.own_ref, f32[2,64]{1,0:T(2,128)S(1)} %collective-permute-done.16.got_ref), custom_call_target="tpu_custom_call" | custom-call | tf_op jit(solution)/shard_map/finish/pallas_call | solution.py:381
  (23 shorter events, 0.5 us)
Async XLA Ops:
  0.6 4.0 %copy-start = (bf16[2,5376]{1,0:T(2,128)(2,1)S(1)}, bf16[2,5376]{1,0:T(2,128)(2,1)}, u32[]{:S(2)}) copy-start(bf16[2,5376]{1,0:T(2,128)(2,1)} %first_ref.1) | copy-start | bytes 64516
  0.6 4.0 %copy-start.1 = (bf16[2,5376]{1,0:T(2,128)(2,1)S(1)}, bf16[2,5376]{1,0:T(2,128)(2,1)}, u32[]{:S(2)}) copy-start(bf16[2,5376]{1,0:T(2,128)(2,1)} %delta_ref.1) | copy-start | bytes 64516
  0.7 9.5 %copy-start.2 = (f32[5376]{0:T(1024)S(1)}, f32[5376]{0:T(1024)}, u32[]{:S(2)}) copy-start(f32[5376]{0:T(1024)} %param.9) | copy-start | bytes 64516
  3.1 1.5 %collective-permute-start = (bf16[16,5376]{1,0:T(8,128)(2,1)S(1)}, bf16[16,5376]{1,0:T(8,128)(2,1)S(1)}, u32[]{:S(2)}, u32[]{:S(2)}) collective-permute-start(bf16[16,5376]{1,0:T(8,128)(2,1)S(1)} %get-tuple-element.17.refs_0_), channel_id=1, source_target_pairs={{0,1},{1,0},{2,3},{3,2},{4,5},{5,4},{6,7},{7,6},{8,9},{9,8},{10,11... | collective-permute-start | bytes 516104 | tf_op jit(solution)/shard_map/ppermute | solution.py:231
  4.7 6.2 %collective-permute-start.2 = (bf16[8,5376]{1,0:T(8,128)(2,1)S(1)}, bf16[8,5376]{1,0:T(8,128)(2,1)S(1)}, u32[]{:S(2)}, u32[]{:S(2)}) collective-permute-start(bf16[8,5376]{1,0:T(8,128)(2,1)S(1)} %get-tuple-element.21), channel_id=1, source_target_pairs={{0,2},{1,3},{2,0},{3,1},{4,6},{5,7},{6,4},{7,5},{8,10},{9,11},{10,... | collective-permute-start | bytes 258056 | tf_op jit(solution)/shard_map/ppermute | solution.py:231
  7.7 6.2 %collective-permute-start.1 = (bf16[4,5376]{1,0:T(4,128)(2,1)S(1)}, bf16[4,5376]{1,0:T(4,128)(2,1)S(1)}, u32[]{:S(2)}, u32[]{:S(2)}) collective-permute-start(bf16[4,5376]{1,0:T(4,128)(2,1)S(1)} %get-tuple-element.19.own_ref), channel_id=1, source_target_pairs={{0,8},{1,9},{2,10},{3,11},{4,12},{5,13},{6,14},{7,15},{8,0},{9,1},... | collective-permute-start | bytes 129032 | tf_op jit(solution)/shard_map/ppermute | solution.py:231
  10.9 6.8 %collective-permute-start.5 = (bf16[8,5376]{1,0:T(8,128)(2,1)S(1)}, bf16[8,5376]{1,0:T(8,128)(2,1)S(1)}, u32[]{:S(2)}, u32[]{:S(2)}) collective-permute-start(bf16[8,5376]{1,0:T(8,128)(2,1)S(1)} %add.23.refs_0_.own_ref), channel_id=1, source_target_pairs={{0,8},{1,9},{2,10},{3,11},{4,12},{5,13},{6,14},{7,15},{8,0},{9,1},... | collective-permute-start | bytes 258056 | tf_op jit(solution)/shard_map/ppermute | solution.py:231
  13.9 4.9 %collective-permute-start.3 = (bf16[8,5376]{1,0:T(8,128)(2,1)S(1)}, bf16[8,5376]{1,0:T(8,128)(2,1)S(1)}, u32[]{:S(2)}, u32[]{:S(2)}) collective-permute-start(bf16[8,5376]{1,0:T(8,128)(2,1)S(1)} %join.1), channel_id=1, source_target_pairs={{0,4},{1,5},{2,6},{3,7},{4,0},{5,1},{6,2},{7,3},{8,12},{9,13},{10,... | collective-permute-start | bytes 258056 | tf_op jit(solution)/shard_map/ppermute | solution.py:231
  17.7 3.2 %collective-permute-start.8 = (bf16[16,5376]{1,0:T(8,128)(2,1)S(1)}, bf16[16,5376]{1,0:T(8,128)(2,1)S(1)}, u32[]{:S(2)}, u32[]{:S(2)}) collective-permute-start(bf16[16,5376]{1,0:T(8,128)(2,1)S(1)} %get-tuple-element.22.refs_0_), channel_id=1, source_target_pairs={{0,1},{1,0},{2,3},{3,2},{4,5},{5,4},{6,7},{7,6},{8,9},{9,8},{10,11... | collective-permute-start | bytes 516104 | tf_op jit(solution)/shard_map/ppermute | solution.py:231
  17.8 5.0 %collective-permute-start.6 = (bf16[8,5376]{1,0:T(8,128)(2,1)S(1)}, bf16[8,5376]{1,0:T(8,128)(2,1)S(1)}, u32[]{:S(2)}, u32[]{:S(2)}) collective-permute-start(bf16[8,5376]{1,0:T(8,128)(2,1)S(1)} %plus.1.own_ref), channel_id=1, source_target_pairs={{0,4},{1,5},{2,6},{3,7},{4,0},{5,1},{6,2},{7,3},{8,12},{9,13},{10,... | collective-permute-start | bytes 258056 | tf_op jit(solution)/shard_map/ppermute | solution.py:231
  19.2 8.9 %collective-permute-start.4 = (bf16[8,5376]{1,0:T(8,128)(2,1)S(1)}, bf16[8,5376]{1,0:T(8,128)(2,1)S(1)}, u32[]{:S(2)}, u32[]{:S(2)}) collective-permute-start(bf16[8,5376]{1,0:T(8,128)(2,1)S(1)} %norm.2.one_ref), channel_id=1, source_target_pairs={{0,2},{1,3},{2,0},{3,1},{4,6},{5,7},{6,4},{7,5},{8,10},{9,11},{10,... | collective-permute-start | bytes 258056 | tf_op jit(solution)/shard_map/ppermute | solution.py:231
  20.9 7.1 %collective-permute-start.9 = (bf16[8,5376]{1,0:T(8,128)(2,1)S(1)}, bf16[8,5376]{1,0:T(8,128)(2,1)S(1)}, u32[]{:S(2)}, u32[]{:S(2)}) collective-permute-start(bf16[8,5376]{1,0:T(8,128)(2,1)S(1)} %slice.81), channel_id=1, source_target_pairs={{0,2},{1,3},{2,0},{3,1},{4,6},{5,7},{6,4},{7,5},{8,10},{9,11},{10,... | collective-permute-start | bytes 258056 | tf_op jit(solution)/shard_map/ppermute | solution.py:231
  23.0 5.1 %collective-permute-start.7 = (bf16[8,5376]{1,0:T(8,128)(2,1)S(1)}, bf16[8,5376]{1,0:T(8,128)(2,1)S(1)}, u32[]{:S(2)}, u32[]{:S(2)}) collective-permute-start(bf16[8,5376]{1,0:T(8,128)(2,1)S(1)} %norm.3.refs_0_.two_ref), channel_id=1, source_target_pairs={{0,2},{1,3},{2,0},{3,1},{4,6},{5,7},{6,4},{7,5},{8,10},{9,11},{10,... | collective-permute-start | bytes 258056 | tf_op jit(solution)/shard_map/ppermute | solution.py:231
  28.2 1.7 %collective-permute-start.10 = (bf16[32,5376]{1,0:T(8,128)(2,1)S(1)}, bf16[32,5376]{1,0:T(8,128)(2,1)S(1)}, u32[]{:S(2)}, u32[]{:S(2)}) collective-permute-start(bf16[32,5376]{1,0:T(8,128)(2,1)S(1)} %chips.1.own_ref), channel_id=1, source_target_pairs={{0,1},{1,0},{2,3},{3,2},{4,5},{5,4},{6,7},{7,6},{8,9},{9,8},{10,11... | collective-permute-start | bytes 1032200 | tf_op jit(solution)/shard_map/ppermute | solution.py:231
  28.3 6.9 %collective-permute-start.13 = (bf16[4,5376]{1,0:T(4,128)(2,1)S(1)}, bf16[4,5376]{1,0:T(4,128)(2,1)S(1)}, u32[]{:S(2)}, u32[]{:S(2)}) collective-permute-start(bf16[4,5376]{1,0:T(4,128)(2,1)S(1)} %slice.83), channel_id=1, source_target_pairs={{0,4},{1,5},{2,6},{3,7},{4,0},{5,1},{6,2},{7,3},{8,12},{9,13},{10,... | collective-permute-start | bytes 129032 | tf_op jit(solution)/shard_map/ppermute | solution.py:231
  33.1 4.5 %collective-permute-start.11 = (f32[2,64]{1,0:T(2,128)S(1)}, f32[2,64]{1,0:T(2,128)S(1)}, u32[]{:S(2)}, u32[]{:S(2)}) collective-permute-start(f32[2,64]{1,0:T(2,128)S(1)} %get-tuple-element.29), channel_id=1, source_target_pairs={{0,8},{1,9},{2,10},{3,11},{4,12},{5,13},{6,14},{7,15},{8,0},{9,1},... | collective-permute-start | bytes 1544 | tf_op jit(solution)/shard_map/ppermute | solution.py:231
  35.2 4.8 %collective-permute-start.14 = (bf16[2,5376]{1,0:T(2,128)(2,1)S(1)}, bf16[2,5376]{1,0:T(2,128)(2,1)S(1)}, u32[]{:S(2)}, u32[]{:S(2)}) collective-permute-start(bf16[2,5376]{1,0:T(2,128)(2,1)S(1)} %slice.85), channel_id=1, source_target_pairs={{0,8},{1,9},{2,10},{3,11},{4,12},{5,13},{6,14},{7,15},{8,0},{9,1},... | collective-permute-start | bytes 64520 | tf_op jit(solution)/shard_map/ppermute | solution.py:231
  37.6 3.6 %collective-permute-start.12 = (f32[2,64]{1,0:T(2,128)S(1)}, f32[2,64]{1,0:T(2,128)S(1)}, u32[]{:S(2)}, u32[]{:S(2)}) collective-permute-start(f32[2,64]{1,0:T(2,128)S(1)} %pad_maximum_fusion.2.own_ref), channel_id=1, source_target_pairs={{0,4},{1,5},{2,6},{3,7},{4,0},{5,1},{6,2},{7,3},{8,12},{9,13},{10,... | collective-permute-start | bytes 1544 | tf_op jit(solution)/shard_map/ppermute | solution.py:231
  41.3 3.6 %collective-permute-start.15 = (f32[2,64]{1,0:T(2,128)S(1)}, f32[2,64]{1,0:T(2,128)S(1)}, u32[]{:S(2)}, u32[]{:S(2)}) collective-permute-start(f32[2,64]{1,0:T(2,128)S(1)} %merge.1), channel_id=1, source_target_pairs={{0,2},{1,3},{2,0},{3,1},{4,6},{5,7},{6,4},{7,5},{8,10},{9,11},{10,... | collective-permute-start | bytes 1544 | tf_op jit(solution)/shard_map/ppermute | solution.py:231
  44.9 1.2 %collective-permute-start.16 = (f32[2,64]{1,0:T(2,128)S(1)}, f32[2,64]{1,0:T(2,128)S(1)}, u32[]{:S(2)}, u32[]{:S(2)}) collective-permute-start(f32[2,64]{1,0:T(2,128)S(1)} %pad_maximum_fusion.3.own_ref), channel_id=1, source_target_pairs={{0,1},{1,0},{2,3},{3,2},{4,5},{5,4},{6,7},{7,6},{8,9},{9,8},{10,11... | collective-permute-start | bytes 1544 | tf_op jit(solution)/shard_map/ppermute | solution.py:231
